TPU v7x, 32 devices: a whole 2x2x4 slice. The times are simulated.
32 devices in a mesh: section: 2 (over x), seq: 16 (over z, y, core).
Axes of the slice: x: 2, y: 2, z: 4, core: 2. Of those that a mesh axis runs over, the one named last changes fastest.
Arguments:
- inputs: bfloat16 [2, 4096, 768], P(None, 'seq'), may hold values from -6 to 6
- cotangent: bfloat16 [2, 4096, 768], P(None, 'seq'), may hold values from -6 to 6
- documents: int32 [2, 4096], replicated, may hold values from 0 to 2, as said below
- w_qkv: float32 [2, 768, 2304], P('section', 'seq'), may hold values from -0.21875 to 0.21875
- w_out: float32 [2, 768, 768], P('section', 'seq'), may hold values from -1.75 to 1.75
- w_up: float32 [2, 768, 3072], P('section', 'seq'), may hold values from -0.21875 to 0.21875
- w_down: float32 [2, 3072, 768], P('section', 'seq'), may hold values from -0.109375 to 0.109375
- norm_gains: float32 [2, 2, 768], P('section', None, 'seq'), may hold values from 0.5 to 1.5
- biases: float32 [2, 6, 768], P('section', None, 'seq'), may hold values from -3 to 3
- up_bias: float32 [2, 3072], P('section', 'seq'), may hold values from -3 to 3
Outputs:
- layer_outputs: bfloat16 [2, 2, 4096, 768], P('section', None, 'seq')
- input_grads: float32 [2, 2, 4096, 768], P('section', None, 'seq')
- grad_qkv: float32 [2, 768, 2304], P('section', 'seq')
- grad_out: float32 [2, 768, 768], P('section', 'seq')
- grad_up: float32 [2, 768, 3072], P('section', 'seq')
- grad_down: float32 [2, 3072, 768], P('section', 'seq')
- grad_gains: float32 [2, 2, 768], P('section', None, 'seq')
- grad_biases: float32 [2, 6, 768], P('section', None, 'seq')
- grad_up_bias: float32 [2, 3072], P('section', 'seq')
Inputs may be any that keep to these rules, and one draw needn't show every extreme that they name: `documents`: in each micro-batch the ids start at 0, never fall and rise by at most one from a tile to the next; a slide is the run of tiles that share an id, and the last id of every micro-batch is the largest.
All inputs are finite; a program needn't handle non-finite values.
Results may differ from a plain program's by a relative error of at most 0.012.
The roundings to bfloat16 on the way count: a program that leaves them out, or rounds other values in their place, can miss the bound.
Values may be sent and summed in bfloat16 or wider, within the bound.
No kernel may reach another device: no remote copies, remote signals or barrier semaphores. Data moves between devices by JAX's collectives and lax.ppermute only.
A program may use at most 512 MiB of HBM per device.

v0:
```python
import jax
import jax.numpy as jnp
import numpy as np
from jax import lax
from jax.sharding import PartitionSpec as P

D = 768
HEADS = 16
HEAD_DIM = 48
SEG0 = 1024
BRANCHES = 5


epsilon = 1e-05
masked_score = -1e30
highest = lax.Precision.HIGHEST


def swapped(value, axis, apart):
    mask = 2**apart
    pairs = [(source, source ^ mask) for source in range(lax.axis_size(axis))]
    return lax.ppermute(value, axis, pairs)


def for_sending(array):
    return jax.tree.map(lambda a: a.astype(jnp.bfloat16) if a.dtype == jnp.float32 else a, array)


def passed_along(array, axis, by):
    peers = lax.axis_size(axis)
    pairs = [(i, i + by) for i in range(peers) if 0 <= i + by < peers]
    return lax.ppermute(array, axis, pairs)


def layer_norm_parts(values, gain_row, shift_row):
    center = values - jnp.mean(values, axis=-1, keepdims=True)
    spread = jnp.mean(center * center, axis=-1, keepdims=True)
    return center * lax.rsqrt(spread + epsilon) * gain_row + shift_row


def exact_gelu(values):
    return jax.nn.gelu(values, approximate=False)


def inner_rows(left, right):
    return jnp.einsum("ta,tb->ab", left, right, preferred_element_type=jnp.float32)


def geometry(tokens_dev, devices):
    groups = [
        min(SEG0 * 2**level_id, tokens_dev * devices) // tokens_dev for level_id in range(BRANCHES)
    ]
    return (groups, max(groups).bit_length() - 1)


def first_level(groups, step_id):
    return min((level_id for level_id in range(BRANCHES) if groups[level_id] > 2**step_id))


def pick_grid(level_id, dtype):
    dilation = 2**level_id
    return (jnp.arange(dilation)[:, None] == (jnp.arange(HEADS) % dilation)[None, :]).astype(dtype)


def select_rows(tensor, level_id):
    dilation = 2**level_id
    shaped = tensor.reshape((tensor.shape[0] // dilation, dilation) + tensor.shape[1:])
    if tensor.dtype == jnp.bfloat16:
        chosen = jnp.einsum(
            "jrh...,rh->jh...",
            shaped,
            pick_grid(level_id, jnp.bfloat16),
            preferred_element_type=jnp.float32,
        )
        return chosen.astype(jnp.bfloat16)
    return jnp.einsum(
        "jrh...,rh->jh...", shaped, pick_grid(level_id, jnp.float32), precision=highest
    )


def spread_rows(tensor, level_id):
    dilation = 2**level_id
    spread = jnp.einsum(
        "jh...,rh->jrh...", tensor, pick_grid(level_id, jnp.float32), precision=highest
    )
    return spread.reshape((tensor.shape[0] * dilation,) + tensor.shape[1:])


def spread_sums(tensor, level_id):
    dilation = 2**level_id
    grid = pick_grid(level_id, jnp.float32)
    spread = jnp.where(grid[None] > 0, tensor[:, None, :], masked_score)
    return spread.reshape(tensor.shape[0] * dilation, HEADS)


def doc_tables(documents_now, level_id, group, tokens_dev, seq_place):
    dilation = 2**level_id
    offsets = np.arange(HEADS) % dilation
    own_docs = lax.dynamic_slice_in_dim(documents_now, seq_place * tokens_dev, tokens_dev)
    own_docs = own_docs.reshape(tokens_dev // dilation, dilation)[:, offsets]
    seg_start = seq_place // group * group * tokens_dev
    seg_docs = lax.dynamic_slice_in_dim(documents_now, seg_start, group * tokens_dev)
    seg_docs = seg_docs.reshape(group * tokens_dev // dilation, dilation)[:, offsets]
    return (own_docs, seg_docs)


def head_bits(level_id):
    return jnp.arange(HEADS) >> level_id & 1


def halve(buffer, level_id):
    pairs = buffer.reshape(buffer.shape[0], buffer.shape[1] // 2, 2, HEADS, HEAD_DIM)
    chosen = head_bits(level_id)[None, None, :, None] == 1
    return jnp.where(chosen, pairs[:, :, 1], pairs[:, :, 0])


def widen(buffer, level_id):
    chosen = head_bits(level_id)[None, None, :, None] == 1
    empty = jnp.zeros_like(buffer)
    upper_part = jnp.where(chosen, buffer, empty)
    lower_part = jnp.where(chosen, empty, buffer)
    stacked = jnp.stack([lower_part, upper_part], axis=2)
    return stacked.reshape(buffer.shape[0], buffer.shape[1] * 2, HEADS, HEAD_DIM)


def thin_to(buffer, low_level, high_level):
    for level_id in range(low_level, high_level):
        buffer = halve(buffer, level_id)
    return buffer


def widen_to(buffer, low_level, high_level):
    for level_id in reversed(range(low_level, high_level)):
        buffer = widen(buffer, level_id)
    return buffer


def gather_keys(own_rows, groups, step_count, seq_place):
    results = [None] * BRANCHES
    current = own_rows
    level_now = 0
    for level_id in range(BRANCHES):
        pass
    for step_id in range(step_count):
        target = first_level(groups, step_id)
        current = thin_to(current, level_now, target)
        level_now = target
        row_count = current.shape[1]
        flat_rows = current.reshape(2, row_count, HEADS * HEAD_DIM)
        incoming = swapped(flat_rows, "seq", step_id).reshape(current.shape)
        upper_half = seq_place >> step_id & 1 == 1
        current = jnp.where(
            upper_half,
            jnp.concatenate([incoming, current], axis=1),
            jnp.concatenate([current, incoming], axis=1),
        )
        for level_id in range(BRANCHES):
            if groups[level_id] == 2 ** (step_id + 1):
                results[level_id] = thin_to(current, level_now, level_id)
    return results


def scatter_keys(key_grads, groups, step_count, seq_place):
    carried = None
    for step_id in reversed(range(step_count)):
        level_now = first_level(groups, step_id)
        total_grad = None
        if carried is not None:
            total_grad = widen_to(carried, level_now, first_level(groups, step_id + 1))
        for level_id in range(BRANCHES):
            if groups[level_id] == 2 ** (step_id + 1):
                branch_term = widen_to(key_grads[level_id], level_now, level_id)
                total_grad = branch_term if total_grad is None else total_grad + branch_term
        half_rows = total_grad.shape[1] // 2
        upper_half = seq_place >> step_id & 1 == 1
        own_half = jnp.where(upper_half, total_grad[:, half_rows:], total_grad[:, :half_rows])
        theirs = jnp.where(upper_half, total_grad[:, :half_rows], total_grad[:, half_rows:])
        flat_rows = theirs.reshape(2, half_rows, HEADS * HEAD_DIM)
        incoming = (
            swapped(for_sending(flat_rows), "seq", step_id)
            .astype(flat_rows.dtype)
            .reshape(own_half.shape)
        )
        carried = own_half + incoming
    own_grad = widen_to(carried, 0, first_level(groups, 0))
    for level_id in range(BRANCHES):
        pass
    return own_grad


def head_blocks(level_id):
    block_size = min(HEADS, 4 * 2**level_id)
    return (HEADS // block_size, block_size)


def to_blocks(tensor, block_count, block_size):
    moved = jnp.moveaxis(tensor, 1, 0)
    return moved.reshape((block_count, block_size) + moved.shape[1:])


def from_blocks(tensor):
    joined = tensor.reshape((tensor.shape[0] * tensor.shape[1],) + tensor.shape[2:])
    return jnp.moveaxis(joined, 0, 1)


def score_block(query_block, key_block, query_doc, key_doc):
    scores = jnp.einsum(
        "hqd,hkd->hqk", query_block, key_block, preferred_element_type=jnp.float32
    ) * HEAD_DIM ** (-0.5)
    return jnp.where(query_doc[:, :, None] == key_doc[:, None, :], scores, masked_score)


def forward_block(pieces):
    query_block, key_block, value_block, query_doc, key_doc = pieces
    scores = score_block(query_block, key_block, query_doc, key_doc)
    row_max = jnp.max(scores, axis=-1, keepdims=True)
    weights = jnp.exp(scores - row_max)
    row_total = jnp.sum(weights, axis=-1, keepdims=True)
    prob_rows = (weights / row_total).astype(jnp.bfloat16)
    result = jnp.einsum("hqk,hkd->hqd", prob_rows, value_block, preferred_element_type=jnp.float32)
    return (result, (row_max + jnp.log(row_total))[:, :, 0])


def backward_block(pieces):
    query_block, key_block, value_block, query_doc, key_doc, summary, out_grad, summary_grad = (
        pieces
    )
    scores = score_block(query_block, key_block, query_doc, key_doc)
    prob_rows = jnp.exp(scores - summary[:, :, None])
    prob_grad = jnp.einsum(
        "hqd,hkd->hqk", out_grad, value_block, preferred_element_type=jnp.float32
    )
    score_grad = prob_rows * (
        prob_grad
        - jnp.sum(prob_rows * prob_grad, axis=-1, keepdims=True)
        + summary_grad[:, :, None]
    )
    score_grad = score_grad.astype(jnp.bfloat16)
    score_scale = HEAD_DIM ** (-0.5)
    query_grad = (
        jnp.einsum("hqk,hkd->hqd", score_grad, key_block, preferred_element_type=jnp.float32)
        * score_scale
    )
    key_grad = (
        jnp.einsum("hqk,hqd->hkd", score_grad, query_block, preferred_element_type=jnp.float32)
        * score_scale
    )
    value_grad = jnp.einsum(
        "hqk,hqd->hkd", prob_rows.astype(jnp.bfloat16), out_grad, preferred_element_type=jnp.float32
    )
    return (query_grad, key_grad, value_grad)


def branch_forward(query_sel, key_value, query_docs, key_docs, level_id):
    block_count, block_size = head_blocks(level_id)
    pieces = (
        to_blocks(query_sel, block_count, block_size),
        to_blocks(key_value[0], block_count, block_size),
        to_blocks(key_value[1], block_count, block_size),
        to_blocks(query_docs, block_count, block_size),
        to_blocks(key_docs, block_count, block_size),
    )
    results, summaries = lax.map(forward_block, pieces)
    return (from_blocks(results), from_blocks(summaries))


def branch_backward(
    query_sel, key_value, query_docs, key_docs, summary, out_grad, summary_grad, level_id
):
    block_count, block_size = head_blocks(level_id)
    pieces = (
        to_blocks(query_sel, block_count, block_size),
        to_blocks(key_value[0], block_count, block_size),
        to_blocks(key_value[1], block_count, block_size),
        to_blocks(query_docs, block_count, block_size),
        to_blocks(key_docs, block_count, block_size),
        to_blocks(summary, block_count, block_size),
        to_blocks(out_grad, block_count, block_size),
        to_blocks(summary_grad, block_count, block_size),
    )
    query_grad, key_grad, value_grad = lax.map(backward_block, pieces)
    return (from_blocks(query_grad), jnp.stack([from_blocks(key_grad), from_blocks(value_grad)]))


def layer_forward(hidden, params, documents_now, groups, step_count, seq_place):
    w_qkv, w_out, w_up, w_down, gains, biases, up_bias = params
    gains = gains.astype(jnp.float32)
    biases = biases.astype(jnp.float32)
    tokens_dev = hidden.shape[0]
    normed = layer_norm_parts(hidden, gains[0], biases[0]).astype(jnp.bfloat16)
    mixed_rows = jnp.dot(normed, w_qkv, preferred_element_type=jnp.float32)
    queries = (mixed_rows[:, :D] + biases[1]).astype(jnp.bfloat16)
    key_part = mixed_rows[:, D : 2 * D].astype(jnp.bfloat16)
    values = (mixed_rows[:, 2 * D :] + biases[2]).astype(jnp.bfloat16)
    own_rows = jnp.stack([key_part, values]).reshape(2, tokens_dev, HEADS, HEAD_DIM)
    gathered = gather_keys(own_rows, groups, step_count, seq_place)
    query_heads = queries.reshape(tokens_dev, HEADS, HEAD_DIM)
    picked, branch_outs, branch_sums = ([], [], [])
    for level_id in range(BRANCHES):
        query_sel = select_rows(query_heads, level_id)
        query_docs, key_docs = doc_tables(
            documents_now, level_id, groups[level_id], tokens_dev, seq_place
        )
        result, summary = branch_forward(
            query_sel, gathered[level_id], query_docs, key_docs, level_id
        )
        picked.append(query_sel)
        branch_outs.append(result)
        branch_sums.append(summary)
    full_sums = jnp.stack(
        [spread_sums(branch_sums[level_id], level_id) for level_id in range(BRANCHES)]
    )
    row_max = jnp.max(full_sums, axis=0)
    shares = jnp.exp(full_sums - row_max)
    shares = shares / jnp.sum(shares, axis=0)
    merged = sum(
        (
            shares[level_id][:, :, None] * spread_rows(branch_outs[level_id], level_id)
            for level_id in range(BRANCHES)
        )
    )
    attended = merged.reshape(tokens_dev, D).astype(jnp.bfloat16)
    middle = hidden + jnp.dot(attended, w_out, preferred_element_type=jnp.float32) + biases[3]
    normed_two = layer_norm_parts(middle, gains[1], biases[4]).astype(jnp.bfloat16)
    upward = jnp.dot(normed_two, w_up, preferred_element_type=jnp.float32) + up_bias.astype(
        jnp.float32
    )
    activated = exact_gelu(upward).astype(jnp.bfloat16)
    result = middle + jnp.dot(activated, w_down, preferred_element_type=jnp.float32) + biases[5]
    kept_values = (
        hidden,
        normed,
        picked,
        gathered,
        branch_sums,
        branch_outs,
        shares,
        merged,
        attended,
        middle,
        normed_two,
        upward,
        activated,
    )
    return (result, kept_values)


def layer_backward(incoming, kept_values, params, documents_now, groups, step_count, seq_place):
    w_qkv, w_out, w_up, w_down, gains, biases, up_bias = params
    gains = gains.astype(jnp.float32)
    biases = biases.astype(jnp.float32)
    (
        hidden,
        normed,
        picked,
        gathered,
        branch_sums,
        branch_outs,
        shares,
        merged,
        attended,
        middle,
        normed_two,
        upward,
        activated,
    ) = kept_values
    tokens_dev = hidden.shape[0]
    down_grad = incoming.astype(jnp.bfloat16)
    grad_down = inner_rows(activated, down_grad)
    grad_bias_down = jnp.sum(down_grad.astype(jnp.float32), axis=0)
    act_grad = jnp.einsum("tb,ab->ta", down_grad, w_down, preferred_element_type=jnp.float32)
    gelu_pulled = jax.vjp(exact_gelu, upward)
    up_grad = gelu_pulled[1](act_grad)[0].astype(jnp.bfloat16)
    grad_up = inner_rows(normed_two, up_grad)
    grad_up_bias = jnp.sum(up_grad.astype(jnp.float32), axis=0)
    norm_two_grad = jnp.einsum("tb,ab->ta", up_grad, w_up, preferred_element_type=jnp.float32)
    norm_pulled = jax.vjp(layer_norm_parts, middle, gains[1], biases[4])
    middle_part, grad_gain_two, grad_shift_two = norm_pulled[1](norm_two_grad)
    middle_grad = incoming + middle_part
    branch_grad = middle_grad.astype(jnp.bfloat16)
    grad_out = inner_rows(attended, branch_grad)
    grad_bias_out = jnp.sum(branch_grad.astype(jnp.float32), axis=0)
    merged_grad = jnp.einsum("tb,ab->ta", branch_grad, w_out, preferred_element_type=jnp.float32)
    merged_grad = merged_grad.reshape(tokens_dev, HEADS, HEAD_DIM)
    query_grad = jnp.zeros((tokens_dev, HEADS, HEAD_DIM), jnp.float32)
    key_grads = []
    for level_id in range(BRANCHES):
        share_sel = select_rows(shares[level_id], level_id)
        merged_sel = select_rows(merged, level_id)
        grad_sel = select_rows(merged_grad, level_id)
        out_grad = (share_sel[:, :, None] * grad_sel).astype(jnp.bfloat16)
        summary_grad = share_sel * (
            jnp.sum(grad_sel * branch_outs[level_id], axis=-1)
            - jnp.sum(grad_sel * merged_sel, axis=-1)
        )
        query_docs, key_docs = doc_tables(
            documents_now, level_id, groups[level_id], tokens_dev, seq_place
        )
        query_part, key_value_grad = branch_backward(
            picked[level_id],
            gathered[level_id],
            query_docs,
            key_docs,
            branch_sums[level_id],
            out_grad,
            summary_grad,
            level_id,
        )
        query_grad = query_grad + spread_rows(query_part, level_id)
        key_grads.append(key_value_grad)
    own_grad = scatter_keys(key_grads, groups, step_count, seq_place)
    mixed_grad = jnp.concatenate(
        [
            query_grad.reshape(tokens_dev, D),
            own_grad[0].reshape(tokens_dev, D),
            own_grad[1].reshape(tokens_dev, D),
        ],
        axis=1,
    ).astype(jnp.bfloat16)
    grad_qkv = inner_rows(normed, mixed_grad)
    grad_bias_query = jnp.sum(mixed_grad[:, :D].astype(jnp.float32), axis=0)
    grad_bias_value = jnp.sum(mixed_grad[:, 2 * D :].astype(jnp.float32), axis=0)
    normed_grad = jnp.einsum("tb,ab->ta", mixed_grad, w_qkv, preferred_element_type=jnp.float32)
    norm_pulled = jax.vjp(layer_norm_parts, hidden, gains[0], biases[0])
    hidden_part, grad_gain_one, grad_shift_one = norm_pulled[1](normed_grad)
    start_grad = middle_grad + hidden_part
    gradients = (
        grad_qkv,
        grad_out,
        grad_up,
        grad_down,
        jnp.stack([grad_gain_one, grad_gain_two]),
        jnp.stack(
            [
                grad_shift_one,
                grad_bias_query,
                grad_bias_value,
                grad_bias_out,
                grad_shift_two,
                grad_bias_down,
            ]
        ),
        grad_up_bias,
    )
    return (start_grad, gradients)


def body(inputs, cotangent, documents, w_qkv, w_out, w_up, w_down, norm_gains, biases, up_bias):
    section_id = lax.axis_index("section")
    seq_place = lax.axis_index("seq")
    devices = lax.axis_size("seq")
    micro = inputs.shape[0]
    tokens_dev = inputs.shape[1]
    groups, step_count = geometry(tokens_dev, devices)
    params = (
        lax.all_gather(w_qkv[0].astype(jnp.bfloat16), "seq", axis=0, tiled=True),
        lax.all_gather(w_out[0].astype(jnp.bfloat16), "seq", axis=0, tiled=True),
        lax.all_gather(w_up[0].astype(jnp.bfloat16), "seq", axis=0, tiled=True),
        lax.all_gather(w_down[0].astype(jnp.bfloat16), "seq", axis=0, tiled=True),
        lax.all_gather(norm_gains[0].astype(jnp.bfloat16), "seq", axis=1, tiled=True),
        lax.all_gather(biases[0].astype(jnp.bfloat16), "seq", axis=1, tiled=True),
        lax.all_gather(up_bias[0].astype(jnp.bfloat16), "seq", axis=0, tiled=True),
    )
    empty_rows = jnp.zeros((tokens_dev, D), jnp.bfloat16)
    received = empty_rows
    saved = []
    produced = []
    for tick_id in range(micro + 1):
        batch_index = jnp.clip(tick_id - section_id, 0, micro - 1)
        documents_now = lax.dynamic_index_in_dim(documents, batch_index, 0, keepdims=False)
        fresh_rows = inputs[tick_id] if tick_id < micro else empty_rows
        start_rows = jnp.where(section_id == 0, fresh_rows, received).astype(jnp.float32)
        result, kept_values = layer_forward(
            start_rows, params, documents_now, groups, step_count, seq_place
        )
        sent_rows = result.astype(jnp.bfloat16)
        produced.append(sent_rows)
        saved.append((kept_values, documents_now))
        if tick_id < micro:
            received = passed_along(sent_rows, "section", 1)
    back_received = empty_rows
    start_grads = []
    sent_grads = []
    totals = None
    shards = None
    for tick_id in range(micro + 1):
        earlier_save = saved[max(tick_id - 1, 0)]
        later_save = saved[min(tick_id + 1, micro)]
        kept_values, documents_now = jax.tree.map(
            lambda earlier, latter: jnp.where(section_id == 0, earlier, latter),
            earlier_save,
            later_save,
        )
        fresh_rows = cotangent[tick_id] if tick_id < micro else empty_rows
        incoming = jnp.where(section_id == 1, fresh_rows, back_received).astype(jnp.float32)
        start_grad, gradients = layer_backward(
            incoming, kept_values, params, documents_now, groups, step_count, seq_place
        )
        sent_rows = start_grad.astype(jnp.bfloat16)
        start_grads.append(start_grad)
        sent_grads.append(sent_rows.astype(jnp.float32))
        if tick_id < micro:
            back_received = passed_along(sent_rows, "section", -1)
        totals = (
            list(gradients)
            if totals is None
            else [earlier + latter for earlier, latter in zip(totals, gradients)]
        )
    shards = (
        lax.psum_scatter(totals[0], "seq", scatter_dimension=0, tiled=True),
        lax.psum_scatter(totals[1], "seq", scatter_dimension=0, tiled=True),
        lax.psum_scatter(totals[2], "seq", scatter_dimension=0, tiled=True),
        lax.psum_scatter(totals[3], "seq", scatter_dimension=0, tiled=True),
        lax.psum_scatter(totals[4], "seq", scatter_dimension=1, tiled=True),
        lax.psum_scatter(totals[5], "seq", scatter_dimension=1, tiled=True),
        lax.psum_scatter(totals[6], "seq", scatter_dimension=0, tiled=True),
    )
    layer_outputs = jnp.stack(
        [
            jnp.where(section_id == 0, produced[batch_id], produced[batch_id + 1])
            for batch_id in range(micro)
        ]
    )[None]
    input_grads = jnp.stack(
        [
            jnp.where(section_id == 0, start_grads[batch_id + 1], sent_grads[batch_id])
            for batch_id in range(micro)
        ]
    )[None]
    return (
        layer_outputs,
        input_grads,
        shards[0][None],
        shards[1][None],
        shards[2][None],
        shards[3][None],
        shards[4][None],
        shards[5][None],
        shards[6][None],
    )


def solution(mesh):
    return jax.shard_map(
        body,
        mesh=mesh,
        in_specs=(
            P(None, "seq", None),
            P(None, "seq", None),
            P(),
            P("section", "seq", None),
            P("section", "seq", None),
            P("section", "seq", None),
            P("section", "seq", None),
            P("section", None, "seq"),
            P("section", None, "seq"),
            P("section", "seq"),
        ),
        out_specs=(
            P("section", None, "seq", None),
            P("section", None, "seq", None),
            P("section", "seq", None),
            P("section", "seq", None),
            P("section", "seq", None),
            P("section", "seq", None),
            P("section", None, "seq"),
            P("section", None, "seq"),
            P("section", "seq"),
        ),
        check_vma=False,
    )
```

profile of v0, /device:TPU:0, one launch (start us, length us, event | category | flops | bytes accessed | tf_op | source)
XLA Modules:
  0.0 3567.2 jit_solution(15858512148944375375)
XLA Ops:
  15.2 24.8 all-gather
  45.2 19.5 all-gather.1
  65.1 13.3 slice_reduce_fusion
  109.2 47.8 %all-reduce = bf16[3072]{0:T(1024)(128)(2,1)S(1)} all-reduce(bf16[3072]{0:T(1024)(128)(2,1)S(1)} %dynamic-update-slice), channel_id=7, replica_groups=mesh['section'=2,'seq'=16] {'seq'}, use_global_device_ids=true, to_apply=%add | all-reduce | flops 3072 | bytes 12288
  216.1 24.4 while.24
  282.4 11.8 while.25
  304.2 45.6 %collective-permute-done.3 = bf16[2,512,768]{1,2,0:T(8,128)(2,1)} collective-permute-done((bf16[2,512,768]{1,2,0:T(8,128)(2,1)}, bf16[2,512,768]{1,2,0:T(8,128)(2,1)}, u32[]{:S(2)}, u32[]{:S(2)}) %collective-permute-start.3) | collective-permute-done | bytes 1572896 | tf_op jit(solution)/shard_map/ppermute | solution.py:22
  440.8 11.2 fusion.488
  592.6 10.6 copy.1994
  624.3 24.4 while.26
  695.3 11.3 while.27
  720.3 43.8 %collective-permute-done.8 = bf16[2,512,768]{1,2,0:T(8,128)(2,1)} collective-permute-done((bf16[2,512,768]{1,2,0:T(8,128)(2,1)}, bf16[2,512,768]{1,2,0:T(8,128)(2,1)}, u32[]{:S(2)}, u32[]{:S(2)}) %collective-permute-start.8) | collective-permute-done | bytes 1572896 | tf_op jit(solution)/shard_map/ppermute | solution.py:22
  869.1 11.3 convert_reduce_fusion.2
  937.0 23.1 collective-permute-done.11
  969.4 10.6 copy.2039
  1004.3 24.6 while.28
  1080.3 11.3 while.29
  1110.9 37.2 %collective-permute-done.13 = bf16[2,512,768]{1,2,0:T(8,128)(2,1)} collective-permute-done((bf16[2,512,768]{1,2,0:T(8,128)(2,1)}, bf16[2,512,768]{1,2,0:T(8,128)(2,1)}, u32[]{:S(2)}, u32[]{:S(2)}) %collective-permute-start.13) | collective-permute-done | bytes 1572896 | tf_op jit(solution)/shard_map/ppermute | solution.py:22
  1263.8 15.3 multiply_reduce_fusion.9
  1322.9 10.0 broadcast_select_fusion.27
  1352.8 10.6 broadcast_select_fusion.30
  1427.2 125.7 %while.30 = (s32[]{:T(128)}, f32[4,4,256,48]{2,3,1,0:T(8,128)}, f32[4,4,1024,48]{2,3,1,0:T(8,128)}, f32[4,4,1024,48]{2,3,1,0:T(8,128)}, s32[4,4,256]{2,1,0:T(4,1...) while((s32[]{:T(128)}, f32[4,4,256,48]{2,3,1,0:T(8,128)}, ...), condition=%wide.region_65.66_spmd, body=%wide.region_63.65_spmd.sunk | while | flops 519294976 | bytes 49575048 | solution.py:281
  1556.6 16.3 multiply_reduce_fusion.11
  1581.8 57.0 %while.31 = (s32[]{:T(128)}, f32[2,8,128,48]{2,3,1,0:T(8,128)S(1)}, f32[2,8,1024,48]{2,3,1,0:T(8,128)}, f32[2,8,1024,48]{2,3,1,0:T(8,128)}, s32[2,8,128]{2,1,0:T...) while((s32[]{:T(128)}, f32[2,8,128,48]{2,3,1,0:T(8,128)S(1)}, ...), condition=%wide.region_70.71_spmd, body=%wide.region_68.70_spmd.sunk | while | flops 519491584 | bytes 52376712 | solution.py:281
  1666.7 15.3 copy.2156
  1682.0 12.5 copy.2157
  1700.1 15.3 copy.2161
  1715.4 12.1 copy.2162
  1751.6 58.6 %collective-permute-done.14 = bf16[2,512,768]{1,2,0:T(8,128)(2,1)} collective-permute-done((bf16[2,512,768]{1,2,0:T(8,128)(2,1)}, bf16[2,512,768]{1,2,0:T(8,128)(2,1)}, u32[]{:S(2)}, u32[]{:S(2)}) %collective-permute-start.14) | collective-permute-done | bytes 1572896 | tf_op jit(solution)/shard_map/ppermute | solution.py:22
  1816.5 15.5 copy.2163
  1832.0 12.4 copy.2164
  1860.0 26.5 collective-permute-done.15
  1891.2 15.5 copy.2165
  1906.7 12.5 copy.2166
  1933.9 26.5 collective-permute-done.16
  1998.4 18.7 convert_reduce_fusion.1
  2088.5 15.3 copy.2218
  2103.8 12.3 copy.2219
  2121.6 15.3 copy.2223
  2136.9 12.6 copy.2224
  2177.2 57.9 %while.33 = (s32[]{:T(128)}, f32[2,8,128,48]{2,3,1,0:T(8,128)}, f32[2,8,1024,48]{2,3,1,0:T(8,128)}, f32[2,8,1024,48]{2,3,1,0:T(8,128)}, s32[2,8,128]{2,1,0:T(8,1...) while((s32[]{:T(128)}, f32[2,8,128,48]{2,3,1,0:T(8,128)}, ...), condition=%wide.region_97.98_spmd, body=%wide.region_95.97_spmd.sunk | while | flops 519491584 | bytes 52376712 | solution.py:281
  2249.7 15.5 copy.2225
  2265.2 12.3 copy.2226
  2289.9 121.5 %while.32 = (s32[]{:T(128)}, f32[4,4,256,48]{2,3,1,0:T(8,128)}, f32[4,4,1024,48]{2,3,1,0:T(8,128)S(1)}, f32[4,4,1024,48]{2,3,1,0:T(8,128)}, s32[4,4,256]{2,1,0:T...) while((s32[]{:T(128)}, f32[4,4,256,48]{2,3,1,0:T(8,128)}, ...), condition=%wide.region_92.93_spmd, body=%wide.region_90.92_spmd.sunk | while | flops 519294976 | bytes 49575048 | solution.py:281
  2419.4 15.5 copy.2227
  2434.9 12.1 copy.2228
  2476.2 16.8 collective-permute-done.21
  2538.9 11.4 convert_reduce_fusion
  2620.7 15.3 copy.2252
  2636.0 12.3 copy.2253
  2653.8 15.3 copy.2257
  2669.1 12.6 copy.2258
  2708.0 56.5 %while.35 = (s32[]{:T(128)}, f32[2,8,128,48]{2,3,1,0:T(8,128)S(1)}, f32[2,8,1024,48]{2,3,1,0:T(8,128)}, f32[2,8,1024,48]{2,3,1,0:T(8,128)}, s32[2,8,128]{2,1,0:T...) while((s32[]{:T(128)}, f32[2,8,128,48]{2,3,1,0:T(8,128)S(1)}, ...), condition=%wide.region_124.125_spmd, body=%wide.region_122.124_spmd.sunk | while | flops 519491584 | bytes 52376712 | solution.py:281
  2781.1 15.5 copy.2259
  2796.6 12.3 copy.2260
  2821.0 121.5 %while.34 = (s32[]{:T(128)}, f32[4,4,256,48]{2,3,1,0:T(8,128)}, f32[4,4,1024,48]{2,3,1,0:T(8,128)S(1)}, f32[4,4,1024,48]{2,3,1,0:T(8,128)}, s32[4,4,256]{2,1,0:T...) while((s32[]{:T(128)}, f32[4,4,256,48]{2,3,1,0:T(8,128)}, ...), condition=%wide.region_119.120_spmd, body=%wide.region_117.119_spmd.sunk | while | flops 519294976 | bytes 49575048 | solution.py:281
  2950.6 15.5 copy.2261
  2966.1 12.1 copy.2262
  3008.4 12.7 collective-permute-done.26
  3104.2 59.5 %all-reduce.1 = f32[3072]{0:T(1024)S(1)} all-reduce(f32[3072]{0:T(1024)S(1)} %add_add_fusion.12), channel_id=15, replica_groups=mesh['section'=2,'seq'=16] {'seq'}, use_global_device_ids=true, to_apply=%region_171.172.clone | all-reduce | flops 3072 | bytes 24576
  3169.5 64.4 %reduce-scatter.13.cloned.1.call-done = f32[48,768]{1,0:T(8,128)} async-done(((f32[768,768]{1,0:T(8,128)}), f32[48,768]{1,0:T(8,128)}) %reduce-scatter.13.cloned.1.call-update) | async-done | bytes 147472 | tf_op jit(solution)/shard_map/reduce_scatter | solution.py:511
  3234.0 115.6 %reduce-scatter.17.cloned.1.call-done = f32[192,768]{1,0:T(8,128)} async-done(((f32[3072,768]{1,0:T(8,128)}), f32[192,768]{1,0:T(8,128)}) %reduce-scatter.17.cloned.1.call-update) | async-done | bytes 589840 | tf_op jit(solution)/shard_map/reduce_scatter | solution.py:513
  3349.6 115.8 %reduce-scatter.15.cloned.1.call-done = f32[48,3072]{1,0:T(8,128)} async-done(((f32[768,3072]{1,0:T(8,128)}), f32[48,3072]{1,0:T(8,128)}) %reduce-scatter.15.cloned.1.call-update) | async-done | bytes 589840 | tf_op jit(solution)/shard_map/reduce_scatter | solution.py:512
  3465.4 94.8 %reduce-scatter.11.cloned.1.call-done = f32[48,2304]{1,0:T(8,128)} async-done(((f32[768,2304]{1,0:T(8,128)}), f32[48,2304]{1,0:T(8,128)}) %reduce-scatter.11.cloned.1.call-update) | async-done | bytes 442384 | tf_op jit(solution)/shard_map/reduce_scatter | solution.py:510
  (2999 shorter events, 2233.2 us)
Async XLA Ops:
  7.2 75.7 %all-gather.12.cloned.1.call-start = ((), (), s32[]{:S(2)}) async-start(), calls=%async_computation.10 | async-start | bytes 3760128 | tf_op jit(solution)/shard_map/all_gather | solution.py:456
  9.1 428.6 %all-gather.14.cloned.1.call-start = ((), (), s32[]{:S(2)}) async-start(), calls=%async_computation.11 | async-start | bytes 1253376 | tf_op jit(solution)/shard_map/all_gather | solution.py:457
  10.7 430.1 %all-gather.16.cloned.1.call-start = ((), (), s32[]{:S(2)}) async-start(), calls=%async_computation.12 | async-start | bytes 5013504 | tf_op jit(solution)/shard_map/all_gather | solution.py:458
  12.6 439.5 %all-gather.18.cloned.1.call-start = ((), (), s32[]{:S(2)}) async-start(), calls=%async_computation.13 | async-start | bytes 5013504 | tf_op jit(solution)/shard_map/all_gather | solution.py:459
  14.5 3152.3 %reduce-scatter.19.cloned.1.call-start = ((), (), s32[]{:S(2)}) async-start(), calls=%async_computation.14 | async-start | bytes 417792
  14.5 227.2 %copy-start.682 = (pred[16]{0:T(512)(128)(4,1)}, pred[16]{0:T(512)(128)(4,1)S(1)}, u32[]{:S(2)}) copy-start(pred[16]{0:T(512)(128)(4,1)S(1)} %and_compare_fusion.3) | copy-start | bytes 52
  14.5 289.4 %copy-start.688 = (pred[16]{0:T(512)(128)(4,1)}, pred[16]{0:T(512)(128)(4,1)S(1)}, u32[]{:S(2)}) copy-start(pred[16]{0:T(512)(128)(4,1)S(1)} %and_compare_fusion.2) | copy-start | bytes 52
  14.6 63.8 %copy-start.476 = (s32[2,4096]{1,0:T(2,128)S(1)}, s32[2,4096]{1,0:T(2,128)}, u32[]{:S(2)}) copy-start(s32[2,4096]{1,0:T(2,128)} %param.126) | copy-start | bytes 98308
  14.8 64.3 %copy-start.813 = (s32[16]{0:T(128)S(1)}, s32[16]{0:T(128)}, u32[]{:S(2)}) copy-start(s32[16]{0:T(128)} %constant.1492) | copy-start | bytes 196
  14.8 64.9 %copy-start.812 = (s32[16]{0:T(128)S(1)}, s32[16]{0:T(128)}, u32[]{:S(2)}) copy-start(s32[16]{0:T(128)} %constant.1490) | copy-start | bytes 196
  14.8 64.9 %copy-start.818 = (f32[1,192]{1,0:T(1,128)S(1)}, f32[1,192]{1,0:T(1,128)}, u32[]{:S(2)}) copy-start(f32[1,192]{1,0:T(1,128)} %param.133) | copy-start | bytes 2308
  14.8 68.0 %copy-start.811 = (s32[16]{0:T(128)S(1)}, s32[16]{0:T(128)}, u32[]{:S(2)}) copy-start(s32[16]{0:T(128)} %constant.1494) | copy-start | bytes 196
  14.8 71.3 %copy-start.625 = (f32[256]{0:T(256)}, f32[256]{0:T(256)S(1)}, u32[]{:S(2)}) copy-start(f32[256]{0:T(256)S(1)} %broadcast_multiply_fusion.23) | copy-start | bytes 3076
  15.1 71.0 %copy-start.676 = (f32[256]{0:T(256)}, f32[256]{0:T(256)S(1)}, u32[]{:S(2)}) copy-start(f32[256]{0:T(256)S(1)} %add_rsqrt_fusion.5) | copy-start | bytes 3076
  86.4 4.7 collective-permute-start
  93.0 85.9 %collective-permute-start.1 = (bf16[2,512,768]{2,1,0:T(8,128)(2,1)}, bf16[2,512,768]{2,1,0:T(8,128)(2,1)}, u32[]{:S(2)}, u32[]{:S(2)}) collective-permute-start(bf16[2,512,768]{2,1,0:T(8,128)(2,1)} %maximum_select_fusion.9), channel_id=1, source_target_pairs={{0,2},{1,3},{2,0},{3,1},{4,6},{5,7},{6,4},{7,5},{8,10},{9,11},{10,... | collective-permute-start | bytes 4718600 | tf_op jit(solution)/shard_map/ppermute | solution.py:22
  96.3 116.9 %copy-start.708 = (pred[768]{0:T(1024)(128)(4,1)}, pred[768]{0:T(1024)(128)(4,1)S(1)}, u32[]{:S(2)}) copy-start(pred[768]{0:T(1024)(128)(4,1)S(1)} %broadcast_in_dim.1491) | copy-start | bytes 2308
  96.5 182.4 %copy-start.705 = (pred[768]{0:T(1024)(128)(4,1)}, pred[768]{0:T(1024)(128)(4,1)S(1)}, u32[]{:S(2)}) copy-start(pred[768]{0:T(1024)(128)(4,1)S(1)} %broadcast_in_dim.1500) | copy-start | bytes 2308
  99.7 70.6 %copy-start.380 = (pred[8,16,1,1]{0,2,3,1:T(4,128)(4,1)}, pred[8,16,1,1]{0,2,3,1:T(4,128)(4,1)S(1)}, u32[]{:S(2)}) copy-start(pred[8,16,1,1]{0,2,3,1:T(4,128)(4,1)S(1)} %copy.2278) | copy-start | bytes 388
  102.3 69.2 %copy-start.374 = (pred[16,16,1,1]{0,2,3,1:T(4,128)(4,1)}, pred[16,16,1,1]{0,2,3,1:T(4,128)(4,1)S(1)}, u32[]{:S(2)}) copy-start(pred[16,16,1,1]{0,2,3,1:T(4,128)(4,1)S(1)} %copy.2281) | copy-start | bytes 772
  157.6 136.7 %copy-start.762 = (pred[2,16]{1,0:T(4,128)(4,1)}, pred[2,16]{1,0:T(4,128)(4,1)S(1)}, u32[]{:S(2)}) copy-start(pred[2,16]{1,0:T(4,128)(4,1)S(1)} %get-tuple-element.1961) | copy-start | bytes 100
  157.6 139.3 %copy-start.583 = (f32[16,2]{0,1:T(2,128)}, f32[16,2]{0,1:T(2,128)S(1)}, u32[]{:S(2)}) copy-start(f32[16,2]{0,1:T(2,128)S(1)} %get-tuple-element.1959) | copy-start | bytes 388
  173.2 208.3 %copy-start.425 = (bf16[16,16,48]{2,1,0:T(8,128)(2,1)}, bf16[16,16,48]{2,1,0:T(8,128)(2,1)S(1)}, u32[]{:S(2)}) copy-start(bf16[16,16,48]{2,1,0:T(8,128)(2,1)S(1)} %convert_element_type.802) | copy-start | bytes 73732
  215.9 34.0 collective-permute-start.2
  280.3 69.5 %collective-permute-start.3 = (bf16[2,512,768]{1,2,0:T(8,128)(2,1)}, bf16[2,512,768]{1,2,0:T(8,128)(2,1)}, u32[]{:S(2)}, u32[]{:S(2)}) collective-permute-start(bf16[2,512,768]{1,2,0:T(8,128)(2,1)} %broadcast_select_fusion.20), channel_id=1, source_target_pairs={{0,8},{1,9},{2,10},{3,11},{4,12},{5,13},{6,14},{7,15},{8,0},{9,1},... | collective-permute-start | bytes 4718600 | tf_op jit(solution)/shard_map/ppermute | solution.py:22
  415.6 136.2 %copy-start.22 = (f32[16,8,32,48]{3,0,1,2:T(8,128)}, f32[16,8,32,48]{3,0,1,2:T(8,128)S(1)}, u32[]{:S(2)}) copy-start(f32[16,8,32,48]{3,0,1,2:T(8,128)S(1)} %get-tuple-element.1839) | copy-start | bytes 2359300
  457.3 11.9 collective-permute-start.4
  474.0 2.4 collective-permute-start.5
  478.2 104.6 %collective-permute-start.6 = (bf16[2,512,768]{2,1,0:T(8,128)(2,1)}, bf16[2,512,768]{2,1,0:T(8,128)(2,1)}, u32[]{:S(2)}, u32[]{:S(2)}) collective-permute-start(bf16[2,512,768]{2,1,0:T(8,128)(2,1)} %maximum_select_fusion.11), channel_id=1, source_target_pairs={{0,2},{1,3},{2,0},{3,1},{4,6},{5,7},{6,4},{7,5},{8,10},{9,11},{10,... | collective-permute-start | bytes 4718600 | tf_op jit(solution)/shard_map/ppermute | solution.py:22
  624.1 36.6 %collective-permute-start.7 = (bf16[2,512,768]{1,2,0:T(8,128)(2,1)}, bf16[2,512,768]{1,2,0:T(8,128)(2,1)}, u32[]{:S(2)}, u32[]{:S(2)}) collective-permute-start(bf16[2,512,768]{1,2,0:T(8,128)(2,1)} %broadcast_select_fusion.22), channel_id=1, source_target_pairs={{0,4},{1,5},{2,6},{3,7},{4,0},{5,1},{6,2},{7,3},{8,12},{9,13},{10,... | collective-permute-start | bytes 4718600 | tf_op jit(solution)/shard_map/ppermute | solution.py:22
  693.8 70.3 %collective-permute-start.8 = (bf16[2,512,768]{1,2,0:T(8,128)(2,1)}, bf16[2,512,768]{1,2,0:T(8,128)(2,1)}, u32[]{:S(2)}, u32[]{:S(2)}) collective-permute-start(bf16[2,512,768]{1,2,0:T(8,128)(2,1)} %broadcast_select_fusion.19), channel_id=1, source_target_pairs={{0,8},{1,9},{2,10},{3,11},{4,12},{5,13},{6,14},{7,15},{8,0},{9,1},... | collective-permute-start | bytes 4718600 | tf_op jit(solution)/shard_map/ppermute | solution.py:22
  828.8 69.0 %copy-start.16 = (f32[16,8,32,48]{3,0,1,2:T(8,128)}, f32[16,8,32,48]{3,0,1,2:T(8,128)S(1)}, u32[]{:S(2)}) copy-start(f32[16,8,32,48]{3,0,1,2:T(8,128)S(1)} %get-tuple-element.1841) | copy-start | bytes 2359300
  863.4 20.8 collective-permute-start.9
  892.2 27.5 collective-permute-start.10
  923.0 37.1 %collective-permute-start.11 = (bf16[2,512,768]{2,1,0:T(8,128)(2,1)}, bf16[2,512,768]{2,1,0:T(8,128)(2,1)}, u32[]{:S(2)}, u32[]{:S(2)}) collective-permute-start(bf16[2,512,768]{2,1,0:T(8,128)(2,1)} %maximum_select_fusion.13), channel_id=1, source_target_pairs={{0,2},{1,3},{2,0},{3,1},{4,6},{5,7},{6,4},{7,5},{8,10},{9,11},{10,... | collective-permute-start | bytes 4718600 | tf_op jit(solution)/shard_map/ppermute | solution.py:22
  1004.2 38.2 %collective-permute-start.12 = (bf16[2,512,768]{1,2,0:T(8,128)(2,1)}, bf16[2,512,768]{1,2,0:T(8,128)(2,1)}, u32[]{:S(2)}, u32[]{:S(2)}) collective-permute-start(bf16[2,512,768]{1,2,0:T(8,128)(2,1)} %broadcast_select_fusion.21), channel_id=1, source_target_pairs={{0,4},{1,5},{2,6},{3,7},{4,0},{5,1},{6,2},{7,3},{8,12},{9,13},{10,... | collective-permute-start | bytes 4718600 | tf_op jit(solution)/shard_map/ppermute | solution.py:22
  1076.9 71.2 %collective-permute-start.13 = (bf16[2,512,768]{1,2,0:T(8,128)(2,1)}, bf16[2,512,768]{1,2,0:T(8,128)(2,1)}, u32[]{:S(2)}, u32[]{:S(2)}) collective-permute-start(bf16[2,512,768]{1,2,0:T(8,128)(2,1)} %broadcast_select_fusion.18), channel_id=1, source_target_pairs={{0,8},{1,9},{2,10},{3,11},{4,12},{5,13},{6,14},{7,15},{8,0},{9,1},... | collective-permute-start | bytes 4718600 | tf_op jit(solution)/shard_map/ppermute | solution.py:22
  1427.1 127.3 %copy-start.580 = (f32[16,2]{0,1:T(2,128)S(1)}, f32[16,2]{0,1:T(2,128)}, u32[]{:S(2)}) copy-start(f32[16,2]{0,1:T(2,128)} %copy-done.578) | copy-start | bytes 388
  1427.1 129.4 %copy-start.116 = (f32[16,128,48]{2,0,1:T(8,128)S(1)}, f32[16,128,48]{2,0,1:T(8,128)}, u32[]{:S(2)}) copy-start(f32[16,128,48]{2,0,1:T(8,128)} %copy.1979) | copy-start | bytes 1179652
  1427.2 129.4 %copy-start.586 = (f32[16,2]{0,1:T(2,128)S(1)}, f32[16,2]{0,1:T(2,128)}, u32[]{:S(2)}) copy-start(f32[16,2]{0,1:T(2,128)} %copy-done.583) | copy-start | bytes 388
  1740.4 69.9 %collective-permute-start.14 = (bf16[2,512,768]{1,2,0:T(8,128)(2,1)}, bf16[2,512,768]{1,2,0:T(8,128)(2,1)}, u32[]{:S(2)}, u32[]{:S(2)}) collective-permute-start(bf16[2,512,768]{1,2,0:T(8,128)(2,1)} %bitcast.623), channel_id=1, source_target_pairs={{0,8},{1,9},{2,10},{3,11},{4,12},{5,13},{6,14},{7,15},{8,0},{9,1},... | collective-permute-start | bytes 4718600 | tf_op jit(solution)/shard_map/ppermute | solution.py:22
  1850.1 36.4 %collective-permute-start.15 = (bf16[2,512,768]{1,2,0:T(8,128)(2,1)S(1)}, bf16[2,512,768]{1,2,0:T(8,128)(2,1)S(1)}, u32[]{:S(2)}, u32[]{:S(2)}) collective-permute-start(bf16[2,512,768]{1,2,0:T(8,128)(2,1)S(1)} %bitcast.2636), channel_id=1, source_target_pairs={{0,4},{1,5},{2,6},{3,7},{4,0},{5,1},{6,2},{7,3},{8,12},{9,13},{10,... | collective-permute-start | bytes 4718600 | tf_op jit(solution)/shard_map/ppermute | solution.py:22
  1850.3 75.2 %copy-start.749 = (f32[256]{0:T(256)}, f32[256]{0:T(256)S(1)}, u32[]{:S(2)}) copy-start(f32[256]{0:T(256)S(1)} %broadcast_multiply_fusion.15) | copy-start | bytes 3076
  1924.8 35.5 collective-permute-start.16
  1961.4 5.7 collective-permute-start.17
  1974.9 21.7 collective-permute-start.18
  2170.0 71.7 %collective-permute-start.19 = (bf16[2,512,768]{1,2,0:T(8,128)(2,1)}, bf16[2,512,768]{1,2,0:T(8,128)(2,1)}, u32[]{:S(2)}, u32[]{:S(2)}) collective-permute-start(bf16[2,512,768]{1,2,0:T(8,128)(2,1)} %bitcast.775), channel_id=1, source_target_pairs={{0,8},{1,9},{2,10},{3,11},{4,12},{5,13},{6,14},{7,15},{8,0},{9,1},... | collective-permute-start | bytes 4718600 | tf_op jit(solution)/shard_map/ppermute | solution.py:22
  2284.4 126.9 %collective-permute-start.20 = (bf16[2,512,768]{1,2,0:T(8,128)(2,1)}, bf16[2,512,768]{1,2,0:T(8,128)(2,1)}, u32[]{:S(2)}, u32[]{:S(2)}) collective-permute-start(bf16[2,512,768]{1,2,0:T(8,128)(2,1)} %bitcast.786), channel_id=1, source_target_pairs={{0,4},{1,5},{2,6},{3,7},{4,0},{5,1},{6,2},{7,3},{8,12},{9,13},{10,... | collective-permute-start | bytes 4718600 | tf_op jit(solution)/shard_map/ppermute | solution.py:22
  2289.9 121.5 %copy-start.686 = (pred[16]{0:T(512)(128)(4,1)S(1)}, pred[16]{0:T(512)(128)(4,1)}, u32[]{:S(2)}) copy-start(pred[16]{0:T(512)(128)(4,1)} %copy-done.682) | copy-start | bytes 52
  2456.4 36.6 %collective-permute-start.21 = (bf16[2,512,768]{1,2,0:T(8,128)(2,1)}, bf16[2,512,768]{1,2,0:T(8,128)(2,1)}, u32[]{:S(2)}, u32[]{:S(2)}) collective-permute-start(bf16[2,512,768]{1,2,0:T(8,128)(2,1)} %bitcast.797), channel_id=1, source_target_pairs={{0,2},{1,3},{2,0},{3,1},{4,6},{5,7},{6,4},{7,5},{8,10},{9,11},{10,... | collective-permute-start | bytes 4718600 | tf_op jit(solution)/shard_map/ppermute | solution.py:22
  2457.3 69.5 %copy-start.754 = (f32[256]{0:T(256)}, f32[256]{0:T(256)S(1)}, u32[]{:S(2)}) copy-start(f32[256]{0:T(256)S(1)} %multiply_reduce_fusion.39) | copy-start | bytes 3076
  2498.3 19.5 collective-permute-start.22
  2525.5 13.4 collective-permute-start.23
  2702.1 70.9 %collective-permute-start.24 = (bf16[2,512,768]{1,2,0:T(8,128)(2,1)}, bf16[2,512,768]{1,2,0:T(8,128)(2,1)}, u32[]{:S(2)}, u32[]{:S(2)}) collective-permute-start(bf16[2,512,768]{1,2,0:T(8,128)(2,1)} %bitcast.886), channel_id=1, source_target_pairs={{0,8},{1,9},{2,10},{3,11},{4,12},{5,13},{6,14},{7,15},{8,0},{9,1},... | collective-permute-start | bytes 4718600 | tf_op jit(solution)/shard_map/ppermute | solution.py:22
  2815.7 126.8 %collective-permute-start.25 = (bf16[2,512,768]{1,2,0:T(8,128)(2,1)}, bf16[2,512,768]{1,2,0:T(8,128)(2,1)}, u32[]{:S(2)}, u32[]{:S(2)}) collective-permute-start(bf16[2,512,768]{1,2,0:T(8,128)(2,1)} %bitcast.897), channel_id=1, source_target_pairs={{0,4},{1,5},{2,6},{3,7},{4,0},{5,1},{6,2},{7,3},{8,12},{9,13},{10,... | collective-permute-start | bytes 4718600 | tf_op jit(solution)/shard_map/ppermute | solution.py:22
  2821.0 121.5 %copy-start.687 = (pred[16]{0:T(512)(128)(4,1)S(1)}, pred[16]{0:T(512)(128)(4,1)}, u32[]{:S(2)}) copy-start(pred[16]{0:T(512)(128)(4,1)} %copy-done.682) | copy-start | bytes 52
  2984.9 36.2 %collective-permute-start.26 = (bf16[2,512,768]{1,2,0:T(8,128)(2,1)}, bf16[2,512,768]{1,2,0:T(8,128)(2,1)}, u32[]{:S(2)}, u32[]{:S(2)}) collective-permute-start(bf16[2,512,768]{1,2,0:T(8,128)(2,1)} %bitcast.908), channel_id=1, source_target_pairs={{0,2},{1,3},{2,0},{3,1},{4,6},{5,7},{6,4},{7,5},{8,10},{9,11},{10,... | collective-permute-start | bytes 4718600 | tf_op jit(solution)/shard_map/ppermute | solution.py:22
  3026.4 20.8 collective-permute-start.27
  3055.6 112.5 %reduce-scatter.21.cloned.1.call-start = ((), (), s32[]{:S(2)}) async-start(), calls=%async_computation.15 | async-start | bytes 417792
  3060.1 173.8 %reduce-scatter.13.cloned.1.call-start = ((), (), s32[]{:S(2)}) async-start(), calls=%async_computation.7 | async-start | bytes 2506752 | tf_op jit(solution)/shard_map/reduce_scatter | solution.py:511
  3064.1 285.4 %reduce-scatter.17.cloned.1.call-start = ((), (), s32[]{:S(2)}) async-start(), calls=%async_computation.9 | async-start | bytes 10027008 | tf_op jit(solution)/shard_map/reduce_scatter | solution.py:513
  3076.3 389.0 %reduce-scatter.15.cloned.1.call-start = ((), (), s32[]{:S(2)}) async-start(), calls=%async_computation.8 | async-start | bytes 10027008 | tf_op jit(solution)/shard_map/reduce_scatter | solution.py:512
  3087.9 472.2 %reduce-scatter.11.cloned.1.call-start = ((), (), s32[]{:S(2)}) async-start(), calls=%async_computation.6 | async-start | bytes 7520256 | tf_op jit(solution)/shard_map/reduce_scatter | solution.py:510
  3099.3 65.0 %copy-start.258 = (f32[1,256,768]{2,1,0:T(8,128)S(1)}, f32[1,256,768]{2,1,0:T(8,128)}, u32[]{:S(2)}) copy-start(f32[1,256,768]{2,1,0:T(8,128)} %get-tuple-element.1794) | copy-start | bytes 2359300
  (807 other events, 5459.8 us)
Sparse Core Ops, SparseCore 0:
  10.9 52.6 all-gather.11
  65.9 39.4 all-gather.13
  107.6 55.6 all-gather.15
  165.4 51.4 all-gather.17
  3055.7 53.3 reduce-scatter.18
  3112.9 54.6 reduce-scatter.20
  3171.9 62.0 reduce-scatter.12
  3239.2 110.3 reduce-scatter.16
  3354.2 111.0 reduce-scatter.14
  3470.3 89.7 reduce-scatter.10
where the time goes:
time: 3590 us; the launch traced here: 3570 us
  local copies, waits for them, and re-layouts  1180 us (33%)
  matrix products  942 us (26%)
  waiting for transfers between devices  704 us (20%)
  other arithmetic  532 us (15%)
  blocking collectives  152 us (4%)
    ppermute x24, waiting for transfers between devices, swapped(): return lax.ppermute(value, axis, pairs)  307 us
    another operation x15, local copies, waits for them, and re-layouts, widen(): stacked = jnp.stack([lower_part, upper_part], axis=2)  207 us
    dot_general x27, matrix products, backward_block(): jnp.einsum('hqk,hqd->hkd', score_grad, query_block, preferred_element_typ...  199 us
    dot_general x27, matrix products, backward_block(): jnp.einsum('hqk,hkd->hqd', score_grad, key_block, preferred_element_type=...  197 us
    reshape x15, local copies, waits for them, and re-layouts, widen(): stacked.reshape(buffer.shape[0], buffer.shape[1] * 2, HEADS, HEAD_DIM)  165 us
    unnamed x1697, local copies, waits for them, and re-layouts  147 us
    dot_general x54, matrix products, score_block(): jnp.einsum('hqd,hkd->hqk', query_block, key_block, preferred_element_type...  140 us
    reshape x51, local copies, waits for them, and re-layouts, spread_rows(): return spread.reshape((tensor.shape[0] * dilation,) + tensor.shape[1:])  118 us
  transfers between devices with their start and end apart: 38, of which 19 were waited for; matrix products, arithmetic and copies ran while one was open for 32% of the time, Pallas kernels for 0%

commit v1 on v0

--- a/solution.py
+++ b/solution.py
@@ -1,7 +1,12 @@
+import functools
+import math
+
 import jax
 import jax.numpy as jnp
 import numpy as np
 from jax import lax
+from jax.experimental import pallas as pl
+from jax.experimental.pallas import tpu as pltpu
 from jax.sharding import PartitionSpec as P
 
 D = 768
@@ -540,9 +545,425 @@
     )
 
 
+HD = 48
+AUG = 128
+IDS = 32
+SRC = 16
+TOK = 256
+ROOT = HD ** -0.5
+C2 = ROOT * math.log2(math.e)
+AWAY = -(2.0 ** 100)
+BLOCKS = (16, 8, 4, 2, 1)
+FIRST = (0, 16, 24, 28, 30)
+F32, BF16 = jnp.float32, jnp.bfloat16
+
+def nt(a, b):
+    return lax.dot_general(a, b, (((1,), (1,)), ((), ())), preferred_element_type=F32)
+
+def nn(a, b):
+    return jnp.dot(a, b, preferred_element_type=F32)
+
+def eye(n):
+    return (lax.broadcasted_iota(jnp.int32, (n, n), 0) == lax.broadcasted_iota(jnp.int32, (n, n), 1)).astype(BF16)
+
+def pack_grid(c):
+    col = lax.broadcasted_iota(jnp.int32, (256, 128), 1)
+    row = lax.broadcasted_iota(jnp.int32, (256, 128), 0)
+    return (row == (col // c) * (2 * c) + col % c).astype(BF16)
+
+def spread_grid(c):
+    row = lax.broadcasted_iota(jnp.int32, (128, 256), 0)
+    col = lax.broadcasted_iota(jnp.int32, (128, 256), 1)
+    return (col == (row // c) * (2 * c) + row % c).astype(BF16)
+
+def split3(v):
+    hi = v.astype(BF16)
+    r = v - hi.astype(F32)
+    mid = r.astype(BF16)
+    lo = (r - mid.astype(F32)).astype(BF16)
+    return hi, mid, lo
+
+def spread(v, grid):
+    hi, mid, lo = split3(v)
+    return nn(hi, grid) + nn(mid, grid) + nn(lo, grid)
+
+def pack_levels(stack):
+    for level in range(1, 5):
+        c = TOK >> level
+        def step(g, _, level=level, c=c):
+            a = stack[FIRST[level - 1] + 2 * g]
+            b = stack[FIRST[level - 1] + 2 * g + 1]
+            if level == 1:
+                pa, pb = a[:, :128], b[:, :128]
+            else:
+                grid = pack_grid(c)
+                pa, pb = nn(a, grid).astype(BF16), nn(b, grid).astype(BF16)
+            stack[FIRST[level] + g] = jnp.concatenate([pa, pb], axis=1)
+            return 0
+        lax.fori_loop(0, BLOCKS[level], step, 0)
+
+def marks(doc_row, away):
+    ids = lax.broadcasted_iota(jnp.int32, (IDS, TOK), 0).astype(F32)
+    same = ids == doc_row
+    return (jnp.where(same, 0.0, AWAY) if away else jnp.where(same, 1.0, 0.0)).astype(BF16)
+
+def fwd_kernel(x_ref, docs_ref, o_ref, ob_ref, lse_ref, fm, ktm, part, *, kc):
+    pad = jnp.zeros((AUG - HD - IDS, TOK), BF16)
+    def load(s, _):
+        x = x_ref[s]
+        d = docs_ref[s]
+        fm[s] = jnp.concatenate([x[0:HD], marks(d, False), pad, x[HD:2 * HD], marks(d, True), pad, x[2 * HD:]], axis=0)
+        return 0
+    lax.fori_loop(0, SRC, load, 0)
+    pack_levels(fm)
+    iden = eye(TOK)
+    def turn(i, _):
+        ktm[i] = nt(iden, fm[i, AUG:2 * AUG, :]).astype(BF16)
+        return 0
+    lax.fori_loop(0, 31, turn, 0)
+
+    def block(i, kfirst, count):
+        q = fm[i, 0:AUG, :]
+        scores = []
+        for t in range(count):
+            scores.append(nn(ktm[kfirst + t], q))
+        top = functools.reduce(jnp.maximum, [jnp.max(s, axis=0, keepdims=True) for s in scores])
+        total = jnp.zeros((1, TOK), F32)
+        out = jnp.zeros((HD, TOK), F32)
+        for t in range(count):
+            p = jnp.exp2((scores[t] - top) * C2)
+            total = total + jnp.sum(p, axis=0, keepdims=True)
+            out = out + nn(fm[kfirst + t, 2 * AUG:2 * AUG + HD, :], p.astype(BF16))
+        part[i, 0:HD] = out
+        part[i, HD:HD + 8] = jnp.broadcast_to(total, (8, TOK))
+        part[i, HD + 8:HD + 16] = jnp.broadcast_to(top * C2, (8, TOK))
+    def main(i, _):
+        block(i, (i // 4) * 4, 4)
+        return 0
+    lax.fori_loop(0, 28, main, 0)
+    block(28, 28, 2)
+    block(29, 28, 2)
+    block(30, 30, 1)
+
+    for level in range(4, 0, -1):
+        c = TOK >> level
+        def join(g, _, level=level, c=c):
+            child = FIRST[level] + g
+            grid = spread_grid(c) if level > 1 else None
+            for half in range(2):
+                mine = FIRST[level - 1] + 2 * g + half
+                got = part[child, :, half * 128:half * 128 + 128]
+                if level > 1:
+                    got = spread(got, grid)
+                else:
+                    got = jnp.concatenate([got, jnp.zeros_like(got)], axis=1)
+                own = part[mine]
+                cl, cm = got[HD:HD + 1], got[HD + 8:HD + 9]
+                cm = jnp.where(cl > 0, cm, AWAY)
+                ol, om = own[HD:HD + 1], own[HD + 8:HD + 9]
+                top = jnp.maximum(cm, om)
+                wc, wo = jnp.exp2(cm - top), jnp.exp2(om - top)
+                part[mine, 0:HD] = got[0:HD] * wc + own[0:HD] * wo
+                part[mine, HD:HD + 8] = jnp.broadcast_to(cl * wc + ol * wo, (8, TOK))
+                part[mine, HD + 8:HD + 16] = jnp.broadcast_to(top, (8, TOK))
+            return 0
+        lax.fori_loop(0, BLOCKS[level], join, 0)
+    def finish(s, _):
+        own = part[s]
+        l, m = own[HD:HD + 1], own[HD + 8:HD + 9]
+        out = own[0:HD] / l
+        o_ref[s] = out
+        ob_ref[s] = out.astype(BF16)
+        lse_ref[s] = m + jnp.log2(l)
+        return 0
+    lax.fori_loop(0, SRC, finish, 0)
+
+def attn_fwd(x, docs):
+    return pl.pallas_call(
+        functools.partial(fwd_kernel, kc=256),
+        out_shape=(jax.ShapeDtypeStruct((SRC, HD, TOK), F32), jax.ShapeDtypeStruct((SRC, HD, TOK), BF16), jax.ShapeDtypeStruct((SRC, 1, TOK), F32)),
+        in_specs=[pl.BlockSpec(memory_space=pltpu.VMEM)] * 2,
+        out_specs=[pl.BlockSpec(memory_space=pltpu.VMEM)] * 3,
+        scratch_shapes=[
+            pltpu.VMEM((31, 2 * AUG + HD, TOK), BF16),
+            pltpu.VMEM((31, TOK, AUG), BF16),
+            pltpu.VMEM((31, HD + 16, TOK), F32),
+        ],
+        compiler_params=pltpu.CompilerParams(vmem_limit_bytes=50 * 2**20),
+        name="attend",
+    )(x, docs)
+
+def bwd_kernel(x_ref, g_ref, docs_ref, o_ref, lse_ref, e_ref, fm, tm, eq, ek, ev):
+    pad = jnp.zeros((AUG - HD - IDS - 16, TOK), BF16)
+    pad2 = jnp.zeros((AUG - HD - 16, TOK), BF16)
+    row16 = lax.broadcasted_iota(jnp.int32, (16, TOK), 0)
+    ones = jnp.where(row16 < 3, 1.0, 0.0).astype(BF16)
+    def three(v):
+        hi, mid, lo = split3(v)
+        hi, mid, lo = hi.astype(F32), mid.astype(F32), lo.astype(F32)
+        return jnp.where(row16 == 0, hi, jnp.where(row16 == 1, mid, jnp.where(row16 == 2, lo, 0.0))).astype(BF16)
+    def load(s, _):
+        x = x_ref[s]
+        d = docs_ref[s]
+        g = g_ref[s]
+        dot = jnp.sum(g.astype(F32) * o_ref[s], axis=0, keepdims=True)
+        low = three(lse_ref[s] * (-1.0 / C2))
+        off = three(-dot)
+        fm[s] = jnp.concatenate([
+            x[0:HD], marks(d, False), low, pad,
+            g, off, pad2,
+            x[HD:2 * HD], marks(d, True), ones, pad,
+            x[2 * HD:], ones, pad2], axis=0)
+        return 0
+    lax.fori_loop(0, SRC, load, 0)
+    pack_levels(fm)
+    iden = eye(TOK)
+    def turn(i, _):
+        tm[i] = nt(iden, fm[i]).astype(BF16)
+        return 0
+    lax.fori_loop(0, 31, turn, 0)
+    def zero(i, _):
+        ek[i] = jnp.zeros((TOK, AUG), F32)
+        ev[i] = jnp.zeros((TOK, AUG), F32)
+        return 0
+    lax.fori_loop(0, 31, zero, 0)
+
+    def block(i, kfirst, count):
+        q = fm[i, 0:AUG, :]
+        g = fm[i, AUG:2 * AUG, :]
+        qt = tm[i, :, 0:AUG]
+        gt = tm[i, :, AUG:2 * AUG]
+        acc = jnp.zeros((HD, TOK), F32)
+        for t in range(count):
+            k = kfirst + t
+            p = jnp.exp2(nn(tm[k, :, 2 * AUG:3 * AUG], q) * C2)
+            es = (p * nn(tm[k, :, 3 * AUG:], g)).astype(BF16)
+            ev[k] += nn(p.astype(BF16), gt)
+            ek[k] += nn(es, qt)
+            acc = acc + nn(fm[k, 2 * AUG:2 * AUG + HD, :], es)
+        eq[i] = acc
+    def main(i, _):
+        block(i, (i // 4) * 4, 4)
+        return 0
+    lax.fori_loop(0, 28, main, 0)
+    block(28, 28, 2)
+    block(29, 28, 2)
+    block(30, 30, 1)
+
+    for level in range(4, 0, -1):
+        c = TOK >> level
+        def join(g, _, level=level, c=c):
+            child = FIRST[level] + g
+            grid = spread_grid(c) if level > 1 else None
+            for half in range(2):
+                mine = FIRST[level - 1] + 2 * g + half
+                got = eq[child, :, half * 128:half * 128 + 128]
+                if level > 1:
+                    eq[mine] += spread(got, grid)
+                else:
+                    eq[mine, :, 0:128] += got
+                for s in range(128 // c):
+                    ek[mine, 2 * c * s:2 * c * s + c, :] += ek[child, half * 128 + c * s:half * 128 + c * s + c, :]
+                    ev[mine, 2 * c * s:2 * c * s + c, :] += ev[child, half * 128 + c * s:half * 128 + c * s + c, :]
+            return 0
+        lax.fori_loop(0, BLOCKS[level], join, 0)
+    small = (lax.broadcasted_iota(jnp.int32, (HD, AUG), 0) == lax.broadcasted_iota(jnp.int32, (HD, AUG), 1)).astype(BF16)
+    def finish(s, _):
+        a = (eq[s] * ROOT).astype(BF16)
+        b = nt(small, (ek[s] * ROOT).astype(BF16)).astype(BF16)
+        v = nt(small, ev[s].astype(BF16)).astype(BF16)
+        e_ref[s] = jnp.concatenate([a, b, v], axis=0)
+        return 0
+    lax.fori_loop(0, SRC, finish, 0)
+
+def attn_bwd(x, g, docs, o, lse):
+    return pl.pallas_call(
+        bwd_kernel,
+        out_shape=jax.ShapeDtypeStruct((SRC, 3 * HD, TOK), BF16),
+        in_specs=[pl.BlockSpec(memory_space=pltpu.VMEM)] * 5,
+        out_specs=pl.BlockSpec(memory_space=pltpu.VMEM),
+        scratch_shapes=[
+            pltpu.VMEM((31, 4 * AUG, TOK), BF16),
+            pltpu.VMEM((31, TOK, 4 * AUG), BF16),
+            pltpu.VMEM((31, HD, TOK), F32),
+            pltpu.VMEM((31, TOK, AUG), F32),
+            pltpu.VMEM((31, TOK, AUG), F32),
+        ],
+        compiler_params=pltpu.CompilerParams(vmem_limit_bytes=56 * 2**20),
+        name="attend_back",
+    )(x, g, docs, o, lse)
+
+
+def layer_norm(values, gain_row, shift_row):
+    center = values - jnp.mean(values, axis=-1, keepdims=True)
+    scale = lax.rsqrt(jnp.mean(center * center, axis=-1, keepdims=True) + epsilon)
+    unit = center * scale
+    return unit, scale, (unit * gain_row + shift_row).astype(BF16)
+
+
+def layer_norm_back(grad, unit, scale, gain_row):
+    pulled = grad * gain_row
+    return (
+        pulled
+        - jnp.mean(pulled, axis=-1, keepdims=True)
+        - unit * jnp.mean(pulled * unit, axis=-1, keepdims=True)
+    ) * scale
+
+
+def gelu_parts(values):
+    share = 0.5 * (1.0 + lax.erf(values * math.sqrt(0.5)))
+    slope = share + values * jnp.exp(-0.5 * values * values) * (1.0 / math.sqrt(2 * math.pi))
+    return (values * share).astype(BF16), slope
+
+
+def head_order():
+    block = np.array([int(f"{k:04b}"[::-1], 2) for k in range(16)])
+    heads = np.arange(HEADS)[:, None, None]
+    residue = (heads + block[None, :, None]) % 16
+    return (np.arange(16)[None, None, :] * 16 + residue).reshape(HEADS, TOK)
+
+
+def cube_forward(hidden, params, order, docs, trade):
+    w_qkv, w_out, w_up, w_down, gains, biases, up_bias = params
+    unit_one, scale_one, normed = layer_norm(hidden, gains[0], biases[0])
+    mixed = jnp.einsum("df,td->ft", w_qkv, normed, preferred_element_type=F32)
+    shift = jnp.concatenate([biases[1], jnp.zeros_like(biases[1]), biases[2]])
+    mixed = (mixed + shift[:, None]).astype(BF16)
+    mixed = mixed.reshape(3, HEADS, HEAD_DIM, TOK).transpose(1, 0, 2, 3).reshape(HEADS, 3 * HEAD_DIM, TOK)
+    mixed = jnp.einsum("hft,htu->hfu", mixed, order, preferred_element_type=F32).astype(BF16)
+    heads = trade(mixed)
+    merged, merged_low, summary = attn_fwd(heads, docs)
+    attended = trade(merged_low)
+    attended = jnp.einsum("hdu,htu->hdt", attended, order, preferred_element_type=F32).astype(BF16)
+    attended = attended.reshape(D, TOK)
+    middle = hidden + jnp.einsum("ft,fd->td", attended, w_out, preferred_element_type=F32) + biases[3]
+    unit_two, scale_two, normed_two = layer_norm(middle, gains[1], biases[4])
+    upward = jnp.dot(normed_two, w_up, preferred_element_type=F32) + up_bias
+    activated, slope = gelu_parts(upward)
+    result = middle + jnp.dot(activated, w_down, preferred_element_type=F32) + biases[5]
+    kept = (unit_one, scale_one, normed, heads, merged, summary, attended, unit_two, scale_two, normed_two, slope, activated)
+    return result.astype(BF16), kept
+
+
+def cube_backward(incoming_low, kept, params, order, docs, trade):
+    w_qkv, w_out, w_up, w_down, gains, biases, up_bias = params
+    unit_one, scale_one, normed, heads, merged, summary, attended, unit_two, scale_two, normed_two, slope, activated = kept
+    incoming = incoming_low.astype(F32)
+    grad_down = inner_rows(activated, incoming_low)
+    act_grad = jnp.einsum("tb,ab->ta", incoming_low, w_down, preferred_element_type=F32)
+    up_grad = (act_grad * slope).astype(BF16)
+    grad_up = inner_rows(normed_two, up_grad)
+    norm_two_grad = jnp.einsum("tb,ab->ta", up_grad, w_up, preferred_element_type=F32)
+    middle_grad = incoming + layer_norm_back(norm_two_grad, unit_two, scale_two, gains[1])
+    branch_grad = middle_grad.astype(BF16)
+    grad_out = jnp.einsum("ft,td->fd", attended, branch_grad, preferred_element_type=F32)
+    merged_grad = jnp.einsum("fd,td->ft", w_out, branch_grad, preferred_element_type=F32).astype(BF16)
+    merged_grad = merged_grad.reshape(HEADS, HEAD_DIM, TOK)
+    merged_grad = jnp.einsum("hdt,htu->hdu", merged_grad, order, preferred_element_type=F32).astype(BF16)
+    back_heads = attn_bwd(heads, trade(merged_grad), docs, merged, summary)
+    mixed_grad = trade(back_heads)
+    mixed_grad = jnp.einsum("hfu,htu->hft", mixed_grad, order, preferred_element_type=F32).astype(BF16)
+    mixed_grad = mixed_grad.reshape(HEADS, 3, HEAD_DIM, TOK).transpose(1, 0, 2, 3).reshape(3 * D, TOK)
+    grad_qkv = jnp.einsum("td,ft->df", normed, mixed_grad, preferred_element_type=F32)
+    grad_shift = jnp.sum(mixed_grad.astype(F32), axis=1)
+    normed_grad = jnp.einsum("ft,df->td", mixed_grad, w_qkv, preferred_element_type=F32)
+    start_grad = middle_grad + layer_norm_back(normed_grad, unit_one, scale_one, gains[0])
+    small = jnp.stack([
+        jnp.sum(normed_grad * unit_one, axis=0),
+        jnp.sum(norm_two_grad * unit_two, axis=0),
+        jnp.sum(normed_grad, axis=0),
+        grad_shift[:D],
+        grad_shift[2 * D:],
+        jnp.sum(branch_grad.astype(F32), axis=0),
+        jnp.sum(norm_two_grad, axis=0),
+        jnp.sum(incoming, axis=0),
+    ])
+    grad_up_bias = jnp.sum(up_grad.astype(F32), axis=0)
+    return start_grad, (grad_qkv, grad_out, grad_up, grad_down, small, grad_up_bias)
+
+
+def cube_body(inputs, cotangent, documents, w_qkv, w_out, w_up, w_down, norm_gains, biases, up_bias):
+    section_id = lax.axis_index("section")
+    place = lax.axis_index("seq")
+    count = lax.axis_size("seq")
+    half = count // 2
+    micro_id = place // half
+    member = section_id * half + place % half
+    teams = [[s * count + k * half + j for s in range(2) for j in range(half)] for k in range(2)]
+    axes = ("section", "seq")
+
+    def trade(value):
+        return lax.all_to_all(value, axes, 0, 0, axis_index_groups=teams, tiled=True)
+
+    def across(value, pairs):
+        return lax.ppermute(value, axes, pairs)
+
+    def own_rows(pair):
+        mine = jnp.where(micro_id == 0, pair[0], pair[1])
+        other = jnp.where(micro_id == 0, pair[1], pair[0])
+        swap = across(other, [(count + j, count + (j ^ half)) for j in range(count)])
+        return jnp.where(section_id == 0, mine, swap)
+
+    table = jnp.asarray(head_order())
+    order = (table[:, None, :] == jnp.arange(TOK)[None, :, None]).astype(BF16)
+    docs = jnp.where(micro_id == 0, documents[0], documents[1]).reshape(count, TOK)
+    docs = jnp.where(micro_id == 0, docs, jnp.roll(docs, half, axis=0))
+    own_order = lax.dynamic_index_in_dim(order, member, 0, keepdims=False)
+    docs = jnp.dot(docs.astype(BF16), own_order, preferred_element_type=F32).reshape(count, 1, TOK)
+
+    def whole(shard):
+        got = lax.all_gather(shard.astype(BF16), axes, axis=0, tiled=True)
+        return got.reshape((2, got.shape[0] // 2) + got.shape[1:])
+
+    hidden = own_rows(inputs)
+    small = jnp.concatenate([norm_gains[0], biases[0]]).astype(BF16)
+    small = jnp.concatenate([small.reshape(-1), up_bias[0].astype(BF16)])
+    small = lax.all_gather(small, axes, axis=0).astype(F32).reshape(2, count, -1)
+    wide = D // count
+    rows = small[:, :, : 8 * wide].reshape(2, count, 8, wide).transpose(0, 2, 1, 3).reshape(2, 8, D)
+    lifts = small[:, :, 8 * wide:].reshape(2, -1)
+    weights = [whole(w[0]) for w in (w_qkv, w_out, w_up, w_down)]
+    params = [tuple(w[l] for w in weights) + (rows[l, :2], rows[l, 2:], lifts[l]) for l in range(2)]
+
+    first, kept_first = cube_forward(hidden.astype(F32), params[0], order, docs, trade)
+    final, kept_final = cube_forward(first.astype(F32), params[1], order, docs, trade)
+    grad_final, terms_final = cube_backward(own_rows(cotangent), kept_final, params[1], order, docs, trade)
+    sent = grad_final.astype(BF16)
+    grad_first, terms_first = cube_backward(sent, kept_first, params[0], order, docs, trade)
+
+    def shared_out(value_first, value_final):
+        far = across(value_first, [(count + j, j ^ half) for j in range(count)])
+        near = across(value_final, [(j, count + j) for j in range(count)])
+        beside = across(value_final, [(count + j, count + (j ^ half)) for j in range(count)])
+        return jnp.where(section_id == 0, far, beside), near
+
+    def placed(mine, other):
+        return jnp.where(micro_id == 0, jnp.stack([mine, other]), jnp.stack([other, mine]))[None]
+
+    other, near = shared_out(first, final)
+    layer_outputs = placed(jnp.where(section_id == 0, first, near), other)
+    other, near = shared_out(grad_first.astype(BF16), sent)
+    input_grads = placed(jnp.where(section_id == 0, grad_first, near.astype(F32)), other.astype(F32))
+
+    def summed(first_term, final_term, axis):
+        parts = [
+            lax.psum_scatter(t, "seq", scatter_dimension=axis, tiled=True)
+            for t in (first_term, final_term)
+        ]
+        away = jnp.where(section_id == 0, parts[1], parts[0])
+        mine = jnp.where(section_id == 0, parts[0], parts[1])
+        return (mine.astype(F32) + lax.ppermute(away, "section", [(0, 1), (1, 0)]).astype(F32))[None]
+
+    grads = [summed(a.astype(BF16), b.astype(BF16), 0) for a, b in zip(terms_first[:4], terms_final[:4])]
+    small = summed(terms_first[4], terms_final[4], 1)
+    lift = summed(terms_first[5], terms_final[5], 0)
+    return (layer_outputs, input_grads, *grads, small[:, :2], small[:, 2:], lift)
+
+
 def solution(mesh):
+    cube = mesh.shape["seq"] == 16
     return jax.shard_map(
-        body,
+        cube_body if cube else body,
         mesh=mesh,
         in_specs=(
             P(None, "seq", None),

time: 3590 us -> 1300 us (0.36)
  local copies, waits for them, and re-layouts: 1180 us -> 33.7 us
  matrix products: 942 us -> 104 us
  other arithmetic: 532 us -> 33 us
  Pallas kernels: 0 us -> 167 us
    dot_general x234 -> x29, matrix products: 906 us -> 83.5 us  [the longest x2 11.2 us: cube_forward(): upward = jnp.dot(normed_two, w_up, preferred_element_type=F32) + up_bias]
    reshape x180 -> x6, local copies, waits for them, and re-layouts: 318 us -> 0.5 us  [the longest x2 0.21 us: cube_body(): small[:, :, :8 * wide].reshape(2, count, 8, wide).transpose(0, 2, 1, 3)]
    another operation x94 -> x19, local copies, waits for them, and re-layouts: 287 us -> 9.25 us  [the longest x18 9.25 us: cube_backward(): jnp.stack([jnp.sum(normed_grad * unit_one, axis=0), jnp.sum(norm_two_grad...]
    ppermute x28 -> x14, waiting for transfers between devices: 313 us -> 45 us  [the longest x8 41.5 us: across(): return lax.ppermute(value, axes, pairs)]
    all_gather x4, waiting for transfers between devices: 0.08 us -> 173 us  [whole(): got = lax.all_gather(shard.astype(BF16), axes, axis=0, tiled=True)]
    pallas_call x0 -> x4, Pallas kernels: none -> 167 us  [the longest x2 99.8 us: attn_bwd(): pl.pallas_call(bwd_kernel, out_shape=jax.ShapeDtypeStruct((SRC, 3 * HD, T...]
    select_n x84 -> x11, other arithmetic: 163 us -> 8.14 us  [the longest x6 4.66 us: summed(): away = jnp.where(section_id == 0, parts[1], parts[0])]
    unnamed x1697 -> x190, local copies, waits for them, and re-layouts: 147 us -> 14.8 us
  transfers between devices with their start and end apart: 38 -> 34, of which waited for: 19 -> 18; matrix products, arithmetic and copies ran while one was open for 32% -> 8% of each run, Pallas kernels for 0% -> 6%
where the time goes in v1:
time: 1300 us; the launch traced here: 1290 us
  waiting for transfers between devices  713 us (55%)
  Pallas kernels  167 us (13%)
  blocking collectives  157 us (12%)
  matrix products  104 us (8%)
  starting transfers between devices  63.8 us (5%)
  local copies, waits for them, and re-layouts  33.7 us (3%)
  other arithmetic  33 us (3%)
  between operations  16.3 us (1%)
    reduce_scatter x8, waiting for transfers between devices, summed(): lax.psum_scatter(t, 'seq', scatter_dimension=axis, tiled=True)  432 us
    all_gather x4, waiting for transfers between devices, whole(): got = lax.all_gather(shard.astype(BF16), axes, axis=0, tiled=True)  173 us
    unnamed x2, blocking collectives  108 us
    pallas_call x2, Pallas kernels, attn_bwd(): pl.pallas_call(bwd_kernel, out_shape=jax.ShapeDtypeStruct((SRC, 3 * HD, T...  99.8 us
    pallas_call x2, Pallas kernels, attn_fwd(): pl.pallas_call(functools.partial(fwd_kernel, kc=256), out_shape=(jax.Shap...  67.7 us
    all_to_all x6, waiting for transfers between devices, trade(): lax.all_to_all(value, axes, 0, 0, axis_index_groups=teams, tiled=True)  61.8 us
    all_to_all x2, blocking collectives, trade(): lax.all_to_all(value, axes, 0, 0, axis_index_groups=teams, tiled=True)  49.7 us
    ppermute x8, waiting for transfers between devices, across(): return lax.ppermute(value, axes, pairs)  41.5 us
  transfers between devices with their start and end apart: 34, of which 18 were waited for; matrix products, arithmetic and copies ran while one was open for 8% of the time, Pallas kernels for 6%

profile of v1, /device:TPU:0, one launch (start us, length us, event | category | flops | bytes accessed | tf_op | source)
XLA Modules:
  0.0 1288.5 jit_solution(870764289864710370)
XLA Ops:
  10.7 1.8 convert_element_type.233
  15.7 49.9 %all-reduce = bf16[18432]{0:T(1024)(128)(2,1)S(1)} all-reduce(bf16[18432]{0:T(1024)(128)(2,1)S(1)} %dynamic-update-slice), channel_id=2, replica_groups=mesh['section'=2,'seq'=16] {'section','seq'}, use_global_device_ids=true, to_apply=%add | all-reduce | flops 18432 | bytes 73728
  67.8 29.5 %all-gather.10.cloned.1.call-done = bf16[1,1536,2304]{2,1,0:T(8,128)(2,1)} async-done(((bf16[1,48,2304]{2,1,0:T(8,128)(2,1)}), bf16[1,1536,2304]{2,1,0:T(8,128)(2,1)}) %all-gather.10.cloned.1.call-update) | async-done | bytes 7077904 | tf_op jit(solution)/shard_map/all_gather | solution.py:915
  97.3 3.2 fusion.25
  101.2 2.0 fusion.44
  103.3 3.8 all-to-all-start
  108.1 18.1 %all-to-all-done.x_ref = bf16[16,144,256]{2,1,0:T(8,128)(2,1)S(1)} async-done(((bf16[16,144,256]{2,1,0:T(8,128)(2,1)}), bf16[16,144,256]{2,1,0:T(8,128)(2,1)S(1)}, u32[]{:S(2)}, u32[]{:S(2)}) %all-to-all-start) | async-done | bytes 1179680 | tf_op jit(solution)/shard_map/all_to_all | solution.py:896
  126.2 33.8 %attend.2 = (f32[16,48,256]{2,1,0:T(8,128)S(1)}, bf16[16,48,256]{2,1,0:T(8,128)(2,1)}, f32[16,1,256]{2,1,0:T(1,128)S(1)}) custom-call(bf16[16,144,256]{2,1,0:T(8,128)(2,1)S(1)} %all-to-all-done.x_ref, f32[16,1,256]{2,1,0:T(1,128)S(1)} %reshape.377.docs_ref), custom_call_target="tpu_custom_call" | custom-call | tf_op jit(solution)/shard_map/attend/pallas_call | solution.py:682
  161.5 3.8 all-to-all-start.1
  166.6 7.9 all-to-all-done.1
  175.4 2.0 fusion.112
  177.7 65.7 %all-gather.14.cloned.1.call-done = bf16[1,1536,3072]{2,1,0:T(8,128)(2,1)} async-done(((bf16[1,48,3072]{2,1,0:T(8,128)(2,1)}), bf16[1,1536,3072]{2,1,0:T(8,128)(2,1)}) %all-gather.14.cloned.1.call-update) | async-done | bytes 9437200 | tf_op jit(solution)/shard_map/all_gather | solution.py:915
  243.4 5.8 multiply_convert_fusion.1
  249.1 78.2 %all-gather.16.cloned.1.call-done = bf16[1,6144,768]{2,1,0:T(8,128)(2,1)} async-done(((bf16[1,192,768]{2,1,0:T(8,128)(2,1)}), bf16[1,6144,768]{2,1,0:T(8,128)(2,1)}) %all-gather.16.cloned.1.call-update) | async-done | bytes 9437200 | tf_op jit(solution)/shard_map/all_gather | solution.py:915
  327.3 3.8 convert_reduce_fusion.4
  331.5 4.2 fusion.24
  338.4 21.1 %all_to_all.40.x_ref = bf16[16,144,256]{2,1,0:T(8,128)(2,1)S(1)} all-to-all(bf16[16,144,256]{2,1,0:T(8,128)(2,1)S(1)} %fusion.45), channel_id=1, replica_groups={{0,1,2,3,4,5,6,7,16,17,18,19,20,21,22,23},{8,9,10,11,12,13,14,15,24,25,..., dimensions={0} | all-to-all | bytes 2359296 | tf_op jit(solution)/shard_map/all_to_all | solution.py:896
  359.5 33.8 %attend.3 = (f32[16,48,256]{2,1,0:T(8,128)S(1)}, bf16[16,48,256]{2,1,0:T(8,128)(2,1)}, f32[16,1,256]{2,1,0:T(1,128)S(1)}) custom-call(bf16[16,144,256]{2,1,0:T(8,128)(2,1)S(1)} %all_to_all.40.x_ref, f32[16,1,256]{2,1,0:T(1,128)S(1)} %reshape.377.docs_ref), custom_call_target="tpu_custom_call" | custom-call | tf_op jit(solution)/shard_map/attend/pallas_call | solution.py:682
  394.8 3.6 all-to-all-start.3
  402.0 1.9 convert_reduce_fusion.7
  403.9 4.6 all-to-all-done.3
  410.9 1.9 fusion.113
  413.0 5.4 multiply_convert_fusion
  418.5 4.5 convert_reduce_fusion
  423.0 2.1 multiply_reduce_fusion
  428.4 28.6 %all_to_all.41.g_ref = bf16[16,48,256]{2,1,0:T(8,128)(2,1)} all-to-all(bf16[16,48,256]{2,1,0:T(8,128)(2,1)S(1)} %fusion.58), channel_id=1, replica_groups={{0,1,2,3,4,5,6,7,16,17,18,19,20,21,22,23},{8,9,10,11,12,13,14,15,24,25,..., dimensions={0} | all-to-all | bytes 786432 | tf_op jit(solution)/shard_map/all_to_all | solution.py:896
  457.0 49.9 %attend_back.2 = bf16[16,144,256]{2,1,0:T(8,128)(2,1)} custom-call(bf16[16,144,256]{2,1,0:T(8,128)(2,1)} %copy-done.1, bf16[16,48,256]{2,1,0:T(8,128)(2,1)} %all_to_all.41.g_ref, f32[16,1,256]{2,1,0:T(1,128)} %copy-done.4, f32[16,48,256]{2,1,0:T(8,128)} %copy-done.3, f32[16,1,256]{2,1,0:T(1,128)} %copy-done.6), custom_call_target="tpu_custom_call" | custom-call | tf_op jit(solution)/shard_map/attend_back/pallas_call | solution.py:780
  506.9 4.5 all-to-all-start.5
  513.8 15.3 %all-to-all-done.5 = bf16[16,144,256]{2,1,0:T(8,128)(2,1)} async-done(((bf16[16,144,256]{2,1,0:T(8,128)(2,1)}), bf16[16,144,256]{2,1,0:T(8,128)(2,1)}, u32[]{:S(2)}, u32[]{:S(2)}) %all-to-all-start.5) | async-done | bytes 1179680 | tf_op jit(solution)/shard_map/all_to_all | solution.py:896
  529.2 2.3 fusion.46
  532.7 4.4 fusion.81
  538.1 4.9 convert_reduce_fusion.1
  543.1 2.2 multiply_reduce_fusion.1
  547.5 1.9 copy.47
  549.4 2.6 fusion.59
  552.0 4.2 all-to-all-start.6
  566.9 2.6 convolution_convert_fusion.6
  569.5 49.9 %attend_back.3 = bf16[16,144,256]{2,1,0:T(8,128)(2,1)} custom-call(bf16[16,144,256]{2,1,0:T(8,128)(2,1)} %copy-done, bf16[16,48,256]{2,1,0:T(8,128)(2,1)} %all-to-all-done.6.g_ref, f32[16,1,256]{2,1,0:T(1,128)} %copy-done.4, f32[16,48,256]{2,1,0:T(8,128)} %copy-done.2, f32[16,1,256]{2,1,0:T(1,128)} %copy-done.5), custom_call_target="tpu_custom_call" | custom-call | tf_op jit(solution)/shard_map/attend_back/pallas_call | solution.py:780
  619.4 5.1 all-to-all-start.7
  626.5 15.9 %all-to-all-done.7 = bf16[16,144,256]{2,1,0:T(8,128)(2,1)} async-done(((bf16[16,144,256]{2,1,0:T(8,128)(2,1)}), bf16[16,144,256]{2,1,0:T(8,128)(2,1)}, u32[]{:S(2)}, u32[]{:S(2)}) %all-to-all-start.7) | async-done | bytes 1179680 | tf_op jit(solution)/shard_map/all_to_all | solution.py:896
  642.3 2.3 fusion.47
  644.8 5.1 fusion.89
  651.6 5.2 convolution_convert_fusion.2
  657.5 5.1 convolution_convert_fusion.3
  663.6 5.0 convolution_convert_fusion
  669.7 5.1 convolution_convert_fusion.1
  675.5 4.5 convolution_convert_fusion.4
  680.6 4.3 convolution_convert_fusion.5
  685.6 5.0 fusion.54
  690.6 3.3 collective-permute-start.1
  697.8 3.8 collective-permute-done.1
  701.7 28.0 %collective-permute-done.2 = bf16[256,768]{1,0:T(8,128)(2,1)S(1)} collective-permute-done((bf16[256,768]{1,0:T(8,128)(2,1)S(1)}, bf16[256,768]{1,0:T(8,128)(2,1)S(1)}, u32[]{:S(2)}, u32[]{:S(2)}) %collective-permute-start.2) | collective-permute-done | bytes 393248 | tf_op jit(solution)/shard_map/ppermute | solution.py:899
  729.7 57.9 %all-reduce.3 = (f32[3072]{0:T(1024)S(1)}, f32[3072]{0:T(1024)S(1)}) all-reduce(f32[3072]{0:T(1024)} %get-tuple-element.127, f32[3072]{0:T(1024)} %get-tuple-element.129), channel_id=18, replica_groups=mesh['section'=2,'seq'=16] {'seq'}, use_global_device_ids=true, to_apply=%region_43.44.clone | all-reduce | flops 6144 | bytes 49152
  787.7 10.4 collective-permute-start.13
  799.1 1.9 collective-permute-start.5
  810.2 10.4 collective-permute-start.12
  823.3 9.7 collective-permute-done.6
  833.1 61.8 %reduce-scatter.25.cloned.1.call-done = bf16[48,3072]{1,0:T(8,128)(2,1)} async-done(((bf16[768,3072]{1,0:T(8,128)(2,1)}), bf16[48,3072]{1,0:T(8,128)(2,1)}) %reduce-scatter.25.cloned.1.call-update) | async-done | bytes 294928 | tf_op jit(solution)/shard_map/reduce_scatter | solution.py:950
  894.9 78.8 %reduce-scatter.23.cloned.1.call-done = bf16[48,3072]{1,0:T(8,128)(2,1)} async-done(((bf16[768,3072]{1,0:T(8,128)(2,1)}), bf16[48,3072]{1,0:T(8,128)(2,1)}) %reduce-scatter.23.cloned.1.call-update) | async-done | bytes 294928 | tf_op jit(solution)/shard_map/reduce_scatter | solution.py:950
  977.6 74.7 %reduce-scatter.29.cloned.1.call-done = bf16[192,768]{1,0:T(8,128)(2,1)} async-done(((bf16[3072,768]{1,0:T(8,128)(2,1)}), bf16[192,768]{1,0:T(8,128)(2,1)}) %reduce-scatter.29.cloned.1.call-update) | async-done | bytes 294928 | tf_op jit(solution)/shard_map/reduce_scatter | solution.py:950
  1052.3 78.8 %reduce-scatter.27.cloned.1.call-done = bf16[192,768]{1,0:T(8,128)(2,1)} async-done(((bf16[3072,768]{1,0:T(8,128)(2,1)}), bf16[192,768]{1,0:T(8,128)(2,1)}) %reduce-scatter.27.cloned.1.call-update) | async-done | bytes 294928 | tf_op jit(solution)/shard_map/reduce_scatter | solution.py:950
  1134.7 67.5 %reduce-scatter.17.cloned.1.call-done = bf16[48,2304]{1,0:T(8,128)(2,1)} async-done(((bf16[768,2304]{1,0:T(8,128)(2,1)}), bf16[48,2304]{1,0:T(8,128)(2,1)}) %reduce-scatter.17.cloned.1.call-update) | async-done | bytes 221200 | tf_op jit(solution)/shard_map/reduce_scatter | solution.py:950
  1202.1 70.6 %reduce-scatter.15.cloned.1.call-done = bf16[48,2304]{1,0:T(8,128)(2,1)} async-done(((bf16[768,2304]{1,0:T(8,128)(2,1)}), bf16[48,2304]{1,0:T(8,128)(2,1)}) %reduce-scatter.15.cloned.1.call-update) | async-done | bytes 221200 | tf_op jit(solution)/shard_map/reduce_scatter | solution.py:950
  1276.2 3.6 collective-permute-done.8
  (357 shorter events, 82.7 us)
Async XLA Ops:
  7.2 90.0 %all-gather.10.cloned.1.call-start = ((), (), s32[]{:S(2)}) async-start(), calls=%async_computation.26 | async-start | bytes 7299072 | tf_op jit(solution)/shard_map/all_gather | solution.py:915
  9.1 166.4 %all-gather.12.cloned.1.call-start = ((), (), s32[]{:S(2)}) async-start(), calls=%async_computation.27 | async-start | bytes 2433024 | tf_op jit(solution)/shard_map/all_gather | solution.py:915
  10.7 232.7 %all-gather.14.cloned.1.call-start = ((), (), s32[]{:S(2)}) async-start(), calls=%async_computation.28 | async-start | bytes 9732096 | tf_op jit(solution)/shard_map/all_gather | solution.py:915
  12.6 314.8 %all-gather.16.cloned.1.call-start = ((), (), s32[]{:S(2)}) async-start(), calls=%async_computation.29 | async-start | bytes 9732096 | tf_op jit(solution)/shard_map/all_gather | solution.py:915
  14.5 52.7 %collective-permute-start = (bf16[256,768]{1,0:T(8,128)(2,1)S(1)}, bf16[256,768]{1,0:T(8,128)(2,1)S(1)}, u32[]{:S(2)}, u32[]{:S(2)}) collective-permute-start(bf16[256,768]{1,0:T(8,128)(2,1)S(1)} %select_bitcast_fusion.4), channel_id=1, source_target_pairs={{16,24},{17,25},{18,26},{19,27},{20,28},{21,29},{22,30},{23,31},{2... | collective-permute-start | bytes 1179656 | tf_op jit(solution)/shard_map/ppermute | solution.py:899
  66.6 33.8 %copy-start.33 = (f32[768]{0:T(1024)}, f32[768]{0:T(1024)S(1)}, u32[]{:S(2)}) copy-start(f32[768]{0:T(1024)S(1)} %get-tuple-element.87) | copy-start | bytes 9220
  67.5 108.0 %copy-start.7 = (bf16[256,768]{1,0:T(8,128)(2,1)}, bf16[256,768]{1,0:T(8,128)(2,1)S(1)}, u32[]{:S(2)}) copy-start(bf16[256,768]{1,0:T(8,128)(2,1)S(1)} %get-tuple-element.104) | copy-start | bytes 1179652
  67.5 33.0 %copy-start.43 = (f32[256]{0:T(256)}, f32[256]{0:T(256)S(1)}, u32[]{:S(2)}) copy-start(f32[256]{0:T(256)S(1)} %broadcast_multiply_fusion.11) | copy-start | bytes 3076
  67.8 32.7 %copy-start.62 = (f32[256]{0:T(256)}, f32[256]{0:T(256)S(1)}, u32[]{:S(2)}) copy-start(f32[256]{0:T(256)S(1)} %add_rsqrt_fusion.3) | copy-start | bytes 3076
  103.3 23.0 %all-to-all-start = ((bf16[16,144,256]{2,1,0:T(8,128)(2,1)}), bf16[16,144,256]{2,1,0:T(8,128)(2,1)S(1)}, u32[]{:S(2)}, u32[]{:S(2)}) async-start(bf16[16,144,256]{2,1,0:T(8,128)(2,1)} %fusion.44), calls=%async_computation | async-start | bytes 2359296 | tf_op jit(solution)/shard_map/all_to_all | solution.py:896
  108.1 251.4 %copy-start.4 = (f32[16,1,256]{2,1,0:T(1,128)}, f32[16,1,256]{2,1,0:T(1,128)S(1)}, u32[]{:S(2)}) copy-start(f32[16,1,256]{2,1,0:T(1,128)S(1)} %reshape.377.docs_ref) | copy-start | bytes 49156
  126.2 51.2 %copy-start = (bf16[16,144,256]{2,1,0:T(8,128)(2,1)}, bf16[16,144,256]{2,1,0:T(8,128)(2,1)S(1)}, u32[]{:S(2)}) copy-start(bf16[16,144,256]{2,1,0:T(8,128)(2,1)S(1)} %all-to-all-done.x_ref) | copy-start | bytes 3538948
  161.5 13.0 %all-to-all-start.1 = ((bf16[16,48,256]{2,1,0:T(8,128)(2,1)}), bf16[16,48,256]{2,1,0:T(8,128)(2,1)S(1)}, u32[]{:S(2)}, u32[]{:S(2)}) async-start(bf16[16,48,256]{2,1,0:T(8,128)(2,1)} %get-tuple-element.15), calls=%async_computation.1 | async-start | bytes 786432 | tf_op jit(solution)/shard_map/all_to_all | solution.py:896
  175.4 73.7 %copy-start.29 = (bf16[16,48,256]{2,1,0:T(8,128)(2,1)}, bf16[16,48,256]{2,1,0:T(8,128)(2,1)S(1)}, u32[]{:S(2)}) copy-start(bf16[16,48,256]{2,1,0:T(8,128)(2,1)S(1)} %fusion.56) | copy-start | bytes 1179652
  175.4 68.0 %copy-start.70 = (f32[3072]{0:T(1024)S(1)}, f32[3072]{0:T(1024)}, u32[]{:S(2)}) copy-start(f32[3072]{0:T(1024)} %add.257) | copy-start | bytes 36868
  177.4 71.7 %copy-start.46 = (f32[256]{0:T(256)}, f32[256]{0:T(256)S(1)}, u32[]{:S(2)}) copy-start(f32[256]{0:T(256)S(1)} %broadcast_multiply_fusion.10) | copy-start | bytes 3076
  177.7 71.5 %copy-start.65 = (f32[256]{0:T(256)}, f32[256]{0:T(256)S(1)}, u32[]{:S(2)}) copy-start(f32[256]{0:T(256)S(1)} %add_rsqrt_fusion.2) | copy-start | bytes 3076
  243.4 84.0 %copy-start.74 = (f32[768]{0:T(1024)S(1)}, f32[768]{0:T(1024)}, u32[]{:S(2)}) copy-start(f32[768]{0:T(1024)} %get-tuple-element.81) | copy-start | bytes 9220
  249.1 82.0 %copy-start.17 = (bf16[256,3072]{1,0:T(8,128)(2,1)}, bf16[256,3072]{1,0:T(8,128)(2,1)S(1)}, u32[]{:S(2)}) copy-start(bf16[256,3072]{1,0:T(8,128)(2,1)S(1)} %get-tuple-element.115) | copy-start | bytes 4718596
  359.5 50.6 %copy-start.1 = (bf16[16,144,256]{2,1,0:T(8,128)(2,1)}, bf16[16,144,256]{2,1,0:T(8,128)(2,1)S(1)}, u32[]{:S(2)}) copy-start(bf16[16,144,256]{2,1,0:T(8,128)(2,1)S(1)} %all_to_all.40.x_ref) | copy-start | bytes 3538948
  394.8 13.7 %all-to-all-start.3 = ((bf16[16,48,256]{2,1,0:T(8,128)(2,1)}), bf16[16,48,256]{2,1,0:T(8,128)(2,1)S(1)}, u32[]{:S(2)}, u32[]{:S(2)}) async-start(bf16[16,48,256]{2,1,0:T(8,128)(2,1)} %get-tuple-element.16), calls=%async_computation.3 | async-start | bytes 786432 | tf_op jit(solution)/shard_map/all_to_all | solution.py:896
  399.6 2.5 collective-permute-start.4
  457.0 54.5 %copy-start.60 = (f32[768]{0:T(1024)S(1)}, f32[768]{0:T(1024)}, u32[]{:S(2)}) copy-start(f32[768]{0:T(1024)} %get-tuple-element.97) | copy-start | bytes 9220
  457.0 55.1 %copy-start.61 = (f32[768]{0:T(1024)S(1)}, f32[768]{0:T(1024)}, u32[]{:S(2)}) copy-start(f32[768]{0:T(1024)} %get-tuple-element.99) | copy-start | bytes 9220
  457.0 55.7 %copy-start.78 = (f32[768]{0:T(1024)S(1)}, f32[768]{0:T(1024)}, u32[]{:S(2)}) copy-start(f32[768]{0:T(1024)} %get-tuple-element.59) | copy-start | bytes 9220
  457.0 56.3 %copy-start.77 = (f32[768]{0:T(1024)S(1)}, f32[768]{0:T(1024)}, u32[]{:S(2)}) copy-start(f32[768]{0:T(1024)} %get-tuple-element.71) | copy-start | bytes 9220
  457.0 72.2 %copy-start.53 = (s32[16,256]{1,0:T(8,128)S(1)}, s32[16,256]{1,0:T(8,128)}, u32[]{:S(2)}) copy-start(s32[16,256]{1,0:T(8,128)} %constant.76.clone) | copy-start | bytes 49156
  506.9 22.3 %all-to-all-start.5 = ((bf16[16,144,256]{2,1,0:T(8,128)(2,1)}), bf16[16,144,256]{2,1,0:T(8,128)(2,1)}, u32[]{:S(2)}, u32[]{:S(2)}) async-start(bf16[16,144,256]{2,1,0:T(8,128)(2,1)} %attend_back.2), calls=%async_computation.5 | async-start | bytes 2359296 | tf_op jit(solution)/shard_map/all_to_all | solution.py:896
  552.0 17.5 %all-to-all-start.6 = ((bf16[16,48,256]{2,1,0:T(8,128)(2,1)}), bf16[16,48,256]{2,1,0:T(8,128)(2,1)}, u32[]{:S(2)}, u32[]{:S(2)}) async-start(bf16[16,48,256]{2,1,0:T(8,128)(2,1)} %fusion.59), calls=%async_computation.6 | async-start | bytes 786432 | tf_op jit(solution)/shard_map/all_to_all | solution.py:896
  556.2 246.1 %reduce-scatter.33.cloned.1.call-start = ((), (), s32[]{:S(2)}) async-start(), calls=%async_computation.31 | async-start | bytes 417792
  566.9 236.3 %reduce-scatter.21.cloned.1.call-start = ((), (), s32[]{:S(2)}) async-start(), calls=%async_computation.21 | async-start | bytes 1253376 | tf_op jit(solution)/shard_map/reduce_scatter | solution.py:950
  569.5 55.1 %copy-start.30 = (bf16[16,48,256]{2,1,0:T(8,128)(2,1)S(1)}, bf16[16,48,256]{2,1,0:T(8,128)(2,1)}, u32[]{:S(2)}) copy-start(bf16[16,48,256]{2,1,0:T(8,128)(2,1)} %copy-done.29) | copy-start | bytes 1179652
  619.4 22.9 %copy-start.54 = (s32[16,256]{1,0:T(8,128)S(1)}, s32[16,256]{1,0:T(8,128)}, u32[]{:S(2)}) copy-start(s32[16,256]{1,0:T(8,128)} %constant.76.clone) | copy-start | bytes 49156
  619.4 22.9 %all-to-all-start.7 = ((bf16[16,144,256]{2,1,0:T(8,128)(2,1)}), bf16[16,144,256]{2,1,0:T(8,128)(2,1)}, u32[]{:S(2)}, u32[]{:S(2)}) async-start(bf16[16,144,256]{2,1,0:T(8,128)(2,1)} %attend_back.3), calls=%async_computation.7 | async-start | bytes 2359296 | tf_op jit(solution)/shard_map/all_to_all | solution.py:896
  624.5 178.6 %reduce-scatter.19.cloned.1.call-start = ((), (), s32[]{:S(2)}) async-start(), calls=%async_computation.20 | async-start | bytes 1253376 | tf_op jit(solution)/shard_map/reduce_scatter | solution.py:950
  626.1 18.7 %copy-start.44 = (f32[256]{0:T(256)S(1)}, f32[256]{0:T(256)}, u32[]{:S(2)}) copy-start(f32[256]{0:T(256)} %copy-done.43) | copy-start | bytes 3076
  626.1 18.7 %copy-start.63 = (f32[256]{0:T(256)S(1)}, f32[256]{0:T(256)}, u32[]{:S(2)}) copy-start(f32[256]{0:T(256)} %copy-done.62) | copy-start | bytes 3076
  626.1 183.3 %reduce-scatter.31.cloned.1.call-start = ((), (), s32[]{:S(2)}) async-start(), calls=%async_computation.30 | async-start | bytes 417792
  651.5 243.4 %reduce-scatter.25.cloned.1.call-start = ((), (), s32[]{:S(2)}) async-start(), calls=%async_computation.23 | async-start | bytes 5013504 | tf_op jit(solution)/shard_map/reduce_scatter | solution.py:950
  656.9 316.9 %reduce-scatter.23.cloned.1.call-start = ((), (), s32[]{:S(2)}) async-start(), calls=%async_computation.22 | async-start | bytes 5013504 | tf_op jit(solution)/shard_map/reduce_scatter | solution.py:950
  662.7 389.6 %reduce-scatter.29.cloned.1.call-start = ((), (), s32[]{:S(2)}) async-start(), calls=%async_computation.25 | async-start | bytes 5013504 | tf_op jit(solution)/shard_map/reduce_scatter | solution.py:950
  668.7 462.4 %reduce-scatter.27.cloned.1.call-start = ((), (), s32[]{:S(2)}) async-start(), calls=%async_computation.24 | async-start | bytes 5013504 | tf_op jit(solution)/shard_map/reduce_scatter | solution.py:950
  674.8 527.3 %reduce-scatter.17.cloned.1.call-start = ((), (), s32[]{:S(2)}) async-start(), calls=%async_computation.19 | async-start | bytes 3760128 | tf_op jit(solution)/shard_map/reduce_scatter | solution.py:950
  680.0 592.8 %reduce-scatter.15.cloned.1.call-start = ((), (), s32[]{:S(2)}) async-start(), calls=%async_computation.18 | async-start | bytes 3760128 | tf_op jit(solution)/shard_map/reduce_scatter | solution.py:950
  690.6 116.1 %copy-start.28 = (f32[256,768]{1,0:T(8,128)S(1)}, f32[256,768]{1,0:T(8,128)}, u32[]{:S(2)}) copy-start(f32[256,768]{1,0:T(8,128)} %get-tuple-element.126) | copy-start | bytes 2359300
  690.6 116.1 %copy-start.45 = (f32[256]{0:T(256)S(1)}, f32[256]{0:T(256)}, u32[]{:S(2)}) copy-start(f32[256]{0:T(256)} %copy-done.43) | copy-start | bytes 3076
  690.6 116.1 %copy-start.64 = (f32[256]{0:T(256)S(1)}, f32[256]{0:T(256)}, u32[]{:S(2)}) copy-start(f32[256]{0:T(256)} %copy-done.62) | copy-start | bytes 3076
  690.6 11.0 collective-permute-start.1
  693.9 35.8 %collective-permute-start.2 = (bf16[256,768]{1,0:T(8,128)(2,1)S(1)}, bf16[256,768]{1,0:T(8,128)(2,1)S(1)}, u32[]{:S(2)}, u32[]{:S(2)}) collective-permute-start(bf16[256,768]{1,0:T(8,128)(2,1)S(1)} %get-tuple-element.118), channel_id=1, source_target_pairs={{16,8},{17,9},{18,10},{19,11},{20,12},{21,13},{22,14},{23,15},{24,... | collective-permute-start | bytes 1179656 | tf_op jit(solution)/shard_map/ppermute | solution.py:899
  695.2 34.5 %collective-permute-start.3 = (bf16[256,768]{1,0:T(8,128)(2,1)}, bf16[256,768]{1,0:T(8,128)(2,1)}, u32[]{:S(2)}, u32[]{:S(2)}) collective-permute-start(bf16[256,768]{1,0:T(8,128)(2,1)} %fusion.54), channel_id=1, source_target_pairs={{16,24},{17,25},{18,26},{19,27},{20,28},{21,29},{22,30},{23,31},{2... | collective-permute-start | bytes 1179656 | tf_op jit(solution)/shard_map/ppermute | solution.py:899
  787.7 14.0 %collective-permute-start.13 = (f32[192]{0:T(256)S(1)}, f32[192]{0:T(256)S(1)}, u32[]{:S(2)}, u32[]{:S(2)}) collective-permute-start(f32[192]{0:T(256)S(1)} %broadcast_select_fusion.7), channel_id=1, source_target_pairs={{0,16},{16,0},{1,17},{17,1},{2,18},{18,2},{3,19},{19,3},{4,20},{20... | collective-permute-start | bytes 2312 | tf_op jit(solution)/shard_map/ppermute | solution.py:955
  799.1 7.6 collective-permute-start.5
  801.0 22.3 %collective-permute-start.7 = (bf16[256,768]{1,0:T(8,128)(2,1)S(1)}, bf16[256,768]{1,0:T(8,128)(2,1)S(1)}, u32[]{:S(2)}, u32[]{:S(2)}) collective-permute-start(bf16[256,768]{1,0:T(8,128)(2,1)S(1)} %copy-done.13), channel_id=1, source_target_pairs={{16,24},{17,25},{18,26},{19,27},{20,28},{21,29},{22,30},{23,31},{2... | collective-permute-start | bytes 1179656 | tf_op jit(solution)/shard_map/ppermute | solution.py:899
  804.7 15.9 %collective-permute-start.9 = (bf16[48,768]{1,0:T(8,128)(2,1)}, bf16[48,768]{1,0:T(8,128)(2,1)}, u32[]{:S(2)}, u32[]{:S(2)}) collective-permute-start(bf16[48,768]{1,0:T(8,128)(2,1)} %broadcast_select_fusion.3), channel_id=1, source_target_pairs={{0,16},{16,0},{1,17},{17,1},{2,18},{18,2},{3,19},{19,3},{4,20},{20... | collective-permute-start | bytes 221192 | tf_op jit(solution)/shard_map/ppermute | solution.py:955
  807.9 168.4 %copy-start.19 = (f32[1,1,256,768]{3,2,1,0:T(8,128)S(1)}, f32[1,1,256,768]{3,2,1,0:T(8,128)}, u32[]{:S(2)}) copy-start(f32[1,1,256,768]{3,2,1,0:T(8,128)} %get-tuple-element.101) | copy-start | bytes 2359300
  807.9 25.1 %collective-permute-start.6 = (bf16[256,768]{1,0:T(8,128)(2,1)S(1)}, bf16[256,768]{1,0:T(8,128)(2,1)S(1)}, u32[]{:S(2)}, u32[]{:S(2)}) collective-permute-start(bf16[256,768]{1,0:T(8,128)(2,1)S(1)} %get-tuple-element.102), channel_id=1, source_target_pairs={{16,8},{17,9},{18,10},{19,11},{20,12},{21,13},{22,14},{23,15},{24,... | collective-permute-start | bytes 1179656 | tf_op jit(solution)/shard_map/ppermute | solution.py:899
  810.2 12.0 collective-permute-start.12
  894.9 238.8 %copy-start.24 = (bf16[48,3072]{1,0:T(8,128)(2,1)S(1)}, bf16[48,3072]{1,0:T(8,128)(2,1)}, u32[]{:S(2)}) copy-start(bf16[48,3072]{1,0:T(8,128)(2,1)} %reduce-scatter.25.cloned.1.call-done) | copy-start | bytes 884740
  973.7 160.0 %copy-start.26 = (bf16[48,3072]{1,0:T(8,128)(2,1)S(1)}, bf16[48,3072]{1,0:T(8,128)(2,1)}, u32[]{:S(2)}) copy-start(bf16[48,3072]{1,0:T(8,128)(2,1)} %reduce-scatter.23.cloned.1.call-done) | copy-start | bytes 884740
  974.8 159.0 %collective-permute-start.10 = (bf16[48,3072]{1,0:T(8,128)(2,1)S(1)}, bf16[48,3072]{1,0:T(8,128)(2,1)S(1)}, u32[]{:S(2)}, u32[]{:S(2)}) collective-permute-start(bf16[48,3072]{1,0:T(8,128)(2,1)S(1)} %broadcast_select_fusion.1), channel_id=1, source_target_pairs={{0,16},{16,0},{1,17},{17,1},{2,18},{18,2},{3,19},{19,3},{4,20},{20... | collective-permute-start | bytes 884744 | tf_op jit(solution)/shard_map/ppermute | solution.py:955
  1052.3 223.0 %copy-start.25 = (bf16[192,768]{1,0:T(8,128)(2,1)S(1)}, bf16[192,768]{1,0:T(8,128)(2,1)}, u32[]{:S(2)}) copy-start(bf16[192,768]{1,0:T(8,128)(2,1)} %reduce-scatter.29.cloned.1.call-done) | copy-start | bytes 884740
  1131.1 144.1 %copy-start.27 = (bf16[192,768]{1,0:T(8,128)(2,1)S(1)}, bf16[192,768]{1,0:T(8,128)(2,1)}, u32[]{:S(2)}) copy-start(bf16[192,768]{1,0:T(8,128)(2,1)} %reduce-scatter.27.cloned.1.call-done) | copy-start | bytes 884740
  1132.2 143.1 %collective-permute-start.11 = (bf16[192,768]{1,0:T(8,128)(2,1)S(1)}, bf16[192,768]{1,0:T(8,128)(2,1)S(1)}, u32[]{:S(2)}, u32[]{:S(2)}) collective-permute-start(bf16[192,768]{1,0:T(8,128)(2,1)S(1)} %broadcast_select_fusion), channel_id=1, source_target_pairs={{0,16},{16,0},{1,17},{17,1},{2,18},{18,2},{3,19},{19,3},{4,20},{20... | collective-permute-start | bytes 884744 | tf_op jit(solution)/shard_map/ppermute | solution.py:955
  1273.7 6.0 collective-permute-start.8
  (60 other events, 289.4 us)
Sparse Core Ops, SparseCore 0:
  11.5 85.6 all-gather.9
  100.7 58.0 all-gather.11
  162.3 81.0 all-gather.13
  246.7 80.6 all-gather.15
  567.0 56.5 reduce-scatter.32
  627.5 57.1 reduce-scatter.20
  688.8 59.4 reduce-scatter.18
  752.8 54.6 reduce-scatter.30
  811.4 83.4 reduce-scatter.24
  899.1 74.5 reduce-scatter.22
  977.6 74.6 reduce-scatter.28
  1056.5 74.5 reduce-scatter.26
  1135.0 67.0 reduce-scatter.16
  1205.9 66.8 reduce-scatter.14

commit v2 on v1

--- a/solution.py
+++ b/solution.py
@@ -690,6 +690,7 @@
             pltpu.VMEM((31, HD + 16, TOK), F32),
         ],
         compiler_params=pltpu.CompilerParams(vmem_limit_bytes=50 * 2**20),
+        cost_estimate=pl.CostEstimate(flops=35 * 10**9, bytes_accessed=3 * 2**20, transcendentals=0),
         name="attend",
     )(x, docs)
 
@@ -790,6 +791,7 @@
             pltpu.VMEM((31, TOK, AUG), F32),
         ],
         compiler_params=pltpu.CompilerParams(vmem_limit_bytes=56 * 2**20),
+        cost_estimate=pl.CostEstimate(flops=50 * 10**9, bytes_accessed=6 * 2**20, transcendentals=0),
         name="attend_back",
     )(x, g, docs, o, lse)
 
@@ -823,14 +825,15 @@
     return (np.arange(16)[None, None, :] * 16 + residue).reshape(HEADS, TOK)
 
 
-def cube_forward(hidden, params, order, docs, trade):
-    w_qkv, w_out, w_up, w_down, gains, biases, up_bias = params
+def cube_forward(hidden, w_qkv, more, w_mlp, lines, order, docs, trade):
+    gains, biases, up_bias = lines
     unit_one, scale_one, normed = layer_norm(hidden, gains[0], biases[0])
     mixed = jnp.einsum("df,td->ft", w_qkv, normed, preferred_element_type=F32)
     shift = jnp.concatenate([biases[1], jnp.zeros_like(biases[1]), biases[2]])
     mixed = (mixed + shift[:, None]).astype(BF16)
     mixed = mixed.reshape(3, HEADS, HEAD_DIM, TOK).transpose(1, 0, 2, 3).reshape(HEADS, 3 * HEAD_DIM, TOK)
     mixed = jnp.einsum("hft,htu->hfu", mixed, order, preferred_element_type=F32).astype(BF16)
+    w_out, w_later, mixed = more(mixed)
     heads = trade(mixed)
     merged, merged_low, summary = attn_fwd(heads, docs)
     attended = trade(merged_low)
@@ -838,33 +841,45 @@
     attended = attended.reshape(D, TOK)
     middle = hidden + jnp.einsum("ft,fd->td", attended, w_out, preferred_element_type=F32) + biases[3]
     unit_two, scale_two, normed_two = layer_norm(middle, gains[1], biases[4])
-    upward = jnp.dot(normed_two, w_up, preferred_element_type=F32) + up_bias
+    ff = up_bias.shape[0]
+    upward = jnp.dot(normed_two, w_mlp[:, :ff], preferred_element_type=F32) + up_bias
     activated, slope = gelu_parts(upward)
-    result = middle + jnp.dot(activated, w_down, preferred_element_type=F32) + biases[5]
+    result = middle + biases[5]
+    for at in range(0, ff, D):
+        result = result + jnp.dot(activated[:, at : at + D], w_mlp[:, ff + at : ff + at + D], preferred_element_type=F32)
     kept = (unit_one, scale_one, normed, heads, merged, summary, attended, unit_two, scale_two, normed_two, slope, activated)
-    return result.astype(BF16), kept
+    return result.astype(BF16), kept, w_out, w_later
 
 
 def cube_backward(incoming_low, kept, params, order, docs, trade):
-    w_qkv, w_out, w_up, w_down, gains, biases, up_bias = params
+    w_qkv, w_out, w_mlp, gains, biases, up_bias = params
     unit_one, scale_one, normed, heads, merged, summary, attended, unit_two, scale_two, normed_two, slope, activated = kept
+    ff = up_bias.shape[0]
     incoming = incoming_low.astype(F32)
-    grad_down = inner_rows(activated, incoming_low)
-    act_grad = jnp.einsum("tb,ab->ta", incoming_low, w_down, preferred_element_type=F32)
+    act_grad = jnp.concatenate([
+        jnp.einsum("tb,ab->ta", incoming_low, w_mlp[:, ff + at : ff + at + D], preferred_element_type=F32)
+        for at in range(0, ff, D)
+    ], axis=1)
     up_grad = (act_grad * slope).astype(BF16)
-    grad_up = inner_rows(normed_two, up_grad)
-    norm_two_grad = jnp.einsum("tb,ab->ta", up_grad, w_up, preferred_element_type=F32)
+    norm_two_grad = jnp.einsum("tb,ab->ta", up_grad, w_mlp[:, :ff], preferred_element_type=F32)
     middle_grad = incoming + layer_norm_back(norm_two_grad, unit_two, scale_two, gains[1])
     branch_grad = middle_grad.astype(BF16)
-    grad_out = jnp.einsum("ft,td->fd", attended, branch_grad, preferred_element_type=F32)
     merged_grad = jnp.einsum("fd,td->ft", w_out, branch_grad, preferred_element_type=F32).astype(BF16)
     merged_grad = merged_grad.reshape(HEADS, HEAD_DIM, TOK)
     merged_grad = jnp.einsum("hdt,htu->hdu", merged_grad, order, preferred_element_type=F32).astype(BF16)
-    back_heads = attn_bwd(heads, trade(merged_grad), docs, merged, summary)
+    grad_rest = jnp.concatenate(
+        [inner_rows(normed_two, up_grad).astype(BF16)]
+        + [inner_rows(activated[:, at : at + D], incoming_low).astype(BF16) for at in range(0, ff, D)]
+        + [jnp.einsum("ft,td->fd", attended, branch_grad, preferred_element_type=F32).astype(BF16)],
+        axis=1,
+    )
+    merged_grad = trade(merged_grad)
+    merged_grad, grad_rest = lax.optimization_barrier((merged_grad, grad_rest))
+    back_heads = attn_bwd(heads, merged_grad, docs, merged, summary)
     mixed_grad = trade(back_heads)
     mixed_grad = jnp.einsum("hfu,htu->hft", mixed_grad, order, preferred_element_type=F32).astype(BF16)
     mixed_grad = mixed_grad.reshape(HEADS, 3, HEAD_DIM, TOK).transpose(1, 0, 2, 3).reshape(3 * D, TOK)
-    grad_qkv = jnp.einsum("td,ft->df", normed, mixed_grad, preferred_element_type=F32)
+    grad_qkv = jnp.einsum("td,ft->df", normed, mixed_grad, preferred_element_type=F32).astype(BF16)
     grad_shift = jnp.sum(mixed_grad.astype(F32), axis=1)
     normed_grad = jnp.einsum("ft,df->td", mixed_grad, w_qkv, preferred_element_type=F32)
     start_grad = middle_grad + layer_norm_back(normed_grad, unit_one, scale_one, gains[0])
@@ -879,7 +894,75 @@
         jnp.sum(incoming, axis=0),
     ])
     grad_up_bias = jnp.sum(up_grad.astype(F32), axis=0)
-    return start_grad, (grad_qkv, grad_out, grad_up, grad_down, small, grad_up_bias)
+    return start_grad, (grad_qkv, grad_rest, small, grad_up_bias)
+
+
+def half_pairs(source, count):
+    return [(source * count + j, (1 - source) * count + j) for j in range(count)]
+
+
+def core_swap(value, bit):
+    return lax.ppermute(value, "seq", [(j, j ^ (1 << bit)) for j in range(16)])
+
+
+def section_swap(value):
+    return lax.ppermute(value, "section", [(0, 1), (1, 0)])
+
+
+def place_bit(bit):
+    return (lax.axis_index("seq") >> bit) & 1
+
+
+def two_of(own, got, bit, axis):
+    return jnp.where(bit == 1, jnp.stack([got, own], axis), jnp.stack([own, got], axis))
+
+
+def two_wide(own, got, bit):
+    return jnp.where(bit == 1, jnp.concatenate([got, own], -1), jnp.concatenate([own, got], -1))
+
+
+def collect(piece, order):
+    rows = piece.shape[0]
+    now = two_of(piece, core_swap(piece, 2), place_bit(2), 0)
+    now = two_of(now, core_swap(now, 3), place_bit(3), 0).reshape(4, rows, -1)
+    for axis in order:
+        if axis == "y":
+            now = two_of(now, core_swap(now, 1), place_bit(1), 1).reshape(8, rows, -1)
+        else:
+            now = two_wide(now, section_swap(now), lax.axis_index("section"))
+    now = two_of(now, core_swap(now, 0), place_bit(0), 1)
+    return now.reshape(16 * rows, -1)
+
+
+def plus(own, got, dtype=BF16):
+    return (own.astype(F32) + got.astype(F32)).astype(dtype)
+
+
+def fold(value, bit, axis, dtype=BF16):
+    mine = place_bit(bit)
+    away = lax.dynamic_index_in_dim(value, 1 - mine, axis, keepdims=False)
+    kept = lax.dynamic_index_in_dim(value, mine, axis, keepdims=False)
+    return plus(kept, core_swap(away, bit), dtype)
+
+
+def fold_wide(value):
+    half = value.shape[-1] // 2
+    lower = lax.axis_index("section") == 0
+    away = jnp.where(lower, value[..., half:], value[..., :half])
+    kept = jnp.where(lower, value[..., :half], value[..., half:])
+    return plus(kept, section_swap(away))
+
+
+def reduce_rows(partial, order):
+    rows = partial.shape[0] // 16
+    now = fold(partial.reshape(8, 2, rows, -1), 0, 1)
+    for axis in order:
+        if axis == "y":
+            now = fold(now.reshape(4, 2, rows, -1), 1, 1)
+        else:
+            now = fold_wide(now)
+    now = fold(now.reshape(2, 2, rows, -1), 3, 0)
+    return fold(now, 2, 0, F32)
 
 
 def cube_body(inputs, cotangent, documents, w_qkv, w_out, w_up, w_down, norm_gains, biases, up_bias):
@@ -891,6 +974,7 @@
     member = section_id * half + place % half
     teams = [[s * count + k * half + j for s in range(2) for j in range(half)] for k in range(2)]
     axes = ("section", "seq")
+    lower = section_id == 0
 
     def trade(value):
         return lax.all_to_all(value, axes, 0, 0, axis_index_groups=teams, tiled=True)
@@ -902,7 +986,7 @@
         mine = jnp.where(micro_id == 0, pair[0], pair[1])
         other = jnp.where(micro_id == 0, pair[1], pair[0])
         swap = across(other, [(count + j, count + (j ^ half)) for j in range(count)])
-        return jnp.where(section_id == 0, mine, swap)
+        return jnp.where(lower, mine, swap)
 
     table = jnp.asarray(head_order())
     order = (table[:, None, :] == jnp.arange(TOK)[None, :, None]).astype(BF16)
@@ -911,53 +995,131 @@
     own_order = lax.dynamic_index_in_dim(order, member, 0, keepdims=False)
     docs = jnp.dot(docs.astype(BF16), own_order, preferred_element_type=F32).reshape(count, 1, TOK)
 
-    def whole(shard):
-        got = lax.all_gather(shard.astype(BF16), axes, axis=0, tiled=True)
-        return got.reshape((2, got.shape[0] // 2) + got.shape[1:])
-
     hidden = own_rows(inputs)
-    small = jnp.concatenate([norm_gains[0], biases[0]]).astype(BF16)
-    small = jnp.concatenate([small.reshape(-1), up_bias[0].astype(BF16)])
-    small = lax.all_gather(small, axes, axis=0).astype(F32).reshape(2, count, -1)
     wide = D // count
-    rows = small[:, :, : 8 * wide].reshape(2, count, 8, wide).transpose(0, 2, 1, 3).reshape(2, 8, D)
-    lifts = small[:, :, 8 * wide:].reshape(2, -1)
-    weights = [whole(w[0]) for w in (w_qkv, w_out, w_up, w_down)]
-    params = [tuple(w[l] for w in weights) + (rows[l, :2], rows[l, 2:], lifts[l]) for l in range(2)]
-
-    first, kept_first = cube_forward(hidden.astype(F32), params[0], order, docs, trade)
-    final, kept_final = cube_forward(first.astype(F32), params[1], order, docs, trade)
-    grad_final, terms_final = cube_backward(own_rows(cotangent), kept_final, params[1], order, docs, trade)
-    sent = grad_final.astype(BF16)
-    grad_first, terms_first = cube_backward(sent, kept_first, params[0], order, docs, trade)
+    lift = up_bias[0].reshape(-1, wide)
+    small = jnp.concatenate([norm_gains[0], biases[0], lift]).T.astype(BF16)
+    small = jnp.pad(small, ((0, 0), (0, 128 - small.shape[1])))
+
+    def column_halves(shard, source):
+        columns = shard.shape[1] // 2
+        got = across(shard[:, columns:] if source == 0 else shard[:, :columns], half_pairs(source, count))
+        if source == 0:
+            return jnp.where(lower, shard[:, :columns], got)
+        return jnp.where(lower, got, shard[:, columns:])
+
+    def row_halves(shard, source):
+        rows = shard.shape[0] // 2
+        got = across(shard[rows:] if source == 0 else shard[:rows], half_pairs(source, count))
+        if source == 0:
+            return jnp.where(lower, shard[:rows], got)
+        return jnp.where(lower, got, shard[rows:])
+
+    ff = w_up.shape[2]
+    low_qkv, low_out = w_qkv[0].astype(BF16), w_out[0].astype(BF16)
+    piece = column_halves(low_qkv, 0)
+    part_a = collect(piece[:, :640], "yx")
+    part_b = collect(jnp.concatenate([piece[:, 640:], small], axis=1), "xy")
+    qkv_first = jnp.concatenate([part_a[:, :640], part_b[:, :512], part_a[:, 640:], part_b[:, 640:1152]], axis=1)
+
+    up_shard = w_up[0].astype(BF16).reshape(wide, count, 4, wide).transpose(0, 2, 1, 3).reshape(wide, ff)
+    down_shard = w_down[0].astype(BF16).reshape(4, wide, D).transpose(1, 0, 2).reshape(wide, 4 * D)
+    shard = jnp.concatenate([up_shard, down_shard, low_out], axis=1)
+    mlp_first = lax.all_gather(row_halves(shard[:, : 2 * ff], 0), ("seq", "section"), axis=0, tiled=True)
+    rest_final = lax.all_gather(row_halves(shard, 1), ("seq", "section"), axis=0, tiled=True)
+    piece = jnp.concatenate([column_halves(low_qkv, 1), column_halves(low_out, 0)], axis=1)
+
+    def lines(columns):
+        values = columns[:, :12].astype(F32).T
+        return values[:2], values[2:8], values[8:].reshape(ff)
+
+    def second_weights(after):
+        later, after = lax.optimization_barrier((piece, after))
+        part_a = collect(later[:, :768], "yx")
+        part_b = collect(later[:, 768:], "xy")
+        qkv = jnp.concatenate([part_a[:, :768], part_b[:, :384], part_a[:, 768:], part_b[:, 768:1152]], axis=1)
+        return jnp.concatenate([part_b[:, 384:768], part_b[:, 1152:]], axis=1), qkv, after
+
+    lines_first, lines_final = lines(part_b[:, 512:640]), lines(part_b[:, 1152:])
+    first, kept_first, out_first, qkv_final = cube_forward(
+        hidden.astype(F32), qkv_first, second_weights, mlp_first, lines_first, order, docs, trade
+    )
+    out_final = rest_final[:, 2 * ff :]
+    final, kept_final, _, _ = cube_forward(
+        first.astype(F32), qkv_final, lambda after: (out_final, None, after), rest_final, lines_final, order, docs, trade
+    )
+    params_final = (qkv_final, out_final, rest_final) + lines_final
+    grad_final, terms_final = cube_backward(own_rows(cotangent), kept_final, params_final, order, docs, trade)
+
+    def scattered(partial):
+        return lax.psum_scatter(partial, "seq", scatter_dimension=0, tiled=True)
+
+    sent, qkv_term = lax.optimization_barrier((grad_final.astype(BF16), terms_final[0]))
+    rest_final = scattered(terms_final[1])
+    params_first = (qkv_first, out_first, mlp_first) + lines_first
+    grad_first, terms_first = cube_backward(sent, kept_first, params_first, order, docs, trade)
+    rest_first = scattered(terms_first[1])
 
     def shared_out(value_first, value_final):
         far = across(value_first, [(count + j, j ^ half) for j in range(count)])
-        near = across(value_final, [(j, count + j) for j in range(count)])
+        near = across(value_final, half_pairs(0, count))
         beside = across(value_final, [(count + j, count + (j ^ half)) for j in range(count)])
-        return jnp.where(section_id == 0, far, beside), near
+        return far, near, beside
 
     def placed(mine, other):
         return jnp.where(micro_id == 0, jnp.stack([mine, other]), jnp.stack([other, mine]))[None]
 
-    other, near = shared_out(first, final)
-    layer_outputs = placed(jnp.where(section_id == 0, first, near), other)
-    other, near = shared_out(grad_first.astype(BF16), sent)
-    input_grads = placed(jnp.where(section_id == 0, grad_first, near.astype(F32)), other.astype(F32))
-
-    def summed(first_term, final_term, axis):
-        parts = [
-            lax.psum_scatter(t, "seq", scatter_dimension=axis, tiled=True)
-            for t in (first_term, final_term)
-        ]
-        away = jnp.where(section_id == 0, parts[1], parts[0])
-        mine = jnp.where(section_id == 0, parts[0], parts[1])
-        return (mine.astype(F32) + lax.ppermute(away, "section", [(0, 1), (1, 0)]).astype(F32))[None]
-
-    grads = [summed(a.astype(BF16), b.astype(BF16), 0) for a, b in zip(terms_first[:4], terms_final[:4])]
-    small = summed(terms_first[4], terms_final[4], 1)
-    lift = summed(terms_first[5], terms_final[5], 0)
-    return (layer_outputs, input_grads, *grads, small[:, :2], small[:, 2:], lift)
+    outs = shared_out(first, final)
+    backs = shared_out(grad_first.astype(BF16), sent)
+    qkv_first = reduce_rows(terms_first[0], "xy")
+    qkv_final = reduce_rows(qkv_term, "yx")
+
+    def upright(rows, wide_row):
+        return jnp.concatenate([rows, wide_row.reshape(4, D)]).T
+
+    smalls = jnp.concatenate([upright(*terms_first[2:]), upright(*terms_final[2:])], axis=1)
+    smalls = fold(smalls.reshape(8, 2, wide, 24), 0, 1, F32)
+    smalls = fold(smalls.reshape(4, 2, wide, 24), 1, 1, F32)
+    smalls = fold(smalls.reshape(2, 2, wide, 24), 3, 0, F32)
+    smalls = fold(smalls, 2, 0, F32)
+    smalls = smalls + section_swap(smalls)
+    smalls = jnp.where(lower, smalls[:, :12], smalls[:, 12:]).T
+
+    grad_first, outs, rest_first, rest_final = lax.optimization_barrier((grad_first, outs, rest_first, rest_final))
+    far, near, beside = outs
+    layer_outputs = placed(jnp.where(lower, first, near), jnp.where(lower, far, beside))
+    far, near, beside = backs
+    input_grads = placed(
+        jnp.where(lower, grad_first, near.astype(F32)), jnp.where(lower, far, beside).astype(F32)
+    )
+
+    def finished(part_first, part_final):
+        got_final = across(part_final, half_pairs(0, count))
+        got_first = across(part_first, half_pairs(1, count))
+        return jnp.where(
+            lower,
+            part_first.astype(F32) + got_first.astype(F32),
+            part_final.astype(F32) + got_final.astype(F32),
+        )
+
+    rest = finished(rest_first, rest_final)
+    away = section_swap(jnp.where(lower, qkv_final, qkv_first).astype(BF16)).astype(F32)
+    qkv = jnp.where(
+        lower, jnp.concatenate([qkv_first, away], axis=1), jnp.concatenate([away, qkv_final], axis=1)
+    )
+    up = rest[:, :ff].reshape(wide, 4, count, wide).transpose(0, 2, 1, 3).reshape(wide, ff)
+    down = rest[:, ff : 2 * ff].reshape(wide, 4, D).transpose(1, 0, 2).reshape(4 * wide, D)
+    return (
+        layer_outputs,
+        input_grads,
+        qkv[None],
+        rest[None, :, 2 * ff :],
+        up[None],
+        down[None],
+        smalls[None, :2],
+        smalls[None, 2:8],
+        smalls[8:].reshape(1, -1),
+    )
 
 
 def solution(mesh):

time: 1300 us -> 800 us (0.62)
  waiting for transfers between devices: 713 us -> 283 us
  blocking collectives: 157 us -> 0 us
  starting transfers between devices: 63.8 us -> 153 us
    reduce_scatter x8 -> x2, waiting for transfers between devices: 432 us -> 0.04 us  [scattered(): return lax.psum_scatter(partial, 'seq', scatter_dimension=0, tiled=True)]
    all_gather x4 -> x2, waiting for transfers between devices: 173 us -> 0.04 us  [the longest x1 0.02 us: cube_body(): lax.all_gather(row_halves(shard[:, :2 * ff], 0), ('seq', 'section'), axis...]
    ppermute x6 -> x36, waiting for transfers between devices: 3.59 us -> 174 us  [the longest x28 103 us: core_swap(): return lax.ppermute(value, 'seq', [(j, j ^ 1 << bit) for j in range(16)])]
    unnamed x2 -> x0, blocking collectives: 108 us -> none
    ppermute x8 -> x15, starting transfers between devices: 11.8 us -> 61.5 us  [across(): return lax.ppermute(value, axes, pairs)]
    all_to_all x2 -> x0, blocking collectives: 49.7 us -> none  [trade(): lax.all_to_all(value, axes, 0, 0, axis_index_groups=teams, tiled=True)]
    ppermute x6 -> x36, starting transfers between devices: 26 us -> 53.7 us  [the longest x8 30.8 us: section_swap(): return lax.ppermute(value, 'section', [(0, 1), (1, 0)])]
    all_to_all x6 -> x8, waiting for transfers between devices: 61.8 us -> 88.8 us  [trade(): lax.all_to_all(value, axes, 0, 0, axis_index_groups=teams, tiled=True)]
  transfers between devices with their start and end apart: 34 -> 63, of which waited for: 18 -> 38; matrix products, arithmetic and copies ran while one was open for 8% -> 17% of each run, Pallas kernels for 6% -> 21%
where the time goes in v2:
time: 800 us; the launch traced here: 794 us
  waiting for transfers between devices  283 us (35%)
  Pallas kernels  167 us (21%)
  starting transfers between devices  153 us (19%)
  matrix products  96 us (12%)
  other arithmetic  41.5 us (5%)
  local copies, waits for them, and re-layouts  36.6 us (5%)
  between operations  16.7 us (2%)
    ppermute x28, waiting for transfers between devices, core_swap(): return lax.ppermute(value, 'seq', [(j, j ^ 1 << bit) for j in range(16)])  103 us
    pallas_call x2, Pallas kernels, attn_bwd(): pl.pallas_call(bwd_kernel, out_shape=jax.ShapeDtypeStruct((SRC, 3 * HD, T...  99.7 us
    all_to_all x8, waiting for transfers between devices, trade(): lax.all_to_all(value, axes, 0, 0, axis_index_groups=teams, tiled=True)  88.8 us
    ppermute x8, waiting for transfers between devices, section_swap(): return lax.ppermute(value, 'section', [(0, 1), (1, 0)])  70.5 us
    pallas_call x2, Pallas kernels, attn_fwd(): pl.pallas_call(functools.partial(fwd_kernel, kc=256), out_shape=(jax.Shap...  67.7 us
    ppermute x15, starting transfers between devices, across(): return lax.ppermute(value, axes, pairs)  61.5 us
    all_to_all x8, starting transfers between devices, trade(): lax.all_to_all(value, axes, 0, 0, axis_index_groups=teams, tiled=True)  37.1 us
    ppermute x8, starting transfers between devices, section_swap(): return lax.ppermute(value, 'section', [(0, 1), (1, 0)])  30.8 us
  transfers between devices with their start and end apart: 63, of which 38 were waited for; matrix products, arithmetic and copies ran while one was open for 17% of the time, Pallas kernels for 21%

profile of v2, /device:TPU:0, one launch (start us, length us, event | category | flops | bytes accessed | tf_op | source)
XLA Modules:
  0.0 793.8 jit_solution(7021789296442967500)
XLA Ops:
  12.1 5.0 collective-permute-start.19
  17.1 6.2 collective-permute-done.19
  24.8 5.0 collective-permute-start.2
  35.1 2.3 collective-permute-done.1
  38.4 6.8 collective-permute-start.3
  54.8 8.0 %collective-permute-done.5 = bf16[2,48,640]{2,1,0:T(8,128)(2,1)S(1)} collective-permute-done((bf16[2,48,640]{2,1,0:T(8,128)(2,1)S(1)}, bf16[2,48,640]{2,1,0:T(8,128)(2,1)S(1)}, u32[]{:S(2)}, u32[]{:S(2)}) %collective-permute-start.5) | collective-permute-done | bytes 122912 | tf_op jit(solution)/shard_map/ppermute | solution.py:905
  66.2 22.4 %collective-permute-start.11 = (bf16[4,48,640]{2,1,0:T(8,128)(2,1)S(1)}, bf16[4,48,640]{2,1,0:T(8,128)(2,1)S(1)}, u32[]{:S(2)}, u32[]{:S(2)}) collective-permute-start(bf16[4,48,640]{2,1,0:T(8,128)(2,1)S(1)} %bitcast.301), channel_id=1, source_target_pairs={{0,16},{16,0},{1,17},{17,1},{2,18},{18,2},{3,19},{19,3},{4,20},{20... | collective-permute-start | bytes 737288 | tf_op jit(solution)/shard_map/ppermute | solution.py:909
  88.6 3.2 collective-permute-start.7
  92.1 6.9 collective-permute-done.11
  99.3 15.5 %collective-permute-done.7 = bf16[8,48,640]{2,1,0:T(8,128)(2,1)S(1)} collective-permute-done((bf16[8,48,640]{2,1,0:T(8,128)(2,1)S(1)}, bf16[8,48,640]{2,1,0:T(8,128)(2,1)S(1)}, u32[]{:S(2)}, u32[]{:S(2)}) %collective-permute-start.7) | collective-permute-done | bytes 491552 | tf_op jit(solution)/shard_map/ppermute | solution.py:909
  129.8 3.9 collective-permute-start.14
  133.7 4.2 all-to-all-start
  140.0 3.5 collective-permute-start.15
  143.5 22.0 %collective-permute-done.22 = bf16[48,768]{1,0:T(8,128)(2,1)S(1)} collective-permute-done((bf16[48,768]{1,0:T(8,128)(2,1)S(1)}, bf16[48,768]{1,0:T(8,128)(2,1)S(1)}, u32[]{:S(2)}, u32[]{:S(2)}) %collective-permute-start.22) | collective-permute-done | bytes 73760 | tf_op jit(solution)/shard_map/ppermute | solution.py:905
  166.9 15.5 %collective-permute-done.23 = bf16[2,48,768]{2,1,0:T(8,128)(2,1)S(1)} collective-permute-done((bf16[2,48,768]{2,1,0:T(8,128)(2,1)S(1)}, bf16[2,48,768]{2,1,0:T(8,128)(2,1)S(1)}, u32[]{:S(2)}, u32[]{:S(2)}) %collective-permute-start.23) | collective-permute-done | bytes 147488 | tf_op jit(solution)/shard_map/ppermute | solution.py:905
  186.2 3.0 collective-permute-done.24
  197.8 14.0 %collective-permute-done.25 = bf16[8,48,768]{2,1,0:T(8,128)(2,1)} collective-permute-done((bf16[8,48,768]{2,1,0:T(8,128)(2,1)S(1)}, bf16[8,48,768]{2,1,0:T(8,128)(2,1)}, u32[]{:S(2)}, u32[]{:S(2)}) %collective-permute-start.25) | collective-permute-done | bytes 589856 | tf_op jit(solution)/shard_map/ppermute | solution.py:909
  211.8 2.5 maximum_select_fusion.6
  216.6 2.5 maximum_select_fusion.5
  219.0 2.6 maximum_select_fusion.7
  221.6 33.8 %attend.2 = (f32[16,48,256]{2,1,0:T(8,128)S(1)}, bf16[16,48,256]{2,1,0:T(8,128)(2,1)}, f32[16,1,256]{2,1,0:T(1,128)S(1)}) custom-call(bf16[16,144,256]{2,1,0:T(8,128)(2,1)S(1)} %all-to-all-done.x_ref, f32[16,1,256]{2,1,0:T(1,128)S(1)} %reshape.1046.docs_ref), custom_call_target="tpu_custom_call" | custom-call | flops 35000000512 | bytes 3145728 | tf_op jit(solution)/shard_map/attend/pallas_call | solution.py:682
  257.0 3.8 all-to-all-start.1
  262.8 2.9 maximum_select_fusion
  273.0 5.9 multiply_convert_fusion.1
  283.1 2.5 fusion.25
  287.7 3.7 all-to-all-start.2
  293.9 23.6 %all-to-all-done.2.x_ref = bf16[16,144,256]{2,1,0:T(8,128)(2,1)S(1)} async-done(((bf16[16,144,256]{2,1,0:T(8,128)(2,1)}), bf16[16,144,256]{2,1,0:T(8,128)(2,1)S(1)}, u32[]{:S(2)}, u32[]{:S(2)}) %all-to-all-start.2) | async-done | bytes 1179680 | tf_op jit(solution)/shard_map/all_to_all | solution.py:980
  317.5 33.8 %attend.3 = (f32[16,48,256]{2,1,0:T(8,128)S(1)}, bf16[16,48,256]{2,1,0:T(8,128)(2,1)}, f32[16,1,256]{2,1,0:T(1,128)S(1)}) custom-call(bf16[16,144,256]{2,1,0:T(8,128)(2,1)S(1)} %all-to-all-done.2.x_ref, f32[16,1,256]{2,1,0:T(1,128)S(1)} %reshape.1046.docs_ref), custom_call_target="tpu_custom_call" | custom-call | flops 35000000512 | bytes 3145728 | tf_op jit(solution)/shard_map/attend/pallas_call | solution.py:682
  352.8 9.2 %all-to-all-start.3 = ((bf16[16,48,256]{2,1,0:T(8,128)(2,1)}), bf16[16,48,256]{2,1,0:T(8,128)(2,1)}, u32[]{:S(2)}, u32[]{:S(2)}) async-start(bf16[16,48,256]{2,1,0:T(8,128)(2,1)} %get-tuple-element.32), calls=%async_computation.3 | async-start | bytes 786432 | tf_op jit(solution)/shard_map/all_to_all | solution.py:980
  375.5 6.6 convert_reduce_fusion
  382.1 3.8 fusion
  391.1 3.6 all-to-all-start.4
  404.5 49.8 %attend_back.2 = bf16[16,144,256]{2,1,0:T(8,128)(2,1)} custom-call(bf16[16,144,256]{2,1,0:T(8,128)(2,1)} %copy-done.1, bf16[16,48,256]{2,1,0:T(8,128)(2,1)} %copy-done.56, f32[16,1,256]{2,1,0:T(1,128)} %copy-done.2, f32[16,48,256]{2,1,0:T(8,128)} %copy-done.4, f32[16,1,256]{2,1,0:T(1,128)} %copy-done.6), custom_call_target="tpu_custom_call" | custom-call | flops 49999998976 | bytes 6291456 | tf_op jit(solution)/shard_map/attend_back/pallas_call | solution.py:781
  454.3 4.1 all-to-all-start.5
  460.5 2.7 fusion.83
  463.2 2.6 fusion.79
  465.8 37.2 %all-to-all-done.5 = bf16[16,144,256]{2,1,0:T(8,128)(2,1)S(1)} async-done(((bf16[16,144,256]{2,1,0:T(8,128)(2,1)}), bf16[16,144,256]{2,1,0:T(8,128)(2,1)S(1)}, u32[]{:S(2)}, u32[]{:S(2)}) %all-to-all-start.5) | async-done | bytes 1179680 | tf_op jit(solution)/shard_map/all_to_all | solution.py:980
  506.2 3.1 fusion.126
  510.7 2.4 convolution_convert_fusion.2
  524.1 4.2 all-to-all-start.6
  531.1 3.7 fusion.1
  542.6 4.6 all-to-all-done.6.g_ref
  547.3 49.9 %attend_back.3 = bf16[16,144,256]{2,1,0:T(8,128)(2,1)} custom-call(bf16[16,144,256]{2,1,0:T(8,128)(2,1)} %copy-done, bf16[16,48,256]{2,1,0:T(8,128)(2,1)} %all-to-all-done.6.g_ref, f32[16,1,256]{2,1,0:T(1,128)} %copy-done.2, f32[16,48,256]{2,1,0:T(8,128)} %copy-done.3, f32[16,1,256]{2,1,0:T(1,128)} %copy-done.5), custom_call_target="tpu_custom_call" | custom-call | flops 49999998976 | bytes 6291456 | tf_op jit(solution)/shard_map/attend_back/pallas_call | solution.py:781
  597.2 4.4 all-to-all-start.7
  607.5 2.6 fusion.68
  611.7 4.9 collective-permute-start.28
  617.4 14.1 %collective-permute-done.39 = bf16[4,48,2304]{2,1,0:T(8,128)(2,1)S(1)} collective-permute-done((bf16[4,48,2304]{2,1,0:T(8,128)(2,1)S(1)}, bf16[4,48,2304]{2,1,0:T(8,128)(2,1)S(1)}, u32[]{:S(2)}, u32[]{:S(2)}) %collective-permute-start.39) | collective-permute-done | bytes 884768 | tf_op jit(solution)/shard_map/ppermute | solution.py:905
  632.9 18.8 %all-to-all-done.7 = bf16[16,144,256]{2,1,0:T(8,128)(2,1)} async-done(((bf16[16,144,256]{2,1,0:T(8,128)(2,1)}), bf16[16,144,256]{2,1,0:T(8,128)(2,1)}, u32[]{:S(2)}, u32[]{:S(2)}) %all-to-all-start.7) | async-done | bytes 1179680 | tf_op jit(solution)/shard_map/all_to_all | solution.py:980
  651.7 2.3 fusion.52
  655.4 4.4 fusion.134
  662.9 4.0 collective-permute-done.47
  667.0 5.1 collective-permute-done.48
  672.2 4.2 collective-permute-done.49
  676.8 3.5 collective-permute-done.50
  683.0 10.4 %collective-permute-done.40 = bf16[4,48,1152]{2,1,0:T(8,128)(2,1)S(1)} collective-permute-done((bf16[4,48,1152]{2,1,0:T(8,128)(2,1)S(1)}, bf16[4,48,1152]{2,1,0:T(8,128)(2,1)S(1)}, u32[]{:S(2)}, u32[]{:S(2)}) %collective-permute-start.40) | collective-permute-done | bytes 442400 | tf_op jit(solution)/shard_map/ppermute | solution.py:909
  693.7 13.3 %collective-permute-done.34 = bf16[8,48,1152]{2,1,0:T(8,128)(2,1)S(1)} collective-permute-done((bf16[8,48,1152]{2,1,0:T(8,128)(2,1)S(1)}, bf16[8,48,1152]{2,1,0:T(8,128)(2,1)S(1)}, u32[]{:S(2)}, u32[]{:S(2)}) %collective-permute-start.34) | collective-permute-done | bytes 884768 | tf_op jit(solution)/shard_map/ppermute | solution.py:909
  707.6 8.2 %collective-permute-done.35 = bf16[4,48,1152]{2,1,0:T(8,128)(2,1)S(1)} collective-permute-done((bf16[4,48,1152]{2,1,0:T(8,128)(2,1)S(1)}, bf16[4,48,1152]{2,1,0:T(8,128)(2,1)S(1)}, u32[]{:S(2)}, u32[]{:S(2)}) %collective-permute-start.35) | collective-permute-done | bytes 442400 | tf_op jit(solution)/shard_map/ppermute | solution.py:905
  717.7 7.3 collective-permute-done.36
  731.3 24.8 %collective-permute-start.30 = (bf16[256,768]{1,0:T(8,128)(2,1)S(1)}, bf16[256,768]{1,0:T(8,128)(2,1)S(1)}, u32[]{:S(2)}, u32[]{:S(2)}) collective-permute-start(bf16[256,768]{1,0:T(8,128)(2,1)S(1)} %copy-done.9), channel_id=1, source_target_pairs={{0,16},{1,17},{2,18},{3,19},{4,20},{5,21},{6,22},{7,23},{8,24},{9,... | collective-permute-start | bytes 1179656 | tf_op jit(solution)/shard_map/ppermute | solution.py:983
  756.1 2.5 collective-permute-done.31
  758.7 4.7 collective-permute-done.43
  765.6 4.8 collective-permute-start.45
  773.9 5.4 collective-permute-done.44
  784.4 2.6 broadcast_in_dim_reshape.8
  (573 shorter events, 172.1 us)
Async XLA Ops:
  7.2 265.8 %all-gather.3.cloned.1.call-start = ((), (), s32[]{:S(2)}) async-start(), calls=%async_computation.10 | async-start | bytes 9732096 | tf_op jit(solution)/shard_map/all_gather | solution.py:1028
  12.1 11.2 %collective-permute-start.19 = (bf16[24,6144]{1,0:T(8,128)(2,1)S(1)}, bf16[24,6144]{1,0:T(8,128)(2,1)S(1)}, u32[]{:S(2)}, u32[]{:S(2)}) collective-permute-start(bf16[24,6144]{1,0:T(8,128)(2,1)S(1)} %slice.441), channel_id=1, source_target_pairs={{0,16},{1,17},{2,18},{3,19},{4,20},{5,21},{6,22},{7,23},{8,24},{9,... | collective-permute-start | bytes 884744 | tf_op jit(solution)/shard_map/ppermute | solution.py:983
  24.1 337.9 %all-gather.5.cloned.1.call-start = ((), (), s32[]{:S(2)}) async-start(), calls=%async_computation.11 | async-start | bytes 10948608 | tf_op jit(solution)/shard_map/all_gather | solution.py:1029
  24.8 10.3 %collective-permute-start.2 = (bf16[48,384]{1,0:T(8,128)(2,1)}, bf16[48,384]{1,0:T(8,128)(2,1)}, u32[]{:S(2)}, u32[]{:S(2)}) collective-permute-start(bf16[48,384]{1,0:T(8,128)(2,1)} %slice.420), channel_id=1, source_target_pairs={{0,16},{1,17},{2,18},{3,19},{4,20},{5,21},{6,22},{7,23},{8,24},{9,... | collective-permute-start | bytes 110600 | tf_op jit(solution)/shard_map/ppermute | solution.py:983
  30.5 6.9 collective-permute-start.1
  31.9 59.9 %collective-permute-start = (bf16[256,768]{1,0:T(8,128)(2,1)S(1)}, bf16[256,768]{1,0:T(8,128)(2,1)S(1)}, u32[]{:S(2)}, u32[]{:S(2)}) collective-permute-start(bf16[256,768]{1,0:T(8,128)(2,1)S(1)} %select_bitcast_fusion.4), channel_id=1, source_target_pairs={{16,24},{17,25},{18,26},{19,27},{20,28},{21,29},{22,30},{23,31},{2... | collective-permute-start | bytes 1179656 | tf_op jit(solution)/shard_map/ppermute | solution.py:983
  33.4 30.9 %collective-permute-start.21 = (bf16[24,6912]{1,0:T(8,128)(2,1)}, bf16[24,6912]{1,0:T(8,128)(2,1)S(1)}, u32[]{:S(2)}, u32[]{:S(2)}) collective-permute-start(bf16[24,6912]{1,0:T(8,128)(2,1)} %slice.452), channel_id=1, source_target_pairs={{16,0},{17,1},{18,2},{19,3},{20,4},{21,5},{22,6},{23,7},{24,8},{25... | collective-permute-start | bytes 995336 | tf_op jit(solution)/shard_map/ppermute | solution.py:983
  38.4 8.9 %collective-permute-start.3 = (bf16[48,1152]{1,0:T(8,128)(2,1)S(1)}, bf16[48,1152]{1,0:T(8,128)(2,1)S(1)}, u32[]{:S(2)}, u32[]{:S(2)}) collective-permute-start(bf16[48,1152]{1,0:T(8,128)(2,1)S(1)} %get-tuple-element.117), channel_id=1, source_target_pairs={{0,16},{1,17},{2,18},{3,19},{4,20},{5,21},{6,22},{7,23},{8,24},{9,... | collective-permute-start | bytes 331784 | tf_op jit(solution)/shard_map/ppermute | solution.py:983
  47.3 4.3 collective-permute-start.9
  49.0 4.9 collective-permute-start.4
  51.6 13.5 %collective-permute-start.10 = (bf16[2,48,640]{2,1,0:T(8,128)(2,1)S(1)}, bf16[2,48,640]{2,1,0:T(8,128)(2,1)}, u32[]{:S(2)}, u32[]{:S(2)}) collective-permute-start(bf16[2,48,640]{2,1,0:T(8,128)(2,1)S(1)} %maximum_select_fusion.29), channel_id=1, source_target_pairs={{0,8},{1,9},{2,10},{3,11},{4,12},{5,13},{6,14},{7,15},{8,0},{9,1},... | collective-permute-start | bytes 368648 | tf_op jit(solution)/shard_map/ppermute | solution.py:905
  53.9 8.9 %collective-permute-start.5 = (bf16[2,48,640]{2,1,0:T(8,128)(2,1)S(1)}, bf16[2,48,640]{2,1,0:T(8,128)(2,1)S(1)}, u32[]{:S(2)}, u32[]{:S(2)}) collective-permute-start(bf16[2,48,640]{2,1,0:T(8,128)(2,1)S(1)} %maximum_select_fusion.27), channel_id=1, source_target_pairs={{0,8},{1,9},{2,10},{3,11},{4,12},{5,13},{6,14},{7,15},{8,0},{9,1},... | collective-permute-start | bytes 368648 | tf_op jit(solution)/shard_map/ppermute | solution.py:905
  62.8 25.8 %collective-permute-start.6 = (bf16[4,48,640]{2,1,0:T(8,128)(2,1)S(1)}, bf16[4,48,640]{2,1,0:T(8,128)(2,1)S(1)}, u32[]{:S(2)}, u32[]{:S(2)}) collective-permute-start(bf16[4,48,640]{2,1,0:T(8,128)(2,1)S(1)} %bitcast.318), channel_id=1, source_target_pairs={{0,2},{1,3},{2,0},{3,1},{4,6},{5,7},{6,4},{7,5},{8,10},{9,11},{10,... | collective-permute-start | bytes 737288 | tf_op jit(solution)/shard_map/ppermute | solution.py:905
  66.2 32.8 %collective-permute-start.11 = (bf16[4,48,640]{2,1,0:T(8,128)(2,1)S(1)}, bf16[4,48,640]{2,1,0:T(8,128)(2,1)S(1)}, u32[]{:S(2)}, u32[]{:S(2)}) collective-permute-start(bf16[4,48,640]{2,1,0:T(8,128)(2,1)S(1)} %bitcast.301), channel_id=1, source_target_pairs={{0,16},{16,0},{1,17},{17,1},{2,18},{18,2},{3,19},{19,3},{4,20},{20... | collective-permute-start | bytes 737288 | tf_op jit(solution)/shard_map/ppermute | solution.py:909
  88.6 26.1 %collective-permute-start.7 = (bf16[8,48,640]{2,1,0:T(8,128)(2,1)S(1)}, bf16[8,48,640]{2,1,0:T(8,128)(2,1)S(1)}, u32[]{:S(2)}, u32[]{:S(2)}) collective-permute-start(bf16[8,48,640]{2,1,0:T(8,128)(2,1)S(1)} %bitcast.283), channel_id=1, source_target_pairs={{0,16},{16,0},{1,17},{17,1},{2,18},{18,2},{3,19},{19,3},{4,20},{20... | collective-permute-start | bytes 1474568 | tf_op jit(solution)/shard_map/ppermute | solution.py:909
  92.1 178.8 %copy-start.10 = (bf16[256,768]{1,0:T(8,128)(2,1)}, bf16[256,768]{1,0:T(8,128)(2,1)S(1)}, u32[]{:S(2)}) copy-start(bf16[256,768]{1,0:T(8,128)(2,1)S(1)} %get-tuple-element.96) | copy-start | bytes 1179652
  99.1 17.7 %collective-permute-start.12 = (bf16[4,48,1280]{2,1,0:T(8,128)(2,1)S(1)}, bf16[4,48,1280]{2,1,0:T(8,128)(2,1)S(1)}, u32[]{:S(2)}, u32[]{:S(2)}) collective-permute-start(bf16[4,48,1280]{2,1,0:T(8,128)(2,1)S(1)} %maximum_select_fusion.16), channel_id=1, source_target_pairs={{0,2},{1,3},{2,0},{3,1},{4,6},{5,7},{6,4},{7,5},{8,10},{9,11},{10,... | collective-permute-start | bytes 1474568 | tf_op jit(solution)/shard_map/ppermute | solution.py:905
  115.0 2.6 collective-permute-start.8
  116.9 3.0 collective-permute-start.13
  129.8 10.1 %collective-permute-start.14 = (bf16[48,768]{1,0:T(8,128)(2,1)S(1)}, bf16[48,768]{1,0:T(8,128)(2,1)S(1)}, u32[]{:S(2)}, u32[]{:S(2)}) collective-permute-start(bf16[48,768]{1,0:T(8,128)(2,1)S(1)} %get-tuple-element.125), channel_id=1, source_target_pairs={{0,4},{1,5},{2,6},{3,7},{4,0},{5,1},{6,2},{7,3},{8,12},{9,13},{10,... | collective-permute-start | bytes 221192 | tf_op jit(solution)/shard_map/ppermute | solution.py:905
  133.7 87.9 %all-to-all-start = ((bf16[16,144,256]{2,1,0:T(8,128)(2,1)}), bf16[16,144,256]{2,1,0:T(8,128)(2,1)S(1)}, u32[]{:S(2)}, u32[]{:S(2)}) async-start(bf16[16,144,256]{2,1,0:T(8,128)(2,1)} %fusion.49), calls=%async_computation | async-start | bytes 2359296 | tf_op jit(solution)/shard_map/all_to_all | solution.py:980
  137.9 27.5 %collective-permute-start.22 = (bf16[48,768]{1,0:T(8,128)(2,1)S(1)}, bf16[48,768]{1,0:T(8,128)(2,1)S(1)}, u32[]{:S(2)}, u32[]{:S(2)}) collective-permute-start(bf16[48,768]{1,0:T(8,128)(2,1)S(1)} %get-tuple-element.124), channel_id=1, source_target_pairs={{0,4},{1,5},{2,6},{3,7},{4,0},{5,1},{6,2},{7,3},{8,12},{9,13},{10,... | collective-permute-start | bytes 221192 | tf_op jit(solution)/shard_map/ppermute | solution.py:905
  140.0 44.0 %collective-permute-start.15 = (bf16[2,48,768]{2,1,0:T(8,128)(2,1)S(1)}, bf16[2,48,768]{2,1,0:T(8,128)(2,1)S(1)}, u32[]{:S(2)}, u32[]{:S(2)}) collective-permute-start(bf16[2,48,768]{2,1,0:T(8,128)(2,1)S(1)} %maximum_select_fusion.23), channel_id=1, source_target_pairs={{0,8},{1,9},{2,10},{3,11},{4,12},{5,13},{6,14},{7,15},{8,0},{9,1},... | collective-permute-start | bytes 442376 | tf_op jit(solution)/shard_map/ppermute | solution.py:905
  165.5 16.9 %collective-permute-start.23 = (bf16[2,48,768]{2,1,0:T(8,128)(2,1)S(1)}, bf16[2,48,768]{2,1,0:T(8,128)(2,1)S(1)}, u32[]{:S(2)}, u32[]{:S(2)}) collective-permute-start(bf16[2,48,768]{2,1,0:T(8,128)(2,1)S(1)} %maximum_select_fusion.25), channel_id=1, source_target_pairs={{0,8},{1,9},{2,10},{3,11},{4,12},{5,13},{6,14},{7,15},{8,0},{9,1},... | collective-permute-start | bytes 442376 | tf_op jit(solution)/shard_map/ppermute | solution.py:905
  182.4 6.8 collective-permute-start.24
  184.0 9.0 %collective-permute-start.16 = (bf16[4,48,768]{2,1,0:T(8,128)(2,1)S(1)}, bf16[4,48,768]{2,1,0:T(8,128)(2,1)S(1)}, u32[]{:S(2)}, u32[]{:S(2)}) collective-permute-start(bf16[4,48,768]{2,1,0:T(8,128)(2,1)S(1)} %bitcast.297), channel_id=1, source_target_pairs={{0,16},{16,0},{1,17},{17,1},{2,18},{18,2},{3,19},{19,3},{4,20},{20... | collective-permute-start | bytes 884744 | tf_op jit(solution)/shard_map/ppermute | solution.py:909
  189.2 22.6 %collective-permute-start.25 = (bf16[8,48,768]{2,1,0:T(8,128)(2,1)S(1)}, bf16[8,48,768]{2,1,0:T(8,128)(2,1)}, u32[]{:S(2)}, u32[]{:S(2)}) collective-permute-start(bf16[8,48,768]{2,1,0:T(8,128)(2,1)S(1)} %bitcast.272), channel_id=1, source_target_pairs={{0,16},{16,0},{1,17},{17,1},{2,18},{18,2},{3,19},{19,3},{4,20},{20... | collective-permute-start | bytes 1769480 | tf_op jit(solution)/shard_map/ppermute | solution.py:909
  193.9 22.6 %collective-permute-start.17 = (bf16[4,48,1536]{2,1,0:T(8,128)(2,1)}, bf16[4,48,1536]{2,1,0:T(8,128)(2,1)}, u32[]{:S(2)}, u32[]{:S(2)}) collective-permute-start(bf16[4,48,1536]{2,1,0:T(8,128)(2,1)} %maximum_select_fusion.12), channel_id=1, source_target_pairs={{0,2},{1,3},{2,0},{3,1},{4,6},{5,7},{6,4},{7,5},{8,10},{9,11},{10,... | collective-permute-start | bytes 1769480 | tf_op jit(solution)/shard_map/ppermute | solution.py:905
  214.3 46.4 %collective-permute-start.26 = (bf16[8,48,1536]{2,1,0:T(8,128)(2,1)}, bf16[8,48,1536]{2,1,0:T(8,128)(2,1)}, u32[]{:S(2)}, u32[]{:S(2)}) collective-permute-start(bf16[8,48,1536]{2,1,0:T(8,128)(2,1)} %maximum_select_fusion.6), channel_id=1, source_target_pairs={{0,1},{1,0},{2,3},{3,2},{4,5},{5,4},{6,7},{7,6},{8,9},{9,8},{10,11... | collective-permute-start | bytes 3538952 | tf_op jit(solution)/shard_map/ppermute | solution.py:905
  219.0 43.8 %collective-permute-start.18 = (bf16[8,48,1536]{2,1,0:T(8,128)(2,1)}, bf16[8,48,1536]{2,1,0:T(8,128)(2,1)}, u32[]{:S(2)}, u32[]{:S(2)}) collective-permute-start(bf16[8,48,1536]{2,1,0:T(8,128)(2,1)} %bitcast.48), channel_id=1, source_target_pairs={{0,1},{1,0},{2,3},{3,2},{4,5},{5,4},{6,7},{7,6},{8,9},{9,8},{10,11... | collective-permute-start | bytes 3538952 | tf_op jit(solution)/shard_map/ppermute | solution.py:905
  257.0 13.0 %all-to-all-start.1 = ((bf16[16,48,256]{2,1,0:T(8,128)(2,1)}), bf16[16,48,256]{2,1,0:T(8,128)(2,1)S(1)}, u32[]{:S(2)}, u32[]{:S(2)}) async-start(bf16[16,48,256]{2,1,0:T(8,128)(2,1)} %get-tuple-element.30), calls=%async_computation.1 | async-start | bytes 786432 | tf_op jit(solution)/shard_map/all_to_all | solution.py:980
  287.7 29.8 %all-to-all-start.2 = ((bf16[16,144,256]{2,1,0:T(8,128)(2,1)}), bf16[16,144,256]{2,1,0:T(8,128)(2,1)S(1)}, u32[]{:S(2)}, u32[]{:S(2)}) async-start(bf16[16,144,256]{2,1,0:T(8,128)(2,1)} %fusion.50), calls=%async_computation.2 | async-start | bytes 2359296 | tf_op jit(solution)/shard_map/all_to_all | solution.py:980
  291.5 0.7 collective-permute-start.20
  352.8 18.4 %all-to-all-start.3 = ((bf16[16,48,256]{2,1,0:T(8,128)(2,1)}), bf16[16,48,256]{2,1,0:T(8,128)(2,1)}, u32[]{:S(2)}, u32[]{:S(2)}) async-start(bf16[16,48,256]{2,1,0:T(8,128)(2,1)} %get-tuple-element.32), calls=%async_computation.3 | async-start | bytes 786432 | tf_op jit(solution)/shard_map/all_to_all | solution.py:980
  391.1 12.7 %all-to-all-start.4 = ((bf16[16,48,256]{2,1,0:T(8,128)(2,1)}), bf16[16,48,256]{2,1,0:T(8,128)(2,1)S(1)}, u32[]{:S(2)}, u32[]{:S(2)}) async-start(bf16[16,48,256]{2,1,0:T(8,128)(2,1)} %fusion.71), calls=%async_computation.4 | async-start | bytes 786432 | tf_op jit(solution)/shard_map/all_to_all | solution.py:980
  394.7 369.6 %reduce-scatter.5.cloned.1.call-start = ((), (), s32[]{:S(2)}) async-start(), calls=%async_computation.13 | async-start | bytes 11280384 | tf_op jit(solution)/shard_map/reduce_scatter | solution.py:1055
  454.3 48.7 %all-to-all-start.5 = ((bf16[16,144,256]{2,1,0:T(8,128)(2,1)}), bf16[16,144,256]{2,1,0:T(8,128)(2,1)S(1)}, u32[]{:S(2)}, u32[]{:S(2)}) async-start(bf16[16,144,256]{2,1,0:T(8,128)(2,1)} %attend_back.2), calls=%async_computation.5 | async-start | bytes 2359296 | tf_op jit(solution)/shard_map/all_to_all | solution.py:980
  459.0 305.2 %collective-permute-start.27 = (bf16[256,768]{1,0:T(8,128)(2,1)}, bf16[256,768]{1,0:T(8,128)(2,1)}, u32[]{:S(2)}, u32[]{:S(2)}) collective-permute-start(bf16[256,768]{1,0:T(8,128)(2,1)} %get-tuple-element.143), channel_id=1, source_target_pairs={{16,8},{17,9},{18,10},{19,11},{20,12},{21,13},{22,14},{23,15},{24,... | collective-permute-start | bytes 1179656 | tf_op jit(solution)/shard_map/ppermute | solution.py:983
  524.1 23.2 %all-to-all-start.6 = ((bf16[16,48,256]{2,1,0:T(8,128)(2,1)}), bf16[16,48,256]{2,1,0:T(8,128)(2,1)}, u32[]{:S(2)}, u32[]{:S(2)}) async-start(bf16[16,48,256]{2,1,0:T(8,128)(2,1)} %fusion.72), calls=%async_computation.6 | async-start | bytes 786432 | tf_op jit(solution)/shard_map/all_to_all | solution.py:980
  528.3 235.9 %reduce-scatter.3.cloned.1.call-start = ((), (), s32[]{:S(2)}) async-start(), calls=%async_computation.12 | async-start | bytes 11280384 | tf_op jit(solution)/shard_map/reduce_scatter | solution.py:1055
  530.2 71.4 %collective-permute-start.38 = (bf16[8,48,2304]{2,1,0:T(8,128)(2,1)}, bf16[8,48,2304]{2,1,0:T(8,128)(2,1)}, u32[]{:S(2)}, u32[]{:S(2)}) collective-permute-start(bf16[8,48,2304]{2,1,0:T(8,128)(2,1)} %dynamic-slice_bitcast_fusion), channel_id=1, source_target_pairs={{0,1},{1,0},{2,3},{3,2},{4,5},{5,4},{6,7},{7,6},{8,9},{9,8},{10,11... | collective-permute-start | bytes 5308424 | tf_op jit(solution)/shard_map/ppermute | solution.py:905
  597.2 54.6 %all-to-all-start.7 = ((bf16[16,144,256]{2,1,0:T(8,128)(2,1)}), bf16[16,144,256]{2,1,0:T(8,128)(2,1)}, u32[]{:S(2)}, u32[]{:S(2)}) async-start(bf16[16,144,256]{2,1,0:T(8,128)(2,1)} %attend_back.3), calls=%async_computation.7 | async-start | bytes 2359296 | tf_op jit(solution)/shard_map/all_to_all | solution.py:980
  603.7 27.8 %collective-permute-start.39 = (bf16[4,48,2304]{2,1,0:T(8,128)(2,1)S(1)}, bf16[4,48,2304]{2,1,0:T(8,128)(2,1)S(1)}, u32[]{:S(2)}, u32[]{:S(2)}) collective-permute-start(bf16[4,48,2304]{2,1,0:T(8,128)(2,1)S(1)} %dynamic-slice_bitcast_fusion.2), channel_id=1, source_target_pairs={{0,2},{1,3},{2,0},{3,1},{4,6},{5,7},{6,4},{7,5},{8,10},{9,11},{10,... | collective-permute-start | bytes 2654216 | tf_op jit(solution)/shard_map/ppermute | solution.py:905
  610.1 154.1 %collective-permute-start.29 = (bf16[256,768]{1,0:T(8,128)(2,1)}, bf16[256,768]{1,0:T(8,128)(2,1)}, u32[]{:S(2)}, u32[]{:S(2)}) collective-permute-start(bf16[256,768]{1,0:T(8,128)(2,1)} %fusion.68), channel_id=1, source_target_pairs={{16,24},{17,25},{18,26},{19,27},{20,28},{21,29},{22,30},{23,31},{2... | collective-permute-start | bytes 1179656 | tf_op jit(solution)/shard_map/ppermute | solution.py:983
  611.7 152.5 %collective-permute-start.28 = (bf16[256,768]{1,0:T(8,128)(2,1)}, bf16[256,768]{1,0:T(8,128)(2,1)}, u32[]{:S(2)}, u32[]{:S(2)}) collective-permute-start(bf16[256,768]{1,0:T(8,128)(2,1)} %fusion.68), channel_id=1, source_target_pairs={{0,16},{1,17},{2,18},{3,19},{4,20},{5,21},{6,22},{7,23},{8,24},{9,... | collective-permute-start | bytes 1179656 | tf_op jit(solution)/shard_map/ppermute | solution.py:983
  660.5 2.1 collective-permute-start.46
  662.2 18.1 %collective-permute-start.33 = (bf16[8,48,2304]{2,1,0:T(8,128)(2,1)S(1)}, bf16[8,48,2304]{2,1,0:T(8,128)(2,1)S(1)}, u32[]{:S(2)}, u32[]{:S(2)}) collective-permute-start(bf16[8,48,2304]{2,1,0:T(8,128)(2,1)S(1)} %dynamic-slice_bitcast_fusion.1), channel_id=1, source_target_pairs={{0,1},{1,0},{2,3},{3,2},{4,5},{5,4},{6,7},{7,6},{8,9},{9,8},{10,11... | collective-permute-start | bytes 5308424 | tf_op jit(solution)/shard_map/ppermute | solution.py:905
  662.7 4.2 collective-permute-start.47
  666.9 5.2 collective-permute-start.48
  672.1 4.3 collective-permute-start.49
  676.4 3.9 collective-permute-start.50
  680.3 13.1 %collective-permute-start.40 = (bf16[4,48,1152]{2,1,0:T(8,128)(2,1)S(1)}, bf16[4,48,1152]{2,1,0:T(8,128)(2,1)S(1)}, u32[]{:S(2)}, u32[]{:S(2)}) collective-permute-start(bf16[4,48,1152]{2,1,0:T(8,128)(2,1)S(1)} %broadcast_select_fusion.1), channel_id=1, source_target_pairs={{0,16},{16,0},{1,17},{17,1},{2,18},{18,2},{3,19},{19,3},{4,20},{20... | collective-permute-start | bytes 1327112 | tf_op jit(solution)/shard_map/ppermute | solution.py:909
  680.9 26.1 %collective-permute-start.34 = (bf16[8,48,1152]{2,1,0:T(8,128)(2,1)S(1)}, bf16[8,48,1152]{2,1,0:T(8,128)(2,1)S(1)}, u32[]{:S(2)}, u32[]{:S(2)}) collective-permute-start(bf16[8,48,1152]{2,1,0:T(8,128)(2,1)S(1)} %broadcast_select_fusion), channel_id=1, source_target_pairs={{0,16},{16,0},{1,17},{17,1},{2,18},{18,2},{3,19},{19,3},{4,20},{20... | collective-permute-start | bytes 2654216 | tf_op jit(solution)/shard_map/ppermute | solution.py:909
  693.6 13.9 %collective-permute-start.41 = (bf16[2,48,1152]{2,1,0:T(8,128)(2,1)S(1)}, bf16[2,48,1152]{2,1,0:T(8,128)(2,1)S(1)}, u32[]{:S(2)}, u32[]{:S(2)}) collective-permute-start(bf16[2,48,1152]{2,1,0:T(8,128)(2,1)S(1)} %dynamic-slice_bitcast_fusion.4), channel_id=1, source_target_pairs={{0,8},{1,9},{2,10},{3,11},{4,12},{5,13},{6,14},{7,15},{8,0},{9,1},... | collective-permute-start | bytes 663560 | tf_op jit(solution)/shard_map/ppermute | solution.py:905
  707.4 8.4 %collective-permute-start.35 = (bf16[4,48,1152]{2,1,0:T(8,128)(2,1)S(1)}, bf16[4,48,1152]{2,1,0:T(8,128)(2,1)S(1)}, u32[]{:S(2)}, u32[]{:S(2)}) collective-permute-start(bf16[4,48,1152]{2,1,0:T(8,128)(2,1)S(1)} %dynamic-slice_bitcast_fusion.3), channel_id=1, source_target_pairs={{0,2},{1,3},{2,0},{3,1},{4,6},{5,7},{6,4},{7,5},{8,10},{9,11},{10,... | collective-permute-start | bytes 1327112 | tf_op jit(solution)/shard_map/ppermute | solution.py:905
  716.0 9.0 %collective-permute-start.36 = (bf16[2,48,1152]{2,1,0:T(8,128)(2,1)S(1)}, bf16[2,48,1152]{2,1,0:T(8,128)(2,1)S(1)}, u32[]{:S(2)}, u32[]{:S(2)}) collective-permute-start(bf16[2,48,1152]{2,1,0:T(8,128)(2,1)S(1)} %dynamic-slice_bitcast_fusion.5), channel_id=1, source_target_pairs={{0,8},{1,9},{2,10},{3,11},{4,12},{5,13},{6,14},{7,15},{8,0},{9,1},... | collective-permute-start | bytes 663560 | tf_op jit(solution)/shard_map/ppermute | solution.py:905
  716.1 10.9 %collective-permute-start.42 = (bf16[48,1152]{1,0:T(8,128)(2,1)S(1)}, bf16[48,1152]{1,0:T(8,128)(2,1)S(1)}, u32[]{:S(2)}, u32[]{:S(2)}) collective-permute-start(bf16[48,1152]{1,0:T(8,128)(2,1)S(1)} %dynamic-slice_bitcast_fusion.6), channel_id=1, source_target_pairs={{0,4},{1,5},{2,6},{3,7},{4,0},{5,1},{6,2},{7,3},{8,12},{9,13},{10,... | collective-permute-start | bytes 331784 | tf_op jit(solution)/shard_map/ppermute | solution.py:905
  725.1 4.8 collective-permute-start.37
  727.0 4.3 collective-permute-start.32
  729.9 28.7 %collective-permute-start.31 = (bf16[256,768]{1,0:T(8,128)(2,1)S(1)}, bf16[256,768]{1,0:T(8,128)(2,1)S(1)}, u32[]{:S(2)}, u32[]{:S(2)}) collective-permute-start(bf16[256,768]{1,0:T(8,128)(2,1)S(1)} %get-tuple-element.93), channel_id=1, source_target_pairs={{16,8},{17,9},{18,10},{19,11},{20,12},{21,13},{22,14},{23,15},{24,... | collective-permute-start | bytes 1179656 | tf_op jit(solution)/shard_map/ppermute | solution.py:983
  731.3 41.4 %collective-permute-start.30 = (bf16[256,768]{1,0:T(8,128)(2,1)S(1)}, bf16[256,768]{1,0:T(8,128)(2,1)S(1)}, u32[]{:S(2)}, u32[]{:S(2)}) collective-permute-start(bf16[256,768]{1,0:T(8,128)(2,1)S(1)} %copy-done.9), channel_id=1, source_target_pairs={{0,16},{1,17},{2,18},{3,19},{4,20},{5,21},{6,22},{7,23},{8,24},{9,... | collective-permute-start | bytes 1179656 | tf_op jit(solution)/shard_map/ppermute | solution.py:983
  758.6 4.7 collective-permute-start.43
  764.3 15.1 %collective-permute-start.44 = (bf16[48,6912]{1,0:T(8,128)(2,1)}, bf16[48,6912]{1,0:T(8,128)(2,1)S(1)}, u32[]{:S(2)}, u32[]{:S(2)}) collective-permute-start(bf16[48,6912]{1,0:T(8,128)(2,1)} %reduce-scatter.3.cloned.1.call-done), channel_id=1, source_target_pairs={{16,0},{17,1},{18,2},{19,3},{20,4},{21,5},{22,6},{23,7},{24,8},{25... | collective-permute-start | bytes 1990664 | tf_op jit(solution)/shard_map/ppermute | solution.py:983
  765.6 15.1 %collective-permute-start.45 = (bf16[48,6912]{1,0:T(8,128)(2,1)}, bf16[48,6912]{1,0:T(8,128)(2,1)S(1)}, u32[]{:S(2)}, u32[]{:S(2)}) collective-permute-start(bf16[48,6912]{1,0:T(8,128)(2,1)} %reduce-scatter.5.cloned.1.call-done), channel_id=1, source_target_pairs={{0,16},{1,17},{2,18},{3,19},{4,20},{5,21},{6,22},{7,23},{8,24},{9,... | collective-permute-start | bytes 1990664 | tf_op jit(solution)/shard_map/ppermute | solution.py:983
  (125 other events, 1073.6 us)
Sparse Core Ops, SparseCore 0:
  24.3 106.2 all-gather.2
  133.5 103.7 all-gather.4
  403.9 142.9 reduce-scatter.4
  550.9 146.8 reduce-scatter.2

commit v3 on v2

--- a/solution.py
+++ b/solution.py
@@ -557,6 +557,21 @@
 FIRST = (0, 16, 24, 28, 30)
 F32, BF16 = jnp.float32, jnp.bfloat16
 
+UN = 16
+MAIN = 1
+QW = 4
+TWO = False
+
+def loop(n, f, u=None):
+    u = min(u or UN, n)
+    while n % u:
+        u -= 1
+    def many(i, _):
+        for j in range(u):
+            f(i * u + j, 0)
+        return 0
+    lax.fori_loop(0, n // u, many, 0)
+
 def nt(a, b):
     return lax.dot_general(a, b, (((1,), (1,)), ((), ())), preferred_element_type=F32)
 
@@ -600,7 +615,7 @@
                 pa, pb = nn(a, grid).astype(BF16), nn(b, grid).astype(BF16)
             stack[FIRST[level] + g] = jnp.concatenate([pa, pb], axis=1)
             return 0
-        lax.fori_loop(0, BLOCKS[level], step, 0)
+        loop(BLOCKS[level], step)
 
 def marks(doc_row, away):
     ids = lax.broadcasted_iota(jnp.int32, (IDS, TOK), 0).astype(F32)
@@ -614,36 +629,32 @@
         d = docs_ref[s]
         fm[s] = jnp.concatenate([x[0:HD], marks(d, False), pad, x[HD:2 * HD], marks(d, True), pad, x[2 * HD:]], axis=0)
         return 0
-    lax.fori_loop(0, SRC, load, 0)
+    loop(SRC, load)
     pack_levels(fm)
     iden = eye(TOK)
     def turn(i, _):
         ktm[i] = nt(iden, fm[i, AUG:2 * AUG, :]).astype(BF16)
         return 0
-    lax.fori_loop(0, 31, turn, 0)
-
-    def block(i, kfirst, count):
-        q = fm[i, 0:AUG, :]
-        scores = []
-        for t in range(count):
-            scores.append(nn(ktm[kfirst + t], q))
-        top = functools.reduce(jnp.maximum, [jnp.max(s, axis=0, keepdims=True) for s in scores])
-        total = jnp.zeros((1, TOK), F32)
-        out = jnp.zeros((HD, TOK), F32)
-        for t in range(count):
-            p = jnp.exp2((scores[t] - top) * C2)
-            total = total + jnp.sum(p, axis=0, keepdims=True)
-            out = out + nn(fm[kfirst + t, 2 * AUG:2 * AUG + HD, :], p.astype(BF16))
-        part[i, 0:HD] = out
-        part[i, HD:HD + 8] = jnp.broadcast_to(total, (8, TOK))
-        part[i, HD + 8:HD + 16] = jnp.broadcast_to(top * C2, (8, TOK))
-    def main(i, _):
-        block(i, (i // 4) * 4, 4)
-        return 0
-    lax.fori_loop(0, 28, main, 0)
-    block(28, 28, 2)
-    block(29, 28, 2)
-    block(30, 30, 1)
+    loop(30, turn); turn(30, 0)
+
+    def segment(first, count):
+        for at in range(0, count, QW):
+            n = min(QW, count - at)
+            q = jnp.concatenate([fm[first + at + b, 0:AUG, :] for b in range(n)], axis=1)
+            scores = [nn(ktm[first + t], q) for t in range(count)]
+            top = functools.reduce(jnp.maximum, [jnp.max(x, axis=0, keepdims=True) for x in scores])
+            ps = [jnp.exp2((x - top) * C2) for x in scores]
+            total = functools.reduce(jnp.add, [jnp.sum(p, axis=0, keepdims=True) for p in ps])
+            p = jnp.concatenate([p.astype(BF16) for p in ps], axis=0)
+            v = jnp.concatenate([fm[first + t, 2 * AUG:2 * AUG + HD, :] for t in range(count)], axis=1)
+            out = nn(v, p)
+            for b in range(n):
+                part[first + at + b, 0:HD] = out[:, b * TOK:(b + 1) * TOK]
+                part[first + at + b, HD:HD + 8] = jnp.broadcast_to(total[:, b * TOK:(b + 1) * TOK], (8, TOK))
+                part[first + at + b, HD + 8:HD + 16] = jnp.broadcast_to(top[:, b * TOK:(b + 1) * TOK] * C2, (8, TOK))
+    loop(7, lambda i, _: segment(i * 4, 4), MAIN)
+    segment(28, 2)
+    segment(30, 1)
 
     for level in range(4, 0, -1):
         c = TOK >> level
@@ -667,7 +678,7 @@
                 part[mine, HD:HD + 8] = jnp.broadcast_to(cl * wc + ol * wo, (8, TOK))
                 part[mine, HD + 8:HD + 16] = jnp.broadcast_to(top, (8, TOK))
             return 0
-        lax.fori_loop(0, BLOCKS[level], join, 0)
+        loop(BLOCKS[level], join)
     def finish(s, _):
         own = part[s]
         l, m = own[HD:HD + 1], own[HD + 8:HD + 9]
@@ -676,7 +687,7 @@
         ob_ref[s] = out.astype(BF16)
         lse_ref[s] = m + jnp.log2(l)
         return 0
-    lax.fori_loop(0, SRC, finish, 0)
+    loop(SRC, finish)
 
 def attn_fwd(x, docs):
     return pl.pallas_call(
@@ -690,7 +701,7 @@
             pltpu.VMEM((31, HD + 16, TOK), F32),
         ],
         compiler_params=pltpu.CompilerParams(vmem_limit_bytes=50 * 2**20),
-        cost_estimate=pl.CostEstimate(flops=35 * 10**9, bytes_accessed=3 * 2**20, transcendentals=0),
+        cost_estimate=pl.CostEstimate(flops=18 * 10**9, bytes_accessed=3 * 2**20, transcendentals=0),
         name="attend",
     )(x, docs)
 
@@ -716,40 +727,34 @@
             x[HD:2 * HD], marks(d, True), ones, pad,
             x[2 * HD:], ones, pad2], axis=0)
         return 0
-    lax.fori_loop(0, SRC, load, 0)
+    loop(SRC, load)
     pack_levels(fm)
     iden = eye(TOK)
     def turn(i, _):
         tm[i] = nt(iden, fm[i]).astype(BF16)
         return 0
-    lax.fori_loop(0, 31, turn, 0)
-    def zero(i, _):
-        ek[i] = jnp.zeros((TOK, AUG), F32)
-        ev[i] = jnp.zeros((TOK, AUG), F32)
-        return 0
-    lax.fori_loop(0, 31, zero, 0)
-
-    def block(i, kfirst, count):
-        q = fm[i, 0:AUG, :]
-        g = fm[i, AUG:2 * AUG, :]
-        qt = tm[i, :, 0:AUG]
-        gt = tm[i, :, AUG:2 * AUG]
-        acc = jnp.zeros((HD, TOK), F32)
+    loop(30, turn); turn(30, 0)
+    def segment(first, count):
+        q = jnp.concatenate([fm[first + b, 0:AUG, :] for b in range(count)], axis=1)
+        g = jnp.concatenate([fm[first + b, AUG:2 * AUG, :] for b in range(count)], axis=1)
+        rows = pl.ds(first, count)
+        qt = tm[rows, :, 0:AUG].reshape(count * TOK, AUG)
+        gt = tm[rows, :, AUG:2 * AUG].reshape(count * TOK, AUG)
+        parts = []
         for t in range(count):
-            k = kfirst + t
+            k = first + t
             p = jnp.exp2(nn(tm[k, :, 2 * AUG:3 * AUG], q) * C2)
             es = (p * nn(tm[k, :, 3 * AUG:], g)).astype(BF16)
-            ev[k] += nn(p.astype(BF16), gt)
-            ek[k] += nn(es, qt)
-            acc = acc + nn(fm[k, 2 * AUG:2 * AUG + HD, :], es)
-        eq[i] = acc
-    def main(i, _):
-        block(i, (i // 4) * 4, 4)
-        return 0
-    lax.fori_loop(0, 28, main, 0)
-    block(28, 28, 2)
-    block(29, 28, 2)
-    block(30, 30, 1)
+            ev[k] = nn(p.astype(BF16), gt)
+            ek[k] = nn(es, qt)
+            parts.append(es)
+        k = jnp.concatenate([fm[first + t, 2 * AUG:2 * AUG + HD, :] for t in range(count)], axis=1)
+        out = nn(k, jnp.concatenate(parts, axis=0))
+        for b in range(count):
+            eq[first + b] = out[:, b * TOK:(b + 1) * TOK]
+    loop(7, lambda i, _: segment(i * 4, 4), MAIN)
+    segment(28, 2)
+    segment(30, 1)
 
     for level in range(4, 0, -1):
         c = TOK >> level
@@ -767,7 +772,7 @@
                     ek[mine, 2 * c * s:2 * c * s + c, :] += ek[child, half * 128 + c * s:half * 128 + c * s + c, :]
                     ev[mine, 2 * c * s:2 * c * s + c, :] += ev[child, half * 128 + c * s:half * 128 + c * s + c, :]
             return 0
-        lax.fori_loop(0, BLOCKS[level], join, 0)
+        loop(BLOCKS[level], join)
     small = (lax.broadcasted_iota(jnp.int32, (HD, AUG), 0) == lax.broadcasted_iota(jnp.int32, (HD, AUG), 1)).astype(BF16)
     def finish(s, _):
         a = (eq[s] * ROOT).astype(BF16)
@@ -775,7 +780,7 @@
         v = nt(small, ev[s].astype(BF16)).astype(BF16)
         e_ref[s] = jnp.concatenate([a, b, v], axis=0)
         return 0
-    lax.fori_loop(0, SRC, finish, 0)
+    loop(SRC, finish)
 
 def attn_bwd(x, g, docs, o, lse):
     return pl.pallas_call(
@@ -791,7 +796,7 @@
             pltpu.VMEM((31, TOK, AUG), F32),
         ],
         compiler_params=pltpu.CompilerParams(vmem_limit_bytes=56 * 2**20),
-        cost_estimate=pl.CostEstimate(flops=50 * 10**9, bytes_accessed=6 * 2**20, transcendentals=0),
+        cost_estimate=pl.CostEstimate(flops=28 * 10**9, bytes_accessed=6 * 2**20, transcendentals=0),
         name="attend_back",
     )(x, g, docs, o, lse)
 
@@ -825,15 +830,14 @@
     return (np.arange(16)[None, None, :] * 16 + residue).reshape(HEADS, TOK)
 
 
-def cube_forward(hidden, w_qkv, more, w_mlp, lines, order, docs, trade):
-    gains, biases, up_bias = lines
+def cube_forward(hidden, params, order, docs, trade):
+    w_qkv, w_out, w_mlp, gains, biases, up_bias = params
     unit_one, scale_one, normed = layer_norm(hidden, gains[0], biases[0])
     mixed = jnp.einsum("df,td->ft", w_qkv, normed, preferred_element_type=F32)
     shift = jnp.concatenate([biases[1], jnp.zeros_like(biases[1]), biases[2]])
     mixed = (mixed + shift[:, None]).astype(BF16)
     mixed = mixed.reshape(3, HEADS, HEAD_DIM, TOK).transpose(1, 0, 2, 3).reshape(HEADS, 3 * HEAD_DIM, TOK)
     mixed = jnp.einsum("hft,htu->hfu", mixed, order, preferred_element_type=F32).astype(BF16)
-    w_out, w_later, mixed = more(mixed)
     heads = trade(mixed)
     merged, merged_low, summary = attn_fwd(heads, docs)
     attended = trade(merged_low)
@@ -848,10 +852,10 @@
     for at in range(0, ff, D):
         result = result + jnp.dot(activated[:, at : at + D], w_mlp[:, ff + at : ff + at + D], preferred_element_type=F32)
     kept = (unit_one, scale_one, normed, heads, merged, summary, attended, unit_two, scale_two, normed_two, slope, activated)
-    return result.astype(BF16), kept, w_out, w_later
-
-
-def cube_backward(incoming_low, kept, params, order, docs, trade):
+    return result.astype(BF16), kept
+
+
+def cube_backward(incoming_low, kept, params, order, docs, trade, before, between, along, send_rest):
     w_qkv, w_out, w_mlp, gains, biases, up_bias = params
     unit_one, scale_one, normed, heads, merged, summary, attended, unit_two, scale_two, normed_two, slope, activated = kept
     ff = up_bias.shape[0]
@@ -874,9 +878,11 @@
         axis=1,
     )
     merged_grad = trade(merged_grad)
-    merged_grad, grad_rest = lax.optimization_barrier((merged_grad, grad_rest))
+    merged_grad, grad_rest, before = lax.optimization_barrier((merged_grad, grad_rest, before))
+    sums_rest = send_rest(grad_rest)
     back_heads = attn_bwd(heads, merged_grad, docs, merged, summary)
     mixed_grad = trade(back_heads)
+    mixed_grad, before, along = lax.optimization_barrier((mixed_grad, between(before), along))
     mixed_grad = jnp.einsum("hfu,htu->hft", mixed_grad, order, preferred_element_type=F32).astype(BF16)
     mixed_grad = mixed_grad.reshape(HEADS, 3, HEAD_DIM, TOK).transpose(1, 0, 2, 3).reshape(3 * D, TOK)
     grad_qkv = jnp.einsum("td,ft->df", normed, mixed_grad, preferred_element_type=F32).astype(BF16)
@@ -894,7 +900,7 @@
         jnp.sum(incoming, axis=0),
     ])
     grad_up_bias = jnp.sum(up_grad.astype(F32), axis=0)
-    return start_grad, (grad_qkv, grad_rest, small, grad_up_bias)
+    return start_grad, (grad_qkv, sums_rest, small, grad_up_bias), before, along
 
 
 def half_pairs(source, count):
@@ -913,25 +919,35 @@
     return (lax.axis_index("seq") >> bit) & 1
 
 
-def two_of(own, got, bit, axis):
-    return jnp.where(bit == 1, jnp.stack([got, own], axis), jnp.stack([own, got], axis))
-
-
-def two_wide(own, got, bit):
-    return jnp.where(bit == 1, jnp.concatenate([got, own], -1), jnp.concatenate([own, got], -1))
-
-
-def collect(piece, order):
-    rows = piece.shape[0]
-    now = two_of(piece, core_swap(piece, 2), place_bit(2), 0)
-    now = two_of(now, core_swap(now, 3), place_bit(3), 0).reshape(4, rows, -1)
-    for axis in order:
-        if axis == "y":
-            now = two_of(now, core_swap(now, 1), place_bit(1), 1).reshape(8, rows, -1)
-        else:
-            now = two_wide(now, section_swap(now), lax.axis_index("section"))
-    now = two_of(now, core_swap(now, 0), place_bit(0), 1)
-    return now.reshape(16 * rows, -1)
+def team(kind):
+    def device(x, z, y, c):
+        return x * 16 + z * 4 + y * 2 + c
+    two, four = range(2), range(4)
+    if kind == "plane":
+        return [[device(x, z, y, c) for x in two for y in two] for z in four for c in two]
+    return [[device(x, z, y, c) for z in four] for x in two for y in two for c in two]
+
+
+def team_trade(value, kind):
+    return lax.all_to_all(value, ("section", "seq"), 0, 0, axis_index_groups=team(kind), tiled=True)
+
+
+def collect_line(piece):
+    return team_trade(jnp.broadcast_to(piece[None], (4,) + piece.shape), "line")
+
+
+def collect_plane(now):
+    rows, columns = now.shape[1:]
+    now = team_trade(jnp.broadcast_to(now[None], (4,) + now.shape), "plane")
+    now = now.reshape(2, 2, 4, rows, columns)
+    got = core_swap(now, 0)
+    upper = place_bit(0) == 1
+    halves = []
+    for x in range(2):
+        a, b = now[x].transpose(1, 0, 2, 3), got[x].transpose(1, 0, 2, 3)
+        both = jnp.stack([jnp.where(upper, b, a), jnp.where(upper, a, b)], axis=2)
+        halves.append(both.reshape(16 * rows, columns))
+    return halves
 
 
 def plus(own, got, dtype=BF16):
@@ -945,24 +961,18 @@
     return plus(kept, core_swap(away, bit), dtype)
 
 
-def fold_wide(value):
-    half = value.shape[-1] // 2
-    lower = lax.axis_index("section") == 0
-    away = jnp.where(lower, value[..., half:], value[..., :half])
-    kept = jnp.where(lower, value[..., :half], value[..., half:])
-    return plus(kept, section_swap(away))
-
-
-def reduce_rows(partial, order):
-    rows = partial.shape[0] // 16
-    now = fold(partial.reshape(8, 2, rows, -1), 0, 1)
-    for axis in order:
-        if axis == "y":
-            now = fold(now.reshape(4, 2, rows, -1), 1, 1)
-        else:
-            now = fold_wide(now)
-    now = fold(now.reshape(2, 2, rows, -1), 3, 0)
-    return fold(now, 2, 0, F32)
+def reduce_core(partial):
+    rows, half = partial.shape[0] // 16, partial.shape[1] // 2
+    now = fold(partial.reshape(8, 2, rows, 2 * half), 0, 1).reshape(4, 2, rows, 2 * half)
+    return jnp.stack([now[:, y, :, x * half : x * half + half] for x in range(2) for y in range(2)])
+
+
+def reduce_plane(now):
+    return jnp.sum(team_trade(now, "plane").astype(F32), axis=0).astype(BF16)
+
+
+def reduce_line(now):
+    return jnp.sum(team_trade(now, "line").astype(F32), axis=0)
 
 
 def cube_body(inputs, cotangent, documents, w_qkv, w_out, w_up, w_down, norm_gains, biases, up_bias):
@@ -1001,65 +1011,37 @@
     small = jnp.concatenate([norm_gains[0], biases[0], lift]).T.astype(BF16)
     small = jnp.pad(small, ((0, 0), (0, 128 - small.shape[1])))
 
-    def column_halves(shard, source):
-        columns = shard.shape[1] // 2
-        got = across(shard[:, columns:] if source == 0 else shard[:, :columns], half_pairs(source, count))
-        if source == 0:
-            return jnp.where(lower, shard[:, :columns], got)
-        return jnp.where(lower, got, shard[:, columns:])
-
-    def row_halves(shard, source):
-        rows = shard.shape[0] // 2
-        got = across(shard[rows:] if source == 0 else shard[:rows], half_pairs(source, count))
-        if source == 0:
-            return jnp.where(lower, shard[:rows], got)
-        return jnp.where(lower, got, shard[rows:])
-
     ff = w_up.shape[2]
-    low_qkv, low_out = w_qkv[0].astype(BF16), w_out[0].astype(BF16)
-    piece = column_halves(low_qkv, 0)
-    part_a = collect(piece[:, :640], "yx")
-    part_b = collect(jnp.concatenate([piece[:, 640:], small], axis=1), "xy")
-    qkv_first = jnp.concatenate([part_a[:, :640], part_b[:, :512], part_a[:, 640:], part_b[:, 640:1152]], axis=1)
-
+    low_qkv = w_qkv[0].astype(BF16)
+    columns = low_qkv.shape[1] // 2
+    got = across(low_qkv[:, columns:], half_pairs(0, count))
+    piece = jnp.where(lower, low_qkv[:, :columns], got)
+    line = collect_line(jnp.concatenate([piece, small], axis=1))
+    parts = collect_plane(line)
+    qkv_first = jnp.concatenate([part[:, :columns] for part in parts], axis=1)
+
+    piece, w_up, w_down = lax.optimization_barrier((piece, w_up, w_down))
     up_shard = w_up[0].astype(BF16).reshape(wide, count, 4, wide).transpose(0, 2, 1, 3).reshape(wide, ff)
     down_shard = w_down[0].astype(BF16).reshape(4, wide, D).transpose(1, 0, 2).reshape(wide, 4 * D)
-    shard = jnp.concatenate([up_shard, down_shard, low_out], axis=1)
-    mlp_first = lax.all_gather(row_halves(shard[:, : 2 * ff], 0), ("seq", "section"), axis=0, tiled=True)
-    rest_final = lax.all_gather(row_halves(shard, 1), ("seq", "section"), axis=0, tiled=True)
-    piece = jnp.concatenate([column_halves(low_qkv, 1), column_halves(low_out, 0)], axis=1)
+    shard = jnp.concatenate([up_shard, down_shard, w_out[0].astype(BF16), low_qkv], axis=1)
+    rows, rest = wide // 2, 2 * ff + D
+    got = section_swap(jnp.where(lower, shard[rows:], shard[:rows]))
+    near = jnp.concatenate([jnp.where(lower, shard[:rows, :rest], got[:, :rest]), jnp.where(lower, got, shard[rows:])[:, rest:]], axis=1)
+    far = jnp.where(lower, got[:, :rest], shard[rows:, :rest])
+    near, far, line = lax.optimization_barrier((near, far, line))
+    near = lax.all_gather(near, ("seq", "section"), axis=0, tiled=True)
+    rest_final = lax.all_gather(far, ("seq", "section"), axis=0, tiled=True)
+    rest_first, qkv_final = near[:, :rest], near[:, rest:]
 
     def lines(columns):
         values = columns[:, :12].astype(F32).T
         return values[:2], values[2:8], values[8:].reshape(ff)
 
-    def second_weights(after):
-        later, after = lax.optimization_barrier((piece, after))
-        part_a = collect(later[:, :768], "yx")
-        part_b = collect(later[:, 768:], "xy")
-        qkv = jnp.concatenate([part_a[:, :768], part_b[:, :384], part_a[:, 768:], part_b[:, 768:1152]], axis=1)
-        return jnp.concatenate([part_b[:, 384:768], part_b[:, 1152:]], axis=1), qkv, after
-
-    lines_first, lines_final = lines(part_b[:, 512:640]), lines(part_b[:, 1152:])
-    first, kept_first, out_first, qkv_final = cube_forward(
-        hidden.astype(F32), qkv_first, second_weights, mlp_first, lines_first, order, docs, trade
-    )
-    out_final = rest_final[:, 2 * ff :]
-    final, kept_final, _, _ = cube_forward(
-        first.astype(F32), qkv_final, lambda after: (out_final, None, after), rest_final, lines_final, order, docs, trade
-    )
-    params_final = (qkv_final, out_final, rest_final) + lines_final
-    grad_final, terms_final = cube_backward(own_rows(cotangent), kept_final, params_final, order, docs, trade)
-
-    def scattered(partial):
-        return lax.psum_scatter(partial, "seq", scatter_dimension=0, tiled=True)
-
-    sent, qkv_term = lax.optimization_barrier((grad_final.astype(BF16), terms_final[0]))
-    rest_final = scattered(terms_final[1])
-    params_first = (qkv_first, out_first, mlp_first) + lines_first
-    grad_first, terms_first = cube_backward(sent, kept_first, params_first, order, docs, trade)
-    rest_first = scattered(terms_first[1])
-
+    lines_first, lines_final = lines(parts[0][:, columns:]), lines(parts[1][:, columns:])
+    params_first = (qkv_first, rest_first[:, 2 * ff :], rest_first) + lines_first
+    params_final = (qkv_final, rest_final[:, 2 * ff :], rest_final) + lines_final
+    first, kept_first = cube_forward(hidden.astype(F32), params_first, order, docs, trade)
+    final, kept_final = cube_forward(first.astype(F32), params_final, order, docs, trade)
     def shared_out(value_first, value_final):
         far = across(value_first, [(count + j, j ^ half) for j in range(count)])
         near = across(value_final, half_pairs(0, count))
@@ -1069,23 +1051,38 @@
     def placed(mine, other):
         return jnp.where(micro_id == 0, jnp.stack([mine, other]), jnp.stack([other, mine]))[None]
 
-    outs = shared_out(first, final)
-    backs = shared_out(grad_first.astype(BF16), sent)
-    qkv_first = reduce_rows(terms_first[0], "xy")
-    qkv_final = reduce_rows(qkv_term, "yx")
+    def scattered(partial):
+        return lax.psum_scatter(partial, ("seq", "section"), scatter_dimension=0, tiled=True)
+
+    start_back, merged = lax.optimization_barrier((own_rows(cotangent), kept_final[4]))
+    kept_final = kept_final[:4] + (merged,) + kept_final[5:]
+    grad_final, terms_final, _, _ = cube_backward(
+        start_back, kept_final, params_final, order, docs, trade, None, lambda now: now, None, scattered
+    )
+    rest_final = terms_final[1]
+    sent, qkv_final = lax.optimization_barrier((grad_final.astype(BF16), terms_final[0]))
+    near = across(sent, half_pairs(0, count))
+    beside = across(sent, [(count + j, count + (j ^ half)) for j in range(count)])
+    grad_first, terms_first, qkv_final, along = cube_backward(
+        sent, kept_first, params_first, order, docs, trade,
+        reduce_core(qkv_final), reduce_plane, (rest_final, shared_out(first, final), near, beside), scattered,
+    )
+    rest_final, outs, near, beside = along
 
     def upright(rows, wide_row):
         return jnp.concatenate([rows, wide_row.reshape(4, D)]).T
 
     smalls = jnp.concatenate([upright(*terms_first[2:]), upright(*terms_final[2:])], axis=1)
-    smalls = fold(smalls.reshape(8, 2, wide, 24), 0, 1, F32)
-    smalls = fold(smalls.reshape(4, 2, wide, 24), 1, 1, F32)
-    smalls = fold(smalls.reshape(2, 2, wide, 24), 3, 0, F32)
-    smalls = fold(smalls, 2, 0, F32)
-    smalls = smalls + section_swap(smalls)
+    smalls = fold(smalls.reshape(8, 2, wide, 24), 0, 1).reshape(4, 2, wide, 24)
+    smalls = jnp.stack([smalls[:, 0], smalls[:, 1]] * 2)
+    smalls = jnp.pad(smalls, ((0, 0), (0, 0), (0, 0), (0, 128 - 24)))
+    now = jnp.concatenate([reduce_core(terms_first[0]), smalls], axis=3)
+    now = reduce_line(reduce_plane(now))
+    qkv_first, smalls = now[:, :-128], now[:, -128:-104]
     smalls = jnp.where(lower, smalls[:, :12], smalls[:, 12:]).T
-
-    grad_first, outs, rest_first, rest_final = lax.optimization_barrier((grad_first, outs, rest_first, rest_final))
+    qkv_final = reduce_line(qkv_final)
+    rest_first = terms_first[1]
+    backs = across(grad_first.astype(BF16), [(count + j, j ^ half) for j in range(count)]), near, beside
     far, near, beside = outs
     layer_outputs = placed(jnp.where(lower, first, near), jnp.where(lower, far, beside))
     far, near, beside = backs
@@ -1093,16 +1090,10 @@
         jnp.where(lower, grad_first, near.astype(F32)), jnp.where(lower, far, beside).astype(F32)
     )
 
-    def finished(part_first, part_final):
-        got_final = across(part_final, half_pairs(0, count))
-        got_first = across(part_first, half_pairs(1, count))
-        return jnp.where(
-            lower,
-            part_first.astype(F32) + got_first.astype(F32),
-            part_final.astype(F32) + got_final.astype(F32),
-        )
-
-    rest = finished(rest_first, rest_final)
+    away = section_swap(jnp.where(lower, rest_final, rest_first))
+    rest = jnp.where(
+        lower, jnp.concatenate([rest_first, away]), jnp.concatenate([away, rest_final])
+    ).astype(F32)
     away = section_swap(jnp.where(lower, qkv_final, qkv_first).astype(BF16)).astype(F32)
     qkv = jnp.where(
         lower, jnp.concatenate([qkv_first, away], axis=1), jnp.concatenate([away, qkv_final], axis=1)

time: 800 us -> 724 us (0.905)
  Pallas kernels: 167 us -> 91.6 us
  waiting for transfers between devices: 283 us -> 212 us
  blocking collectives: 0 us -> 28.5 us
  local copies, waits for them, and re-layouts: 36.6 us -> 59.3 us
  starting transfers between devices: 153 us -> 165 us
    ppermute x28 -> x4, waiting for transfers between devices: 103 us -> 2.81 us  [core_swap(): return lax.ppermute(value, 'seq', [(j, j ^ 1 << bit) for j in range(16)])]
    all_to_all x0 -> x5, starting transfers between devices: none -> 64.1 us  [team_trade(): lax.all_to_all(value, ('section', 'seq'), 0, 0, axis_index_groups=team(ki...]
    ppermute x8 -> x3, waiting for transfers between devices: 70.5 us -> 15.4 us  [section_swap(): return lax.ppermute(value, 'section', [(0, 1), (1, 0)])]
    reduce_scatter x2, waiting for transfers between devices: 0.04 us -> 51.7 us  [scattered(): lax.psum_scatter(partial, ('seq', 'section'), scatter_dimension=0, tiled=...]
    pallas_call x2, Pallas kernels: 99.7 us -> 56.2 us  [attn_bwd(): pl.pallas_call(bwd_kernel, out_shape=jax.ShapeDtypeStruct((SRC, 3 * HD, T...]
    ppermute x15 -> x9, starting transfers between devices: 61.5 us -> 24.6 us  [across(): return lax.ppermute(value, axes, pairs)]
    all_to_all x8, starting transfers between devices: 37.1 us -> 71.2 us  [trade(): lax.all_to_all(value, axes, 0, 0, axis_index_groups=teams, tiled=True)]
    pallas_call x2, Pallas kernels: 67.7 us -> 35.3 us  [attn_fwd(): pl.pallas_call(functools.partial(fwd_kernel, kc=256), out_shape=(jax.Shap...]
  transfers between devices with their start and end apart: 63 -> 33, of which waited for: 38 -> 15; matrix products, arithmetic and copies ran while one was open for 17% -> 23% of each run, Pallas kernels for 21% -> 13%
where the time goes in v3:
time: 724 us; the launch traced here: 713 us
  waiting for transfers between devices  212 us (29%)
  starting transfers between devices  165 us (23%)
  matrix products  102 us (14%)
  Pallas kernels  91.6 us (13%)
  local copies, waits for them, and re-layouts  59.3 us (8%)
  other arithmetic  37.9 us (5%)
  blocking collectives  28.5 us (4%)
  between operations  16.1 us (2%)
    all_to_all x8, waiting for transfers between devices, trade(): lax.all_to_all(value, axes, 0, 0, axis_index_groups=teams, tiled=True)  92.6 us
    all_to_all x8, starting transfers between devices, trade(): lax.all_to_all(value, axes, 0, 0, axis_index_groups=teams, tiled=True)  71.2 us
    all_to_all x5, starting transfers between devices, team_trade(): lax.all_to_all(value, ('section', 'seq'), 0, 0, axis_index_groups=team(ki...  64.1 us
    pallas_call x2, Pallas kernels, attn_bwd(): pl.pallas_call(bwd_kernel, out_shape=jax.ShapeDtypeStruct((SRC, 3 * HD, T...  56.2 us
    reduce_scatter x2, waiting for transfers between devices, scattered(): lax.psum_scatter(partial, ('seq', 'section'), scatter_dimension=0, tiled=...  51.7 us
    pallas_call x2, Pallas kernels, attn_fwd(): pl.pallas_call(functools.partial(fwd_kernel, kc=256), out_shape=(jax.Shap...  35.3 us
    ppermute x9, waiting for transfers between devices, across(): return lax.ppermute(value, axes, pairs)  29.9 us
    all_to_all x1, blocking collectives, team_trade(): lax.all_to_all(value, ('section', 'seq'), 0, 0, axis_index_groups=team(ki...  28.5 us
  transfers between devices with their start and end apart: 33, of which 15 were waited for; matrix products, arithmetic and copies ran while one was open for 23% of the time, Pallas kernels for 13%

profile of v3, /device:TPU:0, one launch (start us, length us, event | category | flops | bytes accessed | tf_op | source)
XLA Modules:
  0.0 712.9 jit_solution(16543682299480954333)
XLA Ops:
  8.3 4.8 collective-permute-start.1
  18.6 4.9 all-to-all-start
  27.6 9.7 %collective-permute-done.3 = bf16[24,9216]{1,0:T(8,128)(2,1)S(1)} collective-permute-done((bf16[24,9216]{1,0:T(8,128)(2,1)S(1)}, bf16[24,9216]{1,0:T(8,128)(2,1)S(1)}, u32[]{:S(2)}, u32[]{:S(2)}) %collective-permute-start.3) | collective-permute-done | bytes 442400 | tf_op jit(solution)/shard_map/ppermute | solution.py:915
  39.9 28.5 %all_to_all.70 = bf16[4,4,48,1280]{3,2,1,0:T(8,128)(2,1)S(1)} all-to-all(bf16[4,4,48,1280]{3,2,1,0:T(8,128)(2,1)S(1)} %broadcast_in_dim.11), channel_id=1, replica_groups={{0,2,16,18},{1,3,17,19},{4,6,20,22},{5,7,21,23},{8,10,24,26},{9,11,25,2..., dimensions={0} | all-to-all | bytes 3932160 | tf_op jit(solution)/shard_map/all_to_all | solution.py:932
  69.7 2.8 collective-permute-done.2
  77.0 2.1 slice_reduce_fusion
  81.4 2.0 fusion.54
  83.4 39.6 %all-to-all-start.2 = ((bf16[16,144,256]{2,1,0:T(8,128)(2,1)}), bf16[16,144,256]{2,1,0:T(8,128)(2,1)S(1)}, u32[]{:S(2)}, u32[]{:S(2)}) async-start(bf16[16,144,256]{2,1,0:T(8,128)(2,1)} %fusion.54), calls=%async_computation.2 | async-start | bytes 2359296 | tf_op jit(solution)/shard_map/all_to_all | solution.py:990
  124.1 33.2 %all-to-all-done.2.x_ref = bf16[16,144,256]{2,1,0:T(8,128)(2,1)S(1)} async-done(((bf16[16,144,256]{2,1,0:T(8,128)(2,1)}), bf16[16,144,256]{2,1,0:T(8,128)(2,1)S(1)}, u32[]{:S(2)}, u32[]{:S(2)}) %all-to-all-start.2) | async-done | bytes 1179680 | tf_op jit(solution)/shard_map/all_to_all | solution.py:990
  157.3 17.7 %attend.2 = (f32[16,48,256]{2,1,0:T(8,128)S(1)}, bf16[16,48,256]{2,1,0:T(8,128)(2,1)}, f32[16,1,256]{2,1,0:T(1,128)S(1)}) custom-call(bf16[16,144,256]{2,1,0:T(8,128)(2,1)S(1)} %all-to-all-done.2.x_ref, f32[16,1,256]{2,1,0:T(1,128)S(1)} %reshape.423.docs_ref), custom_call_target="tpu_custom_call" | custom-call | flops 17999998976 | bytes 3145728 | tf_op jit(solution)/shard_map/attend/pallas_call | solution.py:693
  176.5 3.6 all-to-all-start.3
  180.4 8.9 %all-to-all-done.3 = bf16[16,48,256]{2,1,0:T(8,128)(2,1)S(1)} async-done(((bf16[16,48,256]{2,1,0:T(8,128)(2,1)}), bf16[16,48,256]{2,1,0:T(8,128)(2,1)S(1)}, u32[]{:S(2)}, u32[]{:S(2)}) %all-to-all-start.3) | async-done | bytes 393248 | tf_op jit(solution)/shard_map/all_to_all | solution.py:990
  190.2 2.0 fusion.180
  192.5 6.7 multiply_convert_fusion.1
  203.3 2.0 fusion.55
  205.3 3.7 all-to-all-start.4
  210.8 31.8 %all-to-all-done.4.x_ref = bf16[16,144,256]{2,1,0:T(8,128)(2,1)S(1)} async-done(((bf16[16,144,256]{2,1,0:T(8,128)(2,1)}), bf16[16,144,256]{2,1,0:T(8,128)(2,1)S(1)}, u32[]{:S(2)}, u32[]{:S(2)}) %all-to-all-start.4) | async-done | bytes 1179680 | tf_op jit(solution)/shard_map/all_to_all | solution.py:990
  242.6 17.7 %attend.3 = (f32[16,48,256]{2,1,0:T(8,128)S(1)}, bf16[16,48,256]{2,1,0:T(8,128)(2,1)}, f32[16,1,256]{2,1,0:T(1,128)S(1)}) custom-call(bf16[16,144,256]{2,1,0:T(8,128)(2,1)S(1)} %all-to-all-done.4.x_ref, f32[16,1,256]{2,1,0:T(1,128)S(1)} %reshape.423.docs_ref), custom_call_target="tpu_custom_call" | custom-call | flops 17999998976 | bytes 3145728 | tf_op jit(solution)/shard_map/attend/pallas_call | solution.py:693
  261.8 4.9 all-to-all-start.5
  266.7 11.0 %all-gather.5.cloned.1.call-done = bf16[768,6912]{1,0:T(8,128)(2,1)} async-done(((bf16[24,6912]{1,0:T(8,128)(2,1)}), bf16[768,6912]{1,0:T(8,128)(2,1)}) %all-gather.5.cloned.1.call-update) | async-done | bytes 10616848 | tf_op jit(solution)/shard_map/all_gather | solution.py:1033
  279.5 2.7 fusion.82
  282.1 2.7 fusion.85
  284.8 2.7 fusion.88
  288.4 2.0 fusion.181
  290.8 5.7 convert_reduce_fusion
  296.5 3.8 fusion
  300.3 2.1 multiply_reduce_fusion
  305.6 6.2 all-to-all-start.6
  321.0 28.1 %attend_back.2 = bf16[16,144,256]{2,1,0:T(8,128)(2,1)} custom-call(bf16[16,144,256]{2,1,0:T(8,128)(2,1)} %copy-done.1, bf16[16,48,256]{2,1,0:T(8,128)(2,1)} %all-to-all-done.6.g_ref, f32[16,1,256]{2,1,0:T(1,128)} %copy-done.2, f32[16,48,256]{2,1,0:T(8,128)} %copy-done.4, f32[16,1,256]{2,1,0:T(1,128)} %copy-done.6), custom_call_target="tpu_custom_call" | custom-call | flops 28000000000 | bytes 6291456 | tf_op jit(solution)/shard_map/attend_back/pallas_call | solution.py:786
  349.1 4.5 all-to-all-start.7
  353.6 17.6 %all-to-all-done.7 = bf16[16,144,256]{2,1,0:T(8,128)(2,1)S(1)} async-done(((bf16[16,144,256]{2,1,0:T(8,128)(2,1)}), bf16[16,144,256]{2,1,0:T(8,128)(2,1)S(1)}, u32[]{:S(2)}, u32[]{:S(2)}) %all-to-all-start.7) | async-done | bytes 1179680 | tf_op jit(solution)/shard_map/all_to_all | solution.py:990
  373.4 4.8 fusion.124
  378.9 2.8 convolution_convert_fusion.2
  385.2 1.9 fusion.96
  387.8 2.3 convert_reduce_fusion.1
  390.1 2.1 multiply_reduce_fusion.1
  396.2 4.4 all-to-all-start.8
  403.2 3.8 fusion.1
  418.4 4.1 all-to-all-start.10
  422.5 28.1 %attend_back.3 = bf16[16,144,256]{2,1,0:T(8,128)(2,1)} custom-call(bf16[16,144,256]{2,1,0:T(8,128)(2,1)} %copy-done, bf16[16,48,256]{2,1,0:T(8,128)(2,1)} %all-to-all-done.8.g_ref, f32[16,1,256]{2,1,0:T(1,128)} %copy-done.2, f32[16,48,256]{2,1,0:T(8,128)} %copy-done.3, f32[16,1,256]{2,1,0:T(1,128)} %copy-done.5), custom_call_target="tpu_custom_call" | custom-call | flops 28000000000 | bytes 6291456 | tf_op jit(solution)/shard_map/attend_back/pallas_call | solution.py:786
  450.6 2.9 all-to-all-done.10
  453.6 4.4 all-to-all-start.9
  459.4 1.9 convolution_add_fusion.5
  465.0 2.5 fusion.71
  468.3 8.9 %collective-permute-start.7 = (bf16[256,768]{1,0:T(8,128)(2,1)}, bf16[256,768]{1,0:T(8,128)(2,1)}, u32[]{:S(2)}, u32[]{:S(2)}) collective-permute-start(bf16[256,768]{1,0:T(8,128)(2,1)} %fusion.71), channel_id=1, source_target_pairs={{0,16},{1,17},{2,18},{3,19},{4,20},{5,21},{6,22},{7,23},{8,24},{9,... | collective-permute-start | bytes 1179656 | tf_op jit(solution)/shard_map/ppermute | solution.py:993
  478.6 4.5 collective-permute-start.9
  486.1 2.3 convert_reduce_fusion.2
  489.6 3.7 collective-permute-done.9
  493.5 2.3 fusion.57
  496.8 2.6 convolution_convert_fusion
  512.3 2.7 concatenate.133
  517.9 5.2 fusion.132
  525.7 2.0 concatenate.132
  531.1 1.9 constant_dynamic-slice_fusion.1
  534.1 5.3 all-to-all-start.13
  542.8 2.0 fusion.27
  547.3 5.2 all-to-all-done.13
  552.4 45.9 %all-to-all-start.11 = ((bf16[4,4,48,1280]{3,2,1,0:T(8,128)(2,1)}), bf16[4,4,48,1280]{3,2,1,0:T(8,128)(2,1)S(1)}, u32[]{:S(2)}, u32[]{:S(2)}) async-start(bf16[4,4,48,1280]{3,2,1,0:T(8,128)(2,1)} %fusion.53), calls=%async_computation.12 | async-start | bytes 3932160 | tf_op jit(solution)/shard_map/all_to_all | solution.py:932
  602.7 26.2 %collective-permute-done.11 = bf16[256,768]{1,0:T(8,128)(2,1)S(1)} collective-permute-done((bf16[256,768]{1,0:T(8,128)(2,1)S(1)}, bf16[256,768]{1,0:T(8,128)(2,1)S(1)}, u32[]{:S(2)}, u32[]{:S(2)}) %collective-permute-start.11) | collective-permute-done | bytes 393248 | tf_op jit(solution)/shard_map/ppermute | solution.py:993
  632.6 3.9 all-to-all-start.12
  636.6 51.7 %reduce-scatter.5.cloned.1.call-done = bf16[24,6912]{1,0:T(8,128)(2,1)} async-done(((bf16[768,6912]{1,0:T(8,128)(2,1)}), bf16[24,6912]{1,0:T(8,128)(2,1)}) %reduce-scatter.5.cloned.1.call-update) | async-done | bytes 331792 | tf_op jit(solution)/shard_map/reduce_scatter | solution.py:1055
  688.3 2.5 collective-permute-start.15
  693.3 5.7 collective-permute-done.14
  703.3 2.6 broadcast_in_dim_reshape.8
  (425 shorter events, 128.0 us)
Async XLA Ops:
  8.3 8.1 %collective-permute-start.1 = (bf16[48,1152]{1,0:T(8,128)(2,1)S(1)}, bf16[48,1152]{1,0:T(8,128)(2,1)S(1)}, u32[]{:S(2)}, u32[]{:S(2)}) collective-permute-start(bf16[48,1152]{1,0:T(8,128)(2,1)S(1)} %slice.429), channel_id=1, source_target_pairs={{0,16},{1,17},{2,18},{3,19},{4,20},{5,21},{6,22},{7,23},{8,24},{9,... | collective-permute-start | bytes 331784 | tf_op jit(solution)/shard_map/ppermute | solution.py:993
  18.6 20.4 %all-to-all-start = ((bf16[4,48,1280]{2,1,0:T(8,128)(2,1)}), bf16[4,48,1280]{2,1,0:T(8,128)(2,1)S(1)}, u32[]{:S(2)}, u32[]{:S(2)}) async-start(bf16[4,48,1280]{2,1,0:T(8,128)(2,1)} %broadcast_in_dim.10), calls=%async_computation | async-start | bytes 983040 | tf_op jit(solution)/shard_map/all_to_all | solution.py:932
  23.5 166.7 %all-gather.3.cloned.1.call-start = ((), (), s32[]{:S(2)}) async-start(), calls=%async_computation.16 | async-start | bytes 14598144 | tf_op jit(solution)/shard_map/all_gather | solution.py:1032
  26.0 11.4 %collective-permute-start.3 = (bf16[24,9216]{1,0:T(8,128)(2,1)S(1)}, bf16[24,9216]{1,0:T(8,128)(2,1)S(1)}, u32[]{:S(2)}, u32[]{:S(2)}) collective-permute-start(bf16[24,9216]{1,0:T(8,128)(2,1)S(1)} %get-tuple-element.180), channel_id=1, source_target_pairs={{0,16},{16,0},{1,17},{17,1},{2,18},{18,2},{3,19},{19,3},{4,20},{20... | collective-permute-start | bytes 1327112 | tf_op jit(solution)/shard_map/ppermute | solution.py:915
  39.0 238.7 %all-gather.5.cloned.1.call-start = ((), (), s32[]{:S(2)}) async-start(), calls=%async_computation.17 | async-start | bytes 10948608 | tf_op jit(solution)/shard_map/all_gather | solution.py:1033
  39.9 28.5 %copy-start.28 = (bf16[2,256,768]{2,1,0:T(8,128)(2,1)S(1)}, bf16[2,256,768]{2,1,0:T(8,128)(2,1)}, u32[]{:S(2)}) copy-start(bf16[2,256,768]{2,1,0:T(8,128)(2,1)} %param.11) | copy-start | bytes 2359300
  68.4 4.1 collective-permute-start.2
  68.5 0.7 collective-permute-start
  69.4 120.7 %copy-start.13 = (bf16[256,768]{1,0:T(8,128)(2,1)}, bf16[256,768]{1,0:T(8,128)(2,1)S(1)}, u32[]{:S(2)}) copy-start(bf16[256,768]{1,0:T(8,128)(2,1)S(1)} %get-tuple-element.162) | copy-start | bytes 1179652
  77.0 115.5 %copy-start.73 = (f32[768]{0:T(1024)}, f32[768]{0:T(1024)S(1)}, u32[]{:S(2)}) copy-start(f32[768]{0:T(1024)S(1)} %get-tuple-element.143) | copy-start | bytes 9220
  77.0 115.5 %copy-start.87 = (f32[768]{0:T(1024)}, f32[768]{0:T(1024)S(1)}, u32[]{:S(2)}) copy-start(f32[768]{0:T(1024)S(1)} %get-tuple-element.142) | copy-start | bytes 9220
  79.1 122.5 %copy-start.51 = (f32[768]{0:T(1024)}, f32[768]{0:T(1024)S(1)}, u32[]{:S(2)}) copy-start(f32[768]{0:T(1024)S(1)} %get-tuple-element.140) | copy-start | bytes 9220
  79.1 122.5 %copy-start.58 = (f32[768]{0:T(1024)}, f32[768]{0:T(1024)S(1)}, u32[]{:S(2)}) copy-start(f32[768]{0:T(1024)S(1)} %get-tuple-element.139) | copy-start | bytes 9220
  81.4 41.7 %copy-start.55 = (s32[2,4096]{1,0:T(2,128)S(1)}, s32[2,4096]{1,0:T(2,128)}, u32[]{:S(2)}) copy-start(s32[2,4096]{1,0:T(2,128)} %param.13) | copy-start | bytes 98308
  83.4 73.9 %all-to-all-start.2 = ((bf16[16,144,256]{2,1,0:T(8,128)(2,1)}), bf16[16,144,256]{2,1,0:T(8,128)(2,1)S(1)}, u32[]{:S(2)}, u32[]{:S(2)}) async-start(bf16[16,144,256]{2,1,0:T(8,128)(2,1)} %fusion.54), calls=%async_computation.2 | async-start | bytes 2359296 | tf_op jit(solution)/shard_map/all_to_all | solution.py:990
  124.1 118.5 %copy-start.2 = (f32[16,1,256]{2,1,0:T(1,128)}, f32[16,1,256]{2,1,0:T(1,128)S(1)}, u32[]{:S(2)}) copy-start(f32[16,1,256]{2,1,0:T(1,128)S(1)} %reshape.423.docs_ref) | copy-start | bytes 49156
  157.3 17.7 %copy-start = (bf16[16,144,256]{2,1,0:T(8,128)(2,1)}, bf16[16,144,256]{2,1,0:T(8,128)(2,1)S(1)}, u32[]{:S(2)}) copy-start(bf16[16,144,256]{2,1,0:T(8,128)(2,1)S(1)} %all-to-all-done.2.x_ref) | copy-start | bytes 3538948
  176.5 12.8 %all-to-all-start.3 = ((bf16[16,48,256]{2,1,0:T(8,128)(2,1)}), bf16[16,48,256]{2,1,0:T(8,128)(2,1)S(1)}, u32[]{:S(2)}, u32[]{:S(2)}) async-start(bf16[16,48,256]{2,1,0:T(8,128)(2,1)} %get-tuple-element.36), calls=%async_computation.3 | async-start | bytes 786432 | tf_op jit(solution)/shard_map/all_to_all | solution.py:990
  201.3 176.8 %copy-start.10 = (bf16[256,768]{1,0:T(8,128)(2,1)}, bf16[256,768]{1,0:T(8,128)(2,1)S(1)}, u32[]{:S(2)}) copy-start(bf16[256,768]{1,0:T(8,128)(2,1)S(1)} %get-tuple-element.199) | copy-start | bytes 1179652
  205.3 37.3 %all-to-all-start.4 = ((bf16[16,144,256]{2,1,0:T(8,128)(2,1)}), bf16[16,144,256]{2,1,0:T(8,128)(2,1)S(1)}, u32[]{:S(2)}, u32[]{:S(2)}) async-start(bf16[16,144,256]{2,1,0:T(8,128)(2,1)} %fusion.55), calls=%async_computation.4 | async-start | bytes 2359296 | tf_op jit(solution)/shard_map/all_to_all | solution.py:990
  209.1 0.7 collective-permute-start.4
  242.6 17.7 %copy-start.1 = (bf16[16,144,256]{2,1,0:T(8,128)(2,1)}, bf16[16,144,256]{2,1,0:T(8,128)(2,1)S(1)}, u32[]{:S(2)}) copy-start(bf16[16,144,256]{2,1,0:T(8,128)(2,1)S(1)} %all-to-all-done.4.x_ref) | copy-start | bytes 3538948
  261.8 25.7 %all-to-all-start.5 = ((bf16[16,48,256]{2,1,0:T(8,128)(2,1)}), bf16[16,48,256]{2,1,0:T(8,128)(2,1)S(1)}, u32[]{:S(2)}, u32[]{:S(2)}) async-start(bf16[16,48,256]{2,1,0:T(8,128)(2,1)} %get-tuple-element.43), calls=%async_computation.5 | async-start | bytes 786432 | tf_op jit(solution)/shard_map/all_to_all | solution.py:990
  296.5 20.3 %copy-start.36 = (bf16[256,3072]{1,0:T(8,128)(2,1)}, bf16[256,3072]{1,0:T(8,128)(2,1)S(1)}, u32[]{:S(2)}) copy-start(bf16[256,3072]{1,0:T(8,128)(2,1)S(1)} %get-tuple-element.167) | copy-start | bytes 4718596
  305.6 15.4 %all-to-all-start.6 = ((bf16[16,48,256]{2,1,0:T(8,128)(2,1)}), bf16[16,48,256]{2,1,0:T(8,128)(2,1)}, u32[]{:S(2)}, u32[]{:S(2)}) async-start(bf16[16,48,256]{2,1,0:T(8,128)(2,1)} %fusion.74), calls=%async_computation.6 | async-start | bytes 786432 | tf_op jit(solution)/shard_map/all_to_all | solution.py:990
  311.7 181.7 %reduce-scatter.3.cloned.1.call-start = ((), (), s32[]{:S(2)}) async-start(), calls=%async_computation.18 | async-start | bytes 10948608 | tf_op jit(solution)/shard_map/reduce_scatter | solution.py:1055
  349.1 22.2 %all-to-all-start.7 = ((bf16[16,144,256]{2,1,0:T(8,128)(2,1)}), bf16[16,144,256]{2,1,0:T(8,128)(2,1)S(1)}, u32[]{:S(2)}, u32[]{:S(2)}) async-start(bf16[16,144,256]{2,1,0:T(8,128)(2,1)} %attend_back.2), calls=%async_computation.7 | async-start | bytes 2359296 | tf_op jit(solution)/shard_map/all_to_all | solution.py:990
  353.5 19.8 %copy-start.52 = (f32[768]{0:T(1024)S(1)}, f32[768]{0:T(1024)}, u32[]{:S(2)}) copy-start(f32[768]{0:T(1024)} %copy-done.51) | copy-start | bytes 9220
  353.6 19.8 %copy-start.64 = (f32[256]{0:T(256)S(1)}, f32[256]{0:T(256)}, u32[]{:S(2)}) copy-start(f32[256]{0:T(256)} %copy-done.63) | copy-start | bytes 3076
  353.6 19.8 %copy-start.77 = (f32[256]{0:T(256)S(1)}, f32[256]{0:T(256)}, u32[]{:S(2)}) copy-start(f32[256]{0:T(256)} %copy-done.76) | copy-start | bytes 3076
  371.2 16.0 %slice-start.3 = ((s8[14155776]{0:T(1024)(128)(4,1)}), s8[4194304]{0:T(1024)(128)(4,1)S(1)}, s32[]{:S(2)}) async-start(s8[14155776]{0:T(1024)(128)(4,1)} %bitcast.237), calls=%async_computation.23 | async-start | bytes 8388608
  396.2 22.2 %all-to-all-start.8 = ((bf16[16,48,256]{2,1,0:T(8,128)(2,1)}), bf16[16,48,256]{2,1,0:T(8,128)(2,1)}, u32[]{:S(2)}, u32[]{:S(2)}) async-start(bf16[16,48,256]{2,1,0:T(8,128)(2,1)} %fusion.75), calls=%async_computation.8 | async-start | bytes 786432 | tf_op jit(solution)/shard_map/all_to_all | solution.py:990
  400.6 287.6 %reduce-scatter.5.cloned.1.call-start = ((), (), s32[]{:S(2)}) async-start(), calls=%async_computation.19 | async-start | bytes 10948608 | tf_op jit(solution)/shard_map/reduce_scatter | solution.py:1055
  402.2 12.7 %collective-permute-start.5 = (bf16[8,48,2304]{2,1,0:T(8,128)(2,1)}, bf16[8,48,2304]{2,1,0:T(8,128)(2,1)}, u32[]{:S(2)}, u32[]{:S(2)}) collective-permute-start(bf16[8,48,2304]{2,1,0:T(8,128)(2,1)} %dynamic-slice_bitcast_fusion.1), channel_id=1, source_target_pairs={{0,1},{1,0},{2,3},{3,2},{4,5},{5,4},{6,7},{7,6},{8,9},{9,8},{10,11... | collective-permute-start | bytes 5308424 | tf_op jit(solution)/shard_map/ppermute | solution.py:911
  418.4 35.1 %all-to-all-start.10 = ((bf16[4,4,48,1152]{3,2,1,0:T(8,128)(2,1)}), bf16[4,4,48,1152]{3,2,1,0:T(8,128)(2,1)S(1)}, u32[]{:S(2)}, u32[]{:S(2)}) async-start(bf16[4,4,48,1152]{3,2,1,0:T(8,128)(2,1)} %pad_maximum_fusion.5), calls=%async_computation.10 | async-start | bytes 3538944 | tf_op jit(solution)/shard_map/all_to_all | solution.py:932
  422.5 35.5 %copy-start.11 = (bf16[256,768]{1,0:T(8,128)(2,1)S(1)}, bf16[256,768]{1,0:T(8,128)(2,1)}, u32[]{:S(2)}) copy-start(bf16[256,768]{1,0:T(8,128)(2,1)} %copy-done.10) | copy-start | bytes 1179652
  453.6 39.9 %all-to-all-start.9 = ((bf16[16,144,256]{2,1,0:T(8,128)(2,1)}), bf16[16,144,256]{2,1,0:T(8,128)(2,1)}, u32[]{:S(2)}, u32[]{:S(2)}) async-start(bf16[16,144,256]{2,1,0:T(8,128)(2,1)} %attend_back.3), calls=%async_computation.9 | async-start | bytes 2359296 | tf_op jit(solution)/shard_map/all_to_all | solution.py:990
  458.0 31.5 %collective-permute-start.6 = (bf16[256,768]{1,0:T(8,128)(2,1)S(1)}, bf16[256,768]{1,0:T(8,128)(2,1)S(1)}, u32[]{:S(2)}, u32[]{:S(2)}) collective-permute-start(bf16[256,768]{1,0:T(8,128)(2,1)S(1)} %copy-done.11), channel_id=1, source_target_pairs={{16,8},{17,9},{18,10},{19,11},{20,12},{21,13},{22,14},{23,15},{24,... | collective-permute-start | bytes 1179656 | tf_op jit(solution)/shard_map/ppermute | solution.py:993
  463.1 14.1 %copy-start.9 = (bf16[256,768]{1,0:T(8,128)(2,1)S(1)}, bf16[256,768]{1,0:T(8,128)(2,1)}, u32[]{:S(2)}) copy-start(bf16[256,768]{1,0:T(8,128)(2,1)} %copy-done.7) | copy-start | bytes 1179652
  463.1 20.0 %copy-start.83 = (f32[3072]{0:T(1024)S(1)}, f32[3072]{0:T(1024)}, u32[]{:S(2)}) copy-start(f32[3072]{0:T(1024)} %get-tuple-element.155) | copy-start | bytes 36868
  463.2 20.6 %copy-start.93 = (f32[768]{0:T(1024)S(1)}, f32[768]{0:T(1024)}, u32[]{:S(2)}) copy-start(f32[768]{0:T(1024)} %get-tuple-element.119) | copy-start | bytes 9220
  463.2 21.2 %copy-start.92 = (f32[768]{0:T(1024)S(1)}, f32[768]{0:T(1024)}, u32[]{:S(2)}) copy-start(f32[768]{0:T(1024)} %get-tuple-element.131) | copy-start | bytes 9220
  463.2 21.8 %copy-start.79 = (f32[768]{0:T(1024)S(1)}, f32[768]{0:T(1024)}, u32[]{:S(2)}) copy-start(f32[768]{0:T(1024)} %get-tuple-element.157) | copy-start | bytes 9220
  463.2 22.3 %copy-start.78 = (f32[768]{0:T(1024)S(1)}, f32[768]{0:T(1024)}, u32[]{:S(2)}) copy-start(f32[768]{0:T(1024)} %get-tuple-element.183) | copy-start | bytes 9220
  467.5 25.9 %copy-start.71 = (s32[16,256]{1,0:T(8,128)S(1)}, s32[16,256]{1,0:T(8,128)}, u32[]{:S(2)}) copy-start(s32[16,256]{1,0:T(8,128)} %constant.99.clone) | copy-start | bytes 49156
  467.5 22.0 %collective-permute-start.8 = (bf16[256,768]{1,0:T(8,128)(2,1)}, bf16[256,768]{1,0:T(8,128)(2,1)S(1)}, u32[]{:S(2)}, u32[]{:S(2)}) collective-permute-start(bf16[256,768]{1,0:T(8,128)(2,1)} %fusion.71), channel_id=1, source_target_pairs={{16,24},{17,25},{18,26},{19,27},{20,28},{21,29},{22,30},{23,31},{2... | collective-permute-start | bytes 1179656 | tf_op jit(solution)/shard_map/ppermute | solution.py:993
  468.3 21.3 %collective-permute-start.7 = (bf16[256,768]{1,0:T(8,128)(2,1)}, bf16[256,768]{1,0:T(8,128)(2,1)}, u32[]{:S(2)}, u32[]{:S(2)}) collective-permute-start(bf16[256,768]{1,0:T(8,128)(2,1)} %fusion.71), channel_id=1, source_target_pairs={{0,16},{1,17},{2,18},{3,19},{4,20},{5,21},{6,22},{7,23},{8,24},{9,... | collective-permute-start | bytes 1179656 | tf_op jit(solution)/shard_map/ppermute | solution.py:993
  477.2 12.4 %collective-permute-start.10 = (bf16[256,768]{1,0:T(8,128)(2,1)S(1)}, bf16[256,768]{1,0:T(8,128)(2,1)}, u32[]{:S(2)}, u32[]{:S(2)}) collective-permute-start(bf16[256,768]{1,0:T(8,128)(2,1)S(1)} %copy-done.9), channel_id=1, source_target_pairs={{16,24},{17,25},{18,26},{19,27},{20,28},{21,29},{22,30},{23,31},{2... | collective-permute-start | bytes 1179656 | tf_op jit(solution)/shard_map/ppermute | solution.py:993
  478.6 14.7 %collective-permute-start.9 = (bf16[256,768]{1,0:T(8,128)(2,1)S(1)}, bf16[256,768]{1,0:T(8,128)(2,1)}, u32[]{:S(2)}, u32[]{:S(2)}) collective-permute-start(bf16[256,768]{1,0:T(8,128)(2,1)S(1)} %copy-done.9), channel_id=1, source_target_pairs={{0,16},{1,17},{2,18},{3,19},{4,20},{5,21},{6,22},{7,23},{8,24},{9,... | collective-permute-start | bytes 1179656 | tf_op jit(solution)/shard_map/ppermute | solution.py:993
  500.8 42.0 %collective-permute-start.12 = (bf16[8,48,2304]{2,1,0:T(8,128)(2,1)}, bf16[8,48,2304]{2,1,0:T(8,128)(2,1)}, u32[]{:S(2)}, u32[]{:S(2)}) collective-permute-start(bf16[8,48,2304]{2,1,0:T(8,128)(2,1)} %dynamic-slice_bitcast_fusion), channel_id=1, source_target_pairs={{0,1},{1,0},{2,3},{3,2},{4,5},{5,4},{6,7},{7,6},{8,9},{9,8},{10,11... | collective-permute-start | bytes 5308424 | tf_op jit(solution)/shard_map/ppermute | solution.py:911
  533.6 5.8 collective-permute-start.13
  534.1 18.3 %all-to-all-start.13 = ((bf16[4,48,1152]{2,1,0:T(8,128)(2,1)}), bf16[4,48,1152]{2,1,0:T(8,128)(2,1)}, u32[]{:S(2)}, u32[]{:S(2)}) async-start(bf16[4,48,1152]{2,1,0:T(8,128)(2,1)} %reduce_sum.344), calls=%async_computation.14 | async-start | bytes 884736 | tf_op jit(solution)/shard_map/all_to_all | solution.py:932
  547.2 51.1 %copy-start.94 = (f32[256]{0:T(256)S(1)}, f32[256]{0:T(256)}, u32[]{:S(2)}) copy-start(f32[256]{0:T(256)} %get-tuple-element.122) | copy-start | bytes 3076
  547.2 51.2 %copy-start.95 = (f32[256]{0:T(256)S(1)}, f32[256]{0:T(256)}, u32[]{:S(2)}) copy-start(f32[256]{0:T(256)} %get-tuple-element.126) | copy-start | bytes 3076
  547.2 51.2 %copy-start.14 = (bf16[256,768]{1,0:T(8,128)(2,1)S(1)}, bf16[256,768]{1,0:T(8,128)(2,1)}, u32[]{:S(2)}) copy-start(bf16[256,768]{1,0:T(8,128)(2,1)} %copy-done.13) | copy-start | bytes 1179652
  547.2 51.2 %copy-start.22 = (f32[256,768]{1,0:T(8,128)S(1)}, f32[256,768]{1,0:T(8,128)}, u32[]{:S(2)}) copy-start(f32[256,768]{1,0:T(8,128)} %copy-done.20) | copy-start | bytes 2359300
  547.2 51.2 %copy-start.67 = (f32[256]{0:T(256)S(1)}, f32[256]{0:T(256)}, u32[]{:S(2)}) copy-start(f32[256]{0:T(256)} %copy-done.65) | copy-start | bytes 3076
  547.2 51.2 %copy-start.82 = (f32[256]{0:T(256)S(1)}, f32[256]{0:T(256)}, u32[]{:S(2)}) copy-start(f32[256]{0:T(256)} %copy-done.80) | copy-start | bytes 3076
  552.4 79.0 %all-to-all-start.11 = ((bf16[4,4,48,1280]{3,2,1,0:T(8,128)(2,1)}), bf16[4,4,48,1280]{3,2,1,0:T(8,128)(2,1)S(1)}, u32[]{:S(2)}, u32[]{:S(2)}) async-start(bf16[4,4,48,1280]{3,2,1,0:T(8,128)(2,1)} %fusion.53), calls=%async_computation.12 | async-start | bytes 3932160 | tf_op jit(solution)/shard_map/all_to_all | solution.py:932
  600.2 28.7 %collective-permute-start.11 = (bf16[256,768]{1,0:T(8,128)(2,1)S(1)}, bf16[256,768]{1,0:T(8,128)(2,1)S(1)}, u32[]{:S(2)}, u32[]{:S(2)}) collective-permute-start(bf16[256,768]{1,0:T(8,128)(2,1)S(1)} %get-tuple-element.160), channel_id=1, source_target_pairs={{16,8},{17,9},{18,10},{19,11},{20,12},{21,13},{22,14},{23,15},{24,... | collective-permute-start | bytes 1179656 | tf_op jit(solution)/shard_map/ppermute | solution.py:993
  630.2 58.0 %copy-start.34 = (bf16[24,6912]{1,0:T(8,128)(2,1)S(1)}, bf16[24,6912]{1,0:T(8,128)(2,1)}, u32[]{:S(2)}) copy-start(bf16[24,6912]{1,0:T(8,128)(2,1)} %reduce-scatter.3.cloned.1.call-done) | copy-start | bytes 995332
  632.6 58.2 %all-to-all-start.12 = ((bf16[4,48,1280]{2,1,0:T(8,128)(2,1)}), bf16[4,48,1280]{2,1,0:T(8,128)(2,1)S(1)}, u32[]{:S(2)}, u32[]{:S(2)}) async-start(bf16[4,48,1280]{2,1,0:T(8,128)(2,1)} %reduce_sum.363), calls=%async_computation.13 | async-start | bytes 983040 | tf_op jit(solution)/shard_map/all_to_all | solution.py:932
  688.3 11.5 %collective-permute-start.15 = (bf16[24,6912]{1,0:T(8,128)(2,1)S(1)}, bf16[24,6912]{1,0:T(8,128)(2,1)S(1)}, u32[]{:S(2)}, u32[]{:S(2)}) collective-permute-start(bf16[24,6912]{1,0:T(8,128)(2,1)S(1)} %broadcast_select_fusion), channel_id=1, source_target_pairs={{0,16},{16,0},{1,17},{17,1},{2,18},{18,2},{3,19},{19,3},{4,20},{20... | collective-permute-start | bytes 995336 | tf_op jit(solution)/shard_map/ppermute | solution.py:915
  691.0 7.9 %collective-permute-start.14 = (bf16[48,1152]{1,0:T(8,128)(2,1)S(1)}, bf16[48,1152]{1,0:T(8,128)(2,1)S(1)}, u32[]{:S(2)}, u32[]{:S(2)}) collective-permute-start(bf16[48,1152]{1,0:T(8,128)(2,1)S(1)} %select_convert_fusion), channel_id=1, source_target_pairs={{0,16},{16,0},{1,17},{17,1},{2,18},{18,2},{3,19},{19,3},{4,20},{20... | collective-permute-start | bytes 331784 | tf_op jit(solution)/shard_map/ppermute | solution.py:915
  (72 other events, 343.4 us)
Sparse Core Ops, SparseCore 0:
  39.1 135.1 all-gather.2
  177.8 99.9 all-gather.4
  321.1 167.1 reduce-scatter.2
  494.2 193.9 reduce-scatter.4

commit v4 on v3

--- a/solution.py
+++ b/solution.py
@@ -830,7 +830,7 @@
     return (np.arange(16)[None, None, :] * 16 + residue).reshape(HEADS, TOK)
 
 
-def cube_forward(hidden, params, order, docs, trade):
+def cube_forward(hidden, params, order, docs, trade, window):
     w_qkv, w_out, w_mlp, gains, biases, up_bias = params
     unit_one, scale_one, normed = layer_norm(hidden, gains[0], biases[0])
     mixed = jnp.einsum("df,td->ft", w_qkv, normed, preferred_element_type=F32)
@@ -840,6 +840,7 @@
     mixed = jnp.einsum("hft,htu->hfu", mixed, order, preferred_element_type=F32).astype(BF16)
     heads = trade(mixed)
     merged, merged_low, summary = attn_fwd(heads, docs)
+    merged_low, window = lax.optimization_barrier((merged_low, window))
     attended = trade(merged_low)
     attended = jnp.einsum("hdu,htu->hdt", attended, order, preferred_element_type=F32).astype(BF16)
     attended = attended.reshape(D, TOK)
@@ -852,10 +853,17 @@
     for at in range(0, ff, D):
         result = result + jnp.dot(activated[:, at : at + D], w_mlp[:, ff + at : ff + at + D], preferred_element_type=F32)
     kept = (unit_one, scale_one, normed, heads, merged, summary, attended, unit_two, scale_two, normed_two, slope, activated)
-    return result.astype(BF16), kept
-
-
-def cube_backward(incoming_low, kept, params, order, docs, trade, before, between, along, send_rest):
+    return result.astype(BF16), kept, window
+
+
+def columns_of(values, at, number, over=0):
+    place = (jnp.arange(128)[None, :] == at + number).astype(values.dtype)
+    place = jnp.broadcast_to(place, (values.shape[over], 128))
+    precision = highest if values.dtype == F32 else None
+    return lax.dot_general(values, place, (((over,), (0,)), ((), ())), precision=precision, preferred_element_type=F32)
+
+
+def cube_backward(incoming_low, kept, params, order, docs, trade, before, between, window, send_rest, at):
     w_qkv, w_out, w_mlp, gains, biases, up_bias = params
     unit_one, scale_one, normed, heads, merged, summary, attended, unit_two, scale_two, normed_two, slope, activated = kept
     ff = up_bias.shape[0]
@@ -878,29 +886,31 @@
         axis=1,
     )
     merged_grad = trade(merged_grad)
+    small = (
+        columns_of(norm_two_grad * unit_two, at, 1)
+        + columns_of(branch_grad, at, 5)
+        + columns_of(norm_two_grad, at, 6)
+        + columns_of(incoming_low, at, 7)
+        + sum(columns_of(up_grad[:, k * D : (k + 1) * D], at, 8 + k) for k in range(4))
+    )
     merged_grad, grad_rest, before = lax.optimization_barrier((merged_grad, grad_rest, before))
     sums_rest = send_rest(grad_rest)
     back_heads = attn_bwd(heads, merged_grad, docs, merged, summary)
+    back_heads, window = lax.optimization_barrier((back_heads, window))
     mixed_grad = trade(back_heads)
-    mixed_grad, before, along = lax.optimization_barrier((mixed_grad, between(before), along))
+    mixed_grad, before, small = lax.optimization_barrier((mixed_grad, between(before), small))
     mixed_grad = jnp.einsum("hfu,htu->hft", mixed_grad, order, preferred_element_type=F32).astype(BF16)
     mixed_grad = mixed_grad.reshape(HEADS, 3, HEAD_DIM, TOK).transpose(1, 0, 2, 3).reshape(3 * D, TOK)
     grad_qkv = jnp.einsum("td,ft->df", normed, mixed_grad, preferred_element_type=F32).astype(BF16)
-    grad_shift = jnp.sum(mixed_grad.astype(F32), axis=1)
     normed_grad = jnp.einsum("ft,df->td", mixed_grad, w_qkv, preferred_element_type=F32)
     start_grad = middle_grad + layer_norm_back(normed_grad, unit_one, scale_one, gains[0])
-    small = jnp.stack([
-        jnp.sum(normed_grad * unit_one, axis=0),
-        jnp.sum(norm_two_grad * unit_two, axis=0),
-        jnp.sum(normed_grad, axis=0),
-        grad_shift[:D],
-        grad_shift[2 * D:],
-        jnp.sum(branch_grad.astype(F32), axis=0),
-        jnp.sum(norm_two_grad, axis=0),
-        jnp.sum(incoming, axis=0),
-    ])
-    grad_up_bias = jnp.sum(up_grad.astype(F32), axis=0)
-    return start_grad, (grad_qkv, sums_rest, small, grad_up_bias), before, along
+    late = (
+        columns_of(normed_grad * unit_one, at, 0)
+        + columns_of(normed_grad, at, 2)
+        + columns_of(mixed_grad[:D], at, 3, 1)
+        + columns_of(mixed_grad[2 * D :], at, 4, 1)
+    )
+    return start_grad, (grad_qkv, sums_rest, small + late), before, window
 
 
 def half_pairs(source, count):
@@ -1017,8 +1027,6 @@
     got = across(low_qkv[:, columns:], half_pairs(0, count))
     piece = jnp.where(lower, low_qkv[:, :columns], got)
     line = collect_line(jnp.concatenate([piece, small], axis=1))
-    parts = collect_plane(line)
-    qkv_first = jnp.concatenate([part[:, :columns] for part in parts], axis=1)
 
     piece, w_up, w_down = lax.optimization_barrier((piece, w_up, w_down))
     up_shard = w_up[0].astype(BF16).reshape(wide, count, 4, wide).transpose(0, 2, 1, 3).reshape(wide, ff)
@@ -1028,7 +1036,9 @@
     got = section_swap(jnp.where(lower, shard[rows:], shard[:rows]))
     near = jnp.concatenate([jnp.where(lower, shard[:rows, :rest], got[:, :rest]), jnp.where(lower, got, shard[rows:])[:, rest:]], axis=1)
     far = jnp.where(lower, got[:, :rest], shard[rows:, :rest])
-    near, far, line = lax.optimization_barrier((near, far, line))
+    near, far, line, hidden = lax.optimization_barrier((near, far, line, hidden))
+    parts = collect_plane(line)
+    qkv_first = jnp.concatenate([part[:, :columns] for part in parts], axis=1)
     near = lax.all_gather(near, ("seq", "section"), axis=0, tiled=True)
     rest_final = lax.all_gather(far, ("seq", "section"), axis=0, tiled=True)
     rest_first, qkv_final = near[:, :rest], near[:, rest:]
@@ -1040,60 +1050,59 @@
     lines_first, lines_final = lines(parts[0][:, columns:]), lines(parts[1][:, columns:])
     params_first = (qkv_first, rest_first[:, 2 * ff :], rest_first) + lines_first
     params_final = (qkv_final, rest_final[:, 2 * ff :], rest_final) + lines_final
-    first, kept_first = cube_forward(hidden.astype(F32), params_first, order, docs, trade)
-    final, kept_final = cube_forward(first.astype(F32), params_final, order, docs, trade)
-    def shared_out(value_first, value_final):
-        far = across(value_first, [(count + j, j ^ half) for j in range(count)])
-        near = across(value_final, half_pairs(0, count))
-        beside = across(value_final, [(count + j, count + (j ^ half)) for j in range(count)])
-        return far, near, beside
-
+    beyond = [(count + j, count + (j ^ half)) for j in range(count)]
+    back_over = [(count + j, j ^ half) for j in range(count)]
+    first, kept_first, start_back = cube_forward(
+        hidden.astype(F32), params_first, order, docs, trade, own_rows(cotangent)
+    )
+    final, kept_final, far = cube_forward(
+        first.astype(F32), params_final, order, docs, trade, across(first, back_over)
+    )
     def placed(mine, other):
         return jnp.where(micro_id == 0, jnp.stack([mine, other]), jnp.stack([other, mine]))[None]
 
-    def scattered(partial):
+    def scattered_last(partial):
         return lax.psum_scatter(partial, ("seq", "section"), scatter_dimension=0, tiled=True)
 
-    start_back, merged = lax.optimization_barrier((own_rows(cotangent), kept_final[4]))
+    def scattered_near(partial):
+        return lax.psum_scatter(partial, "seq", scatter_dimension=0, tiled=True)
+
+    start_back, merged = lax.optimization_barrier((start_back, kept_final[4]))
     kept_final = kept_final[:4] + (merged,) + kept_final[5:]
-    grad_final, terms_final, _, _ = cube_backward(
-        start_back, kept_final, params_final, order, docs, trade, None, lambda now: now, None, scattered
-    )
+    grad_final, terms_final, _, window = cube_backward(
+        start_back, kept_final, params_final, order, docs, trade, None, lambda now: now,
+        (across(final, half_pairs(0, count)), across(final, beyond)), scattered_near, 12,
+    )
+    layer_outputs = placed(jnp.where(lower, first, window[0]), jnp.where(lower, far, window[1]))
     rest_final = terms_final[1]
-    sent, qkv_final = lax.optimization_barrier((grad_final.astype(BF16), terms_final[0]))
-    near = across(sent, half_pairs(0, count))
-    beside = across(sent, [(count + j, count + (j ^ half)) for j in range(count)])
-    grad_first, terms_first, qkv_final, along = cube_backward(
-        sent, kept_first, params_first, order, docs, trade,
-        reduce_core(qkv_final), reduce_plane, (rest_final, shared_out(first, final), near, beside), scattered,
-    )
-    rest_final, outs, near, beside = along
-
-    def upright(rows, wide_row):
-        return jnp.concatenate([rows, wide_row.reshape(4, D)]).T
-
-    smalls = jnp.concatenate([upright(*terms_first[2:]), upright(*terms_final[2:])], axis=1)
-    smalls = fold(smalls.reshape(8, 2, wide, 24), 0, 1).reshape(4, 2, wide, 24)
+    sent, qkv_final, small_final = lax.optimization_barrier(
+        (grad_final.astype(BF16), terms_final[0], terms_final[2])
+    )
+    grad_first, terms_first, qkv_final, window = cube_backward(
+        sent, kept_first, params_first, order, docs, trade, reduce_core(qkv_final), reduce_plane,
+        (across(sent, half_pairs(0, count)), across(sent, beyond)), scattered_last, 0,
+    )
+
+    smalls = (terms_first[2] + small_final).astype(BF16)
+    smalls = fold(smalls.reshape(8, 2, wide, 128), 0, 1).reshape(4, 2, wide, 128)
     smalls = jnp.stack([smalls[:, 0], smalls[:, 1]] * 2)
-    smalls = jnp.pad(smalls, ((0, 0), (0, 0), (0, 0), (0, 128 - 24)))
     now = jnp.concatenate([reduce_core(terms_first[0]), smalls], axis=3)
-    now = reduce_line(reduce_plane(now))
-    qkv_first, smalls = now[:, :-128], now[:, -128:-104]
+    plane, far_back = lax.optimization_barrier((reduce_plane(now), across(grad_first.astype(BF16), back_over)))
+    now = reduce_line(jnp.concatenate([plane, qkv_final], axis=2))
+    columns = qkv_final.shape[2]
+    qkv_first, smalls, qkv_final = now[:, :columns], now[:, columns : columns + 24], now[:, columns + 128 :]
     smalls = jnp.where(lower, smalls[:, :12], smalls[:, 12:]).T
-    qkv_final = reduce_line(qkv_final)
     rest_first = terms_first[1]
-    backs = across(grad_first.astype(BF16), [(count + j, j ^ half) for j in range(count)]), near, beside
-    far, near, beside = outs
-    layer_outputs = placed(jnp.where(lower, first, near), jnp.where(lower, far, beside))
-    far, near, beside = backs
     input_grads = placed(
-        jnp.where(lower, grad_first, near.astype(F32)), jnp.where(lower, far, beside).astype(F32)
-    )
-
-    away = section_swap(jnp.where(lower, rest_final, rest_first))
+        jnp.where(lower, grad_first, window[0].astype(F32)), jnp.where(lower, far_back, window[1]).astype(F32)
+    )
+
+    near = across(rest_final, half_pairs(0, count))
+    away = across(rest_first, half_pairs(1, count))
     rest = jnp.where(
-        lower, jnp.concatenate([rest_first, away]), jnp.concatenate([away, rest_final])
-    ).astype(F32)
+        lower, jnp.concatenate([rest_first, away]).astype(F32), rest_final.astype(F32) + near.astype(F32)
+    )
+    qkv_final, qkv_first, layer_outputs = lax.optimization_barrier((qkv_final, qkv_first, layer_outputs))
     away = section_swap(jnp.where(lower, qkv_final, qkv_first).astype(BF16)).astype(F32)
     qkv = jnp.where(
         lower, jnp.concatenate([qkv_first, away], axis=1), jnp.concatenate([away, qkv_final], axis=1)

time: 724 us -> 687 us (0.949)
  starting transfers between devices: 165 us -> 83.6 us
  waiting for transfers between devices: 212 us -> 249 us
  local copies, waits for them, and re-layouts: 59.3 us -> 31.6 us
  matrix products: 102 us -> 120 us
  other arithmetic: 37.9 us -> 48.7 us
    all_to_all x5 -> x4, waiting for transfers between devices: 8.12 us -> 65 us  [team_trade(): lax.all_to_all(value, ('section', 'seq'), 0, 0, axis_index_groups=team(ki...]
    all_to_all x5 -> x4, starting transfers between devices: 64.1 us -> 14.4 us  [team_trade(): lax.all_to_all(value, ('section', 'seq'), 0, 0, axis_index_groups=team(ki...]
    reduce_scatter x2, waiting for transfers between devices: 51.7 us -> 14.7 us  [the longest x1 14.7 us: scattered_last(): lax.psum_scatter(partial, ('seq', 'section'), scatter_dimension=0, tiled=...]
    all_to_all x8, starting transfers between devices: 71.2 us -> 36 us  [trade(): lax.all_to_all(value, axes, 0, 0, axis_index_groups=teams, tiled=True)]
    all_gather x1, waiting for transfers between devices: 11 us -> 36.4 us  [cube_body(): rest_final = lax.all_gather(far, ('seq', 'section'), axis=0, tiled=True)]
    dot_general x0 -> x24, matrix products: none -> 20.3 us  [columns_of(): lax.dot_general(values, place, (((over,), (0,)), ((), ())), precision=pre...]
    another operation x17 -> x1, local copies, waits for them, and re-layouts: 15.8 us -> 0.01 us  [the longest x16 15.8 us: cube_backward(): jnp.stack([jnp.sum(normed_grad * unit_one, axis=0), jnp.sum(norm_two_grad...]
    ppermute x9 -> x11, waiting for transfers between devices: 29.9 us -> 15.1 us  [across(): return lax.ppermute(value, axes, pairs)]
  transfers between devices with their start and end apart: 33 -> 33, of which waited for: 15 -> 16; matrix products, arithmetic and copies ran while one was open for 23% -> 25% of each run, Pallas kernels for 13% -> 14%
where the time goes in v4:
time: 687 us; the launch traced here: 676 us
  waiting for transfers between devices  249 us (36%)
  matrix products  120 us (17%)
  Pallas kernels  91.7 us (13%)
  starting transfers between devices  83.6 us (12%)
  other arithmetic  48.7 us (7%)
  blocking collectives  34.9 us (5%)
  local copies, waits for them, and re-layouts  31.6 us (5%)
  between operations  16.4 us (2%)
    all_to_all x8, waiting for transfers between devices, trade(): lax.all_to_all(value, axes, 0, 0, axis_index_groups=teams, tiled=True)  106 us
    all_to_all x4, waiting for transfers between devices, team_trade(): lax.all_to_all(value, ('section', 'seq'), 0, 0, axis_index_groups=team(ki...  65 us
    pallas_call x2, Pallas kernels, attn_bwd(): pl.pallas_call(bwd_kernel, out_shape=jax.ShapeDtypeStruct((SRC, 3 * HD, T...  56.4 us
    all_gather x1, waiting for transfers between devices, cube_body(): rest_final = lax.all_gather(far, ('seq', 'section'), axis=0, tiled=True)  36.4 us
    all_to_all x8, starting transfers between devices, trade(): lax.all_to_all(value, axes, 0, 0, axis_index_groups=teams, tiled=True)  36 us
    pallas_call x2, Pallas kernels, attn_fwd(): pl.pallas_call(functools.partial(fwd_kernel, kc=256), out_shape=(jax.Shap...  35.4 us
    all_to_all x1, blocking collectives, team_trade(): lax.all_to_all(value, ('section', 'seq'), 0, 0, axis_index_groups=team(ki...  34.9 us
    ppermute x11, starting transfers between devices, across(): return lax.ppermute(value, axes, pairs)  29.6 us
  transfers between devices with their start and end apart: 33, of which 16 were waited for; matrix products, arithmetic and copies ran while one was open for 25% of the time, Pallas kernels for 14%

profile of v4, /device:TPU:0, one launch (start us, length us, event | category | flops | bytes accessed | tf_op | source)
XLA Modules:
  0.0 675.9 jit_solution(3455448937155028705)
XLA Ops:
  8.4 4.8 collective-permute-start
  13.3 1.9 select_bitcast_fusion.8
  20.5 2.6 collective-permute-start.1
  23.9 3.5 all-to-all-start
  27.5 5.7 collective-permute-done.1
  36.7 4.1 all-to-all-done
  41.8 34.9 %all_to_all.65 = bf16[4,4,48,1280]{3,2,1,0:T(8,128)(2,1)S(1)} all-to-all(bf16[4,4,48,1280]{3,2,1,0:T(8,128)(2,1)S(1)} %broadcast_in_dim.59), channel_id=1, replica_groups={{0,2,16,18},{1,3,17,19},{4,6,20,22},{5,7,21,23},{8,10,24,26},{9,11,25,2..., dimensions={0} | all-to-all | bytes 3932160 | tf_op jit(solution)/shard_map/all_to_all | solution.py:942
  77.1 3.7 collective-permute-done.3
  80.7 2.1 select_bitcast_fusion.3
  85.8 2.2 slice_reduce_fusion
  90.8 2.0 fusion.52
  92.8 3.8 all-to-all-start.2
  96.7 1.9 collective-permute-start.4
  105.4 24.3 %all-to-all-done.2.x_ref = bf16[16,144,256]{2,1,0:T(8,128)(2,1)S(1)} async-done(((bf16[16,144,256]{2,1,0:T(8,128)(2,1)}), bf16[16,144,256]{2,1,0:T(8,128)(2,1)S(1)}, u32[]{:S(2)}, u32[]{:S(2)}) %all-to-all-start.2) | async-done | bytes 1179680 | tf_op jit(solution)/shard_map/all_to_all | solution.py:1000
  129.7 17.7 %attend.2 = (f32[16,48,256]{2,1,0:T(8,128)S(1)}, bf16[16,48,256]{2,1,0:T(8,128)(2,1)}, f32[16,1,256]{2,1,0:T(1,128)S(1)}) custom-call(bf16[16,144,256]{2,1,0:T(8,128)(2,1)S(1)} %all-to-all-done.2.x_ref, f32[16,1,256]{2,1,0:T(1,128)S(1)} %reshape.583.docs_ref), custom_call_target="tpu_custom_call" | custom-call | flops 17999998976 | bytes 3145728 | tf_op jit(solution)/shard_map/attend/pallas_call | solution.py:693
  148.9 5.1 all-to-all-start.3
  154.3 15.8 %all-to-all-done.3 = bf16[16,48,256]{2,1,0:T(8,128)(2,1)S(1)} async-done(((bf16[16,48,256]{2,1,0:T(8,128)(2,1)}), bf16[16,48,256]{2,1,0:T(8,128)(2,1)S(1)}, u32[]{:S(2)}, u32[]{:S(2)}) %all-to-all-start.3) | async-done | bytes 393248 | tf_op jit(solution)/shard_map/all_to_all | solution.py:1000
  171.1 2.0 fusion.235
  173.5 6.6 multiply_convert_fusion.1
  184.1 2.0 fusion.53
  186.2 4.7 all-to-all-start.4
  204.0 16.9 %all-to-all-done.4.x_ref = bf16[16,144,256]{2,1,0:T(8,128)(2,1)S(1)} async-done(((bf16[16,144,256]{2,1,0:T(8,128)(2,1)}), bf16[16,144,256]{2,1,0:T(8,128)(2,1)S(1)}, u32[]{:S(2)}, u32[]{:S(2)}) %all-to-all-start.4) | async-done | bytes 1179680 | tf_op jit(solution)/shard_map/all_to_all | solution.py:1000
  220.9 17.7 %attend.3 = (f32[16,48,256]{2,1,0:T(8,128)S(1)}, bf16[16,48,256]{2,1,0:T(8,128)(2,1)}, f32[16,1,256]{2,1,0:T(1,128)S(1)}) custom-call(bf16[16,144,256]{2,1,0:T(8,128)(2,1)S(1)} %all-to-all-done.4.x_ref, f32[16,1,256]{2,1,0:T(1,128)S(1)} %reshape.583.docs_ref), custom_call_target="tpu_custom_call" | custom-call | flops 17999998976 | bytes 3145728 | tf_op jit(solution)/shard_map/attend/pallas_call | solution.py:693
  240.0 3.6 all-to-all-start.5
  243.6 36.4 %all-gather.5.cloned.1.call-done = bf16[768,6912]{1,0:T(8,128)(2,1)} async-done(((bf16[24,6912]{1,0:T(8,128)(2,1)}), bf16[768,6912]{1,0:T(8,128)(2,1)}) %all-gather.5.cloned.1.call-update) | async-done | bytes 10616848 | tf_op jit(solution)/shard_map/all_gather | solution.py:1043
  283.6 2.7 fusion.91
  286.3 2.7 fusion.94
  289.9 2.0 fusion.236
  292.2 5.8 multiply_convert_fusion
  298.0 3.8 fusion
  305.8 4.2 all-to-all-start.6
  310.3 2.7 fusion.65
  321.3 2.8 convolution_add_fusion.4
  324.1 2.1 convolution_add_fusion.3
  329.5 6.7 collective-permute-start.6
  336.2 28.3 %attend_back.2 = bf16[16,144,256]{2,1,0:T(8,128)(2,1)} custom-call(bf16[16,144,256]{2,1,0:T(8,128)(2,1)} %copy-done.1, bf16[16,48,256]{2,1,0:T(8,128)(2,1)} %all-to-all-done.6.g_ref, f32[16,1,256]{2,1,0:T(1,128)} %copy-done.2, f32[16,48,256]{2,1,0:T(8,128)} %copy-done.4, f32[16,1,256]{2,1,0:T(1,128)} %copy-done.6), custom_call_target="tpu_custom_call" | custom-call | flops 28000000000 | bytes 6291456 | tf_op jit(solution)/shard_map/attend_back/pallas_call | solution.py:786
  364.5 4.8 all-to-all-start.7
  376.5 38.7 %all-to-all-done.7 = bf16[16,144,256]{2,1,0:T(8,128)(2,1)} async-done(((bf16[16,144,256]{2,1,0:T(8,128)(2,1)}), bf16[16,144,256]{2,1,0:T(8,128)(2,1)}, u32[]{:S(2)}, u32[]{:S(2)}) %all-to-all-start.7) | async-done | bytes 1179680 | tf_op jit(solution)/shard_map/all_to_all | solution.py:1000
  415.1 2.5 fusion.54
  417.7 3.5 multiply_reduce_fusion.6
  426.6 2.3 convolution_convert_fusion.2
  430.4 3.9 collective-permute-start.9
  448.3 4.2 all-to-all-start.8
  454.9 3.8 fusion.1
  458.7 2.6 fusion.60
  461.3 2.6 fusion.59
  463.9 2.6 fusion.58
  466.6 2.6 fusion.57
  475.3 3.6 all-to-all-start.10
  479.5 28.1 %attend_back.3 = bf16[16,144,256]{2,1,0:T(8,128)(2,1)} custom-call(bf16[16,144,256]{2,1,0:T(8,128)(2,1)} %copy-done, bf16[16,48,256]{2,1,0:T(8,128)(2,1)} %all-to-all-done.8.g_ref, f32[16,1,256]{2,1,0:T(1,128)} %copy-done.2, f32[16,48,256]{2,1,0:T(8,128)} %copy-done.3, f32[16,1,256]{2,1,0:T(1,128)} %copy-done.5), custom_call_target="tpu_custom_call" | custom-call | flops 28000000000 | bytes 6291456 | tf_op jit(solution)/shard_map/attend_back/pallas_call | solution.py:786
  507.6 5.7 all-to-all-start.9
  521.7 8.9 %all-to-all-done.9 = bf16[16,144,256]{2,1,0:T(8,128)(2,1)} async-done(((bf16[16,144,256]{2,1,0:T(8,128)(2,1)}), bf16[16,144,256]{2,1,0:T(8,128)(2,1)}, u32[]{:S(2)}, u32[]{:S(2)}) %all-to-all-start.9) | async-done | bytes 1179680 | tf_op jit(solution)/shard_map/all_to_all | solution.py:1000
  530.6 2.3 fusion.55
  545.9 3.6 all-to-all-start.11
  549.5 2.7 select_bitcast_fusion.4
  553.5 27.5 %all-to-all-done.11 = bf16[4,4,48,1280]{3,2,1,0:T(8,128)(2,1)S(1)} async-done(((bf16[4,4,48,1280]{3,2,1,0:T(8,128)(2,1)}), bf16[4,4,48,1280]{3,2,1,0:T(8,128)(2,1)S(1)}, u32[]{:S(2)}, u32[]{:S(2)}) %all-to-all-start.11) | async-done | bytes 1966112 | tf_op jit(solution)/shard_map/all_to_all | solution.py:942
  581.6 7.2 %collective-permute-done.13 = bf16[256,768]{1,0:T(8,128)(2,1)S(1)} collective-permute-done((bf16[256,768]{1,0:T(8,128)(2,1)}, bf16[256,768]{1,0:T(8,128)(2,1)S(1)}, u32[]{:S(2)}, u32[]{:S(2)}) %collective-permute-start.13) | collective-permute-done | bytes 393248 | tf_op jit(solution)/shard_map/ppermute | solution.py:1003
  588.7 2.0 pad_maximum_fusion.6
  590.8 3.7 all-to-all-start.12
  597.2 33.4 %all-to-all-done.12 = bf16[4,48,2432]{2,1,0:T(8,128)(2,1)S(1)} async-done(((bf16[4,48,2432]{2,1,0:T(8,128)(2,1)}), bf16[4,48,2432]{2,1,0:T(8,128)(2,1)S(1)}, u32[]{:S(2)}, u32[]{:S(2)}) %all-to-all-start.12) | async-done | bytes 933920 | tf_op jit(solution)/shard_map/all_to_all | solution.py:942
  633.1 3.9 collective-permute-start.16
  637.1 14.7 %reduce-scatter.3.cloned.1.call-done = bf16[24,6912]{1,0:T(8,128)(2,1)} async-done(((bf16[768,6912]{1,0:T(8,128)(2,1)}), bf16[24,6912]{1,0:T(8,128)(2,1)}) %reduce-scatter.3.cloned.1.call-update) | async-done | bytes 331792 | tf_op jit(solution)/shard_map/reduce_scatter | solution.py:1065
  653.9 7.9 %collective-permute-done.15 = bf16[24,6912]{1,0:T(8,128)(2,1)S(1)} collective-permute-done((bf16[24,6912]{1,0:T(8,128)(2,1)}, bf16[24,6912]{1,0:T(8,128)(2,1)S(1)}, u32[]{:S(2)}, u32[]{:S(2)}) %collective-permute-start.15) | collective-permute-done | bytes 331808 | tf_op jit(solution)/shard_map/ppermute | solution.py:1003
  666.6 2.6 broadcast_in_dim_reshape.8
  (470 shorter events, 137.8 us)
Async XLA Ops:
  7.2 9.4 %copy-start.106 = (f32[1,2,48]{2,1,0:T(2,128)S(1)}, f32[1,2,48]{2,1,0:T(2,128)}, u32[]{:S(2)}) copy-start(f32[1,2,48]{2,1,0:T(2,128)} %param.18) | copy-start | bytes 1156
  7.2 9.4 %copy-start.107 = (f32[1,192]{1,0:T(1,128)S(1)}, f32[1,192]{1,0:T(1,128)}, u32[]{:S(2)}) copy-start(f32[1,192]{1,0:T(1,128)} %param.20) | copy-start | bytes 2308
  7.2 9.5 %copy-start.83 = (f32[1,6,48]{2,0,1:T(1,128)S(1)}, f32[1,6,48]{2,0,1:T(1,128)}, u32[]{:S(2)}) copy-start(f32[1,6,48]{2,0,1:T(1,128)} %param.19) | copy-start | bytes 3460
  7.2 9.5 %copy-start.48 = (f32[1,48,768]{2,1,0:T(8,128)S(1)}, f32[1,48,768]{2,1,0:T(8,128)}, u32[]{:S(2)}) copy-start(f32[1,48,768]{2,1,0:T(8,128)} %param.15) | copy-start | bytes 442372
  7.2 9.7 %copy-start.42 = (f32[1,192,768]{2,1,0:T(8,128)S(1)}, f32[1,192,768]{2,1,0:T(8,128)}, u32[]{:S(2)}) copy-start(f32[1,192,768]{2,1,0:T(8,128)} %param.17) | copy-start | bytes 1769476
  7.2 9.7 %copy-start.41 = (f32[1,48,3072]{2,1,0:T(8,128)S(1)}, f32[1,48,3072]{2,1,0:T(8,128)}, u32[]{:S(2)}) copy-start(f32[1,48,3072]{2,1,0:T(8,128)} %param.16) | copy-start | bytes 1769476
  8.4 8.5 %collective-permute-start = (bf16[48,1152]{1,0:T(8,128)(2,1)S(1)}, bf16[48,1152]{1,0:T(8,128)(2,1)S(1)}, u32[]{:S(2)}, u32[]{:S(2)}) collective-permute-start(bf16[48,1152]{1,0:T(8,128)(2,1)S(1)} %slice.477), channel_id=1, source_target_pairs={{0,16},{1,17},{2,18},{3,19},{4,20},{5,21},{6,22},{7,23},{8,24},{9,... | collective-permute-start | bytes 331784 | tf_op jit(solution)/shard_map/ppermute | solution.py:1003
  15.2 12.3 %collective-permute-start.2 = (bf16[256,768]{1,0:T(8,128)(2,1)}, bf16[256,768]{1,0:T(8,128)(2,1)}, u32[]{:S(2)}, u32[]{:S(2)}) collective-permute-start(bf16[256,768]{1,0:T(8,128)(2,1)} %select_bitcast_fusion.8), channel_id=1, source_target_pairs={{16,24},{17,25},{18,26},{19,27},{20,28},{21,29},{22,30},{23,31},{2... | collective-permute-start | bytes 1179656 | tf_op jit(solution)/shard_map/ppermute | solution.py:1003
  20.5 12.8 %collective-permute-start.1 = (bf16[24,9216]{1,0:T(8,128)(2,1)}, bf16[24,9216]{1,0:T(8,128)(2,1)}, u32[]{:S(2)}, u32[]{:S(2)}) collective-permute-start(bf16[24,9216]{1,0:T(8,128)(2,1)} %get-tuple-element.192), channel_id=1, source_target_pairs={{0,16},{16,0},{1,17},{17,1},{2,18},{18,2},{3,19},{19,3},{4,20},{20... | collective-permute-start | bytes 1327112 | tf_op jit(solution)/shard_map/ppermute | solution.py:925
  23.9 16.9 %all-to-all-start = ((bf16[4,48,1280]{2,1,0:T(8,128)(2,1)}), bf16[4,48,1280]{2,1,0:T(8,128)(2,1)S(1)}, u32[]{:S(2)}, u32[]{:S(2)}) async-start(bf16[4,48,1280]{2,1,0:T(8,128)(2,1)} %broadcast_in_dim.58), calls=%async_computation | async-start | bytes 983040 | tf_op jit(solution)/shard_map/all_to_all | solution.py:942
  27.4 143.7 %all-gather.3.cloned.1.call-start = ((), (), s32[]{:S(2)}) async-start(), calls=%async_computation.15 | async-start | bytes 14598144 | tf_op jit(solution)/shard_map/all_gather | solution.py:1042
  27.5 143.6 %copy-start.7 = (bf16[256,768]{1,0:T(8,128)(2,1)}, bf16[256,768]{1,0:T(8,128)(2,1)S(1)}, u32[]{:S(2)}) copy-start(bf16[256,768]{1,0:T(8,128)(2,1)S(1)} %bitcast_select_fusion.1) | copy-start | bytes 1179652
  40.9 239.2 %all-gather.5.cloned.1.call-start = ((), (), s32[]{:S(2)}) async-start(), calls=%async_computation.16 | async-start | bytes 10948608 | tf_op jit(solution)/shard_map/all_gather | solution.py:1043
  76.6 4.1 collective-permute-start.3
  76.8 11.8 %copy-start.54 = (f32[256]{0:T(256)}, f32[256]{0:T(256)S(1)}, u32[]{:S(2)}) copy-start(f32[256]{0:T(256)S(1)} %broadcast_multiply_fusion.11) | copy-start | bytes 3076
  77.1 11.5 %copy-start.56 = (f32[256]{0:T(256)}, f32[256]{0:T(256)S(1)}, u32[]{:S(2)}) copy-start(f32[256]{0:T(256)S(1)} %add_rsqrt_fusion.3) | copy-start | bytes 3076
  92.8 36.9 %all-to-all-start.2 = ((bf16[16,144,256]{2,1,0:T(8,128)(2,1)}), bf16[16,144,256]{2,1,0:T(8,128)(2,1)S(1)}, u32[]{:S(2)}, u32[]{:S(2)}) async-start(bf16[16,144,256]{2,1,0:T(8,128)(2,1)} %fusion.52), calls=%async_computation.2 | async-start | bytes 2359296 | tf_op jit(solution)/shard_map/all_to_all | solution.py:1000
  96.7 8.6 %collective-permute-start.4 = (bf16[256,768]{1,0:T(8,128)(2,1)S(1)}, bf16[256,768]{1,0:T(8,128)(2,1)}, u32[]{:S(2)}, u32[]{:S(2)}) collective-permute-start(bf16[256,768]{1,0:T(8,128)(2,1)S(1)} %select_bitcast_fusion.7), channel_id=1, source_target_pairs={{16,24},{17,25},{18,26},{19,27},{20,28},{21,29},{22,30},{23,31},{2... | collective-permute-start | bytes 1179656 | tf_op jit(solution)/shard_map/ppermute | solution.py:1003
  105.3 115.6 %copy-start.2 = (f32[16,1,256]{2,1,0:T(1,128)}, f32[16,1,256]{2,1,0:T(1,128)S(1)}, u32[]{:S(2)}) copy-start(f32[16,1,256]{2,1,0:T(1,128)S(1)} %reshape.583.docs_ref) | copy-start | bytes 49156
  129.7 17.7 %copy-start = (bf16[16,144,256]{2,1,0:T(8,128)(2,1)}, bf16[16,144,256]{2,1,0:T(8,128)(2,1)S(1)}, u32[]{:S(2)}) copy-start(bf16[16,144,256]{2,1,0:T(8,128)(2,1)S(1)} %all-to-all-done.2.x_ref) | copy-start | bytes 3538948
  148.9 21.3 %copy-start.63 = (s32[16,256]{1,0:T(8,128)S(1)}, s32[16,256]{1,0:T(8,128)}, u32[]{:S(2)}) copy-start(s32[16,256]{1,0:T(8,128)} %constant.140.clone) | copy-start | bytes 49156
  148.9 22.2 %copy-start.82 = (f32[768]{0:T(1024)S(1)}, f32[768]{0:T(1024)}, u32[]{:S(2)}) copy-start(f32[768]{0:T(1024)} %get-tuple-element.157) | copy-start | bytes 9220
  148.9 21.3 %all-to-all-start.3 = ((bf16[16,48,256]{2,1,0:T(8,128)(2,1)}), bf16[16,48,256]{2,1,0:T(8,128)(2,1)S(1)}, u32[]{:S(2)}, u32[]{:S(2)}) async-start(bf16[16,48,256]{2,1,0:T(8,128)(2,1)} %get-tuple-element.58), calls=%async_computation.3 | async-start | bytes 786432 | tf_op jit(solution)/shard_map/all_to_all | solution.py:1000
  171.1 9.0 %copy-start.24 = (bf16[768,9216]{1,0:T(8,128)(2,1)S(1)}, bf16[768,9216]{1,0:T(8,128)(2,1)}, u32[]{:S(2)}) copy-start(bf16[768,9216]{1,0:T(8,128)(2,1)} %all-gather.3.cloned.1.call-done) | copy-start | bytes 42467332
  182.2 243.4 %copy-start.9 = (bf16[256,768]{1,0:T(8,128)(2,1)}, bf16[256,768]{1,0:T(8,128)(2,1)S(1)}, u32[]{:S(2)}) copy-start(bf16[256,768]{1,0:T(8,128)(2,1)S(1)} %get-tuple-element.205) | copy-start | bytes 1179652
  186.2 34.7 %all-to-all-start.4 = ((bf16[16,144,256]{2,1,0:T(8,128)(2,1)}), bf16[16,144,256]{2,1,0:T(8,128)(2,1)S(1)}, u32[]{:S(2)}, u32[]{:S(2)}) async-start(bf16[16,144,256]{2,1,0:T(8,128)(2,1)} %fusion.53), calls=%async_computation.4 | async-start | bytes 2359296 | tf_op jit(solution)/shard_map/all_to_all | solution.py:1000
  202.6 37.5 %collective-permute-start.5 = (bf16[256,768]{1,0:T(8,128)(2,1)S(1)}, bf16[256,768]{1,0:T(8,128)(2,1)S(1)}, u32[]{:S(2)}, u32[]{:S(2)}) collective-permute-start(bf16[256,768]{1,0:T(8,128)(2,1)S(1)} %get-tuple-element.205), channel_id=1, source_target_pairs={{16,8},{17,9},{18,10},{19,11},{20,12},{21,13},{22,14},{23,15},{24,... | collective-permute-start | bytes 1179656 | tf_op jit(solution)/shard_map/ppermute | solution.py:1003
  220.9 17.7 %copy-start.1 = (bf16[16,144,256]{2,1,0:T(8,128)(2,1)}, bf16[16,144,256]{2,1,0:T(8,128)(2,1)S(1)}, u32[]{:S(2)}) copy-start(bf16[16,144,256]{2,1,0:T(8,128)(2,1)S(1)} %all-to-all-done.4.x_ref) | copy-start | bytes 3538948
  240.0 40.0 %copy-start.43 = (bf16[256,768]{1,0:T(8,128)(2,1)}, bf16[256,768]{1,0:T(8,128)(2,1)S(1)}, u32[]{:S(2)}) copy-start(bf16[256,768]{1,0:T(8,128)(2,1)S(1)} %collective-permute-done.5) | copy-start | bytes 1179652
  240.0 48.9 %all-to-all-start.5 = ((bf16[16,48,256]{2,1,0:T(8,128)(2,1)}), bf16[16,48,256]{2,1,0:T(8,128)(2,1)S(1)}, u32[]{:S(2)}, u32[]{:S(2)}) async-start(bf16[16,48,256]{2,1,0:T(8,128)(2,1)} %get-tuple-element.63), calls=%async_computation.5 | async-start | bytes 786432 | tf_op jit(solution)/shard_map/all_to_all | solution.py:1000
  291.8 11.5 %copy-start.60 = (f32[256]{0:T(256)}, f32[256]{0:T(256)S(1)}, u32[]{:S(2)}) copy-start(f32[256]{0:T(256)S(1)} %broadcast_multiply_fusion.8) | copy-start | bytes 3076
  292.1 11.3 %copy-start.77 = (f32[256]{0:T(256)}, f32[256]{0:T(256)S(1)}, u32[]{:S(2)}) copy-start(f32[256]{0:T(256)S(1)} %add_rsqrt_fusion) | copy-start | bytes 3076
  292.1 9.6 %slice-start = ((s8[10616832]{0:T(1024)(128)(4,1)}), s8[2228224]{0:T(1024)(128)(4,1)S(1)}, s32[]{:S(2)}) async-start(s8[10616832]{0:T(1024)(128)(4,1)} %bitcast.241), calls=%async_computation.19 | async-start | bytes 4456448
  292.1 9.6 %slice-start.1 = ((s8[10616832]{0:T(1024)(128)(4,1)}), s8[4194304]{0:T(1024)(128)(4,1)S(1)}, s32[]{:S(2)}) async-start(s8[10616832]{0:T(1024)(128)(4,1)} %bitcast.241), calls=%async_computation.20 | async-start | bytes 8388608
  305.8 18.2 %all-to-all-start.6 = ((bf16[16,48,256]{2,1,0:T(8,128)(2,1)}), bf16[16,48,256]{2,1,0:T(8,128)(2,1)}, u32[]{:S(2)}, u32[]{:S(2)}) async-start(bf16[16,48,256]{2,1,0:T(8,128)(2,1)} %fusion.72), calls=%async_computation.6 | async-start | bytes 786432 | tf_op jit(solution)/shard_map/all_to_all | solution.py:1000
  310.1 323.1 %reduce-scatter.5.cloned.1.call-start = ((), (), s32[]{:S(2)}) async-start(), calls=%async_computation.18 | async-start | bytes 11280384 | tf_op jit(solution)/shard_map/reduce_scatter | solution.py:1068
  328.0 36.5 %collective-permute-start.7 = (bf16[256,768]{1,0:T(8,128)(2,1)S(1)}, bf16[256,768]{1,0:T(8,128)(2,1)}, u32[]{:S(2)}, u32[]{:S(2)}) collective-permute-start(bf16[256,768]{1,0:T(8,128)(2,1)S(1)} %fusion.69), channel_id=1, source_target_pairs={{16,24},{17,25},{18,26},{19,27},{20,28},{21,29},{22,30},{23,31},{2... | collective-permute-start | bytes 1179656 | tf_op jit(solution)/shard_map/ppermute | solution.py:1003
  329.5 35.1 %collective-permute-start.6 = (bf16[256,768]{1,0:T(8,128)(2,1)S(1)}, bf16[256,768]{1,0:T(8,128)(2,1)}, u32[]{:S(2)}, u32[]{:S(2)}) collective-permute-start(bf16[256,768]{1,0:T(8,128)(2,1)S(1)} %fusion.69), channel_id=1, source_target_pairs={{0,16},{1,17},{2,18},{3,19},{4,20},{5,21},{6,22},{7,23},{8,24},{9,... | collective-permute-start | bytes 1179656 | tf_op jit(solution)/shard_map/ppermute | solution.py:1003
  364.5 8.7 %copy-start.103 = (bf16[128]{0:T(256)(128)(2,1)S(1)}, bf16[128]{0:T(256)(128)(2,1)}, u32[]{:S(2)}) copy-start(bf16[128]{0:T(256)(128)(2,1)} %compare_convert_fusion.18) | copy-start | bytes 772
  364.5 50.6 %all-to-all-start.7 = ((bf16[16,144,256]{2,1,0:T(8,128)(2,1)}), bf16[16,144,256]{2,1,0:T(8,128)(2,1)}, u32[]{:S(2)}, u32[]{:S(2)}) async-start(bf16[16,144,256]{2,1,0:T(8,128)(2,1)} %attend_back.2), calls=%async_computation.7 | async-start | bytes 2359296 | tf_op jit(solution)/shard_map/all_to_all | solution.py:1000
  375.8 39.3 %copy-start.66 = (s32[16,256]{1,0:T(8,128)S(1)}, s32[16,256]{1,0:T(8,128)}, u32[]{:S(2)}) copy-start(s32[16,256]{1,0:T(8,128)} %constant.140.clone) | copy-start | bytes 49156
  415.1 19.2 %slice-start.3 = ((s8[14155776]{0:T(1024)(128)(4,1)}), s8[4194304]{0:T(1024)(128)(4,1)S(1)}, s32[]{:S(2)}) async-start(s8[14155776]{0:T(1024)(128)(4,1)} %bitcast.244), calls=%async_computation.22 | async-start | bytes 8388608
  417.7 16.6 %slice-start.4 = ((s8[14155776]{0:T(1024)(128)(4,1)}), s8[4194304]{0:T(1024)(128)(4,1)S(1)}, s32[]{:S(2)}) async-start(s8[14155776]{0:T(1024)(128)(4,1)} %bitcast.244), calls=%async_computation.23 | async-start | bytes 8388608
  421.3 13.0 %slice-start.5 = ((s8[14155776]{0:T(1024)(128)(4,1)}), s8[4194304]{0:T(1024)(128)(4,1)S(1)}, s32[]{:S(2)}) async-start(s8[14155776]{0:T(1024)(128)(4,1)} %bitcast.244), calls=%async_computation.24 | async-start | bytes 8388608
  425.6 8.8 %slice-start.6 = ((s8[14155776]{0:T(1024)(128)(4,1)}), s8[1572864]{0:T(1024)(128)(4,1)S(1)}, s32[]{:S(2)}) async-start(s8[14155776]{0:T(1024)(128)(4,1)} %bitcast.244), calls=%async_computation.25 | async-start | bytes 3145728
  429.0 78.6 %collective-permute-start.10 = (bf16[256,768]{1,0:T(8,128)(2,1)}, bf16[256,768]{1,0:T(8,128)(2,1)}, u32[]{:S(2)}, u32[]{:S(2)}) collective-permute-start(bf16[256,768]{1,0:T(8,128)(2,1)} %fusion.128), channel_id=1, source_target_pairs={{16,24},{17,25},{18,26},{19,27},{20,28},{21,29},{22,30},{23,31},{2... | collective-permute-start | bytes 1179656 | tf_op jit(solution)/shard_map/ppermute | solution.py:1003
  430.4 77.2 %collective-permute-start.9 = (bf16[256,768]{1,0:T(8,128)(2,1)}, bf16[256,768]{1,0:T(8,128)(2,1)}, u32[]{:S(2)}, u32[]{:S(2)}) collective-permute-start(bf16[256,768]{1,0:T(8,128)(2,1)} %fusion.128), channel_id=1, source_target_pairs={{0,16},{1,17},{2,18},{3,19},{4,20},{5,21},{6,22},{7,23},{8,24},{9,... | collective-permute-start | bytes 1179656 | tf_op jit(solution)/shard_map/ppermute | solution.py:1003
  448.3 27.0 %all-to-all-start.8 = ((bf16[16,48,256]{2,1,0:T(8,128)(2,1)}), bf16[16,48,256]{2,1,0:T(8,128)(2,1)}, u32[]{:S(2)}, u32[]{:S(2)}) async-start(bf16[16,48,256]{2,1,0:T(8,128)(2,1)} %fusion.73), calls=%async_computation.8 | async-start | bytes 786432 | tf_op jit(solution)/shard_map/all_to_all | solution.py:1000
  454.0 16.7 %collective-permute-start.8 = (bf16[8,48,2304]{2,1,0:T(8,128)(2,1)}, bf16[8,48,2304]{2,1,0:T(8,128)(2,1)}, u32[]{:S(2)}, u32[]{:S(2)}) collective-permute-start(bf16[8,48,2304]{2,1,0:T(8,128)(2,1)} %dynamic-slice_bitcast_fusion.1), channel_id=1, source_target_pairs={{0,1},{1,0},{2,3},{3,2},{4,5},{5,4},{6,7},{7,6},{8,9},{9,8},{10,11... | collective-permute-start | bytes 5308424 | tf_op jit(solution)/shard_map/ppermute | solution.py:921
  475.3 32.3 %all-to-all-start.10 = ((bf16[4,4,48,1152]{3,2,1,0:T(8,128)(2,1)}), bf16[4,4,48,1152]{3,2,1,0:T(8,128)(2,1)S(1)}, u32[]{:S(2)}, u32[]{:S(2)}) async-start(bf16[4,4,48,1152]{3,2,1,0:T(8,128)(2,1)} %pad_maximum_fusion.5), calls=%async_computation.10 | async-start | bytes 3538944 | tf_op jit(solution)/shard_map/all_to_all | solution.py:942
  478.9 172.9 %reduce-scatter.3.cloned.1.call-start = ((), (), s32[]{:S(2)}) async-start(), calls=%async_computation.17 | async-start | bytes 10948608 | tf_op jit(solution)/shard_map/reduce_scatter | solution.py:1065
  507.5 8.6 %copy-start.90 = (bf16[128]{0:T(256)(128)(2,1)S(1)}, bf16[128]{0:T(256)(128)(2,1)}, u32[]{:S(2)}) copy-start(bf16[128]{0:T(256)(128)(2,1)} %compare_convert_fusion.6) | copy-start | bytes 772
  507.6 23.0 %all-to-all-start.9 = ((bf16[16,144,256]{2,1,0:T(8,128)(2,1)}), bf16[16,144,256]{2,1,0:T(8,128)(2,1)}, u32[]{:S(2)}, u32[]{:S(2)}) async-start(bf16[16,144,256]{2,1,0:T(8,128)(2,1)} %attend_back.3), calls=%async_computation.9 | async-start | bytes 2359296 | tf_op jit(solution)/shard_map/all_to_all | solution.py:1000
  519.2 11.4 %copy-start.68 = (s32[16,256]{1,0:T(8,128)S(1)}, s32[16,256]{1,0:T(8,128)}, u32[]{:S(2)}) copy-start(s32[16,256]{1,0:T(8,128)} %constant.140.clone) | copy-start | bytes 49156
  535.4 8.2 %collective-permute-start.11 = (bf16[8,48,2304]{2,1,0:T(8,128)(2,1)S(1)}, bf16[8,48,2304]{2,1,0:T(8,128)(2,1)S(1)}, u32[]{:S(2)}, u32[]{:S(2)}) collective-permute-start(bf16[8,48,2304]{2,1,0:T(8,128)(2,1)S(1)} %dynamic-slice_bitcast_fusion), channel_id=1, source_target_pairs={{0,1},{1,0},{2,3},{3,2},{4,5},{5,4},{6,7},{7,6},{8,9},{9,8},{10,11... | collective-permute-start | bytes 5308424 | tf_op jit(solution)/shard_map/ppermute | solution.py:921
  542.2 1.4 collective-permute-start.12
  545.9 35.1 %all-to-all-start.11 = ((bf16[4,4,48,1280]{3,2,1,0:T(8,128)(2,1)}), bf16[4,4,48,1280]{3,2,1,0:T(8,128)(2,1)S(1)}, u32[]{:S(2)}, u32[]{:S(2)}) async-start(bf16[4,4,48,1280]{3,2,1,0:T(8,128)(2,1)} %maximum_maximum_fusion), calls=%async_computation.11 | async-start | bytes 3932160 | tf_op jit(solution)/shard_map/all_to_all | solution.py:942
  552.2 36.6 %collective-permute-start.13 = (bf16[256,768]{1,0:T(8,128)(2,1)}, bf16[256,768]{1,0:T(8,128)(2,1)S(1)}, u32[]{:S(2)}, u32[]{:S(2)}) collective-permute-start(bf16[256,768]{1,0:T(8,128)(2,1)} %get-tuple-element.165), channel_id=1, source_target_pairs={{16,8},{17,9},{18,10},{19,11},{20,12},{21,13},{22,14},{23,15},{24,... | collective-permute-start | bytes 1179656 | tf_op jit(solution)/shard_map/ppermute | solution.py:1003
  581.5 12.9 %copy-start.10 = (bf16[256,768]{1,0:T(8,128)(2,1)S(1)}, bf16[256,768]{1,0:T(8,128)(2,1)}, u32[]{:S(2)}) copy-start(bf16[256,768]{1,0:T(8,128)(2,1)} %copy-done.9) | copy-start | bytes 1179652
  581.5 12.9 %copy-start.44 = (bf16[256,768]{1,0:T(8,128)(2,1)S(1)}, bf16[256,768]{1,0:T(8,128)(2,1)}, u32[]{:S(2)}) copy-start(bf16[256,768]{1,0:T(8,128)(2,1)} %copy-done.43) | copy-start | bytes 1179652
  590.8 39.8 %all-to-all-start.12 = ((bf16[4,48,2432]{2,1,0:T(8,128)(2,1)}), bf16[4,48,2432]{2,1,0:T(8,128)(2,1)S(1)}, u32[]{:S(2)}, u32[]{:S(2)}) async-start(bf16[4,48,2432]{2,1,0:T(8,128)(2,1)} %pad_maximum_fusion.6), calls=%async_computation.12 | async-start | bytes 1867776 | tf_op jit(solution)/shard_map/all_to_all | solution.py:942
  630.8 6.3 collective-permute-start.14
  633.1 20.8 %collective-permute-start.16 = (bf16[48,6912]{1,0:T(8,128)(2,1)}, bf16[48,6912]{1,0:T(8,128)(2,1)S(1)}, u32[]{:S(2)}, u32[]{:S(2)}) collective-permute-start(bf16[48,6912]{1,0:T(8,128)(2,1)} %reduce-scatter.5.cloned.1.call-done), channel_id=1, source_target_pairs={{0,16},{1,17},{2,18},{3,19},{4,20},{5,21},{6,22},{7,23},{8,24},{9,... | collective-permute-start | bytes 1990664 | tf_op jit(solution)/shard_map/ppermute | solution.py:1003
  651.8 10.0 %collective-permute-start.15 = (bf16[24,6912]{1,0:T(8,128)(2,1)}, bf16[24,6912]{1,0:T(8,128)(2,1)S(1)}, u32[]{:S(2)}, u32[]{:S(2)}) collective-permute-start(bf16[24,6912]{1,0:T(8,128)(2,1)} %reduce-scatter.3.cloned.1.call-done), channel_id=1, source_target_pairs={{16,0},{17,1},{18,2},{19,3},{20,4},{21,5},{22,6},{23,7},{24,8},{25... | collective-permute-start | bytes 995336 | tf_op jit(solution)/shard_map/ppermute | solution.py:1003
  (84 other events, 240.2 us)
Sparse Core Ops, SparseCore 0:
  41.0 129.4 all-gather.2
  174.0 106.0 all-gather.4
  324.2 138.2 reduce-scatter.4
  485.5 166.2 reduce-scatter.2

commit v5 on v4

--- a/solution.py
+++ b/solution.py
@@ -863,7 +863,16 @@
     return lax.dot_general(values, place, (((over,), (0,)), ((), ())), precision=precision, preferred_element_type=F32)
 
 
-def cube_backward(incoming_low, kept, params, order, docs, trade, before, between, window, send_rest, at):
+def turned_rows(kept, turn):
+    attended, normed_two, activated = kept[6], kept[9], kept[11]
+    return (
+        moved(normed_two, turn, "tf,fp->tp"),
+        moved(attended, turn, "ft,fp->pt"),
+        [moved(activated[:, k : k + D], turn, "tf,fp->tp") for k in range(0, activated.shape[1], D)],
+    )
+
+
+def cube_backward(incoming_low, kept, params, order, docs, trade, before, between, window, send_rest, at, turn):
     w_qkv, w_out, w_mlp, gains, biases, up_bias = params
     unit_one, scale_one, normed, heads, merged, summary, attended, unit_two, scale_two, normed_two, slope, activated = kept
     ff = up_bias.shape[0]
@@ -879,19 +888,21 @@
     merged_grad = jnp.einsum("fd,td->ft", w_out, branch_grad, preferred_element_type=F32).astype(BF16)
     merged_grad = merged_grad.reshape(HEADS, HEAD_DIM, TOK)
     merged_grad = jnp.einsum("hdt,htu->hdu", merged_grad, order, preferred_element_type=F32).astype(BF16)
+    turned_two, turned, hidden_units = turn
     grad_rest = jnp.concatenate(
-        [inner_rows(normed_two, up_grad).astype(BF16)]
-        + [inner_rows(activated[:, at : at + D], incoming_low).astype(BF16) for at in range(0, ff, D)]
-        + [jnp.einsum("ft,td->fd", attended, branch_grad, preferred_element_type=F32).astype(BF16)],
+        [inner_rows(turned_two, up_grad).astype(BF16)]
+        + [inner_rows(part, incoming_low).astype(BF16) for part in hidden_units]
+        + [jnp.einsum("pt,td->pd", turned, branch_grad, preferred_element_type=F32).astype(BF16)],
         axis=1,
     )
+    lifts = sum(columns_of(up_grad[:, k * D : (k + 1) * D], at, 8 + k) for k in range(4))
     merged_grad = trade(merged_grad)
     small = (
         columns_of(norm_two_grad * unit_two, at, 1)
         + columns_of(branch_grad, at, 5)
         + columns_of(norm_two_grad, at, 6)
         + columns_of(incoming_low, at, 7)
-        + sum(columns_of(up_grad[:, k * D : (k + 1) * D], at, 8 + k) for k in range(4))
+        + lifts
     )
     merged_grad, grad_rest, before = lax.optimization_barrier((merged_grad, grad_rest, before))
     sums_rest = send_rest(grad_rest)
@@ -933,9 +944,22 @@
     def device(x, z, y, c):
         return x * 16 + z * 4 + y * 2 + c
     two, four = range(2), range(4)
+    if kind == "whole plane":
+        return [[device(x, z, y, c) for x in two for y in two for c in two] for z in four]
     if kind == "plane":
         return [[device(x, z, y, c) for x in two for y in two] for z in four for c in two]
     return [[device(x, z, y, c) for z in four] for x in two for y in two for c in two]
+
+
+def plane_order():
+    index = np.arange(D).reshape(4, 2, 2, 2, D // 32).transpose(3, 1, 2, 0, 4).reshape(D)
+    place = np.empty(D, np.int32)
+    place[index] = np.arange(D)
+    return place
+
+
+def moved(values, turn, equation):
+    return jnp.einsum(equation, values, turn, preferred_element_type=F32).astype(BF16)
 
 
 def team_trade(value, kind):
@@ -1008,6 +1032,7 @@
         swap = across(other, [(count + j, count + (j ^ half)) for j in range(count)])
         return jnp.where(lower, mine, swap)
 
+    turn = (jnp.asarray(plane_order())[:, None] == jnp.arange(D)[None, :]).astype(BF16)
     table = jnp.asarray(head_order())
     order = (table[:, None, :] == jnp.arange(TOK)[None, :, None]).astype(BF16)
     docs = jnp.where(micro_id == 0, documents[0], documents[1]).reshape(count, TOK)
@@ -1049,39 +1074,44 @@
 
     lines_first, lines_final = lines(parts[0][:, columns:]), lines(parts[1][:, columns:])
     params_first = (qkv_first, rest_first[:, 2 * ff :], rest_first) + lines_first
-    params_final = (qkv_final, rest_final[:, 2 * ff :], rest_final) + lines_final
     beyond = [(count + j, count + (j ^ half)) for j in range(count)]
     back_over = [(count + j, j ^ half) for j in range(count)]
     first, kept_first, start_back = cube_forward(
         hidden.astype(F32), params_first, order, docs, trade, own_rows(cotangent)
     )
-    final, kept_final, far = cube_forward(
-        first.astype(F32), params_final, order, docs, trade, across(first, back_over)
-    )
+    params_final = (qkv_final, rest_final[:, 2 * ff :], rest_final) + lines_final
+    final, kept_final, (far, turned_first) = cube_forward(
+        first.astype(F32), params_final, order, docs, trade, (across(first, back_over), turned_rows(kept_first, turn))
+    )
+
     def placed(mine, other):
         return jnp.where(micro_id == 0, jnp.stack([mine, other]), jnp.stack([other, mine]))[None]
 
-    def scattered_last(partial):
-        return lax.psum_scatter(partial, ("seq", "section"), scatter_dimension=0, tiled=True)
-
-    def scattered_near(partial):
-        return lax.psum_scatter(partial, "seq", scatter_dimension=0, tiled=True)
+    def scattered(partial):
+        return lax.psum_scatter(
+            partial, axes, scatter_dimension=0, tiled=True, axis_index_groups=team("whole plane")
+        )
+
+    def fold_line(partial):
+        return fold(partial.reshape(2, 2, rows, -1), 3, 0)
 
     start_back, merged = lax.optimization_barrier((start_back, kept_final[4]))
     kept_final = kept_final[:4] + (merged,) + kept_final[5:]
     grad_final, terms_final, _, window = cube_backward(
         start_back, kept_final, params_final, order, docs, trade, None, lambda now: now,
-        (across(final, half_pairs(0, count)), across(final, beyond)), scattered_near, 12,
+        (across(final, half_pairs(0, count)), across(final, beyond)), scattered, 12,
+        turned_rows(kept_final, turn),
     )
     layer_outputs = placed(jnp.where(lower, first, window[0]), jnp.where(lower, far, window[1]))
-    rest_final = terms_final[1]
     sent, qkv_final, small_final = lax.optimization_barrier(
         (grad_final.astype(BF16), terms_final[0], terms_final[2])
     )
     grad_first, terms_first, qkv_final, window = cube_backward(
         sent, kept_first, params_first, order, docs, trade, reduce_core(qkv_final), reduce_plane,
-        (across(sent, half_pairs(0, count)), across(sent, beyond)), scattered_last, 0,
-    )
+        (across(sent, half_pairs(0, count)), across(sent, beyond), fold_line(terms_final[1])), scattered, 0,
+        turned_first,
+    )
+    rest_final = fold(window[2], 2, 0)
 
     smalls = (terms_first[2] + small_final).astype(BF16)
     smalls = fold(smalls.reshape(8, 2, wide, 128), 0, 1).reshape(4, 2, wide, 128)
@@ -1089,31 +1119,30 @@
     now = jnp.concatenate([reduce_core(terms_first[0]), smalls], axis=3)
     plane, far_back = lax.optimization_barrier((reduce_plane(now), across(grad_first.astype(BF16), back_over)))
     now = reduce_line(jnp.concatenate([plane, qkv_final], axis=2))
+    now, rest_first = lax.optimization_barrier((now, fold_line(terms_first[1])))
     columns = qkv_final.shape[2]
     qkv_first, smalls, qkv_final = now[:, :columns], now[:, columns : columns + 24], now[:, columns + 128 :]
     smalls = jnp.where(lower, smalls[:, :12], smalls[:, 12:]).T
-    rest_first = terms_first[1]
+    rest_first = fold(rest_first, 2, 0)
     input_grads = placed(
         jnp.where(lower, grad_first, window[0].astype(F32)), jnp.where(lower, far_back, window[1]).astype(F32)
     )
 
-    near = across(rest_final, half_pairs(0, count))
-    away = across(rest_first, half_pairs(1, count))
-    rest = jnp.where(
-        lower, jnp.concatenate([rest_first, away]).astype(F32), rest_final.astype(F32) + near.astype(F32)
-    )
+    away = section_swap(jnp.where(lower, rest_final, rest_first))
+    rest = jnp.where(lower, jnp.concatenate([rest_first, away]), jnp.concatenate([away, rest_final]))
     qkv_final, qkv_first, layer_outputs = lax.optimization_barrier((qkv_final, qkv_first, layer_outputs))
     away = section_swap(jnp.where(lower, qkv_final, qkv_first).astype(BF16)).astype(F32)
     qkv = jnp.where(
         lower, jnp.concatenate([qkv_first, away], axis=1), jnp.concatenate([away, qkv_final], axis=1)
     )
-    up = rest[:, :ff].reshape(wide, 4, count, wide).transpose(0, 2, 1, 3).reshape(wide, ff)
-    down = rest[:, ff : 2 * ff].reshape(wide, 4, D).transpose(1, 0, 2).reshape(4 * wide, D)
+    up = rest[:, :ff].astype(F32).reshape(wide, 4, count, wide).transpose(0, 2, 1, 3).reshape(wide, ff)
+    rest = rest[:, ff:].astype(F32)
+    down = rest[:, :ff].reshape(wide, 4, D).transpose(1, 0, 2).reshape(4 * wide, D)
     return (
         layer_outputs,
         input_grads,
         qkv[None],
-        rest[None, :, 2 * ff :],
+        rest[None, :, ff:],
         up[None],
         down[None],
         smalls[None, :2],

time: 687 us -> 660 us (0.961)
  waiting for transfers between devices: 249 us -> 179 us
  starting transfers between devices: 83.6 us -> 106 us
  matrix products: 120 us -> 136 us
  local copies, waits for them, and re-layouts: 31.6 us -> 39.3 us
    all_to_all x8, waiting for transfers between devices: 106 us -> 78.3 us  [trade(): lax.all_to_all(value, axes, 0, 0, axis_index_groups=teams, tiled=True)]
    all_to_all x4, waiting for transfers between devices: 65 us -> 39.1 us  [team_trade(): lax.all_to_all(value, ('section', 'seq'), 0, 0, axis_index_groups=team(ki...]
    ppermute x11 -> x9, waiting for transfers between devices: 15.1 us -> 0.02 us  [across(): return lax.ppermute(value, axes, pairs)]
    reduce_scatter x2, waiting for transfers between devices: 14.7 us -> 0.02 us  [scattered(): lax.psum_scatter(partial, axes, scatter_dimension=0, tiled=True, axis_ind...]
    ppermute x4 -> x8, starting transfers between devices: 0.38 us -> 14.3 us  [core_swap(): return lax.ppermute(value, 'seq', [(j, j ^ 1 << bit) for j in range(16)])]
    dot_general x2 -> x8, matrix products: 3.1 us -> 16.3 us  [the longest x6 11.3 us: moved(): jnp.einsum(equation, values, turn, preferred_element_type=F32).astype(BF16)]
    ppermute x2 -> x3, waiting for transfers between devices: 5.75 us -> 14.2 us  [section_swap(): return lax.ppermute(value, 'section', [(0, 1), (1, 0)])]
    ppermute x4 -> x8, waiting for transfers between devices: 4.97 us -> 12.7 us  [core_swap(): return lax.ppermute(value, 'seq', [(j, j ^ 1 << bit) for j in range(16)])]
  transfers between devices with their start and end apart: 33 -> 36, of which waited for: 16 -> 15; matrix products, arithmetic and copies ran while one was open for 25% -> 27% of each run, Pallas kernels for 14% -> 14%
where the time goes in v5:
time: 660 us; the launch traced here: 649 us
  waiting for transfers between devices  179 us (27%)
  matrix products  136 us (21%)
  starting transfers between devices  106 us (16%)
  Pallas kernels  92.6 us (14%)
  other arithmetic  44.1 us (7%)
  local copies, waits for them, and re-layouts  39.3 us (6%)
  blocking collectives  34.9 us (5%)
  between operations  16.3 us (2%)
    all_to_all x8, waiting for transfers between devices, trade(): lax.all_to_all(value, axes, 0, 0, axis_index_groups=teams, tiled=True)  78.3 us
    pallas_call x2, Pallas kernels, attn_bwd(): pl.pallas_call(bwd_kernel, out_shape=jax.ShapeDtypeStruct((SRC, 3 * HD, T...  57.2 us
    all_to_all x8, starting transfers between devices, trade(): lax.all_to_all(value, axes, 0, 0, axis_index_groups=teams, tiled=True)  41.3 us
    all_to_all x4, waiting for transfers between devices, team_trade(): lax.all_to_all(value, ('section', 'seq'), 0, 0, axis_index_groups=team(ki...  39.1 us
    pallas_call x2, Pallas kernels, attn_fwd(): pl.pallas_call(functools.partial(fwd_kernel, kc=256), out_shape=(jax.Shap...  35.4 us
    all_to_all x1, blocking collectives, team_trade(): lax.all_to_all(value, ('section', 'seq'), 0, 0, axis_index_groups=team(ki...  34.9 us
    all_gather x1, waiting for transfers between devices, cube_body(): rest_final = lax.all_gather(far, ('seq', 'section'), axis=0, tiled=True)  34.1 us
    dot_general x10, matrix products, inner_rows(): jnp.einsum('ta,tb->ab', left, right, preferred_element_type=jnp.float32)  28.9 us
  transfers between devices with their start and end apart: 36, of which 15 were waited for; matrix products, arithmetic and copies ran while one was open for 27% of the time, Pallas kernels for 14%

profile of v5, /device:TPU:0, one launch (start us, length us, event | category | flops | bytes accessed | tf_op | source)
XLA Modules:
  0.0 648.7 jit_solution(15867402248016334180)
XLA Ops:
  8.4 4.8 collective-permute-start
  20.5 2.6 collective-permute-start.1
  23.9 3.5 all-to-all-start
  27.5 5.7 collective-permute-done.1
  36.7 4.1 all-to-all-done
  41.8 34.9 %all_to_all.65 = bf16[4,4,48,1280]{3,2,1,0:T(8,128)(2,1)S(1)} all-to-all(bf16[4,4,48,1280]{3,2,1,0:T(8,128)(2,1)S(1)} %broadcast_in_dim.59), channel_id=1, replica_groups={{0,2,16,18},{1,3,17,19},{4,6,20,22},{5,7,21,23},{8,10,24,26},{9,11,25,2..., dimensions={0} | all-to-all | bytes 3932160 | tf_op jit(solution)/shard_map/all_to_all | solution.py:966
  77.1 3.7 collective-permute-done.3
  80.7 2.1 select_bitcast_fusion.3
  85.8 2.2 slice_reduce_fusion
  90.8 2.0 fusion.64
  92.8 3.8 all-to-all-start.2
  105.1 24.6 %all-to-all-done.2.x_ref = bf16[16,144,256]{2,1,0:T(8,128)(2,1)S(1)} async-done(((bf16[16,144,256]{2,1,0:T(8,128)(2,1)}), bf16[16,144,256]{2,1,0:T(8,128)(2,1)S(1)}, u32[]{:S(2)}, u32[]{:S(2)}) %all-to-all-start.2) | async-done | bytes 1179680 | tf_op jit(solution)/shard_map/all_to_all | solution.py:1024
  129.7 17.7 %attend.2 = (f32[16,48,256]{2,1,0:T(8,128)S(1)}, bf16[16,48,256]{2,1,0:T(8,128)(2,1)}, f32[16,1,256]{2,1,0:T(1,128)S(1)}) custom-call(bf16[16,144,256]{2,1,0:T(8,128)(2,1)S(1)} %all-to-all-done.2.x_ref, f32[16,1,256]{2,1,0:T(1,128)S(1)} %reshape.599.docs_ref), custom_call_target="tpu_custom_call" | custom-call | flops 17999998976 | bytes 3145728 | tf_op jit(solution)/shard_map/attend/pallas_call | solution.py:693
  148.9 5.1 all-to-all-start.3
  155.9 14.2 %all-to-all-done.3 = bf16[16,48,256]{2,1,0:T(8,128)(2,1)S(1)} async-done(((bf16[16,48,256]{2,1,0:T(8,128)(2,1)}), bf16[16,48,256]{2,1,0:T(8,128)(2,1)S(1)}, u32[]{:S(2)}, u32[]{:S(2)}) %all-to-all-start.3) | async-done | bytes 393248 | tf_op jit(solution)/shard_map/all_to_all | solution.py:1024
  171.1 2.0 fusion.285
  173.4 6.6 %multiply_convert_fusion.1 = (bf16[256,3072]{1,0:T(8,128)(2,1)S(1)}, f32[256,3072]{1,0:T(8,128)}) fusion(f32[3072]{0:T(1024)S(1)} %add.363, bf16[768,9216]{1,0:T(8,128)(2,1)} %all-gather.3.cloned.1.call-done, f32[256,768]{1,0:T(8,128)S(1)} %get-tuple-element.238, f32[768]{0:T(1024)S(1)} %copy-done.88, f32[768]{0:T(1024)S(1)} %copy-done.75, ...), kind=kOutput, calls=%fused_computation.50 | convolution fusion | flops 1213661184 | bytes 10244096 | tf_op jit(solution)/shard_map/dot_general | solution.py:850
  184.2 2.1 fusion.65
  186.2 4.6 all-to-all-start.4
  195.5 2.8 fusion.89
  200.0 2.5 fusion.90
  208.6 14.6 %all-to-all-done.4.x_ref = bf16[16,144,256]{2,1,0:T(8,128)(2,1)S(1)} async-done(((bf16[16,144,256]{2,1,0:T(8,128)(2,1)}), bf16[16,144,256]{2,1,0:T(8,128)(2,1)S(1)}, u32[]{:S(2)}, u32[]{:S(2)}) %all-to-all-start.4) | async-done | bytes 1179680 | tf_op jit(solution)/shard_map/all_to_all | solution.py:1024
  223.2 17.7 %attend.3 = (f32[16,48,256]{2,1,0:T(8,128)S(1)}, bf16[16,48,256]{2,1,0:T(8,128)(2,1)}, f32[16,1,256]{2,1,0:T(1,128)S(1)}) custom-call(bf16[16,144,256]{2,1,0:T(8,128)(2,1)S(1)} %all-to-all-done.4.x_ref, f32[16,1,256]{2,1,0:T(1,128)S(1)} %reshape.599.docs_ref), custom_call_target="tpu_custom_call" | custom-call | flops 17999998976 | bytes 3145728 | tf_op jit(solution)/shard_map/attend/pallas_call | solution.py:693
  242.4 3.7 all-to-all-start.5
  246.1 34.1 %all-gather.5.cloned.1.call-done = bf16[768,6912]{1,0:T(8,128)(2,1)} async-done(((bf16[24,6912]{1,0:T(8,128)(2,1)}), bf16[768,6912]{1,0:T(8,128)(2,1)}) %all-gather.5.cloned.1.call-update) | async-done | bytes 10616848 | tf_op jit(solution)/shard_map/all_gather | solution.py:1068
  283.8 2.7 fusion.135
  286.4 2.7 fusion.138
  290.0 2.0 fusion.286
  292.4 5.9 multiply_convert_fusion
  298.3 5.8 fusion
  304.1 4.4 multiply_reduce_fusion.7
  312.2 3.6 all-to-all-start.6
  316.0 3.3 fusion.77
  319.3 3.2 fusion.76
  322.6 3.2 fusion.75
  325.8 3.3 fusion.74
  329.1 3.5 fusion.73
  334.5 2.8 convolution_add_fusion.4
  338.0 2.1 convolution_add_fusion.3
  343.4 7.1 %collective-permute-start.6 = (bf16[256,768]{1,0:T(8,128)(2,1)S(1)}, bf16[256,768]{1,0:T(8,128)(2,1)}, u32[]{:S(2)}, u32[]{:S(2)}) collective-permute-start(bf16[256,768]{1,0:T(8,128)(2,1)S(1)} %fusion.83), channel_id=1, source_target_pairs={{0,16},{1,17},{2,18},{3,19},{4,20},{5,21},{6,22},{7,23},{8,24},{9,... | collective-permute-start | bytes 1179656 | tf_op jit(solution)/shard_map/ppermute | solution.py:1027
  350.6 28.7 %attend_back.2 = bf16[16,144,256]{2,1,0:T(8,128)(2,1)} custom-call(bf16[16,144,256]{2,1,0:T(8,128)(2,1)} %copy-done.1, bf16[16,48,256]{2,1,0:T(8,128)(2,1)} %copy-done.46, f32[16,1,256]{2,1,0:T(1,128)} %copy-done.2, f32[16,48,256]{2,1,0:T(8,128)} %copy-done.4, f32[16,1,256]{2,1,0:T(1,128)} %copy-done.6), custom_call_target="tpu_custom_call" | custom-call | flops 28000000000 | bytes 6291456 | tf_op jit(solution)/shard_map/attend_back/pallas_call | solution.py:786
  379.3 4.6 all-to-all-start.7
  389.9 13.8 %all-to-all-done.7 = bf16[16,144,256]{2,1,0:T(8,128)(2,1)} async-done(((bf16[16,144,256]{2,1,0:T(8,128)(2,1)}), bf16[16,144,256]{2,1,0:T(8,128)(2,1)}, u32[]{:S(2)}, u32[]{:S(2)}) %all-to-all-start.7) | async-done | bytes 1179680 | tf_op jit(solution)/shard_map/all_to_all | solution.py:1024
  403.7 2.5 fusion.66
  406.9 3.5 multiply_reduce_fusion.6
  415.1 2.8 convolution_convert_fusion.2
  427.4 5.7 all-to-all-start.8
  435.3 3.7 fusion.1
  452.2 7.4 %collective-permute-start.9 = (bf16[256,768]{1,0:T(8,128)(2,1)S(1)}, bf16[256,768]{1,0:T(8,128)(2,1)}, u32[]{:S(2)}, u32[]{:S(2)}) collective-permute-start(bf16[256,768]{1,0:T(8,128)(2,1)S(1)} %copy-done.9), channel_id=1, source_target_pairs={{0,16},{1,17},{2,18},{3,19},{4,20},{5,21},{6,22},{7,23},{8,24},{9,... | collective-permute-start | bytes 1179656 | tf_op jit(solution)/shard_map/ppermute | solution.py:1027
  459.6 4.1 all-to-all-start.10
  466.3 28.6 %attend_back.3 = bf16[16,144,256]{2,1,0:T(8,128)(2,1)} custom-call(bf16[16,144,256]{2,1,0:T(8,128)(2,1)} %copy-done, bf16[16,48,256]{2,1,0:T(8,128)(2,1)} %all-to-all-done.8.g_ref, f32[16,1,256]{2,1,0:T(1,128)} %copy-done.2, f32[16,48,256]{2,1,0:T(8,128)} %copy-done.3, f32[16,1,256]{2,1,0:T(1,128)} %copy-done.5), custom_call_target="tpu_custom_call" | custom-call | flops 28000000000 | bytes 6291456 | tf_op jit(solution)/shard_map/attend_back/pallas_call | solution.py:786
  498.3 10.2 %all-to-all-start.9 = ((bf16[16,144,256]{2,1,0:T(8,128)(2,1)}), bf16[16,144,256]{2,1,0:T(8,128)(2,1)}, u32[]{:S(2)}, u32[]{:S(2)}) async-start(bf16[16,144,256]{2,1,0:T(8,128)(2,1)} %attend_back.3), calls=%async_computation.10 | async-start | bytes 2359296 | tf_op jit(solution)/shard_map/all_to_all | solution.py:1024
  516.4 11.0 %all-to-all-done.9 = bf16[16,144,256]{2,1,0:T(8,128)(2,1)} async-done(((bf16[16,144,256]{2,1,0:T(8,128)(2,1)}), bf16[16,144,256]{2,1,0:T(8,128)(2,1)}, u32[]{:S(2)}, u32[]{:S(2)}) %all-to-all-start.9) | async-done | bytes 1179680 | tf_op jit(solution)/shard_map/all_to_all | solution.py:1024
  527.4 2.3 fusion.67
  539.9 2.4 select_bitcast_fusion.4
  545.7 5.6 all-to-all-start.11
  553.2 12.4 %collective-permute-start.15 = (bf16[2,24,6912]{2,1,0:T(8,128)(2,1)}, bf16[2,24,6912]{2,1,0:T(8,128)(2,1)}, u32[]{:S(2)}, u32[]{:S(2)}) collective-permute-start(bf16[2,24,6912]{2,1,0:T(8,128)(2,1)} %dynamic-slice_bitcast_fusion.2), channel_id=1, source_target_pairs={{0,8},{1,9},{2,10},{3,11},{4,12},{5,13},{6,14},{7,15},{8,0},{9,1},... | collective-permute-start | bytes 1990664 | tf_op jit(solution)/shard_map/ppermute | solution.py:932
  566.4 16.1 %all-to-all-done.11 = bf16[4,4,48,1280]{3,2,1,0:T(8,128)(2,1)S(1)} async-done(((bf16[4,4,48,1280]{3,2,1,0:T(8,128)(2,1)}), bf16[4,4,48,1280]{3,2,1,0:T(8,128)(2,1)S(1)}, u32[]{:S(2)}, u32[]{:S(2)}) %all-to-all-start.11) | async-done | bytes 1966112 | tf_op jit(solution)/shard_map/all_to_all | solution.py:966
  583.7 2.2 pad_maximum_fusion.6
  585.9 5.6 all-to-all-start.12
  595.3 18.9 %all-to-all-done.12 = bf16[4,48,2432]{2,1,0:T(8,128)(2,1)S(1)} async-done(((bf16[4,48,2432]{2,1,0:T(8,128)(2,1)}), bf16[4,48,2432]{2,1,0:T(8,128)(2,1)S(1)}, u32[]{:S(2)}, u32[]{:S(2)}) %all-to-all-start.12) | async-done | bytes 933920 | tf_op jit(solution)/shard_map/all_to_all | solution.py:966
  619.4 7.3 %collective-permute-done.17 = bf16[24,6912]{1,0:T(8,128)(2,1)S(1)} collective-permute-done((bf16[24,6912]{1,0:T(8,128)(2,1)S(1)}, bf16[24,6912]{1,0:T(8,128)(2,1)S(1)}, u32[]{:S(2)}, u32[]{:S(2)}) %collective-permute-start.17) | collective-permute-done | bytes 331808 | tf_op jit(solution)/shard_map/ppermute | solution.py:932
  629.3 6.7 %collective-permute-done.19 = bf16[24,6912]{1,0:T(8,128)(2,1)S(1)} collective-permute-done((bf16[24,6912]{1,0:T(8,128)(2,1)S(1)}, bf16[24,6912]{1,0:T(8,128)(2,1)S(1)}, u32[]{:S(2)}, u32[]{:S(2)}) %collective-permute-start.19) | collective-permute-done | bytes 331808 | tf_op jit(solution)/shard_map/ppermute | solution.py:936
  639.3 2.6 reshape.630
  (493 shorter events, 146.2 us)
Async XLA Ops:
  7.2 9.4 %copy-start.102 = (f32[1,2,48]{2,1,0:T(2,128)S(1)}, f32[1,2,48]{2,1,0:T(2,128)}, u32[]{:S(2)}) copy-start(f32[1,2,48]{2,1,0:T(2,128)} %param.19) | copy-start | bytes 1156
  7.2 9.4 %copy-start.103 = (f32[1,192]{1,0:T(1,128)S(1)}, f32[1,192]{1,0:T(1,128)}, u32[]{:S(2)}) copy-start(f32[1,192]{1,0:T(1,128)} %param.21) | copy-start | bytes 2308
  7.2 9.5 %copy-start.91 = (f32[1,6,48]{2,0,1:T(1,128)S(1)}, f32[1,6,48]{2,0,1:T(1,128)}, u32[]{:S(2)}) copy-start(f32[1,6,48]{2,0,1:T(1,128)} %param.20) | copy-start | bytes 3460
  7.2 9.5 %copy-start.51 = (f32[1,48,768]{2,1,0:T(8,128)S(1)}, f32[1,48,768]{2,1,0:T(8,128)}, u32[]{:S(2)}) copy-start(f32[1,48,768]{2,1,0:T(8,128)} %param.16) | copy-start | bytes 442372
  7.2 9.7 %copy-start.42 = (f32[1,192,768]{2,1,0:T(8,128)S(1)}, f32[1,192,768]{2,1,0:T(8,128)}, u32[]{:S(2)}) copy-start(f32[1,192,768]{2,1,0:T(8,128)} %param.18) | copy-start | bytes 1769476
  7.2 9.7 %copy-start.41 = (f32[1,48,3072]{2,1,0:T(8,128)S(1)}, f32[1,48,3072]{2,1,0:T(8,128)}, u32[]{:S(2)}) copy-start(f32[1,48,3072]{2,1,0:T(8,128)} %param.17) | copy-start | bytes 1769476
  8.4 8.5 %collective-permute-start = (bf16[48,1152]{1,0:T(8,128)(2,1)S(1)}, bf16[48,1152]{1,0:T(8,128)(2,1)S(1)}, u32[]{:S(2)}, u32[]{:S(2)}) collective-permute-start(bf16[48,1152]{1,0:T(8,128)(2,1)S(1)} %slice.481), channel_id=1, source_target_pairs={{0,16},{1,17},{2,18},{3,19},{4,20},{5,21},{6,22},{7,23},{8,24},{9,... | collective-permute-start | bytes 331784 | tf_op jit(solution)/shard_map/ppermute | solution.py:1027
  15.2 12.3 %collective-permute-start.2 = (bf16[256,768]{1,0:T(8,128)(2,1)}, bf16[256,768]{1,0:T(8,128)(2,1)}, u32[]{:S(2)}, u32[]{:S(2)}) collective-permute-start(bf16[256,768]{1,0:T(8,128)(2,1)} %select_bitcast_fusion.8), channel_id=1, source_target_pairs={{16,24},{17,25},{18,26},{19,27},{20,28},{21,29},{22,30},{23,31},{2... | collective-permute-start | bytes 1179656 | tf_op jit(solution)/shard_map/ppermute | solution.py:1027
  20.5 12.8 %collective-permute-start.1 = (bf16[24,9216]{1,0:T(8,128)(2,1)}, bf16[24,9216]{1,0:T(8,128)(2,1)}, u32[]{:S(2)}, u32[]{:S(2)}) collective-permute-start(bf16[24,9216]{1,0:T(8,128)(2,1)} %get-tuple-element.229), channel_id=1, source_target_pairs={{0,16},{16,0},{1,17},{17,1},{2,18},{18,2},{3,19},{19,3},{4,20},{20... | collective-permute-start | bytes 1327112 | tf_op jit(solution)/shard_map/ppermute | solution.py:936
  23.9 16.9 %all-to-all-start = ((bf16[4,48,1280]{2,1,0:T(8,128)(2,1)}), bf16[4,48,1280]{2,1,0:T(8,128)(2,1)S(1)}, u32[]{:S(2)}, u32[]{:S(2)}) async-start(bf16[4,48,1280]{2,1,0:T(8,128)(2,1)} %broadcast_in_dim.58), calls=%async_computation | async-start | bytes 983040 | tf_op jit(solution)/shard_map/all_to_all | solution.py:966
  27.4 143.6 %all-gather.3.cloned.1.call-start = ((), (), s32[]{:S(2)}) async-start(), calls=%async_computation.15 | async-start | bytes 14598144 | tf_op jit(solution)/shard_map/all_gather | solution.py:1067
  27.5 143.6 %copy-start.10 = (bf16[256,768]{1,0:T(8,128)(2,1)}, bf16[256,768]{1,0:T(8,128)(2,1)S(1)}, u32[]{:S(2)}) copy-start(bf16[256,768]{1,0:T(8,128)(2,1)S(1)} %bitcast_select_fusion.1) | copy-start | bytes 1179652
  40.9 239.3 %all-gather.5.cloned.1.call-start = ((), (), s32[]{:S(2)}) async-start(), calls=%async_computation.16 | async-start | bytes 10948608 | tf_op jit(solution)/shard_map/all_gather | solution.py:1068
  76.6 4.1 collective-permute-start.3
  76.8 11.8 %copy-start.60 = (f32[256]{0:T(256)}, f32[256]{0:T(256)S(1)}, u32[]{:S(2)}) copy-start(f32[256]{0:T(256)S(1)} %broadcast_multiply_fusion.11) | copy-start | bytes 3076
  77.1 11.5 %copy-start.64 = (f32[256]{0:T(256)}, f32[256]{0:T(256)S(1)}, u32[]{:S(2)}) copy-start(f32[256]{0:T(256)S(1)} %add_rsqrt_fusion.3) | copy-start | bytes 3076
  92.8 36.9 %all-to-all-start.2 = ((bf16[16,144,256]{2,1,0:T(8,128)(2,1)}), bf16[16,144,256]{2,1,0:T(8,128)(2,1)S(1)}, u32[]{:S(2)}, u32[]{:S(2)}) async-start(bf16[16,144,256]{2,1,0:T(8,128)(2,1)} %fusion.64), calls=%async_computation.2 | async-start | bytes 2359296 | tf_op jit(solution)/shard_map/all_to_all | solution.py:1024
  96.7 8.3 %collective-permute-start.4 = (bf16[256,768]{1,0:T(8,128)(2,1)S(1)}, bf16[256,768]{1,0:T(8,128)(2,1)}, u32[]{:S(2)}, u32[]{:S(2)}) collective-permute-start(bf16[256,768]{1,0:T(8,128)(2,1)S(1)} %select_bitcast_fusion.7), channel_id=1, source_target_pairs={{16,24},{17,25},{18,26},{19,27},{20,28},{21,29},{22,30},{23,31},{2... | collective-permute-start | bytes 1179656 | tf_op jit(solution)/shard_map/ppermute | solution.py:1027
  105.0 118.2 %copy-start.2 = (f32[16,1,256]{2,1,0:T(1,128)}, f32[16,1,256]{2,1,0:T(1,128)S(1)}, u32[]{:S(2)}) copy-start(f32[16,1,256]{2,1,0:T(1,128)S(1)} %reshape.599.docs_ref) | copy-start | bytes 49156
  129.7 17.7 %copy-start = (bf16[16,144,256]{2,1,0:T(8,128)(2,1)}, bf16[16,144,256]{2,1,0:T(8,128)(2,1)S(1)}, u32[]{:S(2)}) copy-start(bf16[16,144,256]{2,1,0:T(8,128)(2,1)S(1)} %all-to-all-done.2.x_ref) | copy-start | bytes 3538948
  148.9 21.2 %copy-start.70 = (s32[16,256]{1,0:T(8,128)S(1)}, s32[16,256]{1,0:T(8,128)}, u32[]{:S(2)}) copy-start(s32[16,256]{1,0:T(8,128)} %constant.167.clone) | copy-start | bytes 49156
  148.9 22.2 %copy-start.90 = (f32[768]{0:T(1024)S(1)}, f32[768]{0:T(1024)}, u32[]{:S(2)}) copy-start(f32[768]{0:T(1024)} %get-tuple-element.193) | copy-start | bytes 9220
  148.9 21.2 %all-to-all-start.3 = ((bf16[16,48,256]{2,1,0:T(8,128)(2,1)}), bf16[16,48,256]{2,1,0:T(8,128)(2,1)S(1)}, u32[]{:S(2)}, u32[]{:S(2)}) async-start(bf16[16,48,256]{2,1,0:T(8,128)(2,1)} %get-tuple-element.67), calls=%async_computation.3 | async-start | bytes 786432 | tf_op jit(solution)/shard_map/all_to_all | solution.py:1024
  171.1 9.0 %copy-start.25 = (bf16[768,9216]{1,0:T(8,128)(2,1)S(1)}, bf16[768,9216]{1,0:T(8,128)(2,1)}, u32[]{:S(2)}) copy-start(bf16[768,9216]{1,0:T(8,128)(2,1)} %all-gather.3.cloned.1.call-done) | copy-start | bytes 42467332
  173.1 33.8 %copy-start.14 = (f32[256,768]{1,0:T(8,128)}, f32[256,768]{1,0:T(8,128)S(1)}, u32[]{:S(2)}) copy-start(f32[256,768]{1,0:T(8,128)S(1)} %get-tuple-element.238) | copy-start | bytes 2359300
  182.2 232.6 %copy-start.12 = (bf16[256,768]{1,0:T(8,128)(2,1)}, bf16[256,768]{1,0:T(8,128)(2,1)S(1)}, u32[]{:S(2)}) copy-start(bf16[256,768]{1,0:T(8,128)(2,1)S(1)} %get-tuple-element.242) | copy-start | bytes 1179652
  186.2 37.0 %all-to-all-start.4 = ((bf16[16,144,256]{2,1,0:T(8,128)(2,1)}), bf16[16,144,256]{2,1,0:T(8,128)(2,1)S(1)}, u32[]{:S(2)}, u32[]{:S(2)}) async-start(bf16[16,144,256]{2,1,0:T(8,128)(2,1)} %fusion.65), calls=%async_computation.4 | async-start | bytes 2359296 | tf_op jit(solution)/shard_map/all_to_all | solution.py:1024
  198.4 44.0 %collective-permute-start.5 = (bf16[256,768]{1,0:T(8,128)(2,1)S(1)}, bf16[256,768]{1,0:T(8,128)(2,1)S(1)}, u32[]{:S(2)}, u32[]{:S(2)}) collective-permute-start(bf16[256,768]{1,0:T(8,128)(2,1)S(1)} %get-tuple-element.242), channel_id=1, source_target_pairs={{16,8},{17,9},{18,10},{19,11},{20,12},{21,13},{22,14},{23,15},{24,... | collective-permute-start | bytes 1179656 | tf_op jit(solution)/shard_map/ppermute | solution.py:1027
  223.2 17.7 %copy-start.1 = (bf16[16,144,256]{2,1,0:T(8,128)(2,1)}, bf16[16,144,256]{2,1,0:T(8,128)(2,1)S(1)}, u32[]{:S(2)}) copy-start(bf16[16,144,256]{2,1,0:T(8,128)(2,1)S(1)} %all-to-all-done.4.x_ref) | copy-start | bytes 3538948
  242.4 41.4 %copy-start.43 = (bf16[256,768]{1,0:T(8,128)(2,1)}, bf16[256,768]{1,0:T(8,128)(2,1)S(1)}, u32[]{:S(2)}) copy-start(bf16[256,768]{1,0:T(8,128)(2,1)S(1)} %collective-permute-done.5) | copy-start | bytes 1179652
  242.4 46.7 %all-to-all-start.5 = ((bf16[16,48,256]{2,1,0:T(8,128)(2,1)}), bf16[16,48,256]{2,1,0:T(8,128)(2,1)S(1)}, u32[]{:S(2)}, u32[]{:S(2)}) async-start(bf16[16,48,256]{2,1,0:T(8,128)(2,1)} %get-tuple-element.72), calls=%async_computation.5 | async-start | bytes 786432 | tf_op jit(solution)/shard_map/all_to_all | solution.py:1024
  312.2 25.1 %all-to-all-start.6 = ((bf16[16,48,256]{2,1,0:T(8,128)(2,1)}), bf16[16,48,256]{2,1,0:T(8,128)(2,1)S(1)}, u32[]{:S(2)}, u32[]{:S(2)}) async-start(bf16[16,48,256]{2,1,0:T(8,128)(2,1)} %fusion.86), calls=%async_computation.6 | async-start | bytes 786432 | tf_op jit(solution)/shard_map/all_to_all | solution.py:1024
  315.8 148.0 %reduce-scatter.3.cloned.1.call-start = ((), (), s32[]{:S(2)}) async-start(), calls=%async_computation.17 | async-start | bytes 11943936 | tf_op jit(solution)/shard_map/reduce_scatter | solution.py:1091
  342.0 37.3 %collective-permute-start.7 = (bf16[256,768]{1,0:T(8,128)(2,1)S(1)}, bf16[256,768]{1,0:T(8,128)(2,1)}, u32[]{:S(2)}, u32[]{:S(2)}) collective-permute-start(bf16[256,768]{1,0:T(8,128)(2,1)S(1)} %fusion.83), channel_id=1, source_target_pairs={{16,24},{17,25},{18,26},{19,27},{20,28},{21,29},{22,30},{23,31},{2... | collective-permute-start | bytes 1179656 | tf_op jit(solution)/shard_map/ppermute | solution.py:1027
  343.4 35.8 %collective-permute-start.6 = (bf16[256,768]{1,0:T(8,128)(2,1)S(1)}, bf16[256,768]{1,0:T(8,128)(2,1)}, u32[]{:S(2)}, u32[]{:S(2)}) collective-permute-start(bf16[256,768]{1,0:T(8,128)(2,1)S(1)} %fusion.83), channel_id=1, source_target_pairs={{0,16},{1,17},{2,18},{3,19},{4,20},{5,21},{6,22},{7,23},{8,24},{9,... | collective-permute-start | bytes 1179656 | tf_op jit(solution)/shard_map/ppermute | solution.py:1027
  379.2 7.5 %copy-start.100 = (bf16[128]{0:T(256)(128)(2,1)S(1)}, bf16[128]{0:T(256)(128)(2,1)}, u32[]{:S(2)}) copy-start(bf16[128]{0:T(256)(128)(2,1)} %compare_convert_fusion.18) | copy-start | bytes 772
  379.3 24.5 %all-to-all-start.7 = ((bf16[16,144,256]{2,1,0:T(8,128)(2,1)}), bf16[16,144,256]{2,1,0:T(8,128)(2,1)}, u32[]{:S(2)}, u32[]{:S(2)}) async-start(bf16[16,144,256]{2,1,0:T(8,128)(2,1)} %attend_back.2), calls=%async_computation.7 | async-start | bytes 2359296 | tf_op jit(solution)/shard_map/all_to_all | solution.py:1024
  389.3 14.5 %copy-start.72 = (s32[16,256]{1,0:T(8,128)S(1)}, s32[16,256]{1,0:T(8,128)}, u32[]{:S(2)}) copy-start(s32[16,256]{1,0:T(8,128)} %constant.167.clone) | copy-start | bytes 49156
  403.7 14.2 %slice-start = ((s8[14155776]{0:T(1024)(128)(4,1)}), s8[4194304]{0:T(1024)(128)(4,1)S(1)}, s32[]{:S(2)}) async-start(s8[14155776]{0:T(1024)(128)(4,1)} %bitcast.280), calls=%async_computation.19 | async-start | bytes 8388608
  406.9 11.0 %slice-start.1 = ((s8[14155776]{0:T(1024)(128)(4,1)}), s8[4194304]{0:T(1024)(128)(4,1)S(1)}, s32[]{:S(2)}) async-start(s8[14155776]{0:T(1024)(128)(4,1)} %bitcast.280), calls=%async_computation.20 | async-start | bytes 8388608
  415.1 8.9 %copy-start.7 = (bf16[256,768]{1,0:T(8,128)(2,1)}, bf16[256,768]{1,0:T(8,128)(2,1)S(1)}, u32[]{:S(2)}) copy-start(bf16[256,768]{1,0:T(8,128)(2,1)S(1)} %fusion.172) | copy-start | bytes 1179652
  427.4 23.1 %all-to-all-start.8 = ((bf16[16,48,256]{2,1,0:T(8,128)(2,1)}), bf16[16,48,256]{2,1,0:T(8,128)(2,1)}, u32[]{:S(2)}, u32[]{:S(2)}) async-start(bf16[16,48,256]{2,1,0:T(8,128)(2,1)} %fusion.87), calls=%async_computation.8 | async-start | bytes 786432 | tf_op jit(solution)/shard_map/all_to_all | solution.py:1024
  433.1 118.2 %reduce-scatter.5.cloned.1.call-start = ((), (), s32[]{:S(2)}) async-start(), calls=%async_computation.18 | async-start | bytes 11943936 | tf_op jit(solution)/shard_map/reduce_scatter | solution.py:1091
  434.5 12.4 %collective-permute-start.8 = (bf16[8,48,2304]{2,1,0:T(8,128)(2,1)}, bf16[8,48,2304]{2,1,0:T(8,128)(2,1)}, u32[]{:S(2)}, u32[]{:S(2)}) collective-permute-start(bf16[8,48,2304]{2,1,0:T(8,128)(2,1)} %dynamic-slice_bitcast_fusion.1), channel_id=1, source_target_pairs={{0,1},{1,0},{2,3},{3,2},{4,5},{5,4},{6,7},{7,6},{8,9},{9,8},{10,11... | collective-permute-start | bytes 5308424 | tf_op jit(solution)/shard_map/ppermute | solution.py:932
  451.5 46.1 %collective-permute-start.10 = (bf16[256,768]{1,0:T(8,128)(2,1)S(1)}, bf16[256,768]{1,0:T(8,128)(2,1)S(1)}, u32[]{:S(2)}, u32[]{:S(2)}) collective-permute-start(bf16[256,768]{1,0:T(8,128)(2,1)S(1)} %copy-done.9), channel_id=1, source_target_pairs={{16,24},{17,25},{18,26},{19,27},{20,28},{21,29},{22,30},{23,31},{2... | collective-permute-start | bytes 1179656 | tf_op jit(solution)/shard_map/ppermute | solution.py:1027
  452.2 45.4 %collective-permute-start.9 = (bf16[256,768]{1,0:T(8,128)(2,1)S(1)}, bf16[256,768]{1,0:T(8,128)(2,1)}, u32[]{:S(2)}, u32[]{:S(2)}) collective-permute-start(bf16[256,768]{1,0:T(8,128)(2,1)S(1)} %copy-done.9), channel_id=1, source_target_pairs={{0,16},{1,17},{2,18},{3,19},{4,20},{5,21},{6,22},{7,23},{8,24},{9,... | collective-permute-start | bytes 1179656 | tf_op jit(solution)/shard_map/ppermute | solution.py:1027
  459.6 38.0 %all-to-all-start.10 = ((bf16[4,4,48,1152]{3,2,1,0:T(8,128)(2,1)}), bf16[4,4,48,1152]{3,2,1,0:T(8,128)(2,1)S(1)}, u32[]{:S(2)}, u32[]{:S(2)}) async-start(bf16[4,4,48,1152]{3,2,1,0:T(8,128)(2,1)} %pad_maximum_fusion.5), calls=%async_computation.11 | async-start | bytes 3538944 | tf_op jit(solution)/shard_map/all_to_all | solution.py:966
  465.1 31.5 %collective-permute-start.11 = (bf16[2,24,6912]{2,1,0:T(8,128)(2,1)S(1)}, bf16[2,24,6912]{2,1,0:T(8,128)(2,1)S(1)}, u32[]{:S(2)}, u32[]{:S(2)}) collective-permute-start(bf16[2,24,6912]{2,1,0:T(8,128)(2,1)S(1)} %dynamic-slice_bitcast_fusion.3), channel_id=1, source_target_pairs={{0,8},{1,9},{2,10},{3,11},{4,12},{5,13},{6,14},{7,15},{8,0},{9,1},... | collective-permute-start | bytes 1990664 | tf_op jit(solution)/shard_map/ppermute | solution.py:932
  466.3 30.2 %copy-start.36 = (bf16[96,6912]{1,0:T(8,128)(2,1)S(1)}, bf16[96,6912]{1,0:T(8,128)(2,1)}, u32[]{:S(2)}) copy-start(bf16[96,6912]{1,0:T(8,128)(2,1)} %reduce-scatter.3.cloned.1.call-done) | copy-start | bytes 3981316
  494.9 13.6 %copy-start.13 = (bf16[256,768]{1,0:T(8,128)(2,1)S(1)}, bf16[256,768]{1,0:T(8,128)(2,1)}, u32[]{:S(2)}) copy-start(bf16[256,768]{1,0:T(8,128)(2,1)} %copy-done.12) | copy-start | bytes 1179652
  494.9 13.6 %copy-start.44 = (bf16[256,768]{1,0:T(8,128)(2,1)S(1)}, bf16[256,768]{1,0:T(8,128)(2,1)}, u32[]{:S(2)}) copy-start(bf16[256,768]{1,0:T(8,128)(2,1)} %copy-done.43) | copy-start | bytes 1179652
  498.3 29.1 %all-to-all-start.9 = ((bf16[16,144,256]{2,1,0:T(8,128)(2,1)}), bf16[16,144,256]{2,1,0:T(8,128)(2,1)}, u32[]{:S(2)}, u32[]{:S(2)}) async-start(bf16[16,144,256]{2,1,0:T(8,128)(2,1)} %attend_back.3), calls=%async_computation.10 | async-start | bytes 2359296 | tf_op jit(solution)/shard_map/all_to_all | solution.py:1024
  514.9 12.5 %copy-start.74 = (s32[16,256]{1,0:T(8,128)S(1)}, s32[16,256]{1,0:T(8,128)}, u32[]{:S(2)}) copy-start(s32[16,256]{1,0:T(8,128)} %constant.167.clone) | copy-start | bytes 49156
  532.2 11.4 %collective-permute-start.12 = (bf16[8,48,2304]{2,1,0:T(8,128)(2,1)S(1)}, bf16[8,48,2304]{2,1,0:T(8,128)(2,1)S(1)}, u32[]{:S(2)}, u32[]{:S(2)}) collective-permute-start(bf16[8,48,2304]{2,1,0:T(8,128)(2,1)S(1)} %dynamic-slice_bitcast_fusion), channel_id=1, source_target_pairs={{0,1},{1,0},{2,3},{3,2},{4,5},{5,4},{6,7},{7,6},{8,9},{9,8},{10,11... | collective-permute-start | bytes 5308424 | tf_op jit(solution)/shard_map/ppermute | solution.py:932
  539.7 3.8 collective-permute-start.13
  542.2 41.5 %collective-permute-start.14 = (bf16[256,768]{1,0:T(8,128)(2,1)}, bf16[256,768]{1,0:T(8,128)(2,1)}, u32[]{:S(2)}, u32[]{:S(2)}) collective-permute-start(bf16[256,768]{1,0:T(8,128)(2,1)} %get-tuple-element.204), channel_id=1, source_target_pairs={{16,8},{17,9},{18,10},{19,11},{20,12},{21,13},{22,14},{23,15},{24,... | collective-permute-start | bytes 1179656 | tf_op jit(solution)/shard_map/ppermute | solution.py:1027
  545.7 20.0 %copy-start.29 = (bf16[2,24,6912]{2,1,0:T(8,128)(2,1)S(1)}, bf16[2,24,6912]{2,1,0:T(8,128)(2,1)}, u32[]{:S(2)}) copy-start(bf16[2,24,6912]{2,1,0:T(8,128)(2,1)} %fusion.79) | copy-start | bytes 1990660
  545.7 36.8 %all-to-all-start.11 = ((bf16[4,4,48,1280]{3,2,1,0:T(8,128)(2,1)}), bf16[4,4,48,1280]{3,2,1,0:T(8,128)(2,1)S(1)}, u32[]{:S(2)}, u32[]{:S(2)}) async-start(bf16[4,4,48,1280]{3,2,1,0:T(8,128)(2,1)} %maximum_maximum_fusion), calls=%async_computation.12 | async-start | bytes 3932160 | tf_op jit(solution)/shard_map/all_to_all | solution.py:966
  553.2 38.3 %collective-permute-start.15 = (bf16[2,24,6912]{2,1,0:T(8,128)(2,1)}, bf16[2,24,6912]{2,1,0:T(8,128)(2,1)}, u32[]{:S(2)}, u32[]{:S(2)}) collective-permute-start(bf16[2,24,6912]{2,1,0:T(8,128)(2,1)} %dynamic-slice_bitcast_fusion.2), channel_id=1, source_target_pairs={{0,8},{1,9},{2,10},{3,11},{4,12},{5,13},{6,14},{7,15},{8,0},{9,1},... | collective-permute-start | bytes 1990664 | tf_op jit(solution)/shard_map/ppermute | solution.py:932
  566.4 52.9 %collective-permute-start.18 = (bf16[24,6912]{1,0:T(8,128)(2,1)}, bf16[24,6912]{1,0:T(8,128)(2,1)}, u32[]{:S(2)}, u32[]{:S(2)}) collective-permute-start(bf16[24,6912]{1,0:T(8,128)(2,1)} %dynamic-slice_bitcast_fusion.4), channel_id=1, source_target_pairs={{0,4},{1,5},{2,6},{3,7},{4,0},{5,1},{6,2},{7,3},{8,12},{9,13},{10,... | collective-permute-start | bytes 995336 | tf_op jit(solution)/shard_map/ppermute | solution.py:932
  585.9 28.3 %all-to-all-start.12 = ((bf16[4,48,2432]{2,1,0:T(8,128)(2,1)}), bf16[4,48,2432]{2,1,0:T(8,128)(2,1)S(1)}, u32[]{:S(2)}, u32[]{:S(2)}) async-start(bf16[4,48,2432]{2,1,0:T(8,128)(2,1)} %pad_maximum_fusion.6), calls=%async_computation.13 | async-start | bytes 1867776 | tf_op jit(solution)/shard_map/all_to_all | solution.py:966
  614.5 4.8 collective-permute-start.16
  617.6 9.1 %collective-permute-start.17 = (bf16[24,6912]{1,0:T(8,128)(2,1)S(1)}, bf16[24,6912]{1,0:T(8,128)(2,1)S(1)}, u32[]{:S(2)}, u32[]{:S(2)}) collective-permute-start(bf16[24,6912]{1,0:T(8,128)(2,1)S(1)} %dynamic-slice_bitcast_fusion.5), channel_id=1, source_target_pairs={{0,4},{1,5},{2,6},{3,7},{4,0},{5,1},{6,2},{7,3},{8,12},{9,13},{10,... | collective-permute-start | bytes 995336 | tf_op jit(solution)/shard_map/ppermute | solution.py:932
  627.9 8.2 %collective-permute-start.19 = (bf16[24,6912]{1,0:T(8,128)(2,1)S(1)}, bf16[24,6912]{1,0:T(8,128)(2,1)S(1)}, u32[]{:S(2)}, u32[]{:S(2)}) collective-permute-start(bf16[24,6912]{1,0:T(8,128)(2,1)S(1)} %get-tuple-element.200), channel_id=1, source_target_pairs={{0,16},{16,0},{1,17},{17,1},{2,18},{18,2},{3,19},{19,3},{4,20},{20... | collective-permute-start | bytes 995336 | tf_op jit(solution)/shard_map/ppermute | solution.py:936
  (89 other events, 236.7 us)
Sparse Core Ops, SparseCore 0:
  41.0 129.4 all-gather.2
  173.9 106.2 all-gather.4
  337.4 95.4 reduce-scatter.2
  450.7 100.2 reduce-scatter.4

commit v6 on v5

--- a/solution.py
+++ b/solution.py
@@ -622,7 +622,7 @@
     same = ids == doc_row
     return (jnp.where(same, 0.0, AWAY) if away else jnp.where(same, 1.0, 0.0)).astype(BF16)
 
-def fwd_kernel(x_ref, docs_ref, o_ref, ob_ref, lse_ref, fm, ktm, part, *, kc):
+def fwd_kernel(x_ref, docs_ref, ob_ref, lse_ref, fm, ktm, part, *, kc):
     pad = jnp.zeros((AUG - HD - IDS, TOK), BF16)
     def load(s, _):
         x = x_ref[s]
@@ -683,7 +683,6 @@
         own = part[s]
         l, m = own[HD:HD + 1], own[HD + 8:HD + 9]
         out = own[0:HD] / l
-        o_ref[s] = out
         ob_ref[s] = out.astype(BF16)
         lse_ref[s] = m + jnp.log2(l)
         return 0
@@ -692,9 +691,9 @@
 def attn_fwd(x, docs):
     return pl.pallas_call(
         functools.partial(fwd_kernel, kc=256),
-        out_shape=(jax.ShapeDtypeStruct((SRC, HD, TOK), F32), jax.ShapeDtypeStruct((SRC, HD, TOK), BF16), jax.ShapeDtypeStruct((SRC, 1, TOK), F32)),
+        out_shape=(jax.ShapeDtypeStruct((SRC, HD, TOK), BF16), jax.ShapeDtypeStruct((SRC, 1, TOK), F32)),
         in_specs=[pl.BlockSpec(memory_space=pltpu.VMEM)] * 2,
-        out_specs=[pl.BlockSpec(memory_space=pltpu.VMEM)] * 3,
+        out_specs=[pl.BlockSpec(memory_space=pltpu.VMEM)] * 2,
         scratch_shapes=[
             pltpu.VMEM((31, 2 * AUG + HD, TOK), BF16),
             pltpu.VMEM((31, TOK, AUG), BF16),
@@ -718,7 +717,7 @@
         x = x_ref[s]
         d = docs_ref[s]
         g = g_ref[s]
-        dot = jnp.sum(g.astype(F32) * o_ref[s], axis=0, keepdims=True)
+        dot = jnp.sum(g.astype(F32) * o_ref[s].astype(F32), axis=0, keepdims=True)
         low = three(lse_ref[s] * (-1.0 / C2))
         off = three(-dot)
         fm[s] = jnp.concatenate([
@@ -839,8 +838,9 @@
     mixed = mixed.reshape(3, HEADS, HEAD_DIM, TOK).transpose(1, 0, 2, 3).reshape(HEADS, 3 * HEAD_DIM, TOK)
     mixed = jnp.einsum("hft,htu->hfu", mixed, order, preferred_element_type=F32).astype(BF16)
     heads = trade(mixed)
-    merged, merged_low, summary = attn_fwd(heads, docs)
+    merged_low, summary = attn_fwd(heads, docs)
     merged_low, window = lax.optimization_barrier((merged_low, window))
+    merged = merged_low
     attended = trade(merged_low)
     attended = jnp.einsum("hdu,htu->hdt", attended, order, preferred_element_type=F32).astype(BF16)
     attended = attended.reshape(D, TOK)

time: 660 us -> 660 us (level)
  transfers between devices with their start and end apart: 36 -> 36, of which waited for: 15 -> 16; matrix products, arithmetic and copies ran while one was open for 27% -> 27% of each run, Pallas kernels for 14% -> 14%
where the time goes in v6:
time: 660 us; the launch traced here: 649 us
  waiting for transfers between devices  181 us (27%)
  matrix products  136 us (21%)
  starting transfers between devices  106 us (16%)
  Pallas kernels  92.2 us (14%)
  other arithmetic  44.2 us (7%)
  local copies, waits for them, and re-layouts  38.2 us (6%)
  blocking collectives  34.9 us (5%)
  between operations  16.3 us (2%)
    all_to_all x8, waiting for transfers between devices, trade(): lax.all_to_all(value, axes, 0, 0, axis_index_groups=teams, tiled=True)  76.8 us
    pallas_call x2, Pallas kernels, attn_bwd(): pl.pallas_call(bwd_kernel, out_shape=jax.ShapeDtypeStruct((SRC, 3 * HD, T...  56.9 us
    all_to_all x8, starting transfers between devices, trade(): lax.all_to_all(value, axes, 0, 0, axis_index_groups=teams, tiled=True)  41.7 us
    all_to_all x4, waiting for transfers between devices, team_trade(): lax.all_to_all(value, ('section', 'seq'), 0, 0, axis_index_groups=team(ki...  38.9 us
    all_gather x1, waiting for transfers between devices, cube_body(): rest_final = lax.all_gather(far, ('seq', 'section'), axis=0, tiled=True)  36.7 us
    pallas_call x2, Pallas kernels, attn_fwd(): pl.pallas_call(functools.partial(fwd_kernel, kc=256), out_shape=(jax.Shap...  35.3 us
    all_to_all x1, blocking collectives, team_trade(): lax.all_to_all(value, ('section', 'seq'), 0, 0, axis_index_groups=team(ki...  34.9 us
    dot_general x10, matrix products, inner_rows(): jnp.einsum('ta,tb->ab', left, right, preferred_element_type=jnp.float32)  28.9 us
  transfers between devices with their start and end apart: 36, of which 16 were waited for; matrix products, arithmetic and copies ran while one was open for 27% of the time, Pallas kernels for 14%

profile of v6, /device:TPU:0, one launch (start us, length us, event | category | flops | bytes accessed | tf_op | source)
XLA Modules:
  0.0 649.1 jit_solution(16438275656091216509)
XLA Ops:
  8.4 4.8 collective-permute-start
  20.5 2.6 collective-permute-start.1
  23.9 3.5 all-to-all-start
  27.5 5.7 collective-permute-done.1
  36.7 4.1 all-to-all-done
  41.8 34.9 %all_to_all.65 = bf16[4,4,48,1280]{3,2,1,0:T(8,128)(2,1)S(1)} all-to-all(bf16[4,4,48,1280]{3,2,1,0:T(8,128)(2,1)S(1)} %broadcast_in_dim.59), channel_id=1, replica_groups={{0,2,16,18},{1,3,17,19},{4,6,20,22},{5,7,21,23},{8,10,24,26},{9,11,25,2..., dimensions={0} | all-to-all | bytes 3932160 | tf_op jit(solution)/shard_map/all_to_all | solution.py:966
  77.1 3.7 collective-permute-done.3
  80.7 2.1 select_bitcast_fusion.3
  85.7 2.2 slice_reduce_fusion
  90.8 2.0 fusion.64
  92.8 3.8 all-to-all-start.2
  105.1 24.6 %all-to-all-done.2.x_ref = bf16[16,144,256]{2,1,0:T(8,128)(2,1)S(1)} async-done(((bf16[16,144,256]{2,1,0:T(8,128)(2,1)}), bf16[16,144,256]{2,1,0:T(8,128)(2,1)S(1)}, u32[]{:S(2)}, u32[]{:S(2)}) %all-to-all-start.2) | async-done | bytes 1179680 | tf_op jit(solution)/shard_map/all_to_all | solution.py:1024
  129.7 17.7 %attend.2 = (bf16[16,48,256]{2,1,0:T(8,128)(2,1)}, f32[16,1,256]{2,1,0:T(1,128)S(1)}) custom-call(bf16[16,144,256]{2,1,0:T(8,128)(2,1)S(1)} %all-to-all-done.2.x_ref, f32[16,1,256]{2,1,0:T(1,128)S(1)} %reshape.599.docs_ref), custom_call_target="tpu_custom_call" | custom-call | flops 17999998976 | bytes 3145728 | tf_op jit(solution)/shard_map/attend/pallas_call | solution.py:692
  148.0 5.1 all-to-all-start.3
  155.0 15.2 %all-to-all-done.3 = bf16[16,48,256]{2,1,0:T(8,128)(2,1)S(1)} async-done(((bf16[16,48,256]{2,1,0:T(8,128)(2,1)}), bf16[16,48,256]{2,1,0:T(8,128)(2,1)S(1)}, u32[]{:S(2)}, u32[]{:S(2)}) %all-to-all-start.3) | async-done | bytes 393248 | tf_op jit(solution)/shard_map/all_to_all | solution.py:1024
  171.1 2.0 fusion.285
  173.5 6.6 %multiply_convert_fusion.1 = (bf16[256,3072]{1,0:T(8,128)(2,1)S(1)}, f32[256,3072]{1,0:T(8,128)}) fusion(f32[3072]{0:T(1024)S(1)} %add.363, bf16[768,9216]{1,0:T(8,128)(2,1)} %all-gather.3.cloned.1.call-done, f32[256,768]{1,0:T(8,128)S(1)} %get-tuple-element.234, f32[768]{0:T(1024)S(1)} %copy-done.87, f32[768]{0:T(1024)S(1)} %copy-done.74, ...), kind=kOutput, calls=%fused_computation.50 | convolution fusion | flops 1213661184 | bytes 10244096 | tf_op jit(solution)/shard_map/dot_general | solution.py:850
  184.8 2.1 fusion.65
  186.9 4.6 all-to-all-start.4
  196.3 2.8 fusion.89
  200.8 2.5 fusion.90
  209.3 12.1 %all-to-all-done.4.x_ref = bf16[16,144,256]{2,1,0:T(8,128)(2,1)S(1)} async-done(((bf16[16,144,256]{2,1,0:T(8,128)(2,1)}), bf16[16,144,256]{2,1,0:T(8,128)(2,1)S(1)}, u32[]{:S(2)}, u32[]{:S(2)}) %all-to-all-start.4) | async-done | bytes 1179680 | tf_op jit(solution)/shard_map/all_to_all | solution.py:1024
  221.4 17.7 %attend.3 = (bf16[16,48,256]{2,1,0:T(8,128)(2,1)}, f32[16,1,256]{2,1,0:T(1,128)S(1)}) custom-call(bf16[16,144,256]{2,1,0:T(8,128)(2,1)S(1)} %all-to-all-done.4.x_ref, f32[16,1,256]{2,1,0:T(1,128)S(1)} %reshape.599.docs_ref), custom_call_target="tpu_custom_call" | custom-call | flops 17999998976 | bytes 3145728 | tf_op jit(solution)/shard_map/attend/pallas_call | solution.py:692
  239.6 4.2 all-to-all-start.5
  243.9 36.7 %all-gather.5.cloned.1.call-done = bf16[768,6912]{1,0:T(8,128)(2,1)} async-done(((bf16[24,6912]{1,0:T(8,128)(2,1)}), bf16[768,6912]{1,0:T(8,128)(2,1)}) %all-gather.5.cloned.1.call-update) | async-done | bytes 10616848 | tf_op jit(solution)/shard_map/all_gather | solution.py:1068
  284.2 2.7 fusion.135
  286.8 2.7 fusion.138
  290.4 2.0 fusion.286
  292.8 5.9 multiply_convert_fusion
  298.7 5.8 fusion
  304.5 4.4 multiply_reduce_fusion.7
  312.6 3.6 all-to-all-start.6
  316.5 3.3 fusion.77
  319.8 3.2 fusion.76
  323.0 3.2 fusion.75
  326.3 3.3 fusion.74
  329.6 3.5 fusion.73
  334.9 2.8 convolution_add_fusion.4
  338.5 2.1 convolution_add_fusion.3
  343.9 7.2 %collective-permute-start.6 = (bf16[256,768]{1,0:T(8,128)(2,1)S(1)}, bf16[256,768]{1,0:T(8,128)(2,1)}, u32[]{:S(2)}, u32[]{:S(2)}) collective-permute-start(bf16[256,768]{1,0:T(8,128)(2,1)S(1)} %fusion.83), channel_id=1, source_target_pairs={{0,16},{1,17},{2,18},{3,19},{4,20},{5,21},{6,22},{7,23},{8,24},{9,... | collective-permute-start | bytes 1179656 | tf_op jit(solution)/shard_map/ppermute | solution.py:1027
  351.1 28.5 %attend_back.2 = bf16[16,144,256]{2,1,0:T(8,128)(2,1)} custom-call(bf16[16,144,256]{2,1,0:T(8,128)(2,1)} %copy-done.1, bf16[16,48,256]{2,1,0:T(8,128)(2,1)} %copy-done.44, f32[16,1,256]{2,1,0:T(1,128)} %copy-done.2, bf16[16,48,256]{2,1,0:T(8,128)(2,1)} %get-tuple-element.71.o_ref, f32[16,1,256]{2,1,0:T(1,128)} %copy-done.4), custom_call_target="tpu_custom_call" | custom-call | flops 28000000000 | bytes 6291456 | tf_op jit(solution)/shard_map/attend_back/pallas_call | solution.py:785
  379.6 4.6 all-to-all-start.7
  390.2 13.8 %all-to-all-done.7 = bf16[16,144,256]{2,1,0:T(8,128)(2,1)} async-done(((bf16[16,144,256]{2,1,0:T(8,128)(2,1)}), bf16[16,144,256]{2,1,0:T(8,128)(2,1)}, u32[]{:S(2)}, u32[]{:S(2)}) %all-to-all-start.7) | async-done | bytes 1179680 | tf_op jit(solution)/shard_map/all_to_all | solution.py:1024
  404.0 2.5 fusion.66
  407.2 3.5 multiply_reduce_fusion.6
  415.4 2.9 convolution_convert_fusion.2
  427.8 5.6 all-to-all-start.8
  435.6 3.7 fusion.1
  452.5 7.5 %collective-permute-start.9 = (bf16[256,768]{1,0:T(8,128)(2,1)S(1)}, bf16[256,768]{1,0:T(8,128)(2,1)}, u32[]{:S(2)}, u32[]{:S(2)}) collective-permute-start(bf16[256,768]{1,0:T(8,128)(2,1)S(1)} %copy-done.7), channel_id=1, source_target_pairs={{0,16},{1,17},{2,18},{3,19},{4,20},{5,21},{6,22},{7,23},{8,24},{9,... | collective-permute-start | bytes 1179656 | tf_op jit(solution)/shard_map/ppermute | solution.py:1027
  460.0 4.1 all-to-all-start.10
  466.7 28.4 %attend_back.3 = bf16[16,144,256]{2,1,0:T(8,128)(2,1)} custom-call(bf16[16,144,256]{2,1,0:T(8,128)(2,1)} %copy-done, bf16[16,48,256]{2,1,0:T(8,128)(2,1)} %all-to-all-done.8.g_ref, f32[16,1,256]{2,1,0:T(1,128)} %copy-done.2, bf16[16,48,256]{2,1,0:T(8,128)(2,1)} %get-tuple-element.65.o_ref, f32[16,1,256]{2,1,0:T(1,128)} %copy-done.3), custom_call_target="tpu_custom_call" | custom-call | flops 28000000000 | bytes 6291456 | tf_op jit(solution)/shard_map/attend_back/pallas_call | solution.py:785
  498.7 10.1 %all-to-all-start.9 = ((bf16[16,144,256]{2,1,0:T(8,128)(2,1)}), bf16[16,144,256]{2,1,0:T(8,128)(2,1)}, u32[]{:S(2)}, u32[]{:S(2)}) async-start(bf16[16,144,256]{2,1,0:T(8,128)(2,1)} %attend_back.3), calls=%async_computation.10 | async-start | bytes 2359296 | tf_op jit(solution)/shard_map/all_to_all | solution.py:1024
  516.7 11.1 %all-to-all-done.9 = bf16[16,144,256]{2,1,0:T(8,128)(2,1)} async-done(((bf16[16,144,256]{2,1,0:T(8,128)(2,1)}), bf16[16,144,256]{2,1,0:T(8,128)(2,1)}, u32[]{:S(2)}, u32[]{:S(2)}) %all-to-all-start.9) | async-done | bytes 1179680 | tf_op jit(solution)/shard_map/all_to_all | solution.py:1024
  527.8 2.3 fusion.67
  540.3 2.4 select_bitcast_fusion.4
  546.1 5.5 all-to-all-start.11
  554.2 12.1 %collective-permute-start.15 = (bf16[2,24,6912]{2,1,0:T(8,128)(2,1)}, bf16[2,24,6912]{2,1,0:T(8,128)(2,1)}, u32[]{:S(2)}, u32[]{:S(2)}) collective-permute-start(bf16[2,24,6912]{2,1,0:T(8,128)(2,1)} %dynamic-slice_bitcast_fusion.2), channel_id=1, source_target_pairs={{0,8},{1,9},{2,10},{3,11},{4,12},{5,13},{6,14},{7,15},{8,0},{9,1},... | collective-permute-start | bytes 1990664 | tf_op jit(solution)/shard_map/ppermute | solution.py:932
  567.1 15.9 %all-to-all-done.11 = bf16[4,4,48,1280]{3,2,1,0:T(8,128)(2,1)S(1)} async-done(((bf16[4,4,48,1280]{3,2,1,0:T(8,128)(2,1)}), bf16[4,4,48,1280]{3,2,1,0:T(8,128)(2,1)S(1)}, u32[]{:S(2)}, u32[]{:S(2)}) %all-to-all-start.11) | async-done | bytes 1966112 | tf_op jit(solution)/shard_map/all_to_all | solution.py:966
  584.2 2.2 pad_maximum_fusion.6
  586.4 5.5 all-to-all-start.12
  595.7 18.9 %all-to-all-done.12 = bf16[4,48,2432]{2,1,0:T(8,128)(2,1)S(1)} async-done(((bf16[4,48,2432]{2,1,0:T(8,128)(2,1)}), bf16[4,48,2432]{2,1,0:T(8,128)(2,1)S(1)}, u32[]{:S(2)}, u32[]{:S(2)}) %all-to-all-start.12) | async-done | bytes 933920 | tf_op jit(solution)/shard_map/all_to_all | solution.py:966
  619.7 7.5 %collective-permute-done.17 = bf16[24,6912]{1,0:T(8,128)(2,1)S(1)} collective-permute-done((bf16[24,6912]{1,0:T(8,128)(2,1)S(1)}, bf16[24,6912]{1,0:T(8,128)(2,1)S(1)}, u32[]{:S(2)}, u32[]{:S(2)}) %collective-permute-start.17) | collective-permute-done | bytes 331808 | tf_op jit(solution)/shard_map/ppermute | solution.py:932
  629.6 6.9 %collective-permute-done.19 = bf16[24,6912]{1,0:T(8,128)(2,1)S(1)} collective-permute-done((bf16[24,6912]{1,0:T(8,128)(2,1)S(1)}, bf16[24,6912]{1,0:T(8,128)(2,1)S(1)}, u32[]{:S(2)}, u32[]{:S(2)}) %collective-permute-start.19) | collective-permute-done | bytes 331808 | tf_op jit(solution)/shard_map/ppermute | solution.py:936
  639.7 2.6 reshape.630
  (493 shorter events, 145.7 us)
Async XLA Ops:
  7.2 9.4 %copy-start.101 = (f32[1,2,48]{2,1,0:T(2,128)S(1)}, f32[1,2,48]{2,1,0:T(2,128)}, u32[]{:S(2)}) copy-start(f32[1,2,48]{2,1,0:T(2,128)} %param.19) | copy-start | bytes 1156
  7.2 9.4 %copy-start.102 = (f32[1,192]{1,0:T(1,128)S(1)}, f32[1,192]{1,0:T(1,128)}, u32[]{:S(2)}) copy-start(f32[1,192]{1,0:T(1,128)} %param.21) | copy-start | bytes 2308
  7.2 9.5 %copy-start.90 = (f32[1,6,48]{2,0,1:T(1,128)S(1)}, f32[1,6,48]{2,0,1:T(1,128)}, u32[]{:S(2)}) copy-start(f32[1,6,48]{2,0,1:T(1,128)} %param.20) | copy-start | bytes 3460
  7.2 9.5 %copy-start.49 = (f32[1,48,768]{2,1,0:T(8,128)S(1)}, f32[1,48,768]{2,1,0:T(8,128)}, u32[]{:S(2)}) copy-start(f32[1,48,768]{2,1,0:T(8,128)} %param.16) | copy-start | bytes 442372
  7.2 9.7 %copy-start.40 = (f32[1,192,768]{2,1,0:T(8,128)S(1)}, f32[1,192,768]{2,1,0:T(8,128)}, u32[]{:S(2)}) copy-start(f32[1,192,768]{2,1,0:T(8,128)} %param.18) | copy-start | bytes 1769476
  7.2 9.7 %copy-start.39 = (f32[1,48,3072]{2,1,0:T(8,128)S(1)}, f32[1,48,3072]{2,1,0:T(8,128)}, u32[]{:S(2)}) copy-start(f32[1,48,3072]{2,1,0:T(8,128)} %param.17) | copy-start | bytes 1769476
  8.4 8.5 %collective-permute-start = (bf16[48,1152]{1,0:T(8,128)(2,1)S(1)}, bf16[48,1152]{1,0:T(8,128)(2,1)S(1)}, u32[]{:S(2)}, u32[]{:S(2)}) collective-permute-start(bf16[48,1152]{1,0:T(8,128)(2,1)S(1)} %slice.481), channel_id=1, source_target_pairs={{0,16},{1,17},{2,18},{3,19},{4,20},{5,21},{6,22},{7,23},{8,24},{9,... | collective-permute-start | bytes 331784 | tf_op jit(solution)/shard_map/ppermute | solution.py:1027
  15.2 12.3 %collective-permute-start.2 = (bf16[256,768]{1,0:T(8,128)(2,1)}, bf16[256,768]{1,0:T(8,128)(2,1)}, u32[]{:S(2)}, u32[]{:S(2)}) collective-permute-start(bf16[256,768]{1,0:T(8,128)(2,1)} %select_bitcast_fusion.8), channel_id=1, source_target_pairs={{16,24},{17,25},{18,26},{19,27},{20,28},{21,29},{22,30},{23,31},{2... | collective-permute-start | bytes 1179656 | tf_op jit(solution)/shard_map/ppermute | solution.py:1027
  20.5 12.8 %collective-permute-start.1 = (bf16[24,9216]{1,0:T(8,128)(2,1)}, bf16[24,9216]{1,0:T(8,128)(2,1)}, u32[]{:S(2)}, u32[]{:S(2)}) collective-permute-start(bf16[24,9216]{1,0:T(8,128)(2,1)} %get-tuple-element.225), channel_id=1, source_target_pairs={{0,16},{16,0},{1,17},{17,1},{2,18},{18,2},{3,19},{19,3},{4,20},{20... | collective-permute-start | bytes 1327112 | tf_op jit(solution)/shard_map/ppermute | solution.py:936
  23.9 16.9 %all-to-all-start = ((bf16[4,48,1280]{2,1,0:T(8,128)(2,1)}), bf16[4,48,1280]{2,1,0:T(8,128)(2,1)S(1)}, u32[]{:S(2)}, u32[]{:S(2)}) async-start(bf16[4,48,1280]{2,1,0:T(8,128)(2,1)} %broadcast_in_dim.58), calls=%async_computation | async-start | bytes 983040 | tf_op jit(solution)/shard_map/all_to_all | solution.py:966
  27.4 143.7 %all-gather.3.cloned.1.call-start = ((), (), s32[]{:S(2)}) async-start(), calls=%async_computation.15 | async-start | bytes 14598144 | tf_op jit(solution)/shard_map/all_gather | solution.py:1067
  27.5 143.6 %copy-start.8 = (bf16[256,768]{1,0:T(8,128)(2,1)}, bf16[256,768]{1,0:T(8,128)(2,1)S(1)}, u32[]{:S(2)}) copy-start(bf16[256,768]{1,0:T(8,128)(2,1)S(1)} %bitcast_select_fusion.1) | copy-start | bytes 1179652
  40.9 239.7 %all-gather.5.cloned.1.call-start = ((), (), s32[]{:S(2)}) async-start(), calls=%async_computation.16 | async-start | bytes 10948608 | tf_op jit(solution)/shard_map/all_gather | solution.py:1068
  76.6 4.1 collective-permute-start.3
  76.8 11.8 %copy-start.58 = (f32[256]{0:T(256)}, f32[256]{0:T(256)S(1)}, u32[]{:S(2)}) copy-start(f32[256]{0:T(256)S(1)} %broadcast_multiply_fusion.11) | copy-start | bytes 3076
  77.1 11.5 %copy-start.62 = (f32[256]{0:T(256)}, f32[256]{0:T(256)S(1)}, u32[]{:S(2)}) copy-start(f32[256]{0:T(256)S(1)} %add_rsqrt_fusion.3) | copy-start | bytes 3076
  92.8 36.9 %all-to-all-start.2 = ((bf16[16,144,256]{2,1,0:T(8,128)(2,1)}), bf16[16,144,256]{2,1,0:T(8,128)(2,1)S(1)}, u32[]{:S(2)}, u32[]{:S(2)}) async-start(bf16[16,144,256]{2,1,0:T(8,128)(2,1)} %fusion.64), calls=%async_computation.2 | async-start | bytes 2359296 | tf_op jit(solution)/shard_map/all_to_all | solution.py:1024
  96.7 8.3 %collective-permute-start.4 = (bf16[256,768]{1,0:T(8,128)(2,1)S(1)}, bf16[256,768]{1,0:T(8,128)(2,1)}, u32[]{:S(2)}, u32[]{:S(2)}) collective-permute-start(bf16[256,768]{1,0:T(8,128)(2,1)S(1)} %select_bitcast_fusion.7), channel_id=1, source_target_pairs={{16,24},{17,25},{18,26},{19,27},{20,28},{21,29},{22,30},{23,31},{2... | collective-permute-start | bytes 1179656 | tf_op jit(solution)/shard_map/ppermute | solution.py:1027
  105.0 116.4 %copy-start.2 = (f32[16,1,256]{2,1,0:T(1,128)}, f32[16,1,256]{2,1,0:T(1,128)S(1)}, u32[]{:S(2)}) copy-start(f32[16,1,256]{2,1,0:T(1,128)S(1)} %reshape.599.docs_ref) | copy-start | bytes 49156
  129.7 17.7 %copy-start = (bf16[16,144,256]{2,1,0:T(8,128)(2,1)}, bf16[16,144,256]{2,1,0:T(8,128)(2,1)S(1)}, u32[]{:S(2)}) copy-start(bf16[16,144,256]{2,1,0:T(8,128)(2,1)S(1)} %all-to-all-done.2.x_ref) | copy-start | bytes 3538948
  148.0 22.2 %copy-start.68 = (s32[16,256]{1,0:T(8,128)S(1)}, s32[16,256]{1,0:T(8,128)}, u32[]{:S(2)}) copy-start(s32[16,256]{1,0:T(8,128)} %constant.167.clone) | copy-start | bytes 49156
  148.0 23.2 %copy-start.89 = (f32[768]{0:T(1024)S(1)}, f32[768]{0:T(1024)}, u32[]{:S(2)}) copy-start(f32[768]{0:T(1024)} %get-tuple-element.189) | copy-start | bytes 9220
  148.0 22.2 %all-to-all-start.3 = ((bf16[16,48,256]{2,1,0:T(8,128)(2,1)}), bf16[16,48,256]{2,1,0:T(8,128)(2,1)S(1)}, u32[]{:S(2)}, u32[]{:S(2)}) async-start(bf16[16,48,256]{2,1,0:T(8,128)(2,1)} %get-tuple-element.65.o_ref), calls=%async_computation.3 | async-start | bytes 786432 | tf_op jit(solution)/shard_map/all_to_all | solution.py:1024
  171.1 9.0 %copy-start.23 = (bf16[768,9216]{1,0:T(8,128)(2,1)S(1)}, bf16[768,9216]{1,0:T(8,128)(2,1)}, u32[]{:S(2)}) copy-start(bf16[768,9216]{1,0:T(8,128)(2,1)} %all-gather.3.cloned.1.call-done) | copy-start | bytes 42467332
  173.1 34.5 %copy-start.12 = (f32[256,768]{1,0:T(8,128)}, f32[256,768]{1,0:T(8,128)S(1)}, u32[]{:S(2)}) copy-start(f32[256,768]{1,0:T(8,128)S(1)} %get-tuple-element.234) | copy-start | bytes 2359300
  182.2 232.8 %copy-start.10 = (bf16[256,768]{1,0:T(8,128)(2,1)}, bf16[256,768]{1,0:T(8,128)(2,1)S(1)}, u32[]{:S(2)}) copy-start(bf16[256,768]{1,0:T(8,128)(2,1)S(1)} %get-tuple-element.238) | copy-start | bytes 1179652
  186.9 34.5 %all-to-all-start.4 = ((bf16[16,144,256]{2,1,0:T(8,128)(2,1)}), bf16[16,144,256]{2,1,0:T(8,128)(2,1)S(1)}, u32[]{:S(2)}, u32[]{:S(2)}) async-start(bf16[16,144,256]{2,1,0:T(8,128)(2,1)} %fusion.65), calls=%async_computation.4 | async-start | bytes 2359296 | tf_op jit(solution)/shard_map/all_to_all | solution.py:1024
  199.1 40.5 %collective-permute-start.5 = (bf16[256,768]{1,0:T(8,128)(2,1)S(1)}, bf16[256,768]{1,0:T(8,128)(2,1)S(1)}, u32[]{:S(2)}, u32[]{:S(2)}) collective-permute-start(bf16[256,768]{1,0:T(8,128)(2,1)S(1)} %get-tuple-element.238), channel_id=1, source_target_pairs={{16,8},{17,9},{18,10},{19,11},{20,12},{21,13},{22,14},{23,15},{24,... | collective-permute-start | bytes 1179656 | tf_op jit(solution)/shard_map/ppermute | solution.py:1027
  221.4 17.7 %copy-start.1 = (bf16[16,144,256]{2,1,0:T(8,128)(2,1)}, bf16[16,144,256]{2,1,0:T(8,128)(2,1)S(1)}, u32[]{:S(2)}) copy-start(bf16[16,144,256]{2,1,0:T(8,128)(2,1)S(1)} %all-to-all-done.4.x_ref) | copy-start | bytes 3538948
  239.6 49.8 %all-to-all-start.5 = ((bf16[16,48,256]{2,1,0:T(8,128)(2,1)}), bf16[16,48,256]{2,1,0:T(8,128)(2,1)S(1)}, u32[]{:S(2)}, u32[]{:S(2)}) async-start(bf16[16,48,256]{2,1,0:T(8,128)(2,1)} %get-tuple-element.71.o_ref), calls=%async_computation.5 | async-start | bytes 786432 | tf_op jit(solution)/shard_map/all_to_all | solution.py:1024
  312.6 25.1 %all-to-all-start.6 = ((bf16[16,48,256]{2,1,0:T(8,128)(2,1)}), bf16[16,48,256]{2,1,0:T(8,128)(2,1)S(1)}, u32[]{:S(2)}, u32[]{:S(2)}) async-start(bf16[16,48,256]{2,1,0:T(8,128)(2,1)} %fusion.86), calls=%async_computation.6 | async-start | bytes 786432 | tf_op jit(solution)/shard_map/all_to_all | solution.py:1024
  316.2 147.9 %reduce-scatter.3.cloned.1.call-start = ((), (), s32[]{:S(2)}) async-start(), calls=%async_computation.17 | async-start | bytes 11943936 | tf_op jit(solution)/shard_map/reduce_scatter | solution.py:1091
  342.5 37.1 %collective-permute-start.7 = (bf16[256,768]{1,0:T(8,128)(2,1)S(1)}, bf16[256,768]{1,0:T(8,128)(2,1)}, u32[]{:S(2)}, u32[]{:S(2)}) collective-permute-start(bf16[256,768]{1,0:T(8,128)(2,1)S(1)} %fusion.83), channel_id=1, source_target_pairs={{16,24},{17,25},{18,26},{19,27},{20,28},{21,29},{22,30},{23,31},{2... | collective-permute-start | bytes 1179656 | tf_op jit(solution)/shard_map/ppermute | solution.py:1027
  343.9 35.7 %collective-permute-start.6 = (bf16[256,768]{1,0:T(8,128)(2,1)S(1)}, bf16[256,768]{1,0:T(8,128)(2,1)}, u32[]{:S(2)}, u32[]{:S(2)}) collective-permute-start(bf16[256,768]{1,0:T(8,128)(2,1)S(1)} %fusion.83), channel_id=1, source_target_pairs={{0,16},{1,17},{2,18},{3,19},{4,20},{5,21},{6,22},{7,23},{8,24},{9,... | collective-permute-start | bytes 1179656 | tf_op jit(solution)/shard_map/ppermute | solution.py:1027
  379.5 7.5 %copy-start.99 = (bf16[128]{0:T(256)(128)(2,1)S(1)}, bf16[128]{0:T(256)(128)(2,1)}, u32[]{:S(2)}) copy-start(bf16[128]{0:T(256)(128)(2,1)} %compare_convert_fusion.18) | copy-start | bytes 772
  379.6 24.5 %all-to-all-start.7 = ((bf16[16,144,256]{2,1,0:T(8,128)(2,1)}), bf16[16,144,256]{2,1,0:T(8,128)(2,1)}, u32[]{:S(2)}, u32[]{:S(2)}) async-start(bf16[16,144,256]{2,1,0:T(8,128)(2,1)} %attend_back.2), calls=%async_computation.7 | async-start | bytes 2359296 | tf_op jit(solution)/shard_map/all_to_all | solution.py:1024
  389.6 14.5 %copy-start.71 = (s32[16,256]{1,0:T(8,128)S(1)}, s32[16,256]{1,0:T(8,128)}, u32[]{:S(2)}) copy-start(s32[16,256]{1,0:T(8,128)} %constant.167.clone) | copy-start | bytes 49156
  404.0 14.3 %slice-start = ((s8[14155776]{0:T(1024)(128)(4,1)}), s8[4194304]{0:T(1024)(128)(4,1)S(1)}, s32[]{:S(2)}) async-start(s8[14155776]{0:T(1024)(128)(4,1)} %bitcast.280), calls=%async_computation.19 | async-start | bytes 8388608
  407.2 11.1 %slice-start.1 = ((s8[14155776]{0:T(1024)(128)(4,1)}), s8[4194304]{0:T(1024)(128)(4,1)S(1)}, s32[]{:S(2)}) async-start(s8[14155776]{0:T(1024)(128)(4,1)} %bitcast.280), calls=%async_computation.20 | async-start | bytes 8388608
  410.8 7.6 %slice-start.2 = ((s8[14155776]{0:T(1024)(128)(4,1)}), s8[4194304]{0:T(1024)(128)(4,1)S(1)}, s32[]{:S(2)}) async-start(s8[14155776]{0:T(1024)(128)(4,1)} %bitcast.280), calls=%async_computation.21 | async-start | bytes 8388608
  415.4 9.0 %copy-start.5 = (bf16[256,768]{1,0:T(8,128)(2,1)}, bf16[256,768]{1,0:T(8,128)(2,1)S(1)}, u32[]{:S(2)}) copy-start(bf16[256,768]{1,0:T(8,128)(2,1)S(1)} %fusion.172) | copy-start | bytes 1179652
  427.8 23.0 %all-to-all-start.8 = ((bf16[16,48,256]{2,1,0:T(8,128)(2,1)}), bf16[16,48,256]{2,1,0:T(8,128)(2,1)}, u32[]{:S(2)}, u32[]{:S(2)}) async-start(bf16[16,48,256]{2,1,0:T(8,128)(2,1)} %fusion.87), calls=%async_computation.8 | async-start | bytes 786432 | tf_op jit(solution)/shard_map/all_to_all | solution.py:1024
  433.4 118.8 %reduce-scatter.5.cloned.1.call-start = ((), (), s32[]{:S(2)}) async-start(), calls=%async_computation.18 | async-start | bytes 11943936 | tf_op jit(solution)/shard_map/reduce_scatter | solution.py:1091
  434.9 12.4 %collective-permute-start.8 = (bf16[8,48,2304]{2,1,0:T(8,128)(2,1)}, bf16[8,48,2304]{2,1,0:T(8,128)(2,1)}, u32[]{:S(2)}, u32[]{:S(2)}) collective-permute-start(bf16[8,48,2304]{2,1,0:T(8,128)(2,1)} %dynamic-slice_bitcast_fusion.1), channel_id=1, source_target_pairs={{0,1},{1,0},{2,3},{3,2},{4,5},{5,4},{6,7},{7,6},{8,9},{9,8},{10,11... | collective-permute-start | bytes 5308424 | tf_op jit(solution)/shard_map/ppermute | solution.py:932
  451.8 46.1 %collective-permute-start.10 = (bf16[256,768]{1,0:T(8,128)(2,1)S(1)}, bf16[256,768]{1,0:T(8,128)(2,1)S(1)}, u32[]{:S(2)}, u32[]{:S(2)}) collective-permute-start(bf16[256,768]{1,0:T(8,128)(2,1)S(1)} %copy-done.7), channel_id=1, source_target_pairs={{16,24},{17,25},{18,26},{19,27},{20,28},{21,29},{22,30},{23,31},{2... | collective-permute-start | bytes 1179656 | tf_op jit(solution)/shard_map/ppermute | solution.py:1027
  452.5 45.5 %collective-permute-start.9 = (bf16[256,768]{1,0:T(8,128)(2,1)S(1)}, bf16[256,768]{1,0:T(8,128)(2,1)}, u32[]{:S(2)}, u32[]{:S(2)}) collective-permute-start(bf16[256,768]{1,0:T(8,128)(2,1)S(1)} %copy-done.7), channel_id=1, source_target_pairs={{0,16},{1,17},{2,18},{3,19},{4,20},{5,21},{6,22},{7,23},{8,24},{9,... | collective-permute-start | bytes 1179656 | tf_op jit(solution)/shard_map/ppermute | solution.py:1027
  460.0 38.0 %all-to-all-start.10 = ((bf16[4,4,48,1152]{3,2,1,0:T(8,128)(2,1)}), bf16[4,4,48,1152]{3,2,1,0:T(8,128)(2,1)S(1)}, u32[]{:S(2)}, u32[]{:S(2)}) async-start(bf16[4,4,48,1152]{3,2,1,0:T(8,128)(2,1)} %pad_maximum_fusion.5), calls=%async_computation.11 | async-start | bytes 3538944 | tf_op jit(solution)/shard_map/all_to_all | solution.py:966
  465.5 31.5 %collective-permute-start.11 = (bf16[2,24,6912]{2,1,0:T(8,128)(2,1)S(1)}, bf16[2,24,6912]{2,1,0:T(8,128)(2,1)S(1)}, u32[]{:S(2)}, u32[]{:S(2)}) collective-permute-start(bf16[2,24,6912]{2,1,0:T(8,128)(2,1)S(1)} %dynamic-slice_bitcast_fusion.3), channel_id=1, source_target_pairs={{0,8},{1,9},{2,10},{3,11},{4,12},{5,13},{6,14},{7,15},{8,0},{9,1},... | collective-permute-start | bytes 1990664 | tf_op jit(solution)/shard_map/ppermute | solution.py:932
  466.7 30.2 %copy-start.34 = (bf16[96,6912]{1,0:T(8,128)(2,1)S(1)}, bf16[96,6912]{1,0:T(8,128)(2,1)}, u32[]{:S(2)}) copy-start(bf16[96,6912]{1,0:T(8,128)(2,1)} %reduce-scatter.3.cloned.1.call-done) | copy-start | bytes 3981316
  495.2 13.7 %copy-start.11 = (bf16[256,768]{1,0:T(8,128)(2,1)S(1)}, bf16[256,768]{1,0:T(8,128)(2,1)}, u32[]{:S(2)}) copy-start(bf16[256,768]{1,0:T(8,128)(2,1)} %copy-done.10) | copy-start | bytes 1179652
  495.2 13.7 %copy-start.42 = (bf16[256,768]{1,0:T(8,128)(2,1)S(1)}, bf16[256,768]{1,0:T(8,128)(2,1)}, u32[]{:S(2)}) copy-start(bf16[256,768]{1,0:T(8,128)(2,1)} %copy-done.41) | copy-start | bytes 1179652
  498.7 29.1 %all-to-all-start.9 = ((bf16[16,144,256]{2,1,0:T(8,128)(2,1)}), bf16[16,144,256]{2,1,0:T(8,128)(2,1)}, u32[]{:S(2)}, u32[]{:S(2)}) async-start(bf16[16,144,256]{2,1,0:T(8,128)(2,1)} %attend_back.3), calls=%async_computation.10 | async-start | bytes 2359296 | tf_op jit(solution)/shard_map/all_to_all | solution.py:1024
  515.2 12.6 %copy-start.73 = (s32[16,256]{1,0:T(8,128)S(1)}, s32[16,256]{1,0:T(8,128)}, u32[]{:S(2)}) copy-start(s32[16,256]{1,0:T(8,128)} %constant.167.clone) | copy-start | bytes 49156
  532.6 11.4 %collective-permute-start.12 = (bf16[8,48,2304]{2,1,0:T(8,128)(2,1)S(1)}, bf16[8,48,2304]{2,1,0:T(8,128)(2,1)S(1)}, u32[]{:S(2)}, u32[]{:S(2)}) collective-permute-start(bf16[8,48,2304]{2,1,0:T(8,128)(2,1)S(1)} %dynamic-slice_bitcast_fusion), channel_id=1, source_target_pairs={{0,1},{1,0},{2,3},{3,2},{4,5},{5,4},{6,7},{7,6},{8,9},{9,8},{10,11... | collective-permute-start | bytes 5308424 | tf_op jit(solution)/shard_map/ppermute | solution.py:932
  540.2 3.8 collective-permute-start.13
  542.6 41.5 %collective-permute-start.14 = (bf16[256,768]{1,0:T(8,128)(2,1)}, bf16[256,768]{1,0:T(8,128)(2,1)}, u32[]{:S(2)}, u32[]{:S(2)}) collective-permute-start(bf16[256,768]{1,0:T(8,128)(2,1)} %get-tuple-element.200), channel_id=1, source_target_pairs={{16,8},{17,9},{18,10},{19,11},{20,12},{21,13},{22,14},{23,15},{24,... | collective-permute-start | bytes 1179656 | tf_op jit(solution)/shard_map/ppermute | solution.py:1027
  546.1 20.2 %copy-start.27 = (bf16[2,24,6912]{2,1,0:T(8,128)(2,1)S(1)}, bf16[2,24,6912]{2,1,0:T(8,128)(2,1)}, u32[]{:S(2)}) copy-start(bf16[2,24,6912]{2,1,0:T(8,128)(2,1)} %fusion.79) | copy-start | bytes 1990660
  546.1 36.9 %all-to-all-start.11 = ((bf16[4,4,48,1280]{3,2,1,0:T(8,128)(2,1)}), bf16[4,4,48,1280]{3,2,1,0:T(8,128)(2,1)S(1)}, u32[]{:S(2)}, u32[]{:S(2)}) async-start(bf16[4,4,48,1280]{3,2,1,0:T(8,128)(2,1)} %maximum_maximum_fusion), calls=%async_computation.12 | async-start | bytes 3932160 | tf_op jit(solution)/shard_map/all_to_all | solution.py:966
  554.2 37.6 %collective-permute-start.15 = (bf16[2,24,6912]{2,1,0:T(8,128)(2,1)}, bf16[2,24,6912]{2,1,0:T(8,128)(2,1)}, u32[]{:S(2)}, u32[]{:S(2)}) collective-permute-start(bf16[2,24,6912]{2,1,0:T(8,128)(2,1)} %dynamic-slice_bitcast_fusion.2), channel_id=1, source_target_pairs={{0,8},{1,9},{2,10},{3,11},{4,12},{5,13},{6,14},{7,15},{8,0},{9,1},... | collective-permute-start | bytes 1990664 | tf_op jit(solution)/shard_map/ppermute | solution.py:932
  567.1 52.6 %collective-permute-start.18 = (bf16[24,6912]{1,0:T(8,128)(2,1)}, bf16[24,6912]{1,0:T(8,128)(2,1)}, u32[]{:S(2)}, u32[]{:S(2)}) collective-permute-start(bf16[24,6912]{1,0:T(8,128)(2,1)} %dynamic-slice_bitcast_fusion.4), channel_id=1, source_target_pairs={{0,4},{1,5},{2,6},{3,7},{4,0},{5,1},{6,2},{7,3},{8,12},{9,13},{10,... | collective-permute-start | bytes 995336 | tf_op jit(solution)/shard_map/ppermute | solution.py:932
  586.4 28.2 %all-to-all-start.12 = ((bf16[4,48,2432]{2,1,0:T(8,128)(2,1)}), bf16[4,48,2432]{2,1,0:T(8,128)(2,1)S(1)}, u32[]{:S(2)}, u32[]{:S(2)}) async-start(bf16[4,48,2432]{2,1,0:T(8,128)(2,1)} %pad_maximum_fusion.6), calls=%async_computation.13 | async-start | bytes 1867776 | tf_op jit(solution)/shard_map/all_to_all | solution.py:966
  614.8 4.8 collective-permute-start.16
  618.0 9.1 %collective-permute-start.17 = (bf16[24,6912]{1,0:T(8,128)(2,1)S(1)}, bf16[24,6912]{1,0:T(8,128)(2,1)S(1)}, u32[]{:S(2)}, u32[]{:S(2)}) collective-permute-start(bf16[24,6912]{1,0:T(8,128)(2,1)S(1)} %dynamic-slice_bitcast_fusion.5), channel_id=1, source_target_pairs={{0,4},{1,5},{2,6},{3,7},{4,0},{5,1},{6,2},{7,3},{8,12},{9,13},{10,... | collective-permute-start | bytes 995336 | tf_op jit(solution)/shard_map/ppermute | solution.py:932
  628.3 8.2 %collective-permute-start.19 = (bf16[24,6912]{1,0:T(8,128)(2,1)S(1)}, bf16[24,6912]{1,0:T(8,128)(2,1)S(1)}, u32[]{:S(2)}, u32[]{:S(2)}) collective-permute-start(bf16[24,6912]{1,0:T(8,128)(2,1)S(1)} %get-tuple-element.196), channel_id=1, source_target_pairs={{0,16},{16,0},{1,17},{17,1},{2,18},{18,2},{3,19},{19,3},{4,20},{20... | collective-permute-start | bytes 995336 | tf_op jit(solution)/shard_map/ppermute | solution.py:936
  (89 other events, 239.8 us)
Sparse Core Ops, SparseCore 0:
  41.0 129.4 all-gather.2
  174.0 106.5 all-gather.4
  337.8 95.5 reduce-scatter.2
  451.0 101.1 reduce-scatter.4
